TPU v7x, 32 devices: a whole 2x2x4 slice. The times are simulated.
32 devices in a mesh: dp: 32 (over z, y, x, core).
Axes of the slice: x: 2, y: 2, z: 4, core: 2. Of those that a mesh axis runs over, the one named last changes fastest.
Arguments:
- tokens: bfloat16 [4096, 1024], P('dp'), may hold values from -6 to 6
- lengths: int32 [128], P('dp'), may hold values from 0 to 128, as said below
- in_weight: bfloat16 [1024, 4384], P('dp'), may hold values from -0.1875 to 0.1875
- out_weight: bfloat16 [2048, 1024], P('dp'), may hold values from -0.125 to 0.125
- conv_weight: float32 [4, 2304], replicated, may hold values from -3 to 3
- conv_bias: float32 [2304], replicated, may hold values from -1.5 to 1.5
- dt_bias: float32 [32], replicated, may hold values from -5 to -1
- a_log: float32 [32], replicated, may hold values from 0 to 2.77
- skip_gain: float32 [32], replicated, may hold values from 0.5 to 1.5
- norm_gain: float32 [2048], replicated, may hold values from 0.25 to 1.75
- pre_gain: float32 [1024], replicated, may hold values from 0.25 to 1.75
- cotangent: bfloat16 [4096, 1024], P('dp'), may hold values from -6 to 6
Outputs:
- mixed: bfloat16 [4096, 1024], P('dp')
- tokens_grad: float32 [4096, 1024], P('dp')
- in_weight_grad: float32 [1024, 4384], P('dp')
- out_weight_grad: float32 [2048, 1024], P('dp')
- conv_weight_grad: float32 [4, 2304], replicated
- conv_bias_grad: float32 [2304], replicated
- dt_bias_grad: float32 [32], replicated
- a_log_grad: float32 [32], replicated
- skip_gain_grad: float32 [32], replicated
- norm_gain_grad: float32 [2048], replicated
- pre_gain_grad: float32 [1024], replicated
Inputs may be any that keep to these rules, and one draw needn't show every extreme that they name: Each device's 4 lengths sum to at most 128; in every draw one device holds a single sequence of exactly 128 tokens.
All inputs are finite; a program needn't handle non-finite values.
Results may differ from a plain program's by a relative error of at most 0.0092.
Values may be sent and summed in bfloat16 or wider, within the bound.
No kernel may reach another device: no remote copies, remote signals or barrier semaphores. Data moves between devices by JAX's collectives and lax.ppermute only.
A program may use at most 128 MiB of HBM per device.

v0:
```python
import jax
import jax.numpy as jnp
from jax import lax
from jax.sharding import PartitionSpec as P

SCAN_ROWS = 64


EPS = 1e-05
HIGH = lax.Precision.HIGHEST


def prenorm(hidden_in, gain_row):
    return (
        hidden_in
        * lax.rsqrt(jnp.mean(hidden_in * hidden_in, axis=-1, keepdims=True) + EPS)
        * gain_row
    )


def shifted(array, offset, filler):
    padding = jnp.full((offset,) + array.shape[1:], filler, array.dtype)
    return jnp.concatenate([padding, array[:-offset]], axis=0)


def segments(seq_lengths, row_count):
    seq_ends = jnp.cumsum(seq_lengths, dtype=jnp.int32)
    position = jnp.arange(row_count, dtype=jnp.int32)
    segment = jnp.sum(
        (position[:, None] >= seq_ends[None, :]).astype(jnp.int32), axis=1, dtype=jnp.int32
    )
    live_rows = (position < seq_ends[-1]).astype(jnp.float32)
    return (segment, live_rows)


def block_step(carry, block_item):
    state_mat, prev_segment = carry
    values, key_rows, read_rows, step_size, log_decay, block_segment = block_item
    cumulative = jnp.cumsum(log_decay, axis=0)
    position = jnp.arange(block_segment.shape[0], dtype=jnp.int32)
    causal = (block_segment[:, None] == block_segment[None, :]) & (
        position[:, None] >= position[None, :]
    )
    distance = cumulative[:, None, :] - cumulative[None, :, :]
    decay_mask = jnp.where(
        causal[:, :, None], jnp.exp(jnp.where(causal[:, :, None], distance, 0.0)), 0.0
    )
    scores = jnp.dot(read_rows, key_rows.T, precision=HIGH)
    weighting = scores[:, :, None] * decay_mask * step_size[None, :, :]
    inside = jnp.einsum("ijh,jhp->ihp", weighting, values, precision=HIGH)
    entering = (block_segment == prev_segment).astype(jnp.float32)
    carried = jnp.einsum("in,hnp->ihp", read_rows, state_mat, precision=HIGH)
    carried = carried * (jnp.exp(cumulative) * entering[:, None])[:, :, None]
    last_same = (block_segment == block_segment[-1]).astype(jnp.float32)
    tail_weight = jnp.exp(cumulative[-1][None, :] - cumulative) * last_same[:, None] * step_size
    new_state = state_mat * (jnp.exp(cumulative[-1]) * entering[-1])[:, None, None]
    new_state = new_state + jnp.einsum(
        "jn,jh,jhp->hnp", key_rows, tail_weight, values, precision=HIGH
    )
    return ((new_state, block_segment[-1]), inside + carried)


def mixer_core(projected, conv_weight, conv_bias, dt_bias, a_log, skip_gain, norm_gain, segment):
    inner_width = norm_gain.shape[0]
    head_count = dt_bias.shape[0]
    conv_width = conv_bias.shape[0]
    state_width = (conv_width - inner_width) // 2
    head_size = inner_width // head_count
    row_count = projected.shape[0]
    gate_in = projected[:, :inner_width]
    conv_src = projected[:, inner_width : inner_width + conv_width]
    dt_raw = projected[:, inner_width + conv_width :]
    conv_sum = conv_bias[None, :] + conv_weight[0][None, :] * conv_src
    for offset in range(1, conv_weight.shape[0]):
        same_rows = (segment == shifted(segment, offset, -1)).astype(jnp.float32)
        conv_sum = (
            conv_sum
            + conv_weight[offset][None, :] * shifted(conv_src, offset, 0.0) * same_rows[:, None]
        )
    activated = jax.nn.silu(conv_sum)
    values = activated[:, :inner_width].reshape(row_count, head_count, head_size)
    key_rows = activated[:, inner_width : inner_width + state_width]
    read_rows = activated[:, inner_width + state_width :]
    step_size = jax.nn.softplus(dt_raw + dt_bias[None, :])
    log_decay = -step_size * jnp.exp(a_log)[None, :]
    blocks = row_count // SCAN_ROWS
    items = (
        values.reshape(blocks, SCAN_ROWS, head_count, head_size),
        key_rows.reshape(blocks, SCAN_ROWS, state_width),
        read_rows.reshape(blocks, SCAN_ROWS, state_width),
        step_size.reshape(blocks, SCAN_ROWS, head_count),
        log_decay.reshape(blocks, SCAN_ROWS, head_count),
        segment.reshape(blocks, SCAN_ROWS),
    )
    start = (jnp.zeros((head_count, state_width, head_size), jnp.float32), jnp.array(-1, jnp.int32))
    _, scanned = lax.scan(jax.checkpoint(block_step), start, items)
    scan_out = scanned.reshape(row_count, inner_width) + (
        skip_gain[None, :, None] * values
    ).reshape(row_count, inner_width)
    gated_out = scan_out * jax.nn.silu(gate_in)
    return (
        gated_out
        * lax.rsqrt(jnp.mean(gated_out * gated_out, axis=-1, keepdims=True) + EPS)
        * norm_gain[None, :]
    )


def shards(
    tokens,
    lengths,
    in_weight,
    out_weight,
    conv_weight,
    conv_bias,
    dt_bias,
    a_log,
    skip_gain,
    norm_gain,
    pre_gain,
    cotangent,
):
    w_in, w_out = (
        lax.all_gather(in_weight, "dp", axis=0, tiled=True),
        lax.all_gather(out_weight, "dp", axis=0, tiled=True),
    )
    segment, live_rows = segments(lengths, tokens.shape[0])
    hidden_in = tokens.astype(jnp.float32)
    normed, norm_back = jax.vjp(prenorm, hidden_in, pre_gain)
    normed_low = normed.astype(jnp.bfloat16)
    projected = jnp.dot(normed_low, w_in, preferred_element_type=jnp.float32)
    proj_width = projected.shape[1]

    def mixer_local(proj_rows, conv_w, conv_b, bias_dt, decay_log, skip_w, gain_w):
        return mixer_core(proj_rows, conv_w, conv_b, bias_dt, decay_log, skip_w, gain_w, segment)

    gated_norm, mixer_back = jax.vjp(
        mixer_local, projected, conv_weight, conv_bias, dt_bias, a_log, skip_gain, norm_gain
    )
    gated_low = gated_norm.astype(jnp.bfloat16)
    branch = jnp.dot(gated_low, w_out, preferred_element_type=jnp.float32)
    mixed = (live_rows[:, None] * (hidden_in + branch)).astype(jnp.bfloat16)
    w_in, w_out = (
        lax.all_gather(in_weight, "dp", axis=0, tiled=True),
        lax.all_gather(out_weight, "dp", axis=0, tiled=True),
    )
    out_cot = cotangent.astype(jnp.float32) * live_rows[:, None]
    out_cot_low = out_cot.astype(jnp.bfloat16)
    norm_cot = lax.dot_general(
        out_cot_low, w_out, (((1,), (1,)), ((), ())), preferred_element_type=jnp.float32
    )
    proj_cot, conv_w_grad, conv_b_grad, bias_dt_grad, decay_grad, skip_grad, gain_grad = mixer_back(
        norm_cot
    )
    proj_cot_low = proj_cot.astype(jnp.bfloat16)
    normed_cot = lax.dot_general(
        proj_cot_low, w_in, (((1,), (1,)), ((), ())), preferred_element_type=jnp.float32
    )
    hidden_cot, pre_grad = norm_back(normed_cot)
    tokens_grad = out_cot + hidden_cot
    out_grad = lax.dot_general(
        gated_low, out_cot_low, (((0,), (0,)), ((), ())), preferred_element_type=jnp.float32
    )
    in_grad = lax.dot_general(
        normed_low, proj_cot_low, (((0,), (0,)), ((), ())), preferred_element_type=jnp.float32
    )
    in_wide = in_grad.reshape(2 * in_grad.shape[0], proj_width // 2)
    in_folded, out_shard = (
        lax.psum_scatter(in_wide, "dp", scatter_dimension=0, tiled=True),
        lax.psum_scatter(out_grad, "dp", scatter_dimension=0, tiled=True),
    )
    in_shard = in_folded.reshape(in_weight.shape[0], proj_width)
    summed = lax.psum(
        (conv_w_grad, conv_b_grad, bias_dt_grad, decay_grad, skip_grad, gain_grad, pre_grad), "dp"
    )
    return (
        mixed,
        tokens_grad,
        in_shard,
        out_shard,
        summed[0],
        summed[1],
        summed[2],
        summed[3],
        summed[4],
        summed[5],
        summed[6],
    )


def solution(mesh):
    return jax.shard_map(
        shards,
        mesh=mesh,
        in_specs=(
            P("dp", None),
            P("dp"),
            P("dp", None),
            P("dp", None),
            P(),
            P(),
            P(),
            P(),
            P(),
            P(),
            P(),
            P("dp", None),
        ),
        out_specs=(
            P("dp", None),
            P("dp", None),
            P("dp", None),
            P("dp", None),
            P(),
            P(),
            P(),
            P(),
            P(),
            P(),
            P(),
        ),
        check_vma=False,
    )
```

profile of v0, /device:TPU:0, one launch (start us, length us, event | category | flops | bytes accessed | tf_op | source)
XLA Modules:
  0.0 771.9 jit_solution(6335574929122777526)
XLA Ops:
  15.3 78.9 %all-gather.3.cloned.1.call-done = bf16[1024,4384]{1,0:T(8,128)(2,1)} async-done(((bf16[32,4384]{1,0:T(8,128)(2,1)}), bf16[1024,4384]{1,0:T(8,128)(2,1)}) %all-gather.3.cloned.1.call-update) | async-done | bytes 8978448 | tf_op jit(solution)/shard_map/all_gather | solution.py:123
  94.2 7.4 fusion.96
  106.8 5.5 fusion.76
  113.5 2.5 reshape.402
  116.0 2.3 broadcast.280.clone3
  118.3 82.8 %while.46 = (s32[]{:T(128)}, f32[32,128,64]{1,2,0:T(8,128)S(1)}, s32[]{:T(128)}, f32[2,64,32,64]{1,0,3,2:T(2,128)}, f32[2,32,128,64]{2,3,1,0:T(8,128)}, /*index=...) while((s32[]{:T(128)}, f32[32,128,64]{1,2,0:T(8,128)S(1)}, ...), condition=%wide.region_5.6_spmd.clone, body=%wide.region_3.5_spmd.clone.sunk | while | flops 512117024 | bytes 11374957 | solution.py:96
  118.3 1.4 dynamic_update_slice.90
  125.1 2.7 constant_dynamic-slice_fusion.9
  127.9 2.1 convolution_bitcast_fusion.10
  130.9 25.5 %dynamic_update_slice.89 = f32[2,64,32,64]{1,0,3,2:T(2,128)} dynamic-update-slice(f32[2,64,32,64]{1,0,3,2:T(2,128)} %get-tuple-element.1076, f32[1,64,32,64]{1,0,3,2:T(1,128)S(1)} %bitcast.292, s32[]{:T(128)S(6)} %copy.261, s32[]{:T(128)} %constant.134.clone.1..sunk, s32[]{:T(128)} %constant.134.clone.1..sunk, s32[]{:T(128)} %constant.134.clone.1..sunk) | dynamic-update-slice | bytes 1048580 | tf_op jit(solution)/shard_map/jvp()/while/body/jit(dynamic_update_index_in_dim)/dynamic_update_slice | solution.py:96
  157.5 1.5 fusion.173
  159.8 1.4 dynamic_update_slice.90
  166.6 2.7 constant_dynamic-slice_fusion.9
  169.3 2.1 convolution_bitcast_fusion.10
  172.4 25.4 %dynamic_update_slice.89 = f32[2,64,32,64]{1,0,3,2:T(2,128)} dynamic-update-slice(f32[2,64,32,64]{1,0,3,2:T(2,128)} %get-tuple-element.1076, f32[1,64,32,64]{1,0,3,2:T(1,128)S(1)} %bitcast.292, s32[]{:T(128)S(6)} %copy.261, s32[]{:T(128)} %constant.134.clone.1..sunk, s32[]{:T(128)} %constant.134.clone.1..sunk, s32[]{:T(128)} %constant.134.clone.1..sunk) | dynamic-update-slice | bytes 1048580 | tf_op jit(solution)/shard_map/jvp()/while/body/jit(dynamic_update_index_in_dim)/dynamic_update_slice | solution.py:96
  198.9 1.5 fusion.173
  201.1 3.5 reshape.405
  204.6 2.0 multiply_reduce_fusion.12
  206.7 4.6 multiply_reduce_fusion.9
  211.4 2.7 multiply_reduce_fusion.10
  214.1 3.3 reshape.406
  219.9 2.3 broadcast.280.clone2
  222.3 142.2 %while.47 = (s32[]{:T(128)}, f32[32,128,64]{1,2,0:T(8,128)S(1)}, f32[2,64,32,64]{1,0,3,2:T(2,128)}, f32[2,64,128]{2,1,0:T(8,128)}, f32[2,64,128]{2,1,0:T(8,128)}...) while((s32[]{:T(128)}, f32[32,128,64]{1,2,0:T(8,128)S(1)}, ...), condition=%wide.region_18.19_spmd.clone, body=%wide.region_8.18_spmd.clone.sunk | while | flops 1232269568 | bytes 42039492 | solution.py:96
  229.1 1.9 copy.236
  239.1 4.3 fusion.197
  243.4 1.4 copy.239
  246.2 5.3 multiply_reduce_fusion.19
  251.7 1.5 add_bitcast_fusion.2
  254.0 1.9 convolution_bitcast_fusion.12
  256.8 2.6 convolution_bitcast_fusion.11
  259.4 4.1 fusion.200
  263.5 1.9 fusion.199
  268.0 25.5 %dynamic_update_slice.94 = f32[2,64,32,64]{1,0,3,2:T(2,128)} dynamic-update-slice(f32[2,64,32,64]{1,0,3,2:T(2,128)} %get-tuple-element.1124, f32[1,64,32,64]{1,0,3,2:T(1,128)S(1)} %copy.245, s32[]{:T(128)S(6)} %sub.249, s32[]{:T(128)} %constant.134.clone.1..sunk.1, s32[]{:T(128)} %constant.134.clone.1..sunk.1, s32[]{:T(128)} %constant.134.clone.1..sunk.1) | dynamic-update-slice | bytes 1048580 | tf_op jit(solution)/shard_map/transpose(jvp())/while/body/jit(dynamic_update_index_in_dim)/dynamic_update_slice | solution.py:96
  299.9 1.9 copy.236
  309.9 4.3 fusion.197
  314.2 1.4 copy.239
  317.0 5.3 multiply_reduce_fusion.19
  322.5 1.5 add_bitcast_fusion.2
  324.8 1.9 convolution_bitcast_fusion.12
  327.6 2.6 convolution_bitcast_fusion.11
  330.2 4.1 fusion.200
  334.3 1.9 fusion.199
  338.8 25.5 %dynamic_update_slice.94 = f32[2,64,32,64]{1,0,3,2:T(2,128)} dynamic-update-slice(f32[2,64,32,64]{1,0,3,2:T(2,128)} %get-tuple-element.1124, f32[1,64,32,64]{1,0,3,2:T(1,128)S(1)} %copy.245, s32[]{:T(128)S(6)} %sub.249, s32[]{:T(128)} %constant.134.clone.1..sunk.1, s32[]{:T(128)} %constant.134.clone.1..sunk.1, s32[]{:T(128)} %constant.134.clone.1..sunk.1) | dynamic-update-slice | bytes 1048580 | tf_op jit(solution)/shard_map/transpose(jvp())/while/body/jit(dynamic_update_index_in_dim)/dynamic_update_slice | solution.py:96
  368.2 2.7 reshape.411
  372.5 1.4 multiply_reduce_fusion.8
  374.1 1.9 multiply_reduce_fusion.7
  379.9 1.6 fusion.104
  381.5 7.7 fusion.94
  389.2 20.2 %reshape.412 = f32[2048,2192]{1,0:T(8,128)} reshape(f32[1024,4384]{1,0:T(8,128)} %fusion.94) | data formatting | bytes 35913728 | tf_op jit(solution)/shard_map/reshape | solution.py:166
  410.7 5.8 fusion.90
  416.4 1.4 reduce_sum.336
  417.8 1.3 reshape.414
  419.1 1.3 reshape.415
  420.4 1.3 reshape.416
  421.7 1.3 reshape.417
  423.1 1.4 reduce_sum.337
  425.6 1.4 pad_add_fusion
  427.1 8.8 %fusion.83 = (f32[1024]{0:T(1024)}, f32[128]{0:T(128)}, f32[128,1024]{1,0:T(8,128)}) fusion(bf16[128,1024]{1,0:T(8,128)(2,1)S(1)} %copy-done.18, f32[128]{0:T(128)} %copy-done.56, f32[1024]{0:T(1024)S(1)} %copy-done.37, bf16[1024,4384]{1,0:T(8,128)(2,1)} %all-gather.3.cloned.1.call-done, f32[128,2048]{0,1:T(8,128)S(1)} %copy-done.20, ...), kind=kOutput, calls=%fused_computation.163 | convolution fusion | flops 1151839104 | bytes 12018688 | tf_op jit(solution)/shard_map/dot_general | solution.py:155
  435.8 40.9 %all-reduce.20 = (f32[4,2304]{1,0:T(4,128)}, f32[2304]{0:T(1024)}, f32[32]{0:T(128)}, f32[32]{0:T(128)}, f32[32]{0:T(128)}, /*index=5*/f32[2048]{0:T(1024)}, f32[1024]{0:T(1024)}) all-reduce(f32[4,2304]{1,0:T(4,128)} %pad_add_fusion, f32[2304]{0:T(1024)} %get-tuple-element.712, ...), channel_id=1, replica_groups=mesh['dp'=32] {'dp'}, use_global_device_ids=true, to_apply=%region_26.27 | all-reduce | flops 14688 | bytes 117504 | tf_op jit(solution)/shard_map/psum | solution.py:172
  477.4 2.1 fusion.84
  479.5 4.2 fusion.73
  483.7 131.1 %reduce-scatter.3.cloned.1.call-done = f32[64,2192]{1,0:T(8,128)} async-done(((f32[2048,2192]{1,0:T(8,128)}), f32[64,2192]{1,0:T(8,128)}) %reduce-scatter.3.cloned.1.call-update) | async-done | bytes 561168 | tf_op jit(solution)/shard_map/reduce_scatter | solution.py:168
  614.8 2.0 reshape.413
  616.9 148.3 %reduce-scatter.5.cloned.1.call-done = f32[64,1024]{1,0:T(8,128)} async-done(((f32[2048,1024]{1,0:T(8,128)}), f32[64,1024]{1,0:T(8,128)}) %reduce-scatter.5.cloned.1.call-update) | async-done | bytes 262160 | tf_op jit(solution)/shard_map/reduce_scatter | solution.py:169
  (330 shorter events, 84.6 us)
Async XLA Ops:
  7.2 87.0 %all-gather.3.cloned.1.call-start = ((), (), s32[]{:S(2)}) async-start(), calls=%async_computation.2 | async-start | bytes 9461760 | tf_op jit(solution)/shard_map/all_gather | solution.py:123
  7.9 198.7 %all-gather.5.cloned.1.call-start = ((), (), s32[]{:S(2)}) async-start(), calls=%async_computation.3 | async-start | bytes 4325376 | tf_op jit(solution)/shard_map/all_gather | solution.py:124
  8.7 606.2 %reduce-scatter.3.cloned.1.call-start = ((), (), s32[]{:S(2)}) async-start(), calls=%async_computation.4 | async-start | bytes 19464192 | tf_op jit(solution)/shard_map/reduce_scatter | solution.py:168
  10.8 195.8 %copy-start.54 = (f32[128]{0:T(128)}, f32[128]{0:T(128)S(1)}, u32[]{:S(2)}) copy-start(f32[128]{0:T(128)S(1)} %compare_convert_fusion.7) | copy-start | bytes 1540
  11.6 93.6 %copy-start.66 = (f32[32]{0:T(128)}, f32[32]{0:T(128)S(1)}, u32[]{:S(2)}) copy-start(f32[32]{0:T(128)S(1)} %exp.108) | copy-start | bytes 388
  12.7 89.0 %copy-start.68 = (f32[128]{0:T(128)}, f32[128]{0:T(128)S(1)}, u32[]{:S(2)}) copy-start(f32[128]{0:T(128)S(1)} %fusion.85) | copy-start | bytes 1540
  14.1 197.2 %copy-start.38 = (f32[2048]{0:T(1024)}, f32[2048]{0:T(1024)S(1)}, u32[]{:S(2)}) copy-start(f32[2048]{0:T(1024)S(1)} %mul.796) | copy-start | bytes 24580
  15.1 91.6 %copy-start.40 = (f32[2304]{0:T(1024)}, f32[2304]{0:T(1024)S(1)}, u32[]{:S(2)}) copy-start(f32[2304]{0:T(1024)S(1)} %get-tuple-element.716) | copy-start | bytes 27652
  15.1 91.6 %copy-start.42 = (f32[2304]{0:T(1024)}, f32[2304]{0:T(1024)S(1)}, u32[]{:S(2)}) copy-start(f32[2304]{0:T(1024)S(1)} %get-tuple-element.718) | copy-start | bytes 27652
  15.1 91.6 %copy-start.44 = (f32[2304]{0:T(1024)}, f32[2304]{0:T(1024)S(1)}, u32[]{:S(2)}) copy-start(f32[2304]{0:T(1024)S(1)} %get-tuple-element.717) | copy-start | bytes 27652
  15.2 91.6 %copy-start.46 = (f32[2304]{0:T(1024)}, f32[2304]{0:T(1024)S(1)}, u32[]{:S(2)}) copy-start(f32[2304]{0:T(1024)S(1)} %get-tuple-element.719) | copy-start | bytes 27652
  15.2 91.5 %copy-start.58 = (f32[128]{0:T(128)}, f32[128]{0:T(128)S(1)}, u32[]{:S(2)}) copy-start(f32[128]{0:T(128)S(1)} %get-tuple-element.823) | copy-start | bytes 1540
  15.2 91.5 %copy-start.60 = (f32[128]{0:T(128)}, f32[128]{0:T(128)S(1)}, u32[]{:S(2)}) copy-start(f32[128]{0:T(128)S(1)} %get-tuple-element.825) | copy-start | bytes 1540
  15.3 91.5 %copy-start.62 = (f32[128]{0:T(128)}, f32[128]{0:T(128)S(1)}, u32[]{:S(2)}) copy-start(f32[128]{0:T(128)S(1)} %get-tuple-element.824) | copy-start | bytes 1540
  15.3 86.4 %copy-start.56 = (f32[128]{0:T(128)}, f32[128]{0:T(128)S(1)}, u32[]{:S(2)}) copy-start(f32[128]{0:T(128)S(1)} %fusion.101) | copy-start | bytes 1540
  101.7 5.1 copy-start.3
  104.0 2.8 copy-start.53
  105.2 7.0 copy-start.35
  201.1 3.5 copy-start.4
  204.6 2.0 copy-start.27
  206.6 4.8 copy-start.6
  206.6 4.8 copy-start.50
  206.7 4.7 copy-start.12
  206.7 4.7 copy-start.17
  217.4 4.9 copy-start.8
  224.6 1.8 copy-start.10
  234.6 4.3 copy-start.49
  234.6 17.0 %copy-start.31 = (f32[64]{0:T(128)}, f32[64]{0:T(128)S(1)}, u32[]{:S(2)}) copy-start(f32[64]{0:T(128)S(1)} %get-tuple-element.1047) | copy-start | bytes 772 | tf_op jit(solution)/shard_map/transpose(jvp())/while
  237.6 14.0 %copy-start.33 = (f32[32]{0:T(128)}, f32[32]{0:T(128)S(1)}, u32[]{:S(2)}) copy-start(f32[32]{0:T(128)S(1)} %get-tuple-element.1046) | copy-start | bytes 388 | tf_op jit(solution)/shard_map/transpose(jvp())/while
  237.8 5.6 copy-start.25
  253.2 3.5 copy-start.21
  254.0 1.9 copy-start.23
  255.9 3.4 copy-start
  259.3 4.1 copy-start.52
  263.5 2.0 copy-start.24
  263.5 2.8 copy-start.1
  265.4 1.8 copy-start.22
  265.4 1.9 copy-start.32
  265.4 1.9 copy-start.34
  267.0 26.5 %copy-start.9 = (f32[32,128,64]{1,2,0:T(8,128)S(1)}, f32[32,128,64]{1,2,0:T(8,128)}, u32[]{:S(2)}) copy-start(f32[32,128,64]{1,2,0:T(8,128)} %fusion.199) | copy-start | bytes 3145732 | tf_op jit(solution)/shard_map/transpose(jvp())/while
  268.0 25.5 %copy-start.30 = (f32[2,64,32]{2,1,0:T(8,128)}, f32[2,64,32]{2,1,0:T(8,128)S(1)}, u32[]{:S(2)}) copy-start(f32[2,64,32]{2,1,0:T(8,128)S(1)} %get-tuple-element.1147) | copy-start | bytes 49156 | tf_op jit(solution)/shard_map/transpose(jvp())/while
  295.4 1.8 copy-start.10
  305.4 4.3 copy-start.49
  305.4 17.0 %copy-start.31 = (f32[64]{0:T(128)}, f32[64]{0:T(128)S(1)}, u32[]{:S(2)}) copy-start(f32[64]{0:T(128)S(1)} %get-tuple-element.1047) | copy-start | bytes 772 | tf_op jit(solution)/shard_map/transpose(jvp())/while
  308.4 14.0 %copy-start.33 = (f32[32]{0:T(128)}, f32[32]{0:T(128)S(1)}, u32[]{:S(2)}) copy-start(f32[32]{0:T(128)S(1)} %get-tuple-element.1046) | copy-start | bytes 388 | tf_op jit(solution)/shard_map/transpose(jvp())/while
  308.6 5.6 copy-start.25
  324.0 3.5 copy-start.21
  324.8 1.9 copy-start.23
  326.7 3.4 copy-start
  330.2 4.1 copy-start.52
  334.3 2.0 copy-start.24
  334.3 2.8 copy-start.1
  336.3 1.8 copy-start.22
  336.3 1.9 copy-start.32
  336.3 1.9 copy-start.34
  337.8 26.5 %copy-start.9 = (f32[32,128,64]{1,2,0:T(8,128)S(1)}, f32[32,128,64]{1,2,0:T(8,128)}, u32[]{:S(2)}) copy-start(f32[32,128,64]{1,2,0:T(8,128)} %fusion.199) | copy-start | bytes 3145732 | tf_op jit(solution)/shard_map/transpose(jvp())/while
  338.8 25.5 %copy-start.30 = (f32[2,64,32]{2,1,0:T(8,128)}, f32[2,64,32]{2,1,0:T(8,128)S(1)}, u32[]{:S(2)}) copy-start(f32[2,64,32]{2,1,0:T(8,128)S(1)} %get-tuple-element.1147) | copy-start | bytes 49156 | tf_op jit(solution)/shard_map/transpose(jvp())/while
  368.1 2.7 copy-start.16
  368.2 2.7 copy-start.39
  374.1 1.9 copy-start.47
  377.5 2.3 copy-start.41
  379.8 1.7 copy-start.20
  409.5 355.7 %reduce-scatter.5.cloned.1.call-start = ((), (), s32[]{:S(2)}) async-start(), calls=%async_computation.5 | async-start | bytes 8650752 | tf_op jit(solution)/shard_map/reduce_scatter | solution.py:169
  435.8 43.7 %copy-start.55 = (f32[128]{0:T(128)S(1)}, f32[128]{0:T(128)}, u32[]{:S(2)}) copy-start(f32[128]{0:T(128)} %copy-done.54) | copy-start | bytes 1540
  (28 other events, 39.4 us)
Sparse Core Ops, SparseCore 0:
  10.9 83.3 all-gather.2
  97.1 60.6 all-gather.4
  409.6 205.2 reduce-scatter.2
  617.6 147.5 reduce-scatter.4
where the time goes:
time: 786 us; the launch traced here: 772 us
  waiting for transfers between devices  360 us (46%)
  local copies, waits for them, and re-layouts  210 us (27%)
  matrix products  94 us (12%)
  other arithmetic  49.7 us (6%)
  blocking collectives  40.9 us (5%)
  between operations  14.5 us (2%)
    reduce_scatter x1, waiting for transfers between devices, shards(): lax.psum_scatter(out_grad, 'dp', scatter_dimension=0, tiled=True)  148 us
    reduce_scatter x1, waiting for transfers between devices, shards(): lax.psum_scatter(in_wide, 'dp', scatter_dimension=0, tiled=True)  131 us
    dynamic_update_slice x8, local copies, waits for them, and re-layouts, mixer_core(): _, scanned = lax.scan(jax.checkpoint(block_step), start, items)  106 us
    all_gather x1, waiting for transfers between devices, shards(): lax.all_gather(in_weight, 'dp', axis=0, tiled=True)  78.9 us
    psum x1, blocking collectives, shards(): lax.psum((conv_w_grad, conv_b_grad, bias_dt_grad, decay_grad, skip_grad,...  40.9 us
    dot_general x6, matrix products, block_step(): inside = jnp.einsum('ijh,jhp->ihp', weighting, values, precision=HIGH)  21 us
    reshape x1, local copies, waits for them, and re-layouts, shards(): in_wide = in_grad.reshape(2 * in_grad.shape[0], proj_width // 2)  20.2 us
    dot_general x6, matrix products, block_step(): jnp.einsum('jn,jh,jhp->hnp', key_rows, tail_weight, values, precision=HIGH)  18.8 us
  transfers between devices with their start and end apart: 4, of which 3 were waited for; matrix products, arithmetic and copies ran while one was open for 19% of the time, Pallas kernels for 0%

commit v1 on v0

--- a/solution.py
+++ b/solution.py
@@ -1,6 +1,10 @@
+import functools
+
 import jax
 import jax.numpy as jnp
 from jax import lax
+from jax.experimental import pallas as pl
+from jax.experimental.pallas import tpu as pltpu
 from jax.sharding import PartitionSpec as P
 
 SCAN_ROWS = 64
@@ -8,6 +12,772 @@
 
 EPS = 1e-05
 HIGH = lax.Precision.HIGHEST
+BF = jnp.bfloat16
+F32 = jnp.float32
+NEG = -1e30
+LANES = 128
+QUAD = 4
+WIDE1 = 896
+VMEM_BYTES = 44 * 1024 * 1024
+
+
+def mm(a, b):
+    return lax.dot_general(a, b, (((1,), (0,)), ((), ())), preferred_element_type=F32)
+
+
+def mm_t(a, b):
+    return lax.dot_general(a, b, (((1,), (1,)), ((), ())), preferred_element_type=F32)
+
+
+def mm_l(a, b):
+    return lax.dot_general(a, b, (((0,), (0,)), ((), ())), preferred_element_type=F32)
+
+
+def mm_high(a, b):
+    return lax.dot_general(
+        a, b, (((1,), (0,)), ((), ())), precision=HIGH, preferred_element_type=F32
+    )
+
+
+def call(kernel, out_shapes, inputs, scratch=(), flops=1e8, name=None):
+    in_specs = [
+        pl.BlockSpec(memory_space=pltpu.SMEM if a.dtype == jnp.int32 else pltpu.VMEM)
+        for a in inputs
+    ]
+    shapes = [jax.ShapeDtypeStruct(s, d) for s, d in out_shapes]
+    nbytes = sum(a.size * a.dtype.itemsize for a in inputs) + sum(
+        s.size * s.dtype.itemsize for s in shapes
+    )
+    return pl.pallas_call(
+        kernel,
+        out_shape=shapes,
+        in_specs=in_specs,
+        out_specs=[pl.BlockSpec(memory_space=pltpu.VMEM)] * len(shapes),
+        scratch_shapes=list(scratch),
+        cost_estimate=pl.CostEstimate(flops=int(flops), bytes_accessed=nbytes, transcendentals=0),
+        compiler_params=pltpu.CompilerParams(vmem_limit_bytes=VMEM_BYTES),
+        name=name,
+    )(*inputs)
+
+
+def iota(shape, axis):
+    return lax.broadcasted_iota(jnp.int32, shape, axis)
+
+
+def sigmoid(v):
+    return 1.0 / (1.0 + jnp.exp(-v))
+
+
+def softplus(v):
+    return jnp.maximum(v, 0.0) + jnp.log1p(jnp.exp(-jnp.abs(v)))
+
+
+def segment_of(position, ends):
+    seg = jnp.zeros(position.shape, jnp.int32)
+    for s in range(4):
+        seg = seg + (position >= ends[:, s : s + 1]).astype(jnp.int32)
+    return seg
+
+
+def same_masks(ends, rows, taps):
+    position = iota((rows, 1), 0)
+    seg = segment_of(position, ends)
+    masks = []
+    for k in range(1, taps):
+        seg_k = segment_of(position - k, ends)
+        masks.append(((seg == seg_k) & (position >= k)).astype(F32))
+    return masks
+
+
+def scan_bias(ends, rows):
+    seg_col = segment_of(iota((rows, 1), 0), ends)
+    seg_row = segment_of(iota((1, rows), 1), ends)
+    causal = (seg_col == seg_row) & (iota((rows, rows), 0) >= iota((rows, rows), 1))
+    return jnp.where(causal, 0.0, NEG)
+
+
+def tri_block(rows):
+    i, j = iota((rows, rows), 0), iota((rows, rows), 1)
+    return ((i >= j) & (i // SCAN_ROWS == j // SCAN_ROWS)).astype(F32)
+
+
+def steps_of(dt_raw, dtb, neg_rate, rows):
+    step = softplus(dt_raw + dtb)
+    log_decay = step * neg_rate
+    cum = mm_high(tri_block(rows), log_decay)
+    return step, log_decay, cum
+
+
+def decay_of(cum, cum_t, head, bias, cross):
+    dist = cum[:, head : head + 1] - cum_t[head : head + 1, :]
+    last = cum[SCAN_ROWS - 1 : SCAN_ROWS, head : head + 1]
+    return jnp.exp(dist + cross * last + bias)
+
+
+def conv_sum_of(xbc, cw, cb, masks):
+    total = cb + cw[0:1, :] * xbc
+    for k in range(1, len(masks) + 1):
+        total = total + cw[k : k + 1, :] * (pltpu.roll(xbc, k, 0) * masks[k - 1])
+    return total
+
+
+def prep_kernel(me_ref, len_ref, tok_ref, cot_ref, w_ref, tokx_ref, ocot_ref, *rest):
+    rows = tok_ref.shape[0]
+    outs1, outs2, scr1, scr2 = rest[0:4], rest[4:8], rest[8], rest[9]
+    t = me_ref[0] & (QUAD - 1)
+    inner = outs2[0].shape[1] * QUAD
+    heads = 32
+    size = inner // heads
+    own = heads // QUAD
+    lane = iota((16, tok_ref.shape[1]), 1)
+    end = jnp.int32(0)
+    tail = jnp.zeros((16, tok_ref.shape[1]), jnp.int32)
+    for s in range(4):
+        end = end + len_ref[s]
+        tail = tail + jnp.where(lane == s, end, 0)
+    tokx_ref[0:rows, :] = tok_ref[...]
+    tokx_ref[rows : rows + 16, :] = tail.astype(F32).astype(BF)
+    live = (iota((rows, 1), 0) < end).astype(F32)
+    ocot_ref[...] = (cot_ref[...].astype(F32) * live).astype(BF)
+    w = w_ref[...].astype(F32)
+    nrow = w.shape[0]
+    conv_end = w.shape[1] - heads
+    shared = w[:, 2 * inner : conv_end]
+    dts = w[:, conv_end:].astype(BF)
+    for q in range(QUAD):
+        zs, xs = [], []
+        for k in range(own):
+            at = (k * QUAD + q) * size
+            zs.append(w[:, at : at + size])
+            xs.append(w[:, inner + at : inner + at + size])
+        pick = (iota((heads, LANES), 0) == iota((heads, LANES), 1) * QUAD + q) & (
+            iota((heads, LANES), 1) < own
+        )
+        dt_own = mm(dts, pick.astype(BF))
+        scr2[q] = jnp.concatenate(zs, 1).astype(BF)
+        scr1[q] = jnp.concatenate(xs + [shared, dt_own], 1).astype(BF)
+    for r in range(QUAD):
+        outs1[r][...] = scr1[t ^ r]
+        outs2[r][...] = scr2[t ^ r]
+
+
+def join_kernel(me_ref, *refs):
+    t = me_ref[0] & (QUAD - 1)
+    out = refs[QUAD]
+    nrow = refs[0].shape[0]
+    for r in range(QUAD):
+        out[pl.ds(pl.multiple_of((t ^ r) * nrow, nrow), nrow), :] = refs[r][...]
+
+
+def project_kernel(me_ref, *refs):
+    chunks = 8
+    toks, ws = refs[0:QUAD], refs[QUAD : QUAD + chunks]
+    gain_ref, norm_ref, proj_ref, ends_ref = refs[QUAD + chunks : QUAD + chunks + 4]
+    zy = me_ref[0] // QUAD
+    rows = ends_ref.shape[1]
+    for r in range(QUAD):
+        hidden = toks[r][0:rows, :].astype(F32)
+        scale = lax.rsqrt(jnp.mean(hidden * hidden, axis=1, keepdims=True) + EPS)
+        for k in range(chunks):
+            at = pl.ds(pl.multiple_of((zy ^ k) * LANES, LANES), LANES)
+            part = toks[r][0:rows, at].astype(F32) * scale * gain_ref[:, at]
+            norm_ref[r * rows : (r + 1) * rows, k * LANES : (k + 1) * LANES] = part.astype(BF)
+        ends_ref[r : r + 1, :] = toks[r][rows : rows + 16, 0:LANES].astype(F32)[0:1, :]
+    w = jnp.concatenate([c[...] for c in ws], axis=0)
+    proj_ref[...] = mm(norm_ref[...], w)
+
+
+def scan_kernel(proj_ref, ends_ref, cw_ref, cb_ref, head_ref, out_ref):
+    rows = LANES
+    width = out_ref.shape[1]
+    own = 8
+    size = width // own
+    state = LANES
+    convw = width + 2 * state
+    dtb, rate, skip = head_ref[0:1, :], head_ref[1:2, :], head_ref[2:3, :]
+    neg_rate = -jnp.exp(rate)
+    cross = ((iota((rows, rows), 0) >= SCAN_ROWS) & (iota((rows, rows), 1) < SCAN_ROWS)).astype(F32)
+
+    def body(b, carry):
+        at = pl.ds(pl.multiple_of(b * rows, rows), rows)
+        ends = ends_ref[pl.ds(b, 1), :].astype(jnp.int32)
+        bias = scan_bias(ends, rows)
+        masks = same_masks(ends, rows, 4)
+        xbc = proj_ref[at, 0:convw]
+        conv = conv_sum_of(xbc, cw_ref[...], cb_ref[...], masks)
+        act = conv * sigmoid(conv)
+        key, read = act[:, width : width + state], act[:, width + state : convw]
+        scores = mm_t(read.astype(BF), key.astype(BF))
+        step, _, cum = steps_of(proj_ref[at, convw : convw + LANES], dtb, neg_rate, rows)
+        cum_t = cum.T
+        for h in range(own):
+            x = act[:, h * size : (h + 1) * size]
+            weight = scores * decay_of(cum, cum_t, h, bias, cross)
+            y = mm(weight.astype(BF), (x * step[:, h : h + 1]).astype(BF))
+            out_ref[at, h * size : (h + 1) * size] = y + skip[:, h : h + 1] * x
+        return carry
+
+    lax.fori_loop(0, ends_ref.shape[0], body, 0)
+
+
+def cot_kernel(me_ref, *refs):
+    chunks = 8
+    ws, cots = refs[0:chunks], refs[chunks : chunks + QUAD]
+    wfull_ref, cot_ref, dgn_ref = refs[chunks + QUAD :]
+    zy = me_ref[0] // QUAD
+    size = ws[0].shape[0]
+    rows = cots[0].shape[0]
+    for k in range(chunks):
+        wfull_ref[pl.ds(pl.multiple_of((zy ^ k) * size, size), size), :] = ws[k][...]
+    for r in range(QUAD):
+        cot_ref[r * rows : (r + 1) * rows, :] = cots[r][...]
+    dgn_ref[...] = mm_t(cot_ref[...], wfull_ref[...])
+
+
+def gate_kernel(*refs):
+    chunks = 8
+    ws = refs[0:chunks]
+    norm_ref, scan_ref, dgn_ref, gain_ref, z_ref, stat_ref = refs[chunks:]
+    w = jnp.concatenate([c[...] for c in ws], axis=0)
+    z = mm(norm_ref[...], w)
+    z_ref[...] = z
+    gated = scan_ref[...] * (z * sigmoid(z))
+    s1 = jnp.sum(gated * gated, axis=1, keepdims=True)
+    s2 = jnp.sum(gain_ref[...] * dgn_ref[...] * gated, axis=1, keepdims=True)
+    lane = iota((z.shape[0], LANES), 1)
+    both = jnp.where(lane == 0, s1, 0.0) + jnp.where(lane == 1, s2, 0.0)
+    stat_ref[...] = both.T[0:8, :]
+
+
+def ungate_kernel(inner, *refs):
+    stats = refs[0:QUAD]
+    z_ref, scan_ref, dgn_ref, gain_ref, norm_ref, gn_ref, dscan_ref, dz_ref, ngain_ref = refs[
+        QUAD : QUAD + 9
+    ]
+    outs = refs[QUAD + 9 :]
+    rows = stats[0].shape[1] // QUAD
+    total = stats[0][...]
+    for r in range(1, QUAD):
+        total = total + jnp.concatenate(
+            [stats[r][:, (b ^ r) * rows : ((b ^ r) + 1) * rows] for b in range(QUAD)], 1
+        )
+    pad = jnp.concatenate([total, jnp.zeros((LANES - 8, total.shape[1]), F32)], 0).T
+    s1, s2 = pad[:, 0:1], pad[:, 1:2]
+    r = lax.rsqrt(s1 / inner + EPS)
+    z = z_ref[...]
+    sig = sigmoid(z)
+    silu = z * sig
+    scan = scan_ref[...]
+    gain = gain_ref[...]
+    gated = scan * silu
+    unit = gated * r
+    gn_ref[...] = (unit * gain).astype(BF)
+    dgn = dgn_ref[...]
+    ngain_ref[...] = jnp.sum(dgn * unit, axis=0, keepdims=True)
+    dgated = r * (gain * dgn) - unit * (r * r * s2 / inner)
+    dscan_ref[...] = dgated * silu
+    dz = (dgated * scan * (sig * (1.0 + z * (1.0 - sig)))).astype(BF)
+    dz_ref[...] = dz
+    for k in (1, 3, 5, 7, 2, 4, 6, 0):
+        lhs = norm_ref[:, k * LANES : (k + 1) * LANES]
+        outs[k][...] = mm_l(lhs, dz).astype(BF)
+
+
+def outgrad_kernel(me_ref, gn_ref, cot_ref, *refs):
+    outs, scr = refs[0:8], refs[8]
+    zy = me_ref[0] // QUAD
+    size = outs[0].shape[0]
+    scr[...] = mm_l(gn_ref[...], cot_ref[...]).astype(BF)
+    for k in range(8):
+        outs[k][...] = scr[pl.ds(pl.multiple_of((zy ^ k) * size, size), size), :]
+
+
+def branch_kernel(gn_ref, w_ref, *outs):
+    full = mm(gn_ref[...], w_ref[...])
+    rows = outs[0].shape[0]
+    for r in range(QUAD):
+        outs[r][...] = full[r * rows : (r + 1) * rows, :].astype(outs[r].dtype)
+
+
+def scan_back_kernel(proj_ref, dscan_ref, ends_ref, cw_ref, cb_ref, head_ref, pc_ref, small_ref):
+    rows = LANES
+    width = dscan_ref.shape[1]
+    own = 8
+    size = width // own
+    state = LANES
+    convw = width + 2 * state
+    dtb, rate, skip = head_ref[0:1, :], head_ref[1:2, :], head_ref[2:3, :]
+    neg_rate = -jnp.exp(rate)
+    cross = ((iota((rows, rows), 0) >= SCAN_ROWS) & (iota((rows, rows), 1) < SCAN_ROWS)).astype(F32)
+    after = (iota((rows, rows), 1) >= iota((rows, rows), 0)).astype(F32)
+    lane = iota((rows, LANES), 1)
+    lane1 = iota((1, LANES), 1)
+    small_ref[...] = jnp.zeros(small_ref.shape, F32)
+
+    def body(b, carry):
+        at = pl.ds(pl.multiple_of(b * rows, rows), rows)
+        ends = ends_ref[pl.ds(b, 1), :].astype(jnp.int32)
+        bias = scan_bias(ends, rows)
+        masks = same_masks(ends, rows, 4)
+        xbc = proj_ref[at, 0:convw]
+        cw = cw_ref[...]
+        conv = conv_sum_of(xbc, cw, cb_ref[...], masks)
+        sig = sigmoid(conv)
+        act = conv * sig
+        key = act[:, width : width + state].astype(BF)
+        read = act[:, width + state : convw].astype(BF)
+        scores = mm_t(read, key)
+        raw = proj_ref[at, convw : convw + LANES]
+        step, log_decay, cum = steps_of(raw, dtb, neg_rate, rows)
+        cum_t = cum.T
+        dscores = jnp.zeros((rows, rows), F32)
+        row_sums = jnp.zeros((rows, LANES), F32)
+        dstep = jnp.zeros((rows, LANES), F32)
+        dskip = jnp.zeros((1, LANES), F32)
+        col_sums = []
+        dxs = []
+        for h in range(own):
+            x = act[:, h * size : (h + 1) * size]
+            s = step[:, h : h + 1]
+            decay = decay_of(cum, cum_t, h, bias, cross)
+            weight = scores * decay
+            xs = (x * s).astype(BF)
+            dy = dscan_ref[at, h * size : (h + 1) * size]
+            dyl = dy.astype(BF)
+            dweight = mm_t(dyl, xs)
+            dx_s = mm_l(weight.astype(BF), dyl)
+            dscores = dscores + dweight * decay
+            t = dweight * weight
+            row_sums = row_sums + jnp.where(lane == h, jnp.sum(t, axis=1, keepdims=True), 0.0)
+            col_sums.append(jnp.sum(t, axis=0, keepdims=True))
+            dstep = dstep + jnp.where(lane == h, jnp.sum(dx_s * x, axis=1, keepdims=True), 0.0)
+            dskip = dskip + jnp.where(lane1 == h, jnp.sum(dy * x), 0.0)
+            dxs.append(dx_s * s + skip[:, h : h + 1] * dy)
+        cols = jnp.concatenate(col_sums + [jnp.zeros((rows - own, rows), F32)], 0).T
+        dlog = mm_high(after, row_sums - cols)
+        dstep = dstep + dlog * neg_rate
+        ddt = dstep * sigmoid(raw + dtb)
+        ddt = jnp.where(lane < own, ddt, 0.0)
+        low = dscores.astype(BF)
+        dkey = mm_l(low, read)
+        dread = mm(low, key)
+        dconv = jnp.concatenate(dxs + [dkey, dread], 1) * (sig * (1.0 + conv * (1.0 - sig)))
+        dxbc = cw[0:1, :] * dconv
+        small_ref[0:1, 0:convw] += jnp.sum(dconv * xbc, axis=0, keepdims=True)
+        for k in range(1, 4):
+            masked = dconv * masks[k - 1]
+            dxbc = dxbc + cw[k : k + 1, :] * pltpu.roll(masked, rows - k, 0)
+            small_ref[k : k + 1, 0:convw] += jnp.sum(
+                masked * pltpu.roll(xbc, k, 0), axis=0, keepdims=True
+            )
+        small_ref[4:5, 0:convw] += jnp.sum(dconv, axis=0, keepdims=True)
+        small_ref[5:6, 0:LANES] += jnp.sum(ddt, axis=0, keepdims=True)
+        small_ref[6:7, 0:LANES] += jnp.where(
+            lane1 < own, jnp.sum(dlog * log_decay, axis=0, keepdims=True), 0.0
+        )
+        small_ref[7:8, 0:LANES] += dskip
+        pc_ref[at, 0:convw] = dxbc.astype(BF)
+        pc_ref[at, convw : convw + LANES] = ddt.astype(BF)
+        return carry
+
+    lax.fori_loop(0, ends_ref.shape[0], body, 0)
+
+
+def ingrad_kernel(order, norm_ref, pc_ref, *outs):
+    for n, k in enumerate(order):
+        lhs = norm_ref[:, k * LANES : (k + 1) * LANES]
+        outs[n][...] = mm_l(lhs, pc_ref[...]).astype(BF)
+
+
+def normcot_kernel(me_ref, *refs):
+    chunks = 8
+    w1, w2 = refs[0:chunks], refs[chunks : 2 * chunks]
+    pc_ref, dz_ref, small_in, ngain_ref = refs[2 * chunks : 2 * chunks + 4]
+    toks = refs[2 * chunks + 4 : 2 * chunks + 4 + QUAD]
+    outs = refs[2 * chunks + 4 + QUAD : 2 * chunks + 4 + 2 * QUAD]
+    small_ref = refs[2 * chunks + 4 + 2 * QUAD]
+    zy = me_ref[0] // QUAD
+    rows = outs[0].shape[0]
+    small_ref[...] = small_in[...]
+    small_ref[8:9, 0 : ngain_ref.shape[1]] = ngain_ref[...]
+    for k in range(chunks):
+        part = mm_t(pc_ref[...], w1[k][...]) + mm_t(dz_ref[...], w2[k][...])
+        at = pl.ds(pl.multiple_of((zy ^ k) * LANES, LANES), LANES)
+        for r in range(QUAD):
+            outs[r][:, at] = part[r * rows : (r + 1) * rows, :]
+    pre = jnp.zeros((1, outs[0].shape[1]), F32)
+    for r in range(QUAD):
+        hidden = toks[r][0:rows, :].astype(F32)
+        scale = lax.rsqrt(jnp.mean(hidden * hidden, axis=1, keepdims=True) + EPS)
+        pre = pre + jnp.sum(outs[r][...] * (hidden * scale), axis=0, keepdims=True)
+    small_ref[9:10, :] = pre
+
+
+def pair_add_kernel(a0, b0, a2, b2, o0, o2):
+    o0[...] = a0[...] + b0[...]
+    o2[...] = a2[...] + b2[...]
+
+
+def mixed_kernel(len_ref, tok_ref, a_ref, b_ref, out_ref):
+    rows = tok_ref.shape[0]
+    end = len_ref[0] + len_ref[1] + len_ref[2] + len_ref[3]
+    live = (iota((rows, 1), 0) < end).astype(F32)
+    total = tok_ref[...].astype(F32) + (a_ref[...] + b_ref[...])
+    out_ref[...] = (live * total).astype(BF)
+
+
+def tokgrad_kernel(tok_ref, cot_ref, gain_ref, a_ref, b_ref, out_ref):
+    hidden = tok_ref[...].astype(F32)
+    scale = lax.rsqrt(jnp.mean(hidden * hidden, axis=1, keepdims=True) + EPS)
+    dn = (a_ref[...] + b_ref[...]) * gain_ref[...]
+    inner = jnp.mean(dn * hidden, axis=1, keepdims=True)
+    out_ref[...] = cot_ref[...].astype(F32) + scale * dn - hidden * (scale * scale * scale * inner)
+
+
+def total_kernel(me_ref, *refs):
+    ins, outs, scr = refs[0:5], refs[5:9], refs[9]
+    t = me_ref[0] & (QUAD - 1)
+    total = ins[0][...].astype(F32)
+    for a in ins[1:]:
+        total = total + a[...].astype(F32)
+    scr[...] = total.astype(scr.dtype)
+    nrow = outs[0].shape[0]
+    for r in range(QUAD):
+        outs[r][...] = scr[pl.ds(pl.multiple_of((t ^ r) * nrow, nrow), nrow), :]
+
+
+def sum5_kernel(a, b, c, d, e, out_ref):
+    out_ref[...] = (
+        a[...].astype(F32)
+        + b[...].astype(F32)
+        + c[...].astype(F32)
+        + d[...].astype(F32)
+        + e[...].astype(F32)
+    )
+
+
+def weave(out_ref, at, parts, size):
+    for k in range(8):
+        for half in range(QUAD // 2):
+            pair = [p[:, k * size : (k + 1) * size] for p in parts[2 * half : 2 * half + 2]]
+            lo = at + (k * QUAD + 2 * half) * size
+            out_ref[:, lo : lo + 2 * size] = jnp.concatenate(pair, 1)
+
+
+def pick_heads(parts, heads):
+    total = None
+    for q in range(QUAD):
+        sel = (iota((LANES, heads), 1) == iota((LANES, heads), 0) * QUAD + q).astype(F32)
+        got = mm_high(parts[q], sel)
+        total = got if total is None else total + got
+    return total
+
+
+def finish_kernel(me_ref, *refs):
+    p1, p2 = refs[0:4], refs[4:8]
+    out_ref, scr1, scr2 = refs[8:]
+    t = me_ref[0] & (QUAD - 1)
+    for r in range(QUAD):
+        scr1[t ^ r] = p1[r][...].astype(F32)
+        scr2[t ^ r] = p2[r][...].astype(F32)
+    width = scr2.shape[2]
+    inner = width * QUAD
+    size = inner // 32
+    conv_end = out_ref.shape[1] - 32
+    weave(out_ref, 0, [scr2[q] for q in range(QUAD)], size)
+    weave(out_ref, inner, [scr1[q][:, 0:width] for q in range(QUAD)], size)
+    shared = width + conv_end - 2 * inner
+    out_ref[:, 2 * inner : conv_end] = (
+        scr1[0][:, width:shared] + scr1[1][:, width:shared]
+    ) + (scr1[2][:, width:shared] + scr1[3][:, width:shared])
+    out_ref[:, conv_end:] = pick_heads([scr1[q][:, shared : shared + LANES] for q in range(QUAD)], 32)
+
+
+def small_kernel(me_ref, *refs):
+    parts = refs[0:4]
+    cw_ref, cb_ref, dt_ref, al_ref, sk_ref, ng_ref, pg_ref, scr = refs[4:]
+    t = me_ref[0] & (QUAD - 1)
+    for r in range(QUAD):
+        scr[t ^ r] = parts[r][...]
+    inner = ng_ref.shape[1]
+    width = inner // QUAD
+    size = inner // 32
+    shared = width + cb_ref.shape[1] - inner
+    for out, lo, hi in ((cw_ref, 0, 4), (cb_ref, 4, 5)):
+        weave(out, 0, [scr[q][lo:hi, 0:width] for q in range(QUAD)], size)
+        out[:, inner:] = (scr[0][lo:hi, width:shared] + scr[1][lo:hi, width:shared]) + (
+            scr[2][lo:hi, width:shared] + scr[3][lo:hi, width:shared]
+        )
+    heads = pick_heads([scr[q][0:8, 0:LANES] for q in range(QUAD)], 32)
+    dt_ref[...] = heads[5:6, :]
+    al_ref[...] = heads[6:7, :]
+    sk_ref[...] = heads[7:8, :]
+    weave(ng_ref, 0, [scr[q][8:9, 0:width] for q in range(QUAD)], size)
+    pg_ref[...] = (scr[0][9:10, :] + scr[1][9:10, :]) + (scr[2][9:10, :] + scr[3][9:10, :])
+
+
+def quad_shards(
+    count,
+    tokens,
+    lengths,
+    in_weight,
+    out_weight,
+    conv_weight,
+    conv_bias,
+    dt_bias,
+    a_log,
+    skip_gain,
+    norm_gain,
+    pre_gain,
+    cotangent,
+):
+    chunks = count // QUAD
+    rows, model = tokens.shape
+    inner = norm_gain.shape[0]
+    heads = dt_bias.shape[0]
+    own = heads // QUAD
+    width = inner // QUAD
+    size = inner // heads
+    nrow, proj_width = in_weight.shape
+    state = (conv_bias.shape[0] - inner) // 2
+    wide1 = width + 2 * state + LANES
+    total_rows = QUAD * rows
+
+    def swap(a, mask):
+        return lax.ppermute(a, "dp", [(i, i ^ mask) for i in range(count)])
+
+    def zy_mask(k):
+        return k * QUAD
+
+    def gather(mine):
+        got = [None] * chunks
+        got[0] = mine
+        for k in range(2, chunks, 2):
+            got[k] = swap(mine, zy_mask(k))
+        for k in range(0, chunks, 2):
+            got[k + 1] = swap(got[k], zy_mask(1))
+        return got
+
+    def scatter(parts):
+        sent = {}
+        for k in (2, 4, 6, 0):
+            sent[k] = swap(parts[k + 1], zy_mask(1))
+        back = []
+        for k in (2, 4, 6):
+            both = (parts[k].astype(F32) + sent[k].astype(F32)).astype(BF)
+            back.append(swap(both, zy_mask(k)))
+        return [parts[0], sent[0]] + back
+
+    me_scalar = lax.axis_index("dp").astype(jnp.int32)
+    me = me_scalar.reshape(1)
+    member = me_scalar % QUAD
+
+    def mine(a):
+        return lax.dynamic_index_in_dim(
+            a.reshape(a.shape[:-1] + (own, QUAD, a.shape[-1] // heads)), member, a.ndim, False
+        ).reshape(a.shape[:-1] + (a.shape[-1] // QUAD,))
+
+    cw = jnp.concatenate([mine(conv_weight[:, :inner]), conv_weight[:, inner:]], 1)
+    cb = jnp.concatenate([mine(conv_bias[:inner]), conv_bias[inner:]])[None, :]
+    by_head = jnp.stack([mine(dt_bias), mine(a_log), mine(skip_gain)])
+    by_head = jnp.pad(by_head, ((0, 5), (0, LANES - own)))
+    gain = mine(norm_gain)[None, :]
+    pre = pre_gain[None, :]
+
+    wout = gather(out_weight)
+    prepped = call(
+        prep_kernel,
+        [((rows + 16, model), BF), ((rows, model), BF)]
+        + [((nrow, wide1), BF)] * QUAD
+        + [((nrow, width), BF)] * QUAD,
+        [me, lengths, tokens, cotangent, in_weight],
+        [pltpu.VMEM((QUAD, nrow, wide1), BF), pltpu.VMEM((QUAD, nrow, width), BF)],
+        name="prep",
+    )
+    tokx, ocot, cut1, cut2 = prepped[0], prepped[1], prepped[2:6], prepped[6:10]
+
+    def join(cut):
+        got = [cut[0]] + [swap(cut[r], r) for r in range(1, QUAD)]
+        return call(
+            join_kernel, [((QUAD * nrow, cut[0].shape[1]), BF)], [me] + got, name="join"
+        )[0]
+
+    def share(a):
+        across = swap(a, 2)
+        return [a, swap(a, 1), across, swap(across, 1)]
+
+    own1 = join(cut1)
+    w1 = gather(own1)
+    toks = share(tokx)
+    own2 = join(cut2)
+    w2 = gather(own2)
+    cots = share(ocot)
+
+    normed, proj, ends = call(
+        project_kernel,
+        [((total_rows, model), BF), ((total_rows, wide1), F32), ((QUAD, rows), F32)],
+        [me] + toks + w1 + [pre],
+        flops=2 * total_rows * model * wide1,
+        name="project",
+    )
+    (scan_out,) = call(
+        scan_kernel,
+        [((total_rows, width), F32)],
+        [proj, ends, cw, cb, by_head],
+        flops=2e9,
+        name="scan",
+    )
+    w_full, cot_all, dgn = call(
+        cot_kernel,
+        [((width, model), BF), ((total_rows, model), BF), ((total_rows, width), F32)],
+        [me] + wout + cots,
+        flops=2 * total_rows * model * width,
+        name="normcot",
+    )
+    z, stat = call(
+        gate_kernel,
+        [((total_rows, width), F32), ((8, total_rows), F32)],
+        w2 + [normed, scan_out, dgn, gain],
+        flops=2 * total_rows * model * width,
+        name="gate",
+    )
+    stats = [stat] + [swap(stat, r) for r in range(1, QUAD)]
+    ungated = call(
+        functools.partial(ungate_kernel, float(inner)),
+        [
+            ((total_rows, width), BF),
+            ((total_rows, width), F32),
+            ((total_rows, width), BF),
+            ((1, width), F32),
+        ]
+        + [((LANES, width), BF)] * chunks,
+        stats + [z, scan_out, dgn, gain, normed],
+        flops=2 * total_rows * model * width,
+        name="ungate",
+    )
+    gn, dscan, dz, ngain_part = ungated[0:4]
+    parts2 = scatter(ungated[4:])
+    ograd = call(
+        outgrad_kernel,
+        [((size, model), BF)] * chunks,
+        [me, gn, cot_all],
+        [pltpu.VMEM((width, model), BF)],
+        flops=2 * total_rows * model * width,
+        name="outgrad",
+    )
+    parts3 = scatter(ograd)
+    branch = call(
+        branch_kernel,
+        [((rows, model), F32)] * QUAD,
+        [gn, w_full],
+        flops=2 * total_rows * model * width,
+        name="branch",
+    )
+    pc1, small = call(
+        scan_back_kernel,
+        [((total_rows, wide1), BF), ((16, model), F32)],
+        [proj, dscan, ends, cw, cb, by_head],
+        flops=6e9,
+        name="scanback",
+    )
+    grads = [None] * chunks
+    for order in ((3, 5, 7, 1), (2, 4, 6, 0)):
+        got = call(
+            functools.partial(ingrad_kernel, order),
+            [((LANES, wide1), BF)] * len(order),
+            [normed, pc1],
+            flops=total_rows * model * wide1,
+            name="ingrad",
+        )
+        for n, k in enumerate(order):
+            grads[k] = got[n]
+    parts1 = scatter(grads)
+
+    def pair_sum(blocks):
+        one, three = swap(blocks[1], 1), swap(blocks[3], 1)
+        keep, send = call(
+            pair_add_kernel,
+            [(blocks[0].shape, F32)] * 2,
+            [blocks[0], one, blocks[2], three],
+            name="pair_add",
+        )
+        return keep, swap(send, 2)
+
+    pre_parts = call(
+        normcot_kernel,
+        [((rows, model), F32)] * QUAD + [((16, model), F32)],
+        [me] + w1 + w2 + [pc1, dz, small, ngain_part] + toks,
+        flops=2 * total_rows * model * (wide1 + width),
+        name="normedcot",
+    )
+    keep_m, got_m = pair_sum(branch)
+    (mixed,) = call(
+        mixed_kernel, [((rows, model), BF)], [lengths, tokens, keep_m, got_m], name="mixed"
+    )
+    keep_t, got_t = pair_sum(pre_parts[0:QUAD])
+    (tokens_grad,) = call(
+        tokgrad_kernel,
+        [((rows, model), F32)],
+        [tokens, ocot, pre, keep_t, got_t],
+        name="tokgrad",
+    )
+
+    packed = pre_parts[QUAD]
+    packed = packed + swap(packed, zy_mask(1))
+    around = [swap(packed, zy_mask(k)) for k in range(2, chunks, 2)]
+    packed = (packed + around[0]) + (around[1] + around[2])
+    smalls = [packed] + [swap(packed, r) for r in range(1, QUAD)]
+    small_out = call(
+        small_kernel,
+        [
+            (conv_weight.shape, F32),
+            ((1, conv_bias.shape[0]), F32),
+            ((1, heads), F32),
+            ((1, heads), F32),
+            ((1, heads), F32),
+            ((1, inner), F32),
+            ((1, model), F32),
+        ],
+        [me] + smalls,
+        [pltpu.VMEM((QUAD, 16, model), F32)],
+        name="small",
+    )
+
+    (out_shard,) = call(sum5_kernel, [((size, model), F32)], parts3, name="outsum")
+
+    def member_cut(parts):
+        wide = parts[0].shape[1]
+        cut = call(
+            total_kernel,
+            [((nrow, wide), BF)] * QUAD,
+            [me] + parts,
+            [pltpu.VMEM((QUAD * nrow, wide), BF)],
+            name="total",
+        )
+        return [cut[0]] + [swap(cut[r], r) for r in range(1, QUAD)]
+
+    got2 = member_cut(parts2)
+    got1 = member_cut(parts1)
+    (in_shard,) = call(
+        finish_kernel,
+        [((nrow, proj_width), F32)],
+        [me] + got1 + got2,
+        [pltpu.VMEM((QUAD, nrow, wide1), F32), pltpu.VMEM((QUAD, nrow, width), F32)],
+        name="finish",
+    )
+    return (
+        mixed,
+        tokens_grad,
+        in_shard,
+        out_shard,
+        small_out[0],
+        small_out[1].reshape(-1),
+        small_out[2].reshape(-1),
+        small_out[3].reshape(-1),
+        small_out[4].reshape(-1),
+        small_out[5].reshape(-1),
+        small_out[6].reshape(-1),
+    )
 
 
 def prenorm(hidden_in, gain_row):
@@ -188,8 +958,10 @@
 
 
 def solution(mesh):
+    count = mesh.shape["dp"]
+    body = functools.partial(quad_shards, count) if count == 32 else shards
     return jax.shard_map(
-        shards,
+        body,
         mesh=mesh,
         in_specs=(
             P("dp", None),

time: 786 us -> 237 us (0.30); the launches traced: 772 us -> 236 us
  waiting for transfers between devices: 360 us -> 83.9 us
  local copies, waits for them, and re-layouts: 210 us -> 23.4 us
  matrix products: 94 us -> 0 us
  starting transfers between devices: 0.37 us -> 79 us
  other arithmetic: 49.7 us -> 1.74 us
  Pallas kernels: 0 us -> 47.3 us
  blocking collectives: 40.9 us -> 0 us
  between operations: 14.5 us -> 1.09 us
    reduce_scatter x2 -> x0, waiting for transfers between devices: 279 us -> none  [the longest x1 148 us: shards(): lax.psum_scatter(out_grad, 'dp', scatter_dimension=0, tiled=True)]
    dynamic_update_slice x8 -> x0, local copies, waits for them, and re-layouts: 106 us -> none  [mixer_core(): _, scanned = lax.scan(jax.checkpoint(block_step), start, items)]
    dot_general x32 -> x0, matrix products: 92 us -> none  [the longest x6 21 us: block_step(): inside = jnp.einsum('ijh,jhp->ihp', weighting, values, precision=HIGH)]
    ppermute x0 -> x76, waiting for transfers between devices: none -> 83.9 us  [swap(): return lax.ppermute(a, 'dp', [(i, i ^ mask) for i in range(count)])]
    ppermute x0 -> x76, starting transfers between devices: none -> 79 us  [swap(): return lax.ppermute(a, 'dp', [(i, i ^ mask) for i in range(count)])]
    all_gather x2 -> x0, waiting for transfers between devices: 79 us -> none  [the longest x1 78.9 us: shards(): lax.all_gather(in_weight, 'dp', axis=0, tiled=True)]
    pallas_call x0 -> x23, Pallas kernels: none -> 47.3 us  [call(): pl.pallas_call(kernel, out_shape=shapes, in_specs=in_specs, out_specs=[pl...]
    psum x1 -> x0, blocking collectives: 40.9 us -> none  [shards(): lax.psum((conv_w_grad, conv_b_grad, bias_dt_grad, decay_grad, skip_grad,...]
  transfers between devices with their start and end apart: 4 -> 76, of which waited for: 3 -> 31; matrix products, arithmetic and copies ran while one was open for 19% -> 4% of each run, Pallas kernels for 0% -> 8%
where the time goes in v1:
time: 237 us; the launch traced here: 236 us
  waiting for transfers between devices  83.9 us (35%)
  starting transfers between devices  79 us (33%)
  Pallas kernels  47.3 us (20%)
  local copies, waits for them, and re-layouts  23.4 us (10%)
    ppermute x76, waiting for transfers between devices, swap(): return lax.ppermute(a, 'dp', [(i, i ^ mask) for i in range(count)])  83.9 us
    ppermute x76, starting transfers between devices, swap(): return lax.ppermute(a, 'dp', [(i, i ^ mask) for i in range(count)])  79 us
    pallas_call x23, Pallas kernels, call(): pl.pallas_call(kernel, out_shape=shapes, in_specs=in_specs, out_specs=[pl...  47.3 us
    unnamed x56, local copies, waits for them, and re-layouts  16.8 us
  transfers between devices with their start and end apart: 76, of which 31 were waited for; matrix products, arithmetic and copies ran while one was open for 4% of the time, Pallas kernels for 8%

profile of v1, /device:TPU:0, one launch (start us, length us, event | category | flops | bytes accessed | tf_op | source)
XLA Modules:
  0.0 236.5 jit_solution(1311750495162678339)
XLA Ops:
  5.6 2.9 %collective-permute-start.1 = (bf16[32,512]{1,0:T(8,128)(2,1)S(1)}, bf16[32,512]{1,0:T(8,128)(2,1)S(1)}, u32[]{:S(2)}, u32[]{:S(2)}) collective-permute-start(bf16[32,512]{1,0:T(8,128)(2,1)S(1)} %get-tuple-element.89), channel_id=1, source_target_pairs={{0,2},{1,3},{2,0},{3,1},{4,6},{5,7},{6,4},{7,5},{8,10},{9,11},{10,... | collective-permute-start | bytes 98312 | tf_op jit(solution)/shard_map/ppermute | solution.py:547
  8.5 2.6 %collective-permute-start.26 = (bf16[64,1024]{1,0:T(8,128)(2,1)}, bf16[64,1024]{1,0:T(8,128)(2,1)S(1)}, u32[]{:S(2)}, u32[]{:S(2)}) collective-permute-start(bf16[64,1024]{1,0:T(8,128)(2,1)} %refs_0_.1), channel_id=1, source_target_pairs={{0,16},{1,17},{2,18},{3,19},{4,20},{5,21},{6,22},{7,23},{8,24},{9,... | collective-permute-start | bytes 393224 | tf_op jit(solution)/shard_map/ppermute | solution.py:547
  11.1 1.6 collective-permute-start.24
  12.7 1.1 collective-permute-start.14
  14.5 1.5 collective-permute-start.23
  16.9 1.8 collective-permute-start.28
  18.7 1.2 collective-permute-done.15.refs_3_
  19.9 1.4 collective-permute-start.8
  21.3 1.7 collective-permute-start.6
  23.0 1.4 collective-permute-start.4
  24.9 1.5 collective-permute-start.25
  26.4 1.8 collective-permute-done.8.refs_6_.refs_14_
  28.2 1.0 collective-permute-start.31
  29.2 8.4 %collective-permute-done.6.refs_4_.refs_12_ = bf16[128,512]{1,0:T(8,128)(2,1)S(1)} collective-permute-done((bf16[128,512]{1,0:T(8,128)(2,1)S(1)}, bf16[128,512]{1,0:T(8,128)(2,1)S(1)}, u32[]{:S(2)}, u32[]{:S(2)}) %collective-permute-start.6) | collective-permute-done | bytes 131104 | tf_op jit(solution)/shard_map/ppermute | solution.py:547
  39.4 1.5 collective-permute-start.21
  40.9 1.0 collective-permute-start.11
  41.9 1.5 collective-permute-done.29.refs_7_
  43.6 1.7 collective-permute-start.17
  45.3 4.4 %collective-permute-done.21.refs_10_.refs_6_ = bf16[128,896]{1,0:T(8,128)(2,1)S(1)} collective-permute-done((bf16[128,896]{1,0:T(8,128)(2,1)S(1)}, bf16[128,896]{1,0:T(8,128)(2,1)S(1)}, u32[]{:S(2)}, u32[]{:S(2)}) %collective-permute-start.21) | collective-permute-done | bytes 229408 | tf_op jit(solution)/shard_map/ppermute | solution.py:547
  49.8 1.5 collective-permute-start.16
  51.3 1.2 slice.23
  54.3 6.7 %collective-permute-done.19.refs_8_.refs_4_ = bf16[128,896]{1,0:T(8,128)(2,1)S(1)} collective-permute-done((bf16[128,896]{1,0:T(8,128)(2,1)S(1)}, bf16[128,896]{1,0:T(8,128)(2,1)S(1)}, u32[]{:S(2)}, u32[]{:S(2)}) %collective-permute-start.19) | collective-permute-done | bytes 229408 | tf_op jit(solution)/shard_map/ppermute | solution.py:547
  66.8 1.2 collective-permute-start.20
  76.9 1.3 collective-permute-start.3
  80.2 4.0 %collective-permute-done.18.refs_7_.refs_3_ = bf16[128,896]{1,0:T(8,128)(2,1)S(1)} collective-permute-done((bf16[128,896]{1,0:T(8,128)(2,1)}, bf16[128,896]{1,0:T(8,128)(2,1)S(1)}, u32[]{:S(2)}, u32[]{:S(2)}) %collective-permute-start.18) | collective-permute-done | bytes 229408 | tf_op jit(solution)/shard_map/ppermute | solution.py:547
  85.1 2.6 %project.1 = (bf16[512,1024]{1,0:T(8,128)(2,1)S(1)}, f32[512,896]{1,0:T(8,128)S(1)}, f32[4,128]{1,0:T(4,128)S(1)}) custom-call(s32[1]{0:T(128)} %bitcast.me_ref, bf16[144,1024]{1,0:T(8,128)(2,1)S(1)} %get-tuple-element.91.refs_0_.refs_20_, bf16[144,1024]{1,0:T(8,128)(2,1)S(1)} %collective-permute-done.10.refs_1_.refs_21_, ...), custom_call_target="tpu_custom_call" | custom-call | flops 939524096 | bytes 5904388 | tf_op jit(solution)/shard_map/project/pallas_call | solution.py:51
  87.6 6.1 %scan.1.refs_9_.refs_5_ = f32[512,512]{1,0:T(8,128)S(1)} custom-call(f32[512,896]{1,0:T(8,128)S(1)} %get-tuple-element.97.proj_ref, f32[4,128]{1,0:T(4,128)S(1)} %get-tuple-element.98.ends_ref, f32[4,768]{1,0:T(4,128)S(1)} %pad_maximum_fusion.cw_ref, f32[1,768]{1,0:T(1,128)S(1)} %broadcast_in_dim.7.cb_ref, f32[8,128]{1,0:T(8,128)S(1)} %select_maximum_fusion.head_ref), custom_call_target="tpu_custom_call" | custom-call | flops 2000000000 | bytes 2905088 | tf_op jit(solution)/shard_map/scan/pallas_call | solution.py:51
  94.5 1.2 gate.1
  97.6 1.3 collective-permute-done.35.refs_3_
  99.6 1.8 ungate.1
  101.5 18.2 %scanback.1 = (bf16[512,896]{1,0:T(8,128)(2,1)S(1)}, f32[16,1024]{1,0:T(8,128)S(1)}) custom-call(f32[512,896]{1,0:T(8,128)S(1)} %get-tuple-element.97.proj_ref, f32[512,512]{1,0:T(8,128)S(1)} %get-tuple-element.111.dscan_ref, f32[4,128]{1,0:T(4,128)S(1)} %get-tuple-element.98.ends_ref, f32[4,768]{1,0:T(4,128)S(1)} %pad_maximum_fusion.cw_ref, ...), custom_call_target="tpu_custom_call" | custom-call | flops 6000000000 | bytes 3888128 | tf_op jit(solution)/shard_map/scanback/pallas_call | solution.py:51
  119.7 4.7 %normedcot.1 = (f32[128,1024]{1,0:T(8,128)S(1)}, f32[128,1024]{1,0:T(8,128)S(1)}, f32[128,1024]{1,0:T(8,128)S(1)}, f32[128,1024]{1,0:T(8,128)S(1)}, f32[16,1024]{1,0:T(8,128)S(1)}) custom-call(s32[1]{0:T(128)} %bitcast.me_ref, bf16[128,896]{1,0:T(8,128)(2,1)S(1)} %join.3.refs_4_.refs_0_, bf16[128,896]{1,0:T(8,128)(2,1)} %collective-permute-done.16.refs_5_.refs_1_, ...), custom_call_target="tpu_custom_call" | custom-call | flops 1476395008 | bytes 7735300 | tf_op jit(solution)/shard_map/normedcot/pallas_call | solution.py:51
  126.9 1.8 collective-permute-done.69
  128.7 1.8 collective-permute-start.72
  130.8 2.4 %collective-permute-start.70 = (f32[16,1024]{1,0:T(8,128)S(1)}, f32[16,1024]{1,0:T(8,128)S(1)}, u32[]{:S(2)}, u32[]{:S(2)}) collective-permute-start(f32[16,1024]{1,0:T(8,128)S(1)} %add.67), channel_id=1, source_target_pairs={{0,8},{1,9},{2,10},{3,11},{4,12},{5,13},{6,14},{7,15},{8,0},{9,1},... | collective-permute-start | bytes 196616 | tf_op jit(solution)/shard_map/ppermute | solution.py:547
  134.9 1.1 collective-permute-start.63
  137.7 1.1 collective-permute-start.67
  139.8 3.5 %collective-permute-done.63 = bf16[64,1024]{1,0:T(8,128)(2,1)S(1)} collective-permute-done((bf16[64,1024]{1,0:T(8,128)(2,1)S(1)}, bf16[64,1024]{1,0:T(8,128)(2,1)S(1)}, u32[]{:S(2)}, u32[]{:S(2)}) %collective-permute-start.63) | collective-permute-done | bytes 131104 | tf_op jit(solution)/shard_map/ppermute | solution.py:547
  144.2 1.9 collective-permute-done.65
  147.0 1.9 collective-permute-done.67
  149.8 1.2 collective-permute-start.42
  151.7 2.8 %collective-permute-done.53 = bf16[128,512]{1,0:T(8,128)(2,1)S(1)} collective-permute-done((bf16[128,512]{1,0:T(8,128)(2,1)S(1)}, bf16[128,512]{1,0:T(8,128)(2,1)S(1)}, u32[]{:S(2)}, u32[]{:S(2)}) %collective-permute-start.53) | collective-permute-done | bytes 131104 | tf_op jit(solution)/shard_map/ppermute | solution.py:547
  155.3 2.0 collective-permute-done.55
  157.3 2.2 collective-permute-done.57
  160.6 1.4 collective-permute-done.42.refs_1_
  163.0 5.2 %collective-permute-done.43 = bf16[128,896]{1,0:T(8,128)(2,1)S(1)} collective-permute-done((bf16[128,896]{1,0:T(8,128)(2,1)S(1)}, bf16[128,896]{1,0:T(8,128)(2,1)S(1)}, u32[]{:S(2)}, u32[]{:S(2)}) %collective-permute-start.43) | collective-permute-done | bytes 229408 | tf_op jit(solution)/shard_map/ppermute | solution.py:547
  169.2 5.8 %collective-permute-done.45 = bf16[128,896]{1,0:T(8,128)(2,1)S(1)} collective-permute-done((bf16[128,896]{1,0:T(8,128)(2,1)S(1)}, bf16[128,896]{1,0:T(8,128)(2,1)S(1)}, u32[]{:S(2)}, u32[]{:S(2)}) %collective-permute-start.45) | collective-permute-done | bytes 229408 | tf_op jit(solution)/shard_map/ppermute | solution.py:547
  176.0 5.0 %collective-permute-done.47 = bf16[128,896]{1,0:T(8,128)(2,1)S(1)} collective-permute-done((bf16[128,896]{1,0:T(8,128)(2,1)S(1)}, bf16[128,896]{1,0:T(8,128)(2,1)S(1)}, u32[]{:S(2)}, u32[]{:S(2)}) %collective-permute-start.47) | collective-permute-done | bytes 229408 | tf_op jit(solution)/shard_map/ppermute | solution.py:547
  181.3 1.6 collective-permute-start.66
  182.9 2.6 %collective-permute-start.68 = (bf16[64,1024]{1,0:T(8,128)(2,1)S(1)}, bf16[64,1024]{1,0:T(8,128)(2,1)S(1)}, u32[]{:S(2)}, u32[]{:S(2)}) collective-permute-start(bf16[64,1024]{1,0:T(8,128)(2,1)S(1)} %add_convert_fusion.3), channel_id=1, source_target_pairs={{0,24},{1,25},{2,26},{3,27},{4,28},{5,29},{6,30},{7,31},{8,16},{9,... | collective-permute-start | bytes 393224 | tf_op jit(solution)/shard_map/ppermute | solution.py:547
  185.4 1.9 collective-permute-start.56
  189.2 2.5 %collective-permute-start.58 = (bf16[128,512]{1,0:T(8,128)(2,1)S(1)}, bf16[128,512]{1,0:T(8,128)(2,1)S(1)}, u32[]{:S(2)}, u32[]{:S(2)}) collective-permute-start(bf16[128,512]{1,0:T(8,128)(2,1)S(1)} %add_convert_fusion.6), channel_id=1, source_target_pairs={{0,24},{1,25},{2,26},{3,27},{4,28},{5,29},{6,30},{7,31},{8,16},{9,... | collective-permute-start | bytes 393224 | tf_op jit(solution)/shard_map/ppermute | solution.py:547
  191.7 2.6 %collective-permute-done.66.d = bf16[64,1024]{1,0:T(8,128)(2,1)S(1)} collective-permute-done((bf16[64,1024]{1,0:T(8,128)(2,1)S(1)}, bf16[64,1024]{1,0:T(8,128)(2,1)S(1)}, u32[]{:S(2)}, u32[]{:S(2)}) %collective-permute-start.66) | collective-permute-done | bytes 131104 | tf_op jit(solution)/shard_map/ppermute | solution.py:547
  194.3 8.6 %collective-permute-start.46 = (bf16[128,896]{1,0:T(8,128)(2,1)S(1)}, bf16[128,896]{1,0:T(8,128)(2,1)S(1)}, u32[]{:S(2)}, u32[]{:S(2)}) collective-permute-start(bf16[128,896]{1,0:T(8,128)(2,1)S(1)} %add_convert_fusion.1), channel_id=1, source_target_pairs={{0,16},{1,17},{2,18},{3,19},{4,20},{5,21},{6,22},{7,23},{8,24},{9,... | collective-permute-start | bytes 688136 | tf_op jit(solution)/shard_map/ppermute | solution.py:547
  202.9 1.5 collective-permute-start.38
  204.3 5.8 %collective-permute-done.56.refs_3_ = bf16[128,512]{1,0:T(8,128)(2,1)S(1)} collective-permute-done((bf16[128,512]{1,0:T(8,128)(2,1)S(1)}, bf16[128,512]{1,0:T(8,128)(2,1)S(1)}, u32[]{:S(2)}, u32[]{:S(2)}) %collective-permute-start.56) | collective-permute-done | bytes 131104 | tf_op jit(solution)/shard_map/ppermute | solution.py:547
  211.0 1.8 collective-permute-start.48
  213.1 6.7 %collective-permute-done.46.refs_3_ = bf16[128,896]{1,0:T(8,128)(2,1)S(1)} collective-permute-done((bf16[128,896]{1,0:T(8,128)(2,1)S(1)}, bf16[128,896]{1,0:T(8,128)(2,1)S(1)}, u32[]{:S(2)}, u32[]{:S(2)}) %collective-permute-start.46) | collective-permute-done | bytes 229408 | tf_op jit(solution)/shard_map/ppermute | solution.py:547
  222.2 1.3 collective-permute-start.49
  226.1 1.0 small.1
  228.8 1.2 collective-permute-done.51.refs_3_
  232.3 1.2 finish.1
  234.1 1.3 mixed.1
  235.5 1.0 tokgrad.1
  (202 shorter events, 59.7 us)
Async XLA Ops:
  5.0 11.0 %collective-permute-start.13 = (bf16[32,896]{1,0:T(8,128)(2,1)S(1)}, bf16[32,896]{1,0:T(8,128)(2,1)S(1)}, u32[]{:S(2)}, u32[]{:S(2)}) collective-permute-start(bf16[32,896]{1,0:T(8,128)(2,1)S(1)} %get-tuple-element.93), channel_id=1, source_target_pairs={{0,1},{1,0},{2,3},{3,2},{4,5},{5,4},{6,7},{7,6},{8,9},{9,8},{10,11... | collective-permute-start | bytes 172040 | tf_op jit(solution)/shard_map/ppermute | solution.py:547
  5.5 5.6 %collective-permute-start = (bf16[32,512]{1,0:T(8,128)(2,1)S(1)}, bf16[32,512]{1,0:T(8,128)(2,1)S(1)}, u32[]{:S(2)}, u32[]{:S(2)}) collective-permute-start(bf16[32,512]{1,0:T(8,128)(2,1)S(1)} %get-tuple-element.88), channel_id=1, source_target_pairs={{0,1},{1,0},{2,3},{3,2},{4,5},{5,4},{6,7},{7,6},{8,9},{9,8},{10,11... | collective-permute-start | bytes 98312 | tf_op jit(solution)/shard_map/ppermute | solution.py:547
  5.6 7.1 %collective-permute-start.1 = (bf16[32,512]{1,0:T(8,128)(2,1)S(1)}, bf16[32,512]{1,0:T(8,128)(2,1)S(1)}, u32[]{:S(2)}, u32[]{:S(2)}) collective-permute-start(bf16[32,512]{1,0:T(8,128)(2,1)S(1)} %get-tuple-element.89), channel_id=1, source_target_pairs={{0,2},{1,3},{2,0},{3,1},{4,6},{5,7},{6,4},{7,5},{8,10},{9,11},{10,... | collective-permute-start | bytes 98312 | tf_op jit(solution)/shard_map/ppermute | solution.py:547
  8.5 12.8 %collective-permute-start.26 = (bf16[64,1024]{1,0:T(8,128)(2,1)}, bf16[64,1024]{1,0:T(8,128)(2,1)S(1)}, u32[]{:S(2)}, u32[]{:S(2)}) collective-permute-start(bf16[64,1024]{1,0:T(8,128)(2,1)} %refs_0_.1), channel_id=1, source_target_pairs={{0,16},{1,17},{2,18},{3,19},{4,20},{5,21},{6,22},{7,23},{8,24},{9,... | collective-permute-start | bytes 393224 | tf_op jit(solution)/shard_map/ppermute | solution.py:547
  11.1 11.9 %collective-permute-start.24 = (bf16[64,1024]{1,0:T(8,128)(2,1)}, bf16[64,1024]{1,0:T(8,128)(2,1)S(1)}, u32[]{:S(2)}, u32[]{:S(2)}) collective-permute-start(bf16[64,1024]{1,0:T(8,128)(2,1)} %refs_0_.1), channel_id=1, source_target_pairs={{0,8},{1,9},{2,10},{3,11},{4,12},{5,13},{6,14},{7,15},{8,0},{9,1},... | collective-permute-start | bytes 393224 | tf_op jit(solution)/shard_map/ppermute | solution.py:547
  14.5 9.8 %collective-permute-start.23 = (bf16[64,1024]{1,0:T(8,128)(2,1)}, bf16[64,1024]{1,0:T(8,128)(2,1)S(1)}, u32[]{:S(2)}, u32[]{:S(2)}) collective-permute-start(bf16[64,1024]{1,0:T(8,128)(2,1)} %refs_0_.1), channel_id=1, source_target_pairs={{0,4},{1,5},{2,6},{3,7},{4,0},{5,1},{6,2},{7,3},{8,12},{9,13},{10,... | collective-permute-start | bytes 393224 | tf_op jit(solution)/shard_map/ppermute | solution.py:547
  16.9 8.0 %collective-permute-start.28 = (bf16[64,1024]{1,0:T(8,128)(2,1)}, bf16[64,1024]{1,0:T(8,128)(2,1)S(1)}, u32[]{:S(2)}, u32[]{:S(2)}) collective-permute-start(bf16[64,1024]{1,0:T(8,128)(2,1)} %refs_0_.1), channel_id=1, source_target_pairs={{0,24},{1,25},{2,26},{3,27},{4,28},{5,29},{6,30},{7,31},{8,16},{9,... | collective-permute-start | bytes 393224 | tf_op jit(solution)/shard_map/ppermute | solution.py:547
  19.9 8.2 %collective-permute-start.8 = (bf16[128,512]{1,0:T(8,128)(2,1)S(1)}, bf16[128,512]{1,0:T(8,128)(2,1)S(1)}, u32[]{:S(2)}, u32[]{:S(2)}) collective-permute-start(bf16[128,512]{1,0:T(8,128)(2,1)S(1)} %join.2.refs_0_.refs_8_), channel_id=1, source_target_pairs={{0,24},{1,25},{2,26},{3,27},{4,28},{5,29},{6,30},{7,31},{8,16},{9,... | collective-permute-start | bytes 393224 | tf_op jit(solution)/shard_map/ppermute | solution.py:547
  21.3 16.3 %collective-permute-start.6 = (bf16[128,512]{1,0:T(8,128)(2,1)S(1)}, bf16[128,512]{1,0:T(8,128)(2,1)S(1)}, u32[]{:S(2)}, u32[]{:S(2)}) collective-permute-start(bf16[128,512]{1,0:T(8,128)(2,1)S(1)} %join.2.refs_0_.refs_8_), channel_id=1, source_target_pairs={{0,16},{1,17},{2,18},{3,19},{4,20},{5,21},{6,22},{7,23},{8,24},{9,... | collective-permute-start | bytes 393224 | tf_op jit(solution)/shard_map/ppermute | solution.py:547
  23.0 14.6 %collective-permute-start.4 = (bf16[128,512]{1,0:T(8,128)(2,1)S(1)}, bf16[128,512]{1,0:T(8,128)(2,1)S(1)}, u32[]{:S(2)}, u32[]{:S(2)}) collective-permute-start(bf16[128,512]{1,0:T(8,128)(2,1)S(1)} %join.2.refs_0_.refs_8_), channel_id=1, source_target_pairs={{0,8},{1,9},{2,10},{3,11},{4,12},{5,13},{6,14},{7,15},{8,0},{9,1},... | collective-permute-start | bytes 393224 | tf_op jit(solution)/shard_map/ppermute | solution.py:547
  24.3 14.4 %collective-permute-start.27 = (bf16[64,1024]{1,0:T(8,128)(2,1)S(1)}, bf16[64,1024]{1,0:T(8,128)(2,1)S(1)}, u32[]{:S(2)}, u32[]{:S(2)}) collective-permute-start(bf16[64,1024]{1,0:T(8,128)(2,1)S(1)} %collective-permute-done.26.refs_4_), channel_id=1, source_target_pairs={{0,4},{1,5},{2,6},{3,7},{4,0},{5,1},{6,2},{7,3},{8,12},{9,13},{10,... | collective-permute-start | bytes 393224 | tf_op jit(solution)/shard_map/ppermute | solution.py:547
  24.9 16.0 %collective-permute-start.25 = (bf16[64,1024]{1,0:T(8,128)(2,1)S(1)}, bf16[64,1024]{1,0:T(8,128)(2,1)S(1)}, u32[]{:S(2)}, u32[]{:S(2)}) collective-permute-start(bf16[64,1024]{1,0:T(8,128)(2,1)S(1)} %collective-permute-done.24.refs_2_), channel_id=1, source_target_pairs={{0,4},{1,5},{2,6},{3,7},{4,0},{5,1},{6,2},{7,3},{8,12},{9,13},{10,... | collective-permute-start | bytes 393224 | tf_op jit(solution)/shard_map/ppermute | solution.py:547
  28.2 15.3 %collective-permute-start.31 = (bf16[128,1024]{1,0:T(8,128)(2,1)S(1)}, bf16[128,1024]{1,0:T(8,128)(2,1)S(1)}, u32[]{:S(2)}, u32[]{:S(2)}) collective-permute-start(bf16[128,1024]{1,0:T(8,128)(2,1)S(1)} %get-tuple-element.99.refs_8_.cot_ref), channel_id=1, source_target_pairs={{0,2},{1,3},{2,0},{3,1},{4,6},{5,7},{6,4},{7,5},{8,10},{9,11},{10,... | collective-permute-start | bytes 786440 | tf_op jit(solution)/shard_map/ppermute | solution.py:547
  37.6 6.0 %collective-permute-start.30 = (bf16[128,1024]{1,0:T(8,128)(2,1)S(1)}, bf16[128,1024]{1,0:T(8,128)(2,1)S(1)}, u32[]{:S(2)}, u32[]{:S(2)}) collective-permute-start(bf16[128,1024]{1,0:T(8,128)(2,1)S(1)} %get-tuple-element.99.refs_8_.cot_ref), channel_id=1, source_target_pairs={{0,1},{1,0},{2,3},{3,2},{4,5},{5,4},{6,7},{7,6},{8,9},{9,8},{10,11... | collective-permute-start | bytes 786440 | tf_op jit(solution)/shard_map/ppermute | solution.py:547
  37.6 5.9 %collective-permute-start.29 = (bf16[64,1024]{1,0:T(8,128)(2,1)S(1)}, bf16[64,1024]{1,0:T(8,128)(2,1)S(1)}, u32[]{:S(2)}, u32[]{:S(2)}) collective-permute-start(bf16[64,1024]{1,0:T(8,128)(2,1)S(1)} %collective-permute-done.28.refs_6_), channel_id=1, source_target_pairs={{0,4},{1,5},{2,6},{3,7},{4,0},{5,1},{6,2},{7,3},{8,12},{9,13},{10,... | collective-permute-start | bytes 393224 | tf_op jit(solution)/shard_map/ppermute | solution.py:547
  39.4 10.4 %collective-permute-start.21 = (bf16[128,896]{1,0:T(8,128)(2,1)S(1)}, bf16[128,896]{1,0:T(8,128)(2,1)S(1)}, u32[]{:S(2)}, u32[]{:S(2)}) collective-permute-start(bf16[128,896]{1,0:T(8,128)(2,1)S(1)} %join.3.refs_4_.refs_0_), channel_id=1, source_target_pairs={{0,24},{1,25},{2,26},{3,27},{4,28},{5,29},{6,30},{7,31},{8,16},{9,... | collective-permute-start | bytes 688136 | tf_op jit(solution)/shard_map/ppermute | solution.py:547
  40.9 20.2 %collective-permute-start.11 = (bf16[144,1024]{1,0:T(8,128)(2,1)S(1)}, bf16[144,1024]{1,0:T(8,128)(2,1)S(1)}, u32[]{:S(2)}, u32[]{:S(2)}) collective-permute-start(bf16[144,1024]{1,0:T(8,128)(2,1)S(1)} %get-tuple-element.91.refs_0_.refs_20_), channel_id=1, source_target_pairs={{0,2},{1,3},{2,0},{3,1},{4,6},{5,7},{6,4},{7,5},{8,10},{9,11},{10,... | collective-permute-start | bytes 884744 | tf_op jit(solution)/shard_map/ppermute | solution.py:547
  43.5 17.6 %collective-permute-start.19 = (bf16[128,896]{1,0:T(8,128)(2,1)S(1)}, bf16[128,896]{1,0:T(8,128)(2,1)S(1)}, u32[]{:S(2)}, u32[]{:S(2)}) collective-permute-start(bf16[128,896]{1,0:T(8,128)(2,1)S(1)} %join.3.refs_4_.refs_0_), channel_id=1, source_target_pairs={{0,16},{1,17},{2,18},{3,19},{4,20},{5,21},{6,22},{7,23},{8,24},{9,... | collective-permute-start | bytes 688136 | tf_op jit(solution)/shard_map/ppermute | solution.py:547
  43.5 24.5 %collective-permute-start.32 = (bf16[128,1024]{1,0:T(8,128)(2,1)S(1)}, bf16[128,1024]{1,0:T(8,128)(2,1)S(1)}, u32[]{:S(2)}, u32[]{:S(2)}) collective-permute-start(bf16[128,1024]{1,0:T(8,128)(2,1)S(1)} %collective-permute-done.31.refs_10_), channel_id=1, source_target_pairs={{0,1},{1,0},{2,3},{3,2},{4,5},{5,4},{6,7},{7,6},{8,9},{9,8},{10,11... | collective-permute-start | bytes 786440 | tf_op jit(solution)/shard_map/ppermute | solution.py:547
  43.6 22.3 %collective-permute-start.17 = (bf16[128,896]{1,0:T(8,128)(2,1)S(1)}, bf16[128,896]{1,0:T(8,128)(2,1)}, u32[]{:S(2)}, u32[]{:S(2)}) collective-permute-start(bf16[128,896]{1,0:T(8,128)(2,1)S(1)} %join.3.refs_4_.refs_0_), channel_id=1, source_target_pairs={{0,8},{1,9},{2,10},{3,11},{4,12},{5,13},{6,14},{7,15},{8,0},{9,1},... | collective-permute-start | bytes 688136 | tf_op jit(solution)/shard_map/ppermute | solution.py:547
  49.8 17.0 %collective-permute-start.16 = (bf16[128,896]{1,0:T(8,128)(2,1)S(1)}, bf16[128,896]{1,0:T(8,128)(2,1)}, u32[]{:S(2)}, u32[]{:S(2)}) collective-permute-start(bf16[128,896]{1,0:T(8,128)(2,1)S(1)} %join.3.refs_4_.refs_0_), channel_id=1, source_target_pairs={{0,4},{1,5},{2,6},{3,7},{4,0},{5,1},{6,2},{7,3},{8,12},{9,13},{10,... | collective-permute-start | bytes 688136 | tf_op jit(solution)/shard_map/ppermute | solution.py:547
  61.1 15.8 %collective-permute-start.10 = (bf16[144,1024]{1,0:T(8,128)(2,1)S(1)}, bf16[144,1024]{1,0:T(8,128)(2,1)S(1)}, u32[]{:S(2)}, u32[]{:S(2)}) collective-permute-start(bf16[144,1024]{1,0:T(8,128)(2,1)S(1)} %get-tuple-element.91.refs_0_.refs_20_), channel_id=1, source_target_pairs={{0,1},{1,0},{2,3},{3,2},{4,5},{5,4},{6,7},{7,6},{8,9},{9,8},{10,11... | collective-permute-start | bytes 884744 | tf_op jit(solution)/shard_map/ppermute | solution.py:547
  61.1 24.0 %collective-permute-start.12 = (bf16[144,1024]{1,0:T(8,128)(2,1)S(1)}, bf16[144,1024]{1,0:T(8,128)(2,1)S(1)}, u32[]{:S(2)}, u32[]{:S(2)}) collective-permute-start(bf16[144,1024]{1,0:T(8,128)(2,1)S(1)} %collective-permute-done.11.refs_2_.refs_22_), channel_id=1, source_target_pairs={{0,1},{1,0},{2,3},{3,2},{4,5},{5,4},{6,7},{7,6},{8,9},{9,8},{10,11... | collective-permute-start | bytes 884744 | tf_op jit(solution)/shard_map/ppermute | solution.py:547
  65.9 12.3 %collective-permute-start.22 = (bf16[128,896]{1,0:T(8,128)(2,1)S(1)}, bf16[128,896]{1,0:T(8,128)(2,1)S(1)}, u32[]{:S(2)}, u32[]{:S(2)}) collective-permute-start(bf16[128,896]{1,0:T(8,128)(2,1)S(1)} %collective-permute-done.21.refs_10_.refs_6_), channel_id=1, source_target_pairs={{0,4},{1,5},{2,6},{3,7},{4,0},{5,1},{6,2},{7,3},{8,12},{9,13},{10,... | collective-permute-start | bytes 688136 | tf_op jit(solution)/shard_map/ppermute | solution.py:547
  66.8 12.5 %collective-permute-start.20 = (bf16[128,896]{1,0:T(8,128)(2,1)S(1)}, bf16[128,896]{1,0:T(8,128)(2,1)S(1)}, u32[]{:S(2)}, u32[]{:S(2)}) collective-permute-start(bf16[128,896]{1,0:T(8,128)(2,1)S(1)} %collective-permute-done.19.refs_8_.refs_4_), channel_id=1, source_target_pairs={{0,4},{1,5},{2,6},{3,7},{4,0},{5,1},{6,2},{7,3},{8,12},{9,13},{10,... | collective-permute-start | bytes 688136 | tf_op jit(solution)/shard_map/ppermute | solution.py:547
  68.0 16.3 %collective-permute-start.18 = (bf16[128,896]{1,0:T(8,128)(2,1)}, bf16[128,896]{1,0:T(8,128)(2,1)S(1)}, u32[]{:S(2)}, u32[]{:S(2)}) collective-permute-start(bf16[128,896]{1,0:T(8,128)(2,1)} %collective-permute-done.17.refs_6_.refs_2_), channel_id=1, source_target_pairs={{0,4},{1,5},{2,6},{3,7},{4,0},{5,1},{6,2},{7,3},{8,12},{9,13},{10,... | collective-permute-start | bytes 688136 | tf_op jit(solution)/shard_map/ppermute | solution.py:547
  76.9 16.8 %collective-permute-start.3 = (bf16[128,512]{1,0:T(8,128)(2,1)S(1)}, bf16[128,512]{1,0:T(8,128)(2,1)S(1)}, u32[]{:S(2)}, u32[]{:S(2)}) collective-permute-start(bf16[128,512]{1,0:T(8,128)(2,1)S(1)} %join.2.refs_0_.refs_8_), channel_id=1, source_target_pairs={{0,4},{1,5},{2,6},{3,7},{4,0},{5,1},{6,2},{7,3},{8,12},{9,13},{10,... | collective-permute-start | bytes 393224 | tf_op jit(solution)/shard_map/ppermute | solution.py:547
  78.2 15.5 %collective-permute-start.9 = (bf16[128,512]{1,0:T(8,128)(2,1)S(1)}, bf16[128,512]{1,0:T(8,128)(2,1)S(1)}, u32[]{:S(2)}, u32[]{:S(2)}) collective-permute-start(bf16[128,512]{1,0:T(8,128)(2,1)S(1)} %collective-permute-done.8.refs_6_.refs_14_), channel_id=1, source_target_pairs={{0,4},{1,5},{2,6},{3,7},{4,0},{5,1},{6,2},{7,3},{8,12},{9,13},{10,... | collective-permute-start | bytes 393224 | tf_op jit(solution)/shard_map/ppermute | solution.py:547
  79.3 14.4 %collective-permute-start.7 = (bf16[128,512]{1,0:T(8,128)(2,1)S(1)}, bf16[128,512]{1,0:T(8,128)(2,1)S(1)}, u32[]{:S(2)}, u32[]{:S(2)}) collective-permute-start(bf16[128,512]{1,0:T(8,128)(2,1)S(1)} %collective-permute-done.6.refs_4_.refs_12_), channel_id=1, source_target_pairs={{0,4},{1,5},{2,6},{3,7},{4,0},{5,1},{6,2},{7,3},{8,12},{9,13},{10,... | collective-permute-start | bytes 393224 | tf_op jit(solution)/shard_map/ppermute | solution.py:547
  84.2 10.3 %collective-permute-start.5 = (bf16[128,512]{1,0:T(8,128)(2,1)S(1)}, bf16[128,512]{1,0:T(8,128)(2,1)S(1)}, u32[]{:S(2)}, u32[]{:S(2)}) collective-permute-start(bf16[128,512]{1,0:T(8,128)(2,1)S(1)} %collective-permute-done.4.refs_2_.refs_10_), channel_id=1, source_target_pairs={{0,4},{1,5},{2,6},{3,7},{4,0},{5,1},{6,2},{7,3},{8,12},{9,13},{10,... | collective-permute-start | bytes 393224 | tf_op jit(solution)/shard_map/ppermute | solution.py:547
  128.7 8.0 %collective-permute-start.72 = (f32[16,1024]{1,0:T(8,128)S(1)}, f32[16,1024]{1,0:T(8,128)S(1)}, u32[]{:S(2)}, u32[]{:S(2)}) collective-permute-start(f32[16,1024]{1,0:T(8,128)S(1)} %add.67), channel_id=1, source_target_pairs={{0,24},{1,25},{2,26},{3,27},{4,28},{5,29},{6,30},{7,31},{8,16},{9,... | collective-permute-start | bytes 196616 | tf_op jit(solution)/shard_map/ppermute | solution.py:547
  130.6 7.1 %collective-permute-start.71 = (f32[16,1024]{1,0:T(8,128)S(1)}, f32[16,1024]{1,0:T(8,128)S(1)}, u32[]{:S(2)}, u32[]{:S(2)}) collective-permute-start(f32[16,1024]{1,0:T(8,128)S(1)} %add.67), channel_id=1, source_target_pairs={{0,16},{1,17},{2,18},{3,19},{4,20},{5,21},{6,22},{7,23},{8,24},{9,... | collective-permute-start | bytes 196616 | tf_op jit(solution)/shard_map/ppermute | solution.py:547
  130.8 8.1 %collective-permute-start.70 = (f32[16,1024]{1,0:T(8,128)S(1)}, f32[16,1024]{1,0:T(8,128)S(1)}, u32[]{:S(2)}, u32[]{:S(2)}) collective-permute-start(f32[16,1024]{1,0:T(8,128)S(1)} %add.67), channel_id=1, source_target_pairs={{0,8},{1,9},{2,10},{3,11},{4,12},{5,13},{6,14},{7,15},{8,0},{9,1},... | collective-permute-start | bytes 196616 | tf_op jit(solution)/shard_map/ppermute | solution.py:547
  133.9 15.9 %collective-permute-start.62 = (bf16[64,1024]{1,0:T(8,128)(2,1)S(1)}, bf16[64,1024]{1,0:T(8,128)(2,1)S(1)}, u32[]{:S(2)}, u32[]{:S(2)}) collective-permute-start(bf16[64,1024]{1,0:T(8,128)(2,1)S(1)} %get-tuple-element.148), channel_id=1, source_target_pairs={{0,4},{1,5},{2,6},{3,7},{4,0},{5,1},{6,2},{7,3},{8,12},{9,13},{10,... | collective-permute-start | bytes 393224 | tf_op jit(solution)/shard_map/ppermute | solution.py:547
  134.9 8.4 %collective-permute-start.63 = (bf16[64,1024]{1,0:T(8,128)(2,1)S(1)}, bf16[64,1024]{1,0:T(8,128)(2,1)S(1)}, u32[]{:S(2)}, u32[]{:S(2)}) collective-permute-start(bf16[64,1024]{1,0:T(8,128)(2,1)S(1)} %get-tuple-element.150), channel_id=1, source_target_pairs={{0,4},{1,5},{2,6},{3,7},{4,0},{5,1},{6,2},{7,3},{8,12},{9,13},{10,... | collective-permute-start | bytes 393224 | tf_op jit(solution)/shard_map/ppermute | solution.py:547
  136.8 9.3 %collective-permute-start.65 = (bf16[64,1024]{1,0:T(8,128)(2,1)S(1)}, bf16[64,1024]{1,0:T(8,128)(2,1)S(1)}, u32[]{:S(2)}, u32[]{:S(2)}) collective-permute-start(bf16[64,1024]{1,0:T(8,128)(2,1)S(1)} %get-tuple-element.152), channel_id=1, source_target_pairs={{0,4},{1,5},{2,6},{3,7},{4,0},{5,1},{6,2},{7,3},{8,12},{9,13},{10,... | collective-permute-start | bytes 393224 | tf_op jit(solution)/shard_map/ppermute | solution.py:547
  137.7 11.2 %collective-permute-start.67 = (bf16[64,1024]{1,0:T(8,128)(2,1)S(1)}, bf16[64,1024]{1,0:T(8,128)(2,1)S(1)}, u32[]{:S(2)}, u32[]{:S(2)}) collective-permute-start(bf16[64,1024]{1,0:T(8,128)(2,1)S(1)} %get-tuple-element.154), channel_id=1, source_target_pairs={{0,4},{1,5},{2,6},{3,7},{4,0},{5,1},{6,2},{7,3},{8,12},{9,13},{10,... | collective-permute-start | bytes 393224 | tf_op jit(solution)/shard_map/ppermute | solution.py:547
  138.9 12.8 %collective-permute-start.52 = (bf16[128,512]{1,0:T(8,128)(2,1)S(1)}, bf16[128,512]{1,0:T(8,128)(2,1)S(1)}, u32[]{:S(2)}, u32[]{:S(2)}) collective-permute-start(bf16[128,512]{1,0:T(8,128)(2,1)S(1)} %get-tuple-element.135), channel_id=1, source_target_pairs={{0,4},{1,5},{2,6},{3,7},{4,0},{5,1},{6,2},{7,3},{8,12},{9,13},{10,... | collective-permute-start | bytes 393224 | tf_op jit(solution)/shard_map/ppermute | solution.py:547
  143.3 11.2 %collective-permute-start.53 = (bf16[128,512]{1,0:T(8,128)(2,1)S(1)}, bf16[128,512]{1,0:T(8,128)(2,1)S(1)}, u32[]{:S(2)}, u32[]{:S(2)}) collective-permute-start(bf16[128,512]{1,0:T(8,128)(2,1)S(1)} %get-tuple-element.137), channel_id=1, source_target_pairs={{0,4},{1,5},{2,6},{3,7},{4,0},{5,1},{6,2},{7,3},{8,12},{9,13},{10,... | collective-permute-start | bytes 393224 | tf_op jit(solution)/shard_map/ppermute | solution.py:547
  146.1 11.2 %collective-permute-start.55 = (bf16[128,512]{1,0:T(8,128)(2,1)S(1)}, bf16[128,512]{1,0:T(8,128)(2,1)S(1)}, u32[]{:S(2)}, u32[]{:S(2)}) collective-permute-start(bf16[128,512]{1,0:T(8,128)(2,1)S(1)} %get-tuple-element.139), channel_id=1, source_target_pairs={{0,4},{1,5},{2,6},{3,7},{4,0},{5,1},{6,2},{7,3},{8,12},{9,13},{10,... | collective-permute-start | bytes 393224 | tf_op jit(solution)/shard_map/ppermute | solution.py:547
  148.9 10.7 %collective-permute-start.57 = (bf16[128,512]{1,0:T(8,128)(2,1)S(1)}, bf16[128,512]{1,0:T(8,128)(2,1)S(1)}, u32[]{:S(2)}, u32[]{:S(2)}) collective-permute-start(bf16[128,512]{1,0:T(8,128)(2,1)S(1)} %get-tuple-element.141), channel_id=1, source_target_pairs={{0,4},{1,5},{2,6},{3,7},{4,0},{5,1},{6,2},{7,3},{8,12},{9,13},{10,... | collective-permute-start | bytes 393224 | tf_op jit(solution)/shard_map/ppermute | solution.py:547
  149.8 12.2 %collective-permute-start.42 = (bf16[128,896]{1,0:T(8,128)(2,1)S(1)}, bf16[128,896]{1,0:T(8,128)(2,1)S(1)}, u32[]{:S(2)}, u32[]{:S(2)}) collective-permute-start(bf16[128,896]{1,0:T(8,128)(2,1)S(1)} %get-tuple-element.123), channel_id=1, source_target_pairs={{0,4},{1,5},{2,6},{3,7},{4,0},{5,1},{6,2},{7,3},{8,12},{9,13},{10,... | collective-permute-start | bytes 688136 | tf_op jit(solution)/shard_map/ppermute | solution.py:547
  151.7 7.9 %collective-permute-start.75 = (f32[16,1024]{1,0:T(8,128)S(1)}, f32[16,1024]{1,0:T(8,128)S(1)}, u32[]{:S(2)}, u32[]{:S(2)}) collective-permute-start(f32[16,1024]{1,0:T(8,128)S(1)} %add_add_fusion.refs_0_), channel_id=1, source_target_pairs={{0,3},{1,2},{2,1},{3,0},{4,7},{5,6},{6,5},{7,4},{8,11},{9,10},{10,... | collective-permute-start | bytes 196616 | tf_op jit(solution)/shard_map/ppermute | solution.py:547
  154.5 5.6 %collective-permute-start.74 = (f32[16,1024]{1,0:T(8,128)S(1)}, f32[16,1024]{1,0:T(8,128)S(1)}, u32[]{:S(2)}, u32[]{:S(2)}) collective-permute-start(f32[16,1024]{1,0:T(8,128)S(1)} %add_add_fusion.refs_0_), channel_id=1, source_target_pairs={{0,2},{1,3},{2,0},{3,1},{4,6},{5,7},{6,4},{7,5},{8,10},{9,11},{10,... | collective-permute-start | bytes 196616 | tf_op jit(solution)/shard_map/ppermute | solution.py:547
  159.6 21.7 %collective-permute-start.36 = (f32[128,1024]{1,0:T(8,128)S(1)}, f32[128,1024]{1,0:T(8,128)S(1)}, u32[]{:S(2)}, u32[]{:S(2)}) collective-permute-start(f32[128,1024]{1,0:T(8,128)S(1)} %get-tuple-element.106), channel_id=1, source_target_pairs={{0,1},{1,0},{2,3},{3,2},{4,5},{5,4},{6,7},{7,6},{8,9},{9,8},{10,11... | collective-permute-start | bytes 1572872 | tf_op jit(solution)/shard_map/ppermute | solution.py:547
  159.6 23.3 %collective-permute-start.37 = (f32[128,1024]{1,0:T(8,128)S(1)}, f32[128,1024]{1,0:T(8,128)S(1)}, u32[]{:S(2)}, u32[]{:S(2)}) collective-permute-start(f32[128,1024]{1,0:T(8,128)S(1)} %get-tuple-element.108), channel_id=1, source_target_pairs={{0,1},{1,0},{2,3},{3,2},{4,5},{5,4},{6,7},{7,6},{8,9},{9,8},{10,11... | collective-permute-start | bytes 1572872 | tf_op jit(solution)/shard_map/ppermute | solution.py:547
  160.1 25.3 %collective-permute-start.39 = (f32[128,1024]{1,0:T(8,128)S(1)}, f32[128,1024]{1,0:T(8,128)S(1)}, u32[]{:S(2)}, u32[]{:S(2)}) collective-permute-start(f32[128,1024]{1,0:T(8,128)S(1)} %get-tuple-element.117), channel_id=1, source_target_pairs={{0,1},{1,0},{2,3},{3,2},{4,5},{5,4},{6,7},{7,6},{8,9},{9,8},{10,11... | collective-permute-start | bytes 1572872 | tf_op jit(solution)/shard_map/ppermute | solution.py:547
  160.2 25.3 %collective-permute-start.40 = (f32[128,1024]{1,0:T(8,128)S(1)}, f32[128,1024]{1,0:T(8,128)S(1)}, u32[]{:S(2)}, u32[]{:S(2)}) collective-permute-start(f32[128,1024]{1,0:T(8,128)S(1)} %get-tuple-element.119), channel_id=1, source_target_pairs={{0,1},{1,0},{2,3},{3,2},{4,5},{5,4},{6,7},{7,6},{8,9},{9,8},{10,11... | collective-permute-start | bytes 1572872 | tf_op jit(solution)/shard_map/ppermute | solution.py:547
  162.0 6.2 %collective-permute-start.43 = (bf16[128,896]{1,0:T(8,128)(2,1)S(1)}, bf16[128,896]{1,0:T(8,128)(2,1)S(1)}, u32[]{:S(2)}, u32[]{:S(2)}) collective-permute-start(bf16[128,896]{1,0:T(8,128)(2,1)S(1)} %get-tuple-element.125), channel_id=1, source_target_pairs={{0,4},{1,5},{2,6},{3,7},{4,0},{5,1},{6,2},{7,3},{8,12},{9,13},{10,... | collective-permute-start | bytes 688136 | tf_op jit(solution)/shard_map/ppermute | solution.py:547
  168.2 6.8 %collective-permute-start.45 = (bf16[128,896]{1,0:T(8,128)(2,1)S(1)}, bf16[128,896]{1,0:T(8,128)(2,1)S(1)}, u32[]{:S(2)}, u32[]{:S(2)}) collective-permute-start(bf16[128,896]{1,0:T(8,128)(2,1)S(1)} %get-tuple-element.127), channel_id=1, source_target_pairs={{0,4},{1,5},{2,6},{3,7},{4,0},{5,1},{6,2},{7,3},{8,12},{9,13},{10,... | collective-permute-start | bytes 688136 | tf_op jit(solution)/shard_map/ppermute | solution.py:547
  175.0 6.0 %collective-permute-start.47 = (bf16[128,896]{1,0:T(8,128)(2,1)S(1)}, bf16[128,896]{1,0:T(8,128)(2,1)S(1)}, u32[]{:S(2)}, u32[]{:S(2)}) collective-permute-start(bf16[128,896]{1,0:T(8,128)(2,1)S(1)} %get-tuple-element.129), channel_id=1, source_target_pairs={{0,4},{1,5},{2,6},{3,7},{4,0},{5,1},{6,2},{7,3},{8,12},{9,13},{10,... | collective-permute-start | bytes 688136 | tf_op jit(solution)/shard_map/ppermute | solution.py:547
  181.0 8.2 %collective-permute-start.64 = (bf16[64,1024]{1,0:T(8,128)(2,1)S(1)}, bf16[64,1024]{1,0:T(8,128)(2,1)S(1)}, u32[]{:S(2)}, u32[]{:S(2)}) collective-permute-start(bf16[64,1024]{1,0:T(8,128)(2,1)S(1)} %add_convert_fusion.5), channel_id=1, source_target_pairs={{0,8},{1,9},{2,10},{3,11},{4,12},{5,13},{6,14},{7,15},{8,0},{9,1},... | collective-permute-start | bytes 393224 | tf_op jit(solution)/shard_map/ppermute | solution.py:547
  181.3 13.0 %collective-permute-start.66 = (bf16[64,1024]{1,0:T(8,128)(2,1)S(1)}, bf16[64,1024]{1,0:T(8,128)(2,1)S(1)}, u32[]{:S(2)}, u32[]{:S(2)}) collective-permute-start(bf16[64,1024]{1,0:T(8,128)(2,1)S(1)} %add_convert_fusion.4), channel_id=1, source_target_pairs={{0,16},{1,17},{2,18},{3,19},{4,20},{5,21},{6,22},{7,23},{8,24},{9,... | collective-permute-start | bytes 393224 | tf_op jit(solution)/shard_map/ppermute | solution.py:547
  182.9 11.4 %collective-permute-start.68 = (bf16[64,1024]{1,0:T(8,128)(2,1)S(1)}, bf16[64,1024]{1,0:T(8,128)(2,1)S(1)}, u32[]{:S(2)}, u32[]{:S(2)}) collective-permute-start(bf16[64,1024]{1,0:T(8,128)(2,1)S(1)} %add_convert_fusion.3), channel_id=1, source_target_pairs={{0,24},{1,25},{2,26},{3,27},{4,28},{5,29},{6,30},{7,31},{8,16},{9,... | collective-permute-start | bytes 393224 | tf_op jit(solution)/shard_map/ppermute | solution.py:547
  185.4 17.4 %collective-permute-start.54 = (bf16[128,512]{1,0:T(8,128)(2,1)S(1)}, bf16[128,512]{1,0:T(8,128)(2,1)S(1)}, u32[]{:S(2)}, u32[]{:S(2)}) collective-permute-start(bf16[128,512]{1,0:T(8,128)(2,1)S(1)} %add_convert_fusion.8), channel_id=1, source_target_pairs={{0,8},{1,9},{2,10},{3,11},{4,12},{5,13},{6,14},{7,15},{8,0},{9,1},... | collective-permute-start | bytes 393224 | tf_op jit(solution)/shard_map/ppermute | solution.py:547
  185.4 24.6 %collective-permute-start.56 = (bf16[128,512]{1,0:T(8,128)(2,1)S(1)}, bf16[128,512]{1,0:T(8,128)(2,1)S(1)}, u32[]{:S(2)}, u32[]{:S(2)}) collective-permute-start(bf16[128,512]{1,0:T(8,128)(2,1)S(1)} %add_convert_fusion.7), channel_id=1, source_target_pairs={{0,16},{1,17},{2,18},{3,19},{4,20},{5,21},{6,22},{7,23},{8,24},{9,... | collective-permute-start | bytes 393224 | tf_op jit(solution)/shard_map/ppermute | solution.py:547
  189.2 21.8 %collective-permute-start.58 = (bf16[128,512]{1,0:T(8,128)(2,1)S(1)}, bf16[128,512]{1,0:T(8,128)(2,1)S(1)}, u32[]{:S(2)}, u32[]{:S(2)}) collective-permute-start(bf16[128,512]{1,0:T(8,128)(2,1)S(1)} %add_convert_fusion.6), channel_id=1, source_target_pairs={{0,24},{1,25},{2,26},{3,27},{4,28},{5,29},{6,30},{7,31},{8,16},{9,... | collective-permute-start | bytes 393224 | tf_op jit(solution)/shard_map/ppermute | solution.py:547
  194.3 18.7 %collective-permute-start.44 = (bf16[128,896]{1,0:T(8,128)(2,1)S(1)}, bf16[128,896]{1,0:T(8,128)(2,1)S(1)}, u32[]{:S(2)}, u32[]{:S(2)}) collective-permute-start(bf16[128,896]{1,0:T(8,128)(2,1)S(1)} %add_convert_fusion.2), channel_id=1, source_target_pairs={{0,8},{1,9},{2,10},{3,11},{4,12},{5,13},{6,14},{7,15},{8,0},{9,1},... | collective-permute-start | bytes 688136 | tf_op jit(solution)/shard_map/ppermute | solution.py:547
  194.3 25.5 %collective-permute-start.46 = (bf16[128,896]{1,0:T(8,128)(2,1)S(1)}, bf16[128,896]{1,0:T(8,128)(2,1)S(1)}, u32[]{:S(2)}, u32[]{:S(2)}) collective-permute-start(bf16[128,896]{1,0:T(8,128)(2,1)S(1)} %add_convert_fusion.1), channel_id=1, source_target_pairs={{0,16},{1,17},{2,18},{3,19},{4,20},{5,21},{6,22},{7,23},{8,24},{9,... | collective-permute-start | bytes 688136 | tf_op jit(solution)/shard_map/ppermute | solution.py:547
  202.9 30.6 %collective-permute-start.38 = (f32[128,1024]{1,0:T(8,128)}, f32[128,1024]{1,0:T(8,128)S(1)}, u32[]{:S(2)}, u32[]{:S(2)}) collective-permute-start(f32[128,1024]{1,0:T(8,128)} %get-tuple-element.110), channel_id=1, source_target_pairs={{0,2},{1,3},{2,0},{3,1},{4,6},{5,7},{6,4},{7,5},{8,10},{9,11},{10,... | collective-permute-start | bytes 1572872 | tf_op jit(solution)/shard_map/ppermute | solution.py:547
  210.1 25.4 %collective-permute-start.41 = (f32[128,1024]{1,0:T(8,128)}, f32[128,1024]{1,0:T(8,128)S(1)}, u32[]{:S(2)}, u32[]{:S(2)}) collective-permute-start(f32[128,1024]{1,0:T(8,128)} %get-tuple-element.121), channel_id=1, source_target_pairs={{0,2},{1,3},{2,0},{3,1},{4,6},{5,7},{6,4},{7,5},{8,10},{9,11},{10,... | collective-permute-start | bytes 1572872 | tf_op jit(solution)/shard_map/ppermute | solution.py:547
  211.0 9.6 %collective-permute-start.48 = (bf16[128,896]{1,0:T(8,128)(2,1)S(1)}, bf16[128,896]{1,0:T(8,128)(2,1)S(1)}, u32[]{:S(2)}, u32[]{:S(2)}) collective-permute-start(bf16[128,896]{1,0:T(8,128)(2,1)S(1)} %add_convert_fusion), channel_id=1, source_target_pairs={{0,24},{1,25},{2,26},{3,27},{4,28},{5,29},{6,30},{7,31},{8,16},{9,... | collective-permute-start | bytes 688136 | tf_op jit(solution)/shard_map/ppermute | solution.py:547
  213.0 8.6 %collective-permute-start.59 = (bf16[32,512]{1,0:T(8,128)(2,1)S(1)}, bf16[32,512]{1,0:T(8,128)(2,1)S(1)}, u32[]{:S(2)}, u32[]{:S(2)}) collective-permute-start(bf16[32,512]{1,0:T(8,128)(2,1)S(1)} %get-tuple-element.143), channel_id=1, source_target_pairs={{0,1},{1,0},{2,3},{3,2},{4,5},{5,4},{6,7},{7,6},{8,9},{9,8},{10,11... | collective-permute-start | bytes 98312 | tf_op jit(solution)/shard_map/ppermute | solution.py:547
  222.2 6.2 %collective-permute-start.49 = (bf16[32,896]{1,0:T(8,128)(2,1)}, bf16[32,896]{1,0:T(8,128)(2,1)S(1)}, u32[]{:S(2)}, u32[]{:S(2)}) collective-permute-start(bf16[32,896]{1,0:T(8,128)(2,1)} %get-tuple-element.131), channel_id=1, source_target_pairs={{0,1},{1,0},{2,3},{3,2},{4,5},{5,4},{6,7},{7,6},{8,9},{9,8},{10,11... | collective-permute-start | bytes 172040 | tf_op jit(solution)/shard_map/ppermute | solution.py:547
  (41 other events, 312.4 us)

commit v2 on v0

--- a/solution.py
+++ b/solution.py
@@ -1,6 +1,10 @@
+import functools
+
 import jax
 import jax.numpy as jnp
 from jax import lax
+from jax.experimental import pallas as pl
+from jax.experimental.pallas import tpu as pltpu
 from jax.sharding import PartitionSpec as P
 
 SCAN_ROWS = 64
@@ -8,6 +12,878 @@
 
 EPS = 1e-05
 HIGH = lax.Precision.HIGHEST
+BF = jnp.bfloat16
+F32 = jnp.float32
+NEG = -1e30
+LANES = 128
+QUAD = 4
+SMALL = 8
+VMEM_BYTES = 44 * 1024 * 1024
+RAW_BYTES = 60 * 1024 * 1024
+
+
+def mm(a, b):
+    return lax.dot_general(a, b, (((1,), (0,)), ((), ())), preferred_element_type=F32)
+
+
+def mm_t(a, b):
+    return lax.dot_general(a, b, (((1,), (1,)), ((), ())), preferred_element_type=F32)
+
+
+def mm_l(a, b):
+    return lax.dot_general(a, b, (((0,), (0,)), ((), ())), preferred_element_type=F32)
+
+
+def mm_high(a, b):
+    return lax.dot_general(
+        a, b, (((1,), (0,)), ((), ())), precision=HIGH, preferred_element_type=F32
+    )
+
+
+def call(kernel, out_shapes, inputs, scratch=(), flops=1e3, name=None, raw=(), limit=VMEM_BYTES):
+    in_specs = [
+        pl.BlockSpec(
+            memory_space=pltpu.HBM
+            if n in raw
+            else (pltpu.SMEM if a.dtype == jnp.int32 else pltpu.VMEM)
+        )
+        for n, a in enumerate(inputs)
+    ]
+    shapes = [jax.ShapeDtypeStruct(s, d) for s, d in out_shapes]
+    return pl.pallas_call(
+        kernel,
+        out_shape=shapes,
+        in_specs=in_specs,
+        out_specs=[pl.BlockSpec(memory_space=pltpu.VMEM)] * len(shapes),
+        scratch_shapes=list(scratch),
+        cost_estimate=pl.CostEstimate(flops=int(flops), bytes_accessed=1024, transcendentals=0),
+        compiler_params=pltpu.CompilerParams(vmem_limit_bytes=limit),
+        name=name,
+    )(*inputs)
+
+
+def iota(shape, axis):
+    return lax.broadcasted_iota(jnp.int32, shape, axis)
+
+
+def sigmoid(v):
+    return 1.0 / (1.0 + jnp.exp(-v))
+
+
+def softplus(v):
+    return jnp.maximum(v, 0.0) + jnp.log1p(jnp.exp(-jnp.abs(v)))
+
+
+def segment_of(position, ends):
+    seg = jnp.zeros(position.shape, jnp.int32)
+    for s in range(4):
+        seg = seg + (position >= ends[:, s : s + 1]).astype(jnp.int32)
+    return seg
+
+
+def same_masks(ends, rows, taps):
+    position = iota((rows, 1), 0)
+    seg = segment_of(position, ends)
+    masks = []
+    for k in range(1, taps):
+        seg_k = segment_of(position - k, ends)
+        masks.append(((seg == seg_k) & (position >= k)).astype(F32))
+    return masks
+
+
+def scan_bias(ends, rows):
+    seg_col = segment_of(iota((rows, 1), 0), ends)
+    seg_row = segment_of(iota((1, rows), 1), ends)
+    causal = (seg_col == seg_row) & (iota((rows, rows), 0) >= iota((rows, rows), 1))
+    return jnp.where(causal, 0.0, NEG)
+
+
+def tri_block(rows):
+    i, j = iota((rows, rows), 0), iota((rows, rows), 1)
+    return ((i >= j) & (i // SCAN_ROWS == j // SCAN_ROWS)).astype(F32)
+
+
+def steps_of(dt_raw, dtb, neg_rate, rows):
+    step = softplus(dt_raw + dtb)
+    log_decay = step * neg_rate
+    cum = mm_high(tri_block(rows), log_decay)
+    return step, log_decay, cum
+
+
+def decay_of(cum, cum_t, head, bias, cross):
+    dist = cum[:, head : head + 1] - cum_t[head : head + 1, :]
+    last = cum[SCAN_ROWS - 1 : SCAN_ROWS, head : head + 1]
+    return jnp.exp(dist + cross * last + bias)
+
+
+def conv_sum_of(xbc, cw, cb, masks):
+    total = cb + cw[0:1, :] * xbc
+    for k in range(1, len(masks) + 1):
+        total = total + cw[k : k + 1, :] * (pltpu.roll(xbc, k, 0) * masks[k - 1])
+    return total
+
+
+def pair_lanes(row, pair, low):
+    return jnp.where(low, row[:, 2 * pair : 2 * pair + 1], row[:, 2 * pair + 1 : 2 * pair + 2])
+
+
+def scan_kernel(proj_ref, ends_ref, cw_ref, head_ref, out_ref):
+    rows = LANES
+    width = out_ref.shape[1]
+    pairs = width // LANES
+    convw = width + 2 * LANES
+    dtb, rate, skip = head_ref[0:1, :], head_ref[1:2, :], head_ref[2:3, :]
+    neg_rate = -jnp.exp(rate)
+    cross = ((iota((rows, rows), 0) >= SCAN_ROWS) & (iota((rows, rows), 1) < SCAN_ROWS)).astype(F32)
+    low = iota((rows, LANES), 1) < LANES // 2
+
+    def body(b, carry):
+        at = pl.ds(pl.multiple_of(b * rows, rows), rows)
+        ends = ends_ref[pl.ds(b, 1), :].astype(jnp.int32)
+        bias = scan_bias(ends, rows)
+        masks = same_masks(ends, rows, 4)
+        xbc = proj_ref[at, 0:convw]
+        conv = conv_sum_of(xbc, cw_ref[...], cw_ref[4:5, :], masks)
+        act = conv * sigmoid(conv)
+        key, read = act[:, width : width + LANES], act[:, width + LANES : convw]
+        scores = mm_t(read.astype(BF), key.astype(BF))
+        step, _, cum = steps_of(proj_ref[at, convw : convw + LANES], dtb, neg_rate, rows)
+        cum_t = cum.T
+        for p in range(pairs):
+            lanes = slice(p * LANES, (p + 1) * LANES)
+            x = act[:, lanes]
+            xs = x * pair_lanes(step, p, low)
+            weight = jnp.concatenate(
+                [scores * decay_of(cum, cum_t, h, bias, cross) for h in (2 * p, 2 * p + 1)], 1
+            )
+            split = jnp.concatenate([jnp.where(low, xs, 0.0), jnp.where(low, 0.0, xs)], 0)
+            y = mm(weight.astype(BF), split.astype(BF))
+            out_ref[at, lanes] = y + pair_lanes(skip, p, low[0:1, :]) * x
+        return carry
+
+    lax.fori_loop(0, ends_ref.shape[0], body, 0)
+
+
+def scan_back_kernel(proj_ref, dscan_ref, ends_ref, cw_ref, head_ref, pc_ref, small_ref):
+    rows = LANES
+    width = dscan_ref.shape[1]
+    pairs = width // LANES
+    own = 2 * pairs
+    convw = width + 2 * LANES
+    dtb, rate, skip = head_ref[0:1, :], head_ref[1:2, :], head_ref[2:3, :]
+    neg_rate = -jnp.exp(rate)
+    src, dst = iota((rows, rows), 0), iota((rows, rows), 1)
+    cross = ((src < SCAN_ROWS) & (dst >= SCAN_ROWS)).astype(F32)
+    before = (src < dst).astype(F32)
+    reach = (src >= dst).astype(BF)
+    lane = iota((rows, LANES), 1)
+    low = lane < LANES // 2
+    by_head = (iota((width, LANES), 0) // (width // own) == iota((width, LANES), 1)).astype(F32)
+    small_ref[...] = jnp.zeros(small_ref.shape, F32)
+
+    def body(b, dskip):
+        at = pl.ds(pl.multiple_of(b * rows, rows), rows)
+        ends = ends_ref[pl.ds(b, 1), :].astype(jnp.int32)
+        seg_col = segment_of(iota((rows, 1), 0), ends)
+        seg_row = segment_of(iota((1, rows), 1), ends)
+        bias = jnp.where((seg_col == seg_row) & (src <= dst), 0.0, NEG)
+        masks = same_masks(ends, rows, 4)
+        xbc = proj_ref[at, 0:convw]
+        cw = cw_ref[...]
+        conv = conv_sum_of(xbc, cw, cw[4:5, :], masks)
+        sig = sigmoid(conv)
+        act = conv * sig
+        key = act[:, width : width + LANES].astype(BF)
+        read = act[:, width + LANES : convw].astype(BF)
+        scores = mm_t(key, read)
+        scores = jnp.concatenate([scores, scores], 1)
+        raw = proj_ref[at, convw : convw + LANES]
+        step, log_decay, cum = steps_of(raw, dtb, neg_rate, rows)
+        cum_t = cum.T
+        dscores = jnp.zeros((rows, 2 * rows), F32)
+        dlogs, dxs, prods, dsk = [], [], [], []
+        for p in range(pairs):
+            lanes = slice(p * LANES, (p + 1) * LANES)
+            x = act[:, lanes]
+            s = pair_lanes(step, p, low)
+            decays = []
+            for h in (2 * p, 2 * p + 1):
+                last = cum[SCAN_ROWS - 1 : SCAN_ROWS, h : h + 1]
+                dist = cum_t[h : h + 1, :] - cum[:, h : h + 1]
+                decays.append(jnp.exp(dist + (cross * last + bias)))
+            decay = jnp.concatenate(decays, 1)
+            weight = scores * decay
+            dy = dscan_ref[at, lanes]
+            split = jnp.concatenate([jnp.where(low, dy, 0.0), jnp.where(low, 0.0, dy)], 0).astype(BF)
+            dweight = mm_t((x * s).astype(BF), split)
+            dx_s = mm(weight.astype(BF), split)
+            dscores = dscores + dweight * decay
+            t = (dweight * weight).astype(BF)
+            span = mm(jnp.concatenate([t[:, 0:rows], t[:, rows:]], 0), reach)
+            dlogs.append(jnp.sum(span[0:rows, :] * before, axis=0, keepdims=True))
+            dlogs.append(jnp.sum(span[rows:, :] * before, axis=0, keepdims=True))
+            prods.append(dx_s * x)
+            dsk.append(jnp.sum(dy * x, axis=0, keepdims=True))
+            dxs.append(dx_s * s + pair_lanes(skip, p, low[0:1, :]) * dy)
+        dlog = jnp.concatenate(dlogs + [jnp.zeros((rows - own, rows), F32)], 0).T
+        dstep = mm_high(jnp.concatenate(prods, 1), by_head) + dlog * neg_rate
+        ddt = jnp.where(lane < own, dstep * sigmoid(raw + dtb), 0.0)
+        dsc = (dscores[:, 0:rows] + dscores[:, rows:]).astype(BF)
+        dkey = mm(dsc, read)
+        dread = mm_l(dsc, key)
+        dconv = jnp.concatenate(dxs + [dkey, dread], 1) * (sig * (1.0 + conv * (1.0 - sig)))
+        dxbc = cw[0:1, :] * dconv
+        small_ref[0:1, 0:convw] += jnp.sum(dconv * xbc, axis=0, keepdims=True)
+        for k in range(1, 4):
+            masked = dconv * masks[k - 1]
+            dxbc = dxbc + cw[k : k + 1, :] * pltpu.roll(masked, rows - k, 0)
+            small_ref[k : k + 1, 0:convw] += jnp.sum(
+                masked * pltpu.roll(xbc, k, 0), axis=0, keepdims=True
+            )
+        small_ref[4:5, 0:convw] += jnp.sum(dconv, axis=0, keepdims=True)
+        small_ref[5:6, width : width + LANES] += jnp.sum(ddt, axis=0, keepdims=True)
+        small_ref[5:6, width + LANES : width + 2 * LANES] += jnp.sum(
+            dlog * log_decay, axis=0, keepdims=True
+        )
+        pc_ref[at, 0:convw] = dxbc.astype(BF)
+        pc_ref[at, convw : convw + LANES] = ddt.astype(BF)
+        return dskip + jnp.concatenate(dsk, 1)
+
+    dskip = lax.fori_loop(0, ends_ref.shape[0], body, jnp.zeros((1, width), F32))
+    small_ref[5:6, width + 2 * LANES : width + 3 * LANES] = mm_high(dskip, by_head)
+
+
+def weave(out_ref, at, parts, size):
+    for k in range(8):
+        for half in range(QUAD // 2):
+            pair = [p[:, k * size : (k + 1) * size] for p in parts[2 * half : 2 * half + 2]]
+            lo = at + (k * QUAD + 2 * half) * size
+            out_ref[:, lo : lo + 2 * size] = jnp.concatenate(pair, 1)
+
+
+def pick_heads(parts, heads):
+    total = None
+    for q in range(QUAD):
+        sel = (iota((LANES, heads), 1) == iota((LANES, heads), 0) * QUAD + q).astype(F32)
+        got = mm_high(parts[q], sel)
+        total = got if total is None else total + got
+    return total
+
+
+def prep_kernel(me_ref, len_ref, w_hbm, tok_hbm, cot_hbm, wout_hbm, act_ref, wout_ref, *rest):
+    outs, scr, w_ref, tok_ref, cot_ref, sems = rest[0:4], *rest[4:]
+    copies = [
+        pltpu.make_async_copy(src, dst, sems.at[n])
+        for n, (src, dst) in enumerate(
+            ((w_hbm, w_ref), (tok_hbm, tok_ref), (cot_hbm, cot_ref), (wout_hbm, wout_ref))
+        )
+    ]
+    for c in copies:
+        c.start()
+    rows, model = tok_ref.shape
+    t = me_ref[0] & (QUAD - 1)
+    heads = 32
+    own = heads // QUAD
+    copies[0].wait()
+    w = w_ref[...].astype(F32)
+    inner = (w.shape[1] - heads - outs[0].shape[1] + LANES) * QUAD // (2 * (QUAD - 1))
+    size = inner // heads
+    conv_end = w.shape[1] - heads
+    shared = w[:, 2 * inner : conv_end]
+    dts = w[:, conv_end:].astype(BF)
+    for q in range(QUAD):
+        zs, xs = [], []
+        for k in range(own):
+            at = (k * QUAD + q) * size
+            zs.append(w[:, at : at + size])
+            xs.append(w[:, inner + at : inner + at + size])
+        pick = (iota((heads, LANES), 0) == iota((heads, LANES), 1) * QUAD + q) & (
+            iota((heads, LANES), 1) < own
+        )
+        scr[q] = jnp.concatenate(zs + xs + [shared, mm(dts, pick.astype(BF))], 1).astype(BF)
+    for r in range(QUAD):
+        outs[r][...] = scr[t ^ r]
+    lane = iota((16, model), 1)
+    end = jnp.int32(0)
+    tail = jnp.zeros((16, model), jnp.int32)
+    for s in range(4):
+        end = end + len_ref[s]
+        tail = tail + jnp.where(lane == s, end, 0)
+    act_ref[rows : rows + 16, :] = tail.astype(F32).astype(BF)
+    copies[1].wait()
+    act_ref[0:rows, :] = tok_ref[...]
+    copies[2].wait()
+    live = (iota((rows, 1), 0) < end).astype(F32)
+    act_ref[rows + 16 :, :] = (cot_ref[...].astype(F32) * live).astype(BF)
+    copies[3].wait()
+
+
+def params_kernel(me_ref, *refs):
+    raws, (cwb_ref, head_ref, gain_ref, pre_ref) = refs[0:7], refs[7:11]
+    cw_ref, cb_ref, dt_ref, al_ref, sk_ref, ng_ref, pg_ref = refs[11:18]
+    sems = refs[18]
+    copies = [
+        pltpu.make_async_copy(src, dst, sems.at[n])
+        for n, (src, dst) in enumerate(zip(raws, refs[11:18]))
+    ]
+    for c in copies:
+        c.start()
+    for c in copies:
+        c.wait()
+    pre_ref[...] = pg_ref[...]
+    t = me_ref[0] & (QUAD - 1)
+    heads = dt_ref.shape[1]
+    own = heads // QUAD
+    inner = ng_ref.shape[1]
+    width = inner // QUAD
+    size = inner // heads
+
+    def mine(a):
+        total = jnp.zeros((a.shape[0], width), F32)
+        for q in range(QUAD):
+            cut = [a[:, (k * QUAD + q) * size : (k * QUAD + q + 1) * size] for k in range(own)]
+            total = jnp.where(t == q, jnp.concatenate(cut, 1), total)
+        return total
+
+    taps = cw_ref.shape[0]
+    cwb_ref[...] = jnp.zeros(cwb_ref.shape, F32)
+    cwb_ref[0:taps, 0:width] = mine(cw_ref[...])
+    cwb_ref[0:taps, width:] = cw_ref[:, inner:]
+    cwb_ref[taps : taps + 1, 0:width] = mine(cb_ref[...])
+    cwb_ref[taps : taps + 1, width:] = cb_ref[:, inner:]
+    gain_ref[...] = mine(ng_ref[...])
+    pick = (iota((heads, LANES), 0) == iota((heads, LANES), 1) * QUAD + t) & (
+        iota((heads, LANES), 1) < own
+    )
+    rows = jnp.concatenate(
+        [dt_ref[...], al_ref[...], sk_ref[...], jnp.zeros((5, heads), F32)], 0
+    )
+    head_ref[...] = mm_high(rows, pick.astype(F32))
+
+
+def join_kernel(me_ref, c0, c1, c2, c3, wout_ref, a_ref, b_ref):
+    t = me_ref[0] & (QUAD - 1)
+    nrow = c0.shape[0]
+    width = b_ref.shape[1]
+    for r, c in enumerate((c0, c1, c2, c3)):
+        at = pl.ds(pl.multiple_of((t ^ r) * nrow, nrow), nrow)
+        a_ref[at, :] = c[:, width:]
+        b_ref[at, :] = c[:, 0:width]
+    size = wout_ref.shape[0]
+    b_ref[QUAD * nrow : QUAD * nrow + size, :] = wout_ref[:, 0:width]
+    b_ref[QUAD * nrow + size :, :] = wout_ref[:, width:]
+
+
+def project_kernel(me_ref, *refs):
+    chunks = 8
+    acts, ws = refs[0:QUAD], refs[QUAD : QUAD + chunks]
+    gain_ref, norm_ref, proj_ref, ends_ref = refs[QUAD + chunks :]
+    zy = me_ref[0] // QUAD
+    rows = ends_ref.shape[1]
+    for r in range(QUAD):
+        hidden = acts[r][0:rows, :].astype(F32)
+        scale = lax.rsqrt(jnp.mean(hidden * hidden, axis=1, keepdims=True) + EPS)
+        for k in range(chunks):
+            at = pl.ds(pl.multiple_of((zy ^ k) * LANES, LANES), LANES)
+            part = acts[r][0:rows, at].astype(F32) * scale * gain_ref[:, at]
+            norm_ref[r * rows : (r + 1) * rows, k * LANES : (k + 1) * LANES] = part.astype(BF)
+        ends_ref[r : r + 1, :] = acts[r][rows : rows + 16, 0:LANES].astype(F32)[0:1, :]
+    w = jnp.concatenate([c[...] for c in ws], axis=0)
+    proj_ref[...] = mm(norm_ref[...], w)
+
+
+def cot_kernel(me_ref, *refs):
+    chunks = 8
+    ws, acts = refs[0:chunks], refs[chunks : chunks + QUAD]
+    wfull_ref, cot_ref, dgn_ref = refs[chunks + QUAD :]
+    zy = me_ref[0] // QUAD
+    width = ws[0].shape[1]
+    size = width // chunks
+    rows = cot_ref.shape[0] // QUAD
+    for k in range(chunks):
+        at = pl.ds(pl.multiple_of((zy ^ k) * size, size), size)
+        base = ws[k].shape[0] - 2 * size
+        wfull_ref[at, 0:width] = ws[k][base : base + size, :]
+        wfull_ref[at, width:] = ws[k][base + size :, :]
+    for r in range(QUAD):
+        cot_ref[r * rows : (r + 1) * rows, :] = acts[r][rows + 16 :, :]
+    dgn_ref[...] = mm_t(cot_ref[...], wfull_ref[...])
+
+
+def gate_kernel(*refs):
+    chunks = 8
+    ws = refs[0:chunks]
+    norm_ref, scan_ref, dgn_ref, gain_ref, z_ref, stat_ref = refs[chunks:]
+    w = jnp.concatenate([c[0:LANES, :] for c in ws], axis=0)
+    z = mm(norm_ref[...], w)
+    z_ref[...] = z
+    gated = scan_ref[...] * (z * sigmoid(z))
+    s1 = jnp.sum(gated * gated, axis=1, keepdims=True)
+    s2 = jnp.sum(gain_ref[...] * dgn_ref[...] * gated, axis=1, keepdims=True)
+    lane = iota((z.shape[0], LANES), 1)
+    both = jnp.where(lane == 0, s1, 0.0) + jnp.where(lane == 1, s2, 0.0)
+    stat_ref[...] = both.T[0:8, :]
+
+
+def ungate_kernel(inner, me_ref, *refs):
+    chunks = 8
+    stats, ws = refs[0:QUAD], refs[QUAD : QUAD + chunks]
+    z_ref, scan_ref, dgn_ref, gain_ref, norm_ref, cot_ref = refs[QUAD + chunks : QUAD + chunks + 6]
+    gn_ref, dscan_ref, dz_ref, ngain_ref, pre_ref = refs[QUAD + chunks + 6 : QUAD + chunks + 11]
+    keeps, send67, send3, send1, scr = refs[QUAD + chunks + 11 : QUAD + chunks + 15], *refs[
+        QUAD + chunks + 15 :
+    ]
+    full = keeps[0].shape[0]
+    outs = {0: keeps[0], 2: keeps[1], 4: keeps[2], 5: keeps[3], 3: send3, 1: send1}
+    outs[6], outs[7] = send67.at[0:full, :], send67.at[full:, :]
+    zy = me_ref[0] // QUAD
+    rows = stats[0].shape[1] // QUAD
+    total = stats[0][...]
+    for r in range(1, QUAD):
+        total = total + jnp.concatenate(
+            [stats[r][:, (b ^ r) * rows : ((b ^ r) + 1) * rows] for b in range(QUAD)], 1
+        )
+    pad = jnp.concatenate([total, jnp.zeros((LANES - 8, total.shape[1]), F32)], 0).T
+    s1, s2 = pad[:, 0:1], pad[:, 1:2]
+    r = lax.rsqrt(s1 / inner + EPS)
+    z = z_ref[...]
+    sig = sigmoid(z)
+    silu = z * sig
+    scan = scan_ref[...]
+    gain = gain_ref[...]
+    unit = scan * silu * r
+    gn = (unit * gain).astype(BF)
+    gn_ref[...] = gn
+    scr[...] = mm_l(gn, cot_ref[...])
+    dgn = dgn_ref[...]
+    ngain_ref[...] = jnp.sum(dgn * unit, axis=0, keepdims=True)
+    dgated = r * (gain * dgn) - unit * (r * r * s2 / inner)
+    dscan_ref[...] = dgated * silu
+    dz = (dgated * scan * (sig * (1.0 + z * (1.0 - sig)))).astype(BF)
+    dz_ref[...] = dz
+    width = dz.shape[1]
+    size = width // chunks
+    lane = iota((LANES, LANES), 1)
+    pre = jnp.zeros((LANES, LANES), F32)
+    for k in range(chunks):
+        grad = mm_l(norm_ref[:, k * LANES : (k + 1) * LANES], dz)
+        dot = jnp.sum(grad * ws[k][0:LANES, :].astype(F32), axis=1, keepdims=True)
+        pre = pre + jnp.where(lane == k, dot, 0.0)
+        out = outs[k]
+        out[0:LANES, :] = grad.astype(out.dtype)
+        at = pl.ds(pl.multiple_of((zy ^ k) * size, size), size)
+        out[LANES : LANES + size, :] = scr[at, 0:width].astype(out.dtype)
+        out[LANES + size : LANES + 2 * size, :] = scr[at, width:].astype(out.dtype)
+    pre_ref[...] = pre
+
+
+def split_small(out_ref, base, small):
+    high = small.astype(BF)
+    low = (small - high.astype(F32)).astype(BF)
+    out_ref[base : base + 2 * SMALL, :] = jnp.concatenate(
+        [high.astype(F32), low.astype(F32)], 0
+    ).astype(BF)
+
+
+def joined_small(ref, base):
+    both = ref[base : base + 2 * SMALL, :].astype(F32)
+    return both[0:SMALL, :] + both[SMALL:, :]
+
+
+def ingrad_kernel(me_ref, norm_ref, pc_ref, small_ref, ngain_ref, preb_ref, gain_ref, *refs):
+    chunks = 8
+    ws = refs[0:chunks]
+    keeps, send67, send3, send1, mine_ref, scr = refs[chunks : chunks + 4], *refs[chunks + 4 :]
+    outs = {0: keeps[0], 2: keeps[1], 4: keeps[2], 5: keeps[3], 3: send3, 1: send1}
+    outs[6], outs[7] = send67.at[0:LANES, :], send67.at[LANES:, :]
+    zy = me_ref[0] // QUAD
+    lane = iota((LANES, LANES), 1)
+    pre = preb_ref[...]
+    for k in range(chunks):
+        grad = mm_l(norm_ref[:, k * LANES : (k + 1) * LANES], pc_ref[...])
+        dot = jnp.sum(grad * ws[k][...].astype(F32), axis=1, keepdims=True)
+        pre = pre + jnp.where(lane == k, dot, 0.0)
+        outs[k][0:LANES, :] = grad.astype(outs[k].dtype)
+    pre = pre.T
+    for k in range(chunks):
+        scr[pl.ds(zy ^ k, 1), :] = pre[k : k + 1, :]
+    wide = mine_ref.shape[1]
+    per = wide // LANES
+    gain = gain_ref[...]
+    placed = jnp.concatenate([scr[k : k + 1, :] for k in range(chunks)], 1) / gain
+    width = ngain_ref.shape[1]
+    mine_ref[...] = small_ref[...]
+    mine_ref[5:6, 0:width] = ngain_ref[...]
+    mine_ref[6:7, :] = placed[:, 0:wide]
+    mine_ref[7:8, 0 : (chunks - per) * LANES] = placed[:, wide:]
+    split_small(send3, LANES, mine_ref[...])
+
+
+def add_near_kernel(keep_ref, got_ref, small_ref, out_ref, sum_ref):
+    out_ref[0:LANES, :] = (keep_ref[...] + got_ref[0:LANES, :].astype(F32)).astype(BF)
+    total = small_ref[...] + joined_small(got_ref, LANES)
+    sum_ref[...] = total
+    split_small(out_ref, LANES, total)
+
+
+def add_two_kernel(keep_ref, got_ref, out_ref):
+    out_ref[...] = (keep_ref[...] + got_ref[...].astype(F32)).astype(BF)
+
+
+def add_side_kernel(keep_ref, got_ref, out_ref):
+    full = keep_ref.shape[0]
+    out_ref[...] = (keep_ref[...] + got_ref[full:, :].astype(F32)).astype(BF)
+
+
+def add_far_kernel(keep_ref, got_ref, side_ref, out_ref):
+    full = keep_ref.shape[0]
+    out_ref[...] = (
+        keep_ref[...] + got_ref[0:full, :].astype(F32) + side_ref[...].astype(F32)
+    ).astype(BF)
+
+
+def add_last_kernel(keep_ref, got_ref, side_ref, small_ref, near_ref, out_ref, sum_ref):
+    out_ref[0:LANES, :] = (
+        keep_ref[...] + got_ref[0:LANES, :].astype(F32) + side_ref[...].astype(F32)
+    ).astype(BF)
+    total = small_ref[...] + joined_small(near_ref, LANES)
+    sum_ref[...] = total
+    split_small(out_ref, LANES, total)
+
+
+def tail_kernel(me_ref, *refs):
+    chunks = 8
+    w1, w2 = refs[0:chunks], refs[chunks : 2 * chunks]
+    pc_ref, dz_ref, gn_ref, wfull_ref, keep_ref, send_ref = refs[2 * chunks :]
+    zy = me_ref[0] // QUAD
+    rows = keep_ref.shape[0] // 2
+    model = wfull_ref.shape[1]
+
+    def put(part, at):
+        keep_ref[0:rows, at] = part[0:rows, :]
+        send_ref[0:rows, at] = part[rows : 2 * rows, :].astype(BF)
+        keep_ref[rows:, at] = part[2 * rows : 3 * rows, :]
+        send_ref[rows:, at] = part[3 * rows :, :].astype(BF)
+
+    put(mm(gn_ref[...], wfull_ref[...]), pl.ds(0, model))
+    for k in range(chunks):
+        part = mm_t(pc_ref[...], w1[k][...]) + mm_t(dz_ref[...], w2[k][0:LANES, :])
+        put(part, pl.ds(pl.multiple_of(model + (zy ^ k) * LANES, LANES), LANES))
+
+
+def pair_kernel(keep_ref, got_ref, mine_ref, send_ref):
+    rows = mine_ref.shape[0]
+    total = keep_ref[...] + got_ref[...].astype(F32)
+    mine_ref[...] = total[0:rows, :]
+    send_ref[...] = total[rows:, :].astype(BF)
+
+
+def rows_kernel(act_ref, gain_ref, a_ref, b_ref, mixed_ref, grad_ref):
+    rows, model = mixed_ref.shape
+    hidden = act_ref[0:rows, :].astype(F32)
+    end = act_ref[rows : rows + 16, 0:LANES].astype(F32)[0:1, 3:4]
+    live = (iota((rows, 1), 0).astype(F32) < end).astype(F32)
+    total = a_ref[...] + b_ref[...].astype(F32)
+    mixed_ref[...] = (live * (hidden + total[:, 0:model])).astype(BF)
+    scale = lax.rsqrt(jnp.mean(hidden * hidden, axis=1, keepdims=True) + EPS)
+    dn = total[:, model:] * gain_ref[...]
+    inner = jnp.mean(dn * hidden, axis=1, keepdims=True)
+    back = scale * dn - hidden * (scale * scale * scale * inner)
+    grad_ref[...] = act_ref[rows + 16 :, :].astype(F32) + back
+
+
+def total_kernel(me_ref, *refs):
+    a, b, small_ref = refs[0:4], refs[4:8], refs[8]
+    wout_ref, mine_ref, msmall_ref, s1, s2, s3, scr = refs[9:]
+    t = me_ref[0] & (QUAD - 1)
+    nrow = mine_ref.shape[0]
+    chunk = QUAD * nrow
+    ta = a[0][...]
+    for got in a[1:]:
+        ta = ta + got[0:chunk, :].astype(F32)
+    small = small_ref[...] + joined_small(a[3], chunk)
+    tb = b[0][...].astype(F32)
+    for got in b[1:]:
+        tb = tb + got[...].astype(F32)
+    size = wout_ref.shape[0]
+    width = tb.shape[1]
+    wout_ref[:, 0:width] = tb[chunk : chunk + size, :]
+    wout_ref[:, width:] = tb[chunk + size :, :]
+    scr[:, 0:width] = tb[0:chunk, :]
+    scr[:, width:] = ta
+    msmall_ref[...] = small
+    for r, out in enumerate((mine_ref, s1, s2, s3)):
+        at = pl.ds(pl.multiple_of((t ^ r) * nrow, nrow), nrow)
+        out[0:nrow, :] = scr[at, :].astype(out.dtype)
+    wide = small.shape[1]
+    for out in (s1, s2, s3):
+        split_small(out.at[:, 0:wide], nrow, small)
+
+
+def finish_kernel(me_ref, mine_ref, msmall_ref, *refs):
+    got = refs[0:3]
+    out_ref, cw_ref, cb_ref, dt_ref, al_ref, sk_ref, ng_ref, pg_ref, scr, sscr, row_ref = refs[3:]
+    t = me_ref[0] & (QUAD - 1)
+    nrow = mine_ref.shape[0]
+    wide = msmall_ref.shape[1]
+    scr[t] = mine_ref[...]
+    sscr[t] = msmall_ref[...]
+    for r in range(1, QUAD):
+        scr[t ^ r] = got[r - 1][0:nrow, :].astype(F32)
+        sscr[t ^ r] = joined_small(got[r - 1].at[:, 0:wide], nrow)
+    inner = ng_ref.shape[1]
+    width = inner // QUAD
+    heads = dt_ref.shape[1]
+    size = inner // heads
+    conv_end = out_ref.shape[1] - heads
+    shared = 2 * width + conv_end - 2 * inner
+
+    def added(ref, rows, lanes):
+        return (ref[0][rows, lanes] + ref[1][rows, lanes]) + (ref[2][rows, lanes] + ref[3][rows, lanes])
+
+    every = slice(0, nrow)
+    weave(out_ref, 0, [scr[q][:, 0:width] for q in range(QUAD)], size)
+    weave(out_ref, inner, [scr[q][:, width : 2 * width] for q in range(QUAD)], size)
+    out_ref[:, 2 * inner : conv_end] = added(scr, every, slice(2 * width, shared))
+    out_ref[:, conv_end:] = pick_heads(
+        [scr[q][:, shared : shared + LANES] for q in range(QUAD)], heads
+    )
+    conv = shared - width
+    weave(cw_ref, 0, [sscr[q][0:4, 0:width] for q in range(QUAD)], size)
+    cw_ref[:, inner:] = added(sscr, slice(0, 4), slice(width, conv))
+    weave(row_ref, 0, [sscr[q][4:5, 0:width] for q in range(QUAD)], size)
+    row_ref[:, inner:] = added(sscr, slice(4, 5), slice(width, conv))
+    for n in range(cb_ref.shape[0]):
+        cb_ref[n : n + 1, :] = row_ref[:, n * LANES : (n + 1) * LANES]
+    weave(ng_ref, 0, [sscr[q][5:6, 0:width] for q in range(QUAD)], size)
+    lists = [
+        pick_heads([sscr[q][:, at : at + LANES] for q in range(QUAD)], heads)[5:6, :]
+        for at in (width, width + LANES, width + 2 * LANES)
+    ]
+    dt_ref[...], al_ref[...], sk_ref[...] = lists
+    pg_ref[:, 0:wide] = added(sscr, slice(6, 7), slice(0, wide))
+    pg_ref[:, wide:] = added(sscr, slice(7, 8), slice(0, pg_ref.shape[1] - wide))
+
+
+def quad_shards(
+    count,
+    tokens,
+    lengths,
+    in_weight,
+    out_weight,
+    conv_weight,
+    conv_bias,
+    dt_bias,
+    a_log,
+    skip_gain,
+    norm_gain,
+    pre_gain,
+    cotangent,
+):
+    chunks = count // QUAD
+    rows, model = tokens.shape
+    inner = norm_gain.shape[0]
+    heads = dt_bias.shape[0]
+    width = inner // QUAD
+    size = inner // heads
+    nrow, proj_width = in_weight.shape
+    convw = width + conv_bias.shape[0] - inner
+    wide = convw + LANES
+    both = width + wide
+    total_rows = QUAD * rows
+    chunk = QUAD * nrow
+    chunk_b = chunk + 2 * size
+
+    def swap(a, mask):
+        return lax.ppermute(a, "dp", [(i, i ^ mask) for i in range(count)])
+
+    def after(a, *others):
+        return lax.optimization_barrier((a,) + others)[0]
+
+    def gather(mine, later=()):
+        z = after(mine, *later) if later else mine
+        got = [mine, None, None, None, swap(z, 4 * QUAD), None, None, None]
+        got[2] = swap(z, 2 * QUAD)
+        got[1] = swap(mine, QUAD)
+        got[5] = swap(got[4], QUAD)
+        got[6] = swap(got[4], 2 * QUAD)
+        got[3] = swap(got[2], QUAD)
+        got[7] = swap(got[5], 2 * QUAD)
+        return got
+
+    me = lax.axis_index("dp").astype(jnp.int32).reshape(1)
+
+    prepped = call(
+        prep_kernel,
+        [((2 * rows + 16, model), BF), (out_weight.shape, BF)] + [((nrow, both), BF)] * QUAD,
+        [me, lengths, in_weight, tokens, cotangent, out_weight],
+        [
+            pltpu.VMEM((QUAD, nrow, both), BF),
+            pltpu.VMEM(in_weight.shape, BF),
+            pltpu.VMEM(tokens.shape, BF),
+            pltpu.VMEM(tokens.shape, BF),
+            pltpu.SemaphoreType.DMA((4,)),
+        ],
+        name="prep",
+        raw=(2, 3, 4, 5),
+        limit=RAW_BYTES,
+    )
+    act, own_out, cut = prepped[0], prepped[1], prepped[2:]
+    got = [swap(cut[r], r) for r in range(1, QUAD)]
+    shapes = [(4, conv_bias.shape[0])] + [(1, n) for n in (conv_bias.shape[0], heads, heads, heads, inner, model)]
+    cwb, by_head, gain, pre = call(
+        params_kernel,
+        [((8, convw), F32), ((8, LANES), F32), ((1, width), F32), ((1, model), F32)],
+        [me, conv_weight]
+        + [a[None, :] for a in (conv_bias, dt_bias, a_log, skip_gain, norm_gain, pre_gain)],
+        [pltpu.VMEM(a, F32) for a in shapes] + [pltpu.SemaphoreType.DMA((7,))],
+        name="params",
+        raw=tuple(range(1, 8)),
+        limit=RAW_BYTES,
+    )
+    got[1] = after(got[1], cwb, by_head, gain, pre)
+    own_a, own_b = call(
+        join_kernel,
+        [((chunk, wide), BF), ((chunk_b, width), BF)],
+        [me, cut[0]] + got + [own_out],
+        name="join",
+    )
+    w1 = gather(own_a)
+    w2 = gather(own_b, (w1[2],))
+    across = swap(act, 2)
+    acts = [act, swap(act, 1), across, swap(across, 1)]
+    normed, proj, ends = call(
+        project_kernel,
+        [((total_rows, model), BF), ((total_rows, wide), F32), ((QUAD, rows), F32)],
+        [me] + acts + w1 + [pre],
+        name="project",
+    )
+    (scan_out,) = call(
+        scan_kernel,
+        [((total_rows, width), F32)],
+        [proj, ends, cwb, by_head],
+        name="scan",
+    )
+    w_full, cot_all, dgn = call(
+        cot_kernel,
+        [((width, model), BF), ((total_rows, model), BF), ((total_rows, width), F32)],
+        [me] + w2 + acts,
+        name="normcot",
+    )
+    z, stat = call(
+        gate_kernel,
+        [((total_rows, width), F32), ((8, total_rows), F32)],
+        w2 + [normed, scan_out, dgn, gain],
+        name="gate",
+    )
+    stats = [stat] + [swap(stat, r) for r in range(1, QUAD)]
+    ungated = call(
+        functools.partial(ungate_kernel, float(inner)),
+        [
+            ((total_rows, width), BF),
+            ((total_rows, width), F32),
+            ((total_rows, width), BF),
+            ((1, width), F32),
+            ((LANES, LANES), F32),
+        ]
+        + [((chunk_b, width), F32)] * 4
+        + [((2 * chunk_b, width), BF)]
+        + [((chunk_b, width), BF)] * 2,
+        [me] + stats + w2 + [z, scan_out, dgn, gain, normed, cot_all],
+        [pltpu.VMEM((width, model), F32)],
+        name="ungate",
+    )
+    gn, dscan, dz, ngain_part, pre_b = ungated[0:5]
+    keep_b, (send67, send3, send1) = ungated[5:9], ungated[9:]
+    got67_b, got3_b, got1_b = swap(send67, 2 * QUAD), swap(send3, QUAD), swap(send1, QUAD)
+    pc1, small = call(
+        scan_back_kernel,
+        [((total_rows, wide), BF), ((SMALL, wide), F32)],
+        [proj, dscan, ends, cwb, by_head],
+        name="scanback",
+    )
+    ingrads = call(
+        ingrad_kernel,
+        [((chunk, wide), F32)] * 4
+        + [((2 * chunk, wide), BF), ((chunk + 2 * SMALL, wide), BF), ((chunk, wide), BF)]
+        + [((SMALL, wide), F32)],
+        [me, normed, pc1, small, ngain_part, pre_b, pre] + w1,
+        [pltpu.VMEM((chunks, LANES), F32)],
+        name="ingrad",
+    )
+    keep_a, (send67, send3, send1, small) = list(ingrads[0:4]), ingrads[4:8]
+    got67_a, got3_a, got1_a = swap(send67, 2 * QUAD), swap(send3, QUAD), swap(send1, QUAD)
+    got67_b = after(got67_b, small)
+    got3_b = after(got3_b, small)
+
+    (side,) = call(add_side_kernel, [((chunk_b, width), BF)], [keep_b[3], got67_b], name="side")
+    got5_b = swap(side, QUAD)
+    (near,) = call(add_two_kernel, [((chunk_b, width), BF)], [keep_b[1], got3_b], name="near")
+    got2_b = swap(near, 2 * QUAD)
+    (far,) = call(
+        add_far_kernel, [((chunk_b, width), BF)], [keep_b[2], got67_b, got5_b], name="far"
+    )
+    got4_b = swap(far, 4 * QUAD)
+
+    (side,) = call(add_side_kernel, [((chunk, wide), BF)], [keep_a[3], got67_a], name="side")
+    got5_a = swap(side, QUAD)
+    riding = [((chunk + 2 * SMALL, wide), BF), ((SMALL, wide), F32)]
+    near, small1 = call(add_near_kernel, riding, [keep_a[1], got3_a, small], name="near")
+    got2_a = swap(near, 2 * QUAD)
+    far, small2 = call(
+        add_last_kernel, riding, [keep_a[2], got67_a, got5_a, small1, got2_a], name="far"
+    )
+    got4_a = swap(far, 4 * QUAD)
+
+    pc1, dz = lax.optimization_barrier((pc1, dz, small))[0:2]
+    keep, send = call(
+        tail_kernel,
+        [((2 * rows, 2 * model), F32), ((2 * rows, 2 * model), BF)],
+        [me] + w1 + w2 + [pc1, dz, gn, w_full],
+        name="tail",
+    )
+    mine, send = call(
+        pair_kernel,
+        [((rows, 2 * model), F32), ((rows, 2 * model), BF)],
+        [keep, swap(send, 1)],
+        name="pair",
+    )
+    crossed = swap(send, 2)
+    mixed, tokens_grad = call(
+        rows_kernel,
+        [((rows, model), BF), ((rows, model), F32)],
+        [act, pre, mine, crossed],
+        name="rows",
+    )
+
+    out_shard, own, own_small, *cuts = call(
+        total_kernel,
+        [((size, model), F32), ((nrow, both), F32), ((SMALL, wide), F32)]
+        + [((nrow + 2 * SMALL, both), BF)] * 3,
+        [me, keep_a[0], got1_a, got2_a, got4_a, keep_b[0], got1_b, got2_b, got4_b, small2],
+        [pltpu.VMEM((chunk, both), F32)],
+        name="total",
+    )
+    own, mixed, tokens_grad = lax.optimization_barrier((own, mixed, tokens_grad))
+    done = call(
+        finish_kernel,
+        [
+            ((nrow, proj_width), F32),
+            (conv_weight.shape, F32),
+            ((conv_bias.shape[0] // LANES, LANES), F32),
+            ((1, heads), F32),
+            ((1, heads), F32),
+            ((1, heads), F32),
+            ((1, inner), F32),
+            ((1, model), F32),
+        ],
+        [me, own, own_small] + [swap(a, r + 1) for r, a in enumerate(cuts)],
+        [pltpu.VMEM((QUAD, nrow, both), F32), pltpu.VMEM((QUAD, SMALL, wide), F32), pltpu.VMEM((1, conv_bias.shape[0]), F32)],
+        name="finish",
+    )
+    return (mixed, tokens_grad, done[0], out_shard, done[1]) + tuple(
+        a.reshape(-1) for a in done[2:]
+    )
 
 
 def prenorm(hidden_in, gain_row):
@@ -188,8 +1064,10 @@
 
 
 def solution(mesh):
+    count = mesh.shape["dp"]
+    body = functools.partial(quad_shards, count) if count == 32 else shards
     return jax.shard_map(
-        shards,
+        body,
         mesh=mesh,
         in_specs=(
             P("dp", None),

time: 786 us -> 158 us (0.20); the launches traced: 772 us -> 158 us
  waiting for transfers between devices: 360 us -> 81.8 us
  local copies, waits for them, and re-layouts: 210 us -> 4.96 us
  matrix products: 94 us -> 0 us
  other arithmetic: 49.7 us -> 0 us
  blocking collectives: 40.9 us -> 0 us
  starting transfers between devices: 0.37 us -> 36 us
  Pallas kernels: 0 us -> 34.3 us
  between operations: 14.5 us -> 0.93 us
    reduce_scatter x2 -> x0, waiting for transfers between devices: 279 us -> none  [the longest x1 148 us: shards(): lax.psum_scatter(out_grad, 'dp', scatter_dimension=0, tiled=True)]
    dynamic_update_slice x8 -> x0, local copies, waits for them, and re-layouts: 106 us -> none  [mixer_core(): _, scanned = lax.scan(jax.checkpoint(block_step), start, items)]
    dot_general x32 -> x0, matrix products: 92 us -> none  [the longest x6 21 us: block_step(): inside = jnp.einsum('ijh,jhp->ihp', weighting, values, precision=HIGH)]
    ppermute x0 -> x40, waiting for transfers between devices: none -> 81.8 us  [swap(): return lax.ppermute(a, 'dp', [(i, i ^ mask) for i in range(count)])]
    all_gather x2 -> x0, waiting for transfers between devices: 79 us -> none  [the longest x1 78.9 us: shards(): lax.all_gather(in_weight, 'dp', axis=0, tiled=True)]
    reshape x15 -> x0, local copies, waits for them, and re-layouts: 43.8 us -> none  [the longest x1 20.2 us: shards(): in_wide = in_grad.reshape(2 * in_grad.shape[0], proj_width // 2)]
    psum x1 -> x0, blocking collectives: 40.9 us -> none  [shards(): lax.psum((conv_w_grad, conv_b_grad, bias_dt_grad, decay_grad, skip_grad,...]
    ppermute x0 -> x40, starting transfers between devices: none -> 36 us  [swap(): return lax.ppermute(a, 'dp', [(i, i ^ mask) for i in range(count)])]
  transfers between devices with their start and end apart: 4 -> 40, of which waited for: 3 -> 20; matrix products, arithmetic and copies ran while one was open for 19% -> 1% of each run, Pallas kernels for 0% -> 6%
where the time goes in v2:
time: 158 us
  waiting for transfers between devices  81.8 us (52%)
  starting transfers between devices  36 us (23%)
  Pallas kernels  34.3 us (22%)
  local copies, waits for them, and re-layouts  4.96 us (3%)
    ppermute x40, waiting for transfers between devices, swap(): return lax.ppermute(a, 'dp', [(i, i ^ mask) for i in range(count)])  81.8 us
    ppermute x40, starting transfers between devices, swap(): return lax.ppermute(a, 'dp', [(i, i ^ mask) for i in range(count)])  36 us
    pallas_call x21, Pallas kernels, call(): pl.pallas_call(kernel, out_shape=shapes, in_specs=in_specs, out_specs=[pl...  34.3 us
    unnamed x26, local copies, waits for them, and re-layouts  3.65 us
  transfers between devices with their start and end apart: 40, of which 20 were waited for; matrix products, arithmetic and copies ran while one was open for 1% of the time, Pallas kernels for 6%

profile of v2, /device:TPU:0, one launch (start us, length us, event | category | flops | bytes accessed | tf_op | source)
XLA Modules:
  0.0 158.0 jit_solution(14947662288462402467)
XLA Ops:
  0.6 2.9 %prep.1 = (bf16[272,1024]{1,0:T(8,128)(2,1)}, bf16[64,1024]{1,0:T(8,128)(2,1)}, bf16[32,1408]{1,0:T(8,128)(2,1)}, bf16[32,1408]{1,0:T(8,128)(2,1)}, bf16[32,1408]{1,0:T(8,128)(2,1)}, /*index=5*/bf16[32,1408]{1,0:T(8,128)(2,1)}) custom-call(s32[1]{0:T(128)} %bitcast.me_ref, s32[4]{0:T(128)} %len_ref.1, bf16[32,4384]{1,0:T(8,128)(2,1)} %w_hbm.1, ...), custom_call_target="tpu_custom_call" | custom-call | flops 1000 | bytes 1024 | tf_op jit(solution)/shard_map/prep/pallas_call | solution.py:53
  3.5 3.0 %collective-permute-start.4 = (bf16[32,1408]{1,0:T(8,128)(2,1)}, bf16[32,1408]{1,0:T(8,128)(2,1)S(1)}, u32[]{:S(2)}, u32[]{:S(2)}) collective-permute-start(bf16[32,1408]{1,0:T(8,128)(2,1)} %get-tuple-element.89), channel_id=1, source_target_pairs={{0,2},{1,3},{2,0},{3,1},{4,6},{5,7},{6,4},{7,5},{8,10},{9,11},{10,... | collective-permute-start | bytes 270344 | tf_op jit(solution)/shard_map/ppermute | solution.py:698
  6.8 1.3 broadcast_in_dim.18.refs_1_
  8.1 1.6 %params.1 = (f32[8,768]{1,0:T(8,128)}, f32[8,128]{1,0:T(8,128)}, f32[1,512]{1,0:T(1,128)}, f32[1,1024]{1,0:T(1,128)}) custom-call(s32[1]{0:T(128)} %bitcast.me_ref, f32[4,2304]{1,0:T(4,128)} %refs_0_.1, f32[1,2304]{1,0:T(1,128)} %broadcast_in_dim.18.refs_1_, f32[1,32]{1,0:T(1,128)} %bitcast.14, f32[1,32]{1,0:T(1,128)} %bitcast.15, f32[1,32]{1,0:T(1,128)} %bitcast.16, ...), custom_call_target="tpu_custom_call" | custom-call | flops 1000 | bytes 1024 | tf_op jit(solution)/shard_map/params/pallas_call | solution.py:53
  9.7 1.3 collective-permute-done.5.c3
  11.0 0.9 copy-done.6
  11.9 0.9 copy-done.8
  12.9 2.7 %collective-permute-start.9 = (bf16[128,896]{1,0:T(8,128)(2,1)S(1)}, bf16[128,896]{1,0:T(8,128)(2,1)S(1)}, u32[]{:S(2)}, u32[]{:S(2)}) collective-permute-start(bf16[128,896]{1,0:T(8,128)(2,1)S(1)} %get-tuple-element.97.refs_4_.refs_0_), channel_id=1, source_target_pairs={{0,16},{1,17},{2,18},{3,19},{4,20},{5,21},{6,22},{7,23},{8,24},{9,... | collective-permute-start | bytes 688136 | tf_op jit(solution)/shard_map/ppermute | solution.py:698
  15.6 1.1 collective-permute-start.1
  16.7 1.6 collective-permute-start.7
  18.3 1.5 collective-permute-start.6
  19.8 7.0 %collective-permute-done.9.refs_8_.refs_4_ = bf16[128,896]{1,0:T(8,128)(2,1)S(1)} collective-permute-done((bf16[128,896]{1,0:T(8,128)(2,1)S(1)}, bf16[128,896]{1,0:T(8,128)(2,1)S(1)}, u32[]{:S(2)}, u32[]{:S(2)}) %collective-permute-start.9) | collective-permute-done | bytes 229408 | tf_op jit(solution)/shard_map/ppermute | solution.py:698
  26.8 0.7 collective-permute-start.11
  27.5 0.7 collective-permute-done.7.refs_6_.refs_2_
  28.2 2.8 %collective-permute-start.16 = (bf16[256,512]{1,0:T(8,128)(2,1)S(1)}, bf16[256,512]{1,0:T(8,128)(2,1)S(1)}, u32[]{:S(2)}, u32[]{:S(2)}) collective-permute-start(bf16[256,512]{1,0:T(8,128)(2,1)S(1)} %get-tuple-element.101.refs_0_.refs_4_.refs_8_), channel_id=1, source_target_pairs={{0,16},{1,17},{2,18},{3,19},{4,20},{5,21},{6,22},{7,23},{8,24},{9,... | collective-permute-start | bytes 786440 | tf_op jit(solution)/shard_map/ppermute | solution.py:698
  31.0 1.5 collective-permute-start.10
  32.5 5.4 %collective-permute-done.11.refs_10_.refs_6_ = bf16[128,896]{1,0:T(8,128)(2,1)S(1)} collective-permute-done((bf16[128,896]{1,0:T(8,128)(2,1)S(1)}, bf16[128,896]{1,0:T(8,128)(2,1)S(1)}, u32[]{:S(2)}, u32[]{:S(2)}) %collective-permute-start.11) | collective-permute-done | bytes 229408 | tf_op jit(solution)/shard_map/ppermute | solution.py:698
  37.9 1.5 collective-permute-start.8
  39.4 0.3 collective-permute-start.14
  39.8 4.0 %collective-permute-done.16.refs_4_.refs_8_.refs_12_ = bf16[256,512]{1,0:T(8,128)(2,1)S(1)} collective-permute-done((bf16[256,512]{1,0:T(8,128)(2,1)S(1)}, bf16[256,512]{1,0:T(8,128)(2,1)S(1)}, u32[]{:S(2)}, u32[]{:S(2)}) %collective-permute-start.16) | collective-permute-done | bytes 262176 | tf_op jit(solution)/shard_map/ppermute | solution.py:698
  43.7 1.5 collective-permute-start.17
  45.2 0.6 collective-permute-start.13
  45.8 3.5 %collective-permute-done.14.refs_2_.refs_6_.refs_10_ = bf16[256,512]{1,0:T(8,128)(2,1)S(1)} collective-permute-done((bf16[256,512]{1,0:T(8,128)(2,1)S(1)}, bf16[256,512]{1,0:T(8,128)(2,1)S(1)}, u32[]{:S(2)}, u32[]{:S(2)}) %collective-permute-start.14) | collective-permute-done | bytes 262176 | tf_op jit(solution)/shard_map/ppermute | solution.py:698
  49.3 4.9 %collective-permute-done.12.refs_11_.refs_7_ = bf16[128,896]{1,0:T(8,128)(2,1)S(1)} collective-permute-done((bf16[128,896]{1,0:T(8,128)(2,1)S(1)}, bf16[128,896]{1,0:T(8,128)(2,1)S(1)}, u32[]{:S(2)}, u32[]{:S(2)}) %collective-permute-start.12) | collective-permute-done | bytes 229408 | tf_op jit(solution)/shard_map/ppermute | solution.py:698
  54.2 1.5 collective-permute-start.15
  55.7 1.0 copy-done.2
  56.8 0.7 copy-done.9
  57.5 1.5 project.1
  59.0 4.2 %scan.1.refs_9_.refs_13_ = f32[512,512]{1,0:T(8,128)S(1)} custom-call(f32[512,896]{1,0:T(8,128)S(1)} %get-tuple-element.99.proj_ref, f32[4,128]{1,0:T(4,128)S(1)} %get-tuple-element.102.ends_ref, f32[8,768]{1,0:T(8,128)S(1)} %copy-done.7, f32[8,128]{1,0:T(8,128)S(1)} %copy-done.11), custom_call_target="tpu_custom_call" | custom-call | flops 1000 | bytes 1024 | tf_op jit(solution)/shard_map/scan/pallas_call | solution.py:53
  63.2 2.1 %collective-permute-done.19.refs_7_.refs_11_.refs_15_ = bf16[256,512]{1,0:T(8,128)(2,1)S(1)} collective-permute-done((bf16[256,512]{1,0:T(8,128)(2,1)S(1)}, bf16[256,512]{1,0:T(8,128)(2,1)S(1)}, u32[]{:S(2)}, u32[]{:S(2)}) %collective-permute-start.19) | collective-permute-done | bytes 262176 | tf_op jit(solution)/shard_map/ppermute | solution.py:698
  65.4 0.8 normcot.1
  66.2 1.2 gate.1
  67.5 1.0 collective-permute-start.22
  68.5 0.7 collective-permute-start.21
  69.4 1.3 collective-permute-done.22.refs_3_
  70.7 1.6 collective-permute-done.21.refs_2_
  72.2 4.2 %ungate.1 = (bf16[512,512]{1,0:T(8,128)(2,1)S(1)}, f32[512,512]{1,0:T(8,128)S(1)}, bf16[512,512]{1,0:T(8,128)(2,1)S(1)}, f32[1,512]{1,0:T(1,128)S(1)}, f32[128,1...) custom-call(s32[1]{0:T(128)} %bitcast.me_ref, ...), custom_call_target="tpu_custom_call" | custom-call | flops 1000 | bytes 1024 | tf_op jit(solution)/shard_map/ungate/pallas_call | solution.py:53
  76.5 7.9 %scanback.1 = (bf16[512,896]{1,0:T(8,128)(2,1)S(1)}, f32[8,896]{1,0:T(8,128)S(1)}) custom-call(f32[512,896]{1,0:T(8,128)S(1)} %get-tuple-element.99.proj_ref, f32[512,512]{1,0:T(8,128)S(1)} %get-tuple-element.107.dscan_ref, f32[4,128]{1,0:T(4,128)S(1)} %get-tuple-element.102.ends_ref, f32[8,768]{1,0:T(8,128)S(1)} %copy-done.7, f32[8,128]{1,0:T(8,128)S(1)} %copy-done.11), custom_call_target="tpu_custom_call" | custom-call | flops 1000 | bytes 1024 | tf_op jit(solution)/shard_map/scanback/pallas_call | solution.py:53
  84.3 1.6 %ingrad.1 = (f32[128,896]{1,0:T(8,128)S(1)}, f32[128,896]{1,0:T(8,128)S(1)}, f32[128,896]{1,0:T(8,128)S(1)}, f32[128,896]{1,0:T(8,128)S(1)}, bf16[256,896]{1,0:T...) custom-call(s32[1]{0:T(128)} %bitcast.me_ref, ...), custom_call_target="tpu_custom_call" | custom-call | flops 1000 | bytes 1024 | tf_op jit(solution)/shard_map/ingrad/pallas_call | solution.py:53
  86.0 3.7 %tail.1 = (f32[256,2048]{1,0:T(8,128)S(1)}, bf16[256,2048]{1,0:T(8,128)(2,1)S(1)}) custom-call(s32[1]{0:T(128)} %bitcast.me_ref, bf16[128,896]{1,0:T(8,128)(2,1)S(1)} %get-tuple-element.97.refs_4_.refs_0_, bf16[128,896]{1,0:T(8,128)(2,1)S(1)} %collective-permute-done.6.refs_5_.refs_1_, bf16[128,896]{1,0:T(8,128)(2,1)S(1)} %collective-permute-done.7.refs_6_.refs_2_, ...), custom_call_target="tpu_custom_call" | custom-call | flops 1000 | bytes 1024 | tf_op jit(solution)/shard_map/tail/pallas_call | solution.py:53
  89.9 2.0 %collective-permute-start.26 = (bf16[256,896]{1,0:T(8,128)(2,1)S(1)}, bf16[256,896]{1,0:T(8,128)(2,1)S(1)}, u32[]{:S(2)}, u32[]{:S(2)}) collective-permute-start(bf16[256,896]{1,0:T(8,128)(2,1)S(1)} %get-tuple-element.119), channel_id=1, source_target_pairs={{0,8},{1,9},{2,10},{3,11},{4,12},{5,13},{6,14},{7,15},{8,0},{9,1},... | collective-permute-start | bytes 1376264 | tf_op jit(solution)/shard_map/ppermute | solution.py:698
  91.9 1.5 collective-permute-start.24
  93.4 0.5 collective-permute-start.30
  93.9 10.7 %collective-permute-done.32.got_ref = bf16[512,512]{1,0:T(8,128)(2,1)S(1)} collective-permute-done((bf16[512,512]{1,0:T(8,128)(2,1)S(1)}, bf16[512,512]{1,0:T(8,128)(2,1)S(1)}, u32[]{:S(2)}, u32[]{:S(2)}) %collective-permute-start.32) | collective-permute-done | bytes 524320 | tf_op jit(solution)/shard_map/ppermute | solution.py:698
  104.6 1.6 %collective-permute-start.33 = (bf16[256,512]{1,0:T(8,128)(2,1)S(1)}, bf16[256,512]{1,0:T(8,128)(2,1)S(1)}, u32[]{:S(2)}, u32[]{:S(2)}) collective-permute-start(bf16[256,512]{1,0:T(8,128)(2,1)S(1)} %side.3), channel_id=1, source_target_pairs={{0,4},{1,5},{2,6},{3,7},{4,0},{5,1},{6,2},{7,3},{8,12},{9,13},{10,... | collective-permute-start | bytes 786440 | tf_op jit(solution)/shard_map/ppermute | solution.py:698
  106.4 8.0 %collective-permute-done.26.got_ref = bf16[256,896]{1,0:T(8,128)(2,1)S(1)} collective-permute-done((bf16[256,896]{1,0:T(8,128)(2,1)S(1)}, bf16[256,896]{1,0:T(8,128)(2,1)S(1)}, u32[]{:S(2)}, u32[]{:S(2)}) %collective-permute-start.26) | collective-permute-done | bytes 458784 | tf_op jit(solution)/shard_map/ppermute | solution.py:698
  114.4 1.6 %collective-permute-start.27 = (bf16[128,896]{1,0:T(8,128)(2,1)S(1)}, bf16[128,896]{1,0:T(8,128)(2,1)S(1)}, u32[]{:S(2)}, u32[]{:S(2)}) collective-permute-start(bf16[128,896]{1,0:T(8,128)(2,1)S(1)} %side.2), channel_id=1, source_target_pairs={{0,4},{1,5},{2,6},{3,7},{4,0},{5,1},{6,2},{7,3},{8,12},{9,13},{10,... | collective-permute-start | bytes 688136 | tf_op jit(solution)/shard_map/ppermute | solution.py:698
  116.0 0.5 collective-permute-start.23
  116.8 0.8 collective-permute-start.36
  117.6 1.3 collective-permute-start.29
  119.0 0.5 collective-permute-done.25.near_ref.refs_2_
  119.8 3.3 %collective-permute-done.27.side_ref = bf16[128,896]{1,0:T(8,128)(2,1)S(1)} collective-permute-done((bf16[128,896]{1,0:T(8,128)(2,1)S(1)}, bf16[128,896]{1,0:T(8,128)(2,1)S(1)}, u32[]{:S(2)}, u32[]{:S(2)}) %collective-permute-start.27) | collective-permute-done | bytes 229408 | tf_op jit(solution)/shard_map/ppermute | solution.py:698
  123.1 0.7 collective-permute-start.34
  123.8 4.2 %collective-permute-done.23.refs_1_ = bf16[128,896]{1,0:T(8,128)(2,1)S(1)} collective-permute-done((bf16[128,896]{1,0:T(8,128)(2,1)S(1)}, bf16[128,896]{1,0:T(8,128)(2,1)S(1)}, u32[]{:S(2)}, u32[]{:S(2)}) %collective-permute-start.23) | collective-permute-done | bytes 229408 | tf_op jit(solution)/shard_map/ppermute | solution.py:698
  128.0 0.7 collective-permute-start.28
  128.6 3.1 %collective-permute-done.29.refs_5_ = bf16[256,512]{1,0:T(8,128)(2,1)S(1)} collective-permute-done((bf16[256,512]{1,0:T(8,128)(2,1)S(1)}, bf16[256,512]{1,0:T(8,128)(2,1)S(1)}, u32[]{:S(2)}, u32[]{:S(2)}) %collective-permute-start.29) | collective-permute-done | bytes 262176 | tf_op jit(solution)/shard_map/ppermute | solution.py:698
  131.8 14.8 %collective-permute-done.28.refs_3_ = bf16[144,896]{1,0:T(8,128)(2,1)S(1)} collective-permute-done((bf16[144,896]{1,0:T(8,128)(2,1)S(1)}, bf16[144,896]{1,0:T(8,128)(2,1)S(1)}, u32[]{:S(2)}, u32[]{:S(2)}) %collective-permute-start.28) | collective-permute-done | bytes 258080 | tf_op jit(solution)/shard_map/ppermute | solution.py:698
  146.6 1.1 total.1
  147.7 0.5 collective-permute-start.38
  148.2 1.4 collective-permute-start.39
  149.6 1.2 rows.1
  150.8 3.3 %collective-permute-done.38.refs_1_ = bf16[48,1408]{1,0:T(8,128)(2,1)S(1)} collective-permute-done((bf16[48,1408]{1,0:T(8,128)(2,1)S(1)}, bf16[48,1408]{1,0:T(8,128)(2,1)S(1)}, u32[]{:S(2)}, u32[]{:S(2)}) %collective-permute-start.38) | collective-permute-done | bytes 135200 | tf_op jit(solution)/shard_map/ppermute | solution.py:698
  154.1 2.1 %collective-permute-done.39.refs_2_ = bf16[48,1408]{1,0:T(8,128)(2,1)S(1)} collective-permute-done((bf16[48,1408]{1,0:T(8,128)(2,1)S(1)}, bf16[48,1408]{1,0:T(8,128)(2,1)S(1)}, u32[]{:S(2)}, u32[]{:S(2)}) %collective-permute-start.39) | collective-permute-done | bytes 135200 | tf_op jit(solution)/shard_map/ppermute | solution.py:698
  156.2 1.7 %finish.1 = (f32[32,4384]{1,0:T(8,128)}, f32[4,2304]{1,0:T(4,128)}, f32[18,128]{1,0:T(8,128)}, f32[1,32]{1,0:T(1,128)}, f32[1,32]{1,0:T(1,128)}, /*index=5*/f32[...) custom-call(s32[1]{0:T(128)} %bitcast.me_ref, f32[32,1408]{1,0:T(8,128)S(1)} %get-tuple-element.147.mine_ref, ...), custom_call_target="tpu_custom_call" | custom-call | flops 1000 | bytes 1024 | tf_op jit(solution)/shard_map/finish/pallas_call | solution.py:53
  (64 shorter events, 1.8 us)
Async XLA Ops:
  3.5 6.2 %collective-permute-start.4 = (bf16[32,1408]{1,0:T(8,128)(2,1)}, bf16[32,1408]{1,0:T(8,128)(2,1)S(1)}, u32[]{:S(2)}, u32[]{:S(2)}) collective-permute-start(bf16[32,1408]{1,0:T(8,128)(2,1)} %get-tuple-element.89), channel_id=1, source_target_pairs={{0,2},{1,3},{2,0},{3,1},{4,6},{5,7},{6,4},{7,5},{8,10},{9,11},{10,... | collective-permute-start | bytes 270344 | tf_op jit(solution)/shard_map/ppermute | solution.py:698
  6.5 3.2 %collective-permute-start.3 = (bf16[32,1408]{1,0:T(8,128)(2,1)}, bf16[32,1408]{1,0:T(8,128)(2,1)S(1)}, u32[]{:S(2)}, u32[]{:S(2)}) collective-permute-start(bf16[32,1408]{1,0:T(8,128)(2,1)} %get-tuple-element.88), channel_id=1, source_target_pairs={{0,1},{1,0},{2,3},{3,2},{4,5},{5,4},{6,7},{7,6},{8,9},{9,8},{10,11... | collective-permute-start | bytes 270344 | tf_op jit(solution)/shard_map/ppermute | solution.py:698
  6.5 4.5 %collective-permute-start.5 = (bf16[32,1408]{1,0:T(8,128)(2,1)}, bf16[32,1408]{1,0:T(8,128)(2,1)S(1)}, u32[]{:S(2)}, u32[]{:S(2)}) collective-permute-start(bf16[32,1408]{1,0:T(8,128)(2,1)} %get-tuple-element.95), channel_id=1, source_target_pairs={{0,3},{1,2},{2,1},{3,0},{4,7},{5,6},{6,5},{7,4},{8,11},{9,10},{10,... | collective-permute-start | bytes 270344 | tf_op jit(solution)/shard_map/ppermute | solution.py:698
  11.0 0.9 copy-start.6
  11.9 0.9 copy-start.8
  12.8 46.2 %copy-start.7 = (f32[8,768]{1,0:T(8,128)S(1)}, f32[8,768]{1,0:T(8,128)}, u32[]{:S(2)}) copy-start(f32[8,768]{1,0:T(8,128)} %get-tuple-element.90.cw_ref) | copy-start | bytes 73732
  12.9 46.2 %copy-start.11 = (f32[8,128]{1,0:T(8,128)S(1)}, f32[8,128]{1,0:T(8,128)}, u32[]{:S(2)}) copy-start(f32[8,128]{1,0:T(8,128)} %get-tuple-element.91.head_ref) | copy-start | bytes 12292
  12.9 14.0 %collective-permute-start.9 = (bf16[128,896]{1,0:T(8,128)(2,1)S(1)}, bf16[128,896]{1,0:T(8,128)(2,1)S(1)}, u32[]{:S(2)}, u32[]{:S(2)}) collective-permute-start(bf16[128,896]{1,0:T(8,128)(2,1)S(1)} %get-tuple-element.97.refs_4_.refs_0_), channel_id=1, source_target_pairs={{0,16},{1,17},{2,18},{3,19},{4,20},{5,21},{6,22},{7,23},{8,24},{9,... | collective-permute-start | bytes 688136 | tf_op jit(solution)/shard_map/ppermute | solution.py:698
  15.6 23.8 %collective-permute-start.1 = (bf16[272,1024]{1,0:T(8,128)(2,1)}, bf16[272,1024]{1,0:T(8,128)(2,1)S(1)}, u32[]{:S(2)}, u32[]{:S(2)}) collective-permute-start(bf16[272,1024]{1,0:T(8,128)(2,1)} %get-tuple-element.86.refs_0_.refs_8_.act_ref), channel_id=1, source_target_pairs={{0,2},{1,3},{2,0},{3,1},{4,6},{5,7},{6,4},{7,5},{8,10},{9,11},{10,... | collective-permute-start | bytes 1671176 | tf_op jit(solution)/shard_map/ppermute | solution.py:698
  16.7 11.5 %collective-permute-start.7 = (bf16[128,896]{1,0:T(8,128)(2,1)S(1)}, bf16[128,896]{1,0:T(8,128)(2,1)S(1)}, u32[]{:S(2)}, u32[]{:S(2)}) collective-permute-start(bf16[128,896]{1,0:T(8,128)(2,1)S(1)} %get-tuple-element.97.refs_4_.refs_0_), channel_id=1, source_target_pairs={{0,8},{1,9},{2,10},{3,11},{4,12},{5,13},{6,14},{7,15},{8,0},{9,1},... | collective-permute-start | bytes 688136 | tf_op jit(solution)/shard_map/ppermute | solution.py:698
  18.3 12.7 %collective-permute-start.6 = (bf16[128,896]{1,0:T(8,128)(2,1)S(1)}, bf16[128,896]{1,0:T(8,128)(2,1)S(1)}, u32[]{:S(2)}, u32[]{:S(2)}) collective-permute-start(bf16[128,896]{1,0:T(8,128)(2,1)S(1)} %get-tuple-element.97.refs_4_.refs_0_), channel_id=1, source_target_pairs={{0,4},{1,5},{2,6},{3,7},{4,0},{5,1},{6,2},{7,3},{8,12},{9,13},{10,... | collective-permute-start | bytes 688136 | tf_op jit(solution)/shard_map/ppermute | solution.py:698
  26.8 11.0 %collective-permute-start.11 = (bf16[128,896]{1,0:T(8,128)(2,1)S(1)}, bf16[128,896]{1,0:T(8,128)(2,1)S(1)}, u32[]{:S(2)}, u32[]{:S(2)}) collective-permute-start(bf16[128,896]{1,0:T(8,128)(2,1)S(1)} %collective-permute-done.9.refs_8_.refs_4_), channel_id=1, source_target_pairs={{0,8},{1,9},{2,10},{3,11},{4,12},{5,13},{6,14},{7,15},{8,0},{9,1},... | collective-permute-start | bytes 688136 | tf_op jit(solution)/shard_map/ppermute | solution.py:698
  27.5 17.7 %collective-permute-start = (bf16[272,1024]{1,0:T(8,128)(2,1)}, bf16[272,1024]{1,0:T(8,128)(2,1)S(1)}, u32[]{:S(2)}, u32[]{:S(2)}) collective-permute-start(bf16[272,1024]{1,0:T(8,128)(2,1)} %get-tuple-element.86.refs_0_.refs_8_.act_ref), channel_id=1, source_target_pairs={{0,1},{1,0},{2,3},{3,2},{4,5},{5,4},{6,7},{7,6},{8,9},{9,8},{10,11... | collective-permute-start | bytes 1671176 | tf_op jit(solution)/shard_map/ppermute | solution.py:698
  28.2 15.5 %collective-permute-start.16 = (bf16[256,512]{1,0:T(8,128)(2,1)S(1)}, bf16[256,512]{1,0:T(8,128)(2,1)S(1)}, u32[]{:S(2)}, u32[]{:S(2)}) collective-permute-start(bf16[256,512]{1,0:T(8,128)(2,1)S(1)} %get-tuple-element.101.refs_0_.refs_4_.refs_8_), channel_id=1, source_target_pairs={{0,16},{1,17},{2,18},{3,19},{4,20},{5,21},{6,22},{7,23},{8,24},{9,... | collective-permute-start | bytes 786440 | tf_op jit(solution)/shard_map/ppermute | solution.py:698
  31.0 8.5 %collective-permute-start.10 = (bf16[128,896]{1,0:T(8,128)(2,1)S(1)}, bf16[128,896]{1,0:T(8,128)(2,1)S(1)}, u32[]{:S(2)}, u32[]{:S(2)}) collective-permute-start(bf16[128,896]{1,0:T(8,128)(2,1)S(1)} %collective-permute-done.9.refs_8_.refs_4_), channel_id=1, source_target_pairs={{0,4},{1,5},{2,6},{3,7},{4,0},{5,1},{6,2},{7,3},{8,12},{9,13},{10,... | collective-permute-start | bytes 688136 | tf_op jit(solution)/shard_map/ppermute | solution.py:698
  37.9 7.4 %collective-permute-start.8 = (bf16[128,896]{1,0:T(8,128)(2,1)S(1)}, bf16[128,896]{1,0:T(8,128)(2,1)S(1)}, u32[]{:S(2)}, u32[]{:S(2)}) collective-permute-start(bf16[128,896]{1,0:T(8,128)(2,1)S(1)} %collective-permute-done.7.refs_6_.refs_2_), channel_id=1, source_target_pairs={{0,4},{1,5},{2,6},{3,7},{4,0},{5,1},{6,2},{7,3},{8,12},{9,13},{10,... | collective-permute-start | bytes 688136 | tf_op jit(solution)/shard_map/ppermute | solution.py:698
  39.4 16.3 %collective-permute-start.2 = (bf16[272,1024]{1,0:T(8,128)(2,1)S(1)}, bf16[272,1024]{1,0:T(8,128)(2,1)S(1)}, u32[]{:S(2)}, u32[]{:S(2)}) collective-permute-start(bf16[272,1024]{1,0:T(8,128)(2,1)S(1)} %collective-permute-done.1.refs_2_.refs_10_), channel_id=1, source_target_pairs={{0,1},{1,0},{2,3},{3,2},{4,5},{5,4},{6,7},{7,6},{8,9},{9,8},{10,11... | collective-permute-start | bytes 1671176 | tf_op jit(solution)/shard_map/ppermute | solution.py:698
  39.4 9.8 %collective-permute-start.14 = (bf16[256,512]{1,0:T(8,128)(2,1)S(1)}, bf16[256,512]{1,0:T(8,128)(2,1)S(1)}, u32[]{:S(2)}, u32[]{:S(2)}) collective-permute-start(bf16[256,512]{1,0:T(8,128)(2,1)S(1)} %get-tuple-element.101.refs_0_.refs_4_.refs_8_), channel_id=1, source_target_pairs={{0,8},{1,9},{2,10},{3,11},{4,12},{5,13},{6,14},{7,15},{8,0},{9,1},... | collective-permute-start | bytes 786440 | tf_op jit(solution)/shard_map/ppermute | solution.py:698
  43.7 12.0 %collective-permute-start.17 = (bf16[256,512]{1,0:T(8,128)(2,1)S(1)}, bf16[256,512]{1,0:T(8,128)(2,1)S(1)}, u32[]{:S(2)}, u32[]{:S(2)}) collective-permute-start(bf16[256,512]{1,0:T(8,128)(2,1)S(1)} %collective-permute-done.16.refs_4_.refs_8_.refs_12_), channel_id=1, source_target_pairs={{0,4},{1,5},{2,6},{3,7},{4,0},{5,1},{6,2},{7,3},{8,12},{9,13},{10,... | collective-permute-start | bytes 786440 | tf_op jit(solution)/shard_map/ppermute | solution.py:698
  45.2 8.9 %collective-permute-start.12 = (bf16[128,896]{1,0:T(8,128)(2,1)S(1)}, bf16[128,896]{1,0:T(8,128)(2,1)S(1)}, u32[]{:S(2)}, u32[]{:S(2)}) collective-permute-start(bf16[128,896]{1,0:T(8,128)(2,1)S(1)} %collective-permute-done.10.refs_9_.refs_5_), channel_id=1, source_target_pairs={{0,8},{1,9},{2,10},{3,11},{4,12},{5,13},{6,14},{7,15},{8,0},{9,1},... | collective-permute-start | bytes 688136 | tf_op jit(solution)/shard_map/ppermute | solution.py:698
  45.2 18.0 %collective-permute-start.13 = (bf16[256,512]{1,0:T(8,128)(2,1)S(1)}, bf16[256,512]{1,0:T(8,128)(2,1)S(1)}, u32[]{:S(2)}, u32[]{:S(2)}) collective-permute-start(bf16[256,512]{1,0:T(8,128)(2,1)S(1)} %get-tuple-element.101.refs_0_.refs_4_.refs_8_), channel_id=1, source_target_pairs={{0,4},{1,5},{2,6},{3,7},{4,0},{5,1},{6,2},{7,3},{8,12},{9,13},{10,... | collective-permute-start | bytes 786440 | tf_op jit(solution)/shard_map/ppermute | solution.py:698
  49.3 14.0 %collective-permute-start.18 = (bf16[256,512]{1,0:T(8,128)(2,1)S(1)}, bf16[256,512]{1,0:T(8,128)(2,1)S(1)}, u32[]{:S(2)}, u32[]{:S(2)}) collective-permute-start(bf16[256,512]{1,0:T(8,128)(2,1)S(1)} %collective-permute-done.16.refs_4_.refs_8_.refs_12_), channel_id=1, source_target_pairs={{0,8},{1,9},{2,10},{3,11},{4,12},{5,13},{6,14},{7,15},{8,0},{9,1},... | collective-permute-start | bytes 786440 | tf_op jit(solution)/shard_map/ppermute | solution.py:698
  54.2 9.1 %collective-permute-start.15 = (bf16[256,512]{1,0:T(8,128)(2,1)S(1)}, bf16[256,512]{1,0:T(8,128)(2,1)S(1)}, u32[]{:S(2)}, u32[]{:S(2)}) collective-permute-start(bf16[256,512]{1,0:T(8,128)(2,1)S(1)} %collective-permute-done.14.refs_2_.refs_6_.refs_10_), channel_id=1, source_target_pairs={{0,4},{1,5},{2,6},{3,7},{4,0},{5,1},{6,2},{7,3},{8,12},{9,13},{10,... | collective-permute-start | bytes 786440 | tf_op jit(solution)/shard_map/ppermute | solution.py:698
  55.7 9.6 %collective-permute-start.19 = (bf16[256,512]{1,0:T(8,128)(2,1)S(1)}, bf16[256,512]{1,0:T(8,128)(2,1)S(1)}, u32[]{:S(2)}, u32[]{:S(2)}) collective-permute-start(bf16[256,512]{1,0:T(8,128)(2,1)S(1)} %collective-permute-done.17.refs_5_.refs_9_.refs_13_), channel_id=1, source_target_pairs={{0,8},{1,9},{2,10},{3,11},{4,12},{5,13},{6,14},{7,15},{8,0},{9,1},... | collective-permute-start | bytes 786440 | tf_op jit(solution)/shard_map/ppermute | solution.py:698
  55.7 1.1 copy-start.2
  56.8 0.7 copy-start.9
  59.0 7.2 %copy-start = (bf16[512,1024]{1,0:T(8,128)(2,1)}, bf16[512,1024]{1,0:T(8,128)(2,1)S(1)}, u32[]{:S(2)}) copy-start(bf16[512,1024]{1,0:T(8,128)(2,1)S(1)} %get-tuple-element.98.refs_8_.refs_16_.norm_ref) | copy-start | bytes 3145732
  59.0 6.4 %copy-start.3 = (bf16[272,1024]{1,0:T(8,128)(2,1)S(1)}, bf16[272,1024]{1,0:T(8,128)(2,1)}, u32[]{:S(2)}) copy-start(bf16[272,1024]{1,0:T(8,128)(2,1)} %get-tuple-element.86.refs_0_.refs_8_.act_ref) | copy-start | bytes 1671172
  63.2 3.0 %copy-start.12 = (f32[1,512]{1,0:T(1,128)S(1)}, f32[1,512]{1,0:T(1,128)}, u32[]{:S(2)}) copy-start(f32[1,512]{1,0:T(1,128)} %get-tuple-element.92.refs_11_.refs_15_) | copy-start | bytes 6148
  66.2 1.2 copy-start.4
  66.2 1.3 copy-start.5
  67.5 3.2 %collective-permute-start.22 = (f32[8,512]{1,0:T(8,128)S(1)}, f32[8,512]{1,0:T(8,128)S(1)}, u32[]{:S(2)}, u32[]{:S(2)}) collective-permute-start(f32[8,512]{1,0:T(8,128)S(1)} %get-tuple-element.104.refs_0_), channel_id=1, source_target_pairs={{0,3},{1,2},{2,1},{3,0},{4,7},{5,6},{6,5},{7,4},{8,11},{9,10},{10,... | collective-permute-start | bytes 49160 | tf_op jit(solution)/shard_map/ppermute | solution.py:698
  68.5 3.7 %collective-permute-start.21 = (f32[8,512]{1,0:T(8,128)S(1)}, f32[8,512]{1,0:T(8,128)S(1)}, u32[]{:S(2)}, u32[]{:S(2)}) collective-permute-start(f32[8,512]{1,0:T(8,128)S(1)} %get-tuple-element.104.refs_0_), channel_id=1, source_target_pairs={{0,2},{1,3},{2,0},{3,1},{4,6},{5,7},{6,4},{7,5},{8,10},{9,11},{10,... | collective-permute-start | bytes 49160 | tf_op jit(solution)/shard_map/ppermute | solution.py:698
  69.2 3.0 %collective-permute-start.20 = (f32[8,512]{1,0:T(8,128)S(1)}, f32[8,512]{1,0:T(8,128)S(1)}, u32[]{:S(2)}, u32[]{:S(2)}) collective-permute-start(f32[8,512]{1,0:T(8,128)S(1)} %get-tuple-element.104.refs_0_), channel_id=1, source_target_pairs={{0,1},{1,0},{2,3},{3,2},{4,5},{5,4},{6,7},{7,6},{8,9},{9,8},{10,11... | collective-permute-start | bytes 49160 | tf_op jit(solution)/shard_map/ppermute | solution.py:698
  76.5 7.9 %copy-start.1 = (bf16[512,1024]{1,0:T(8,128)(2,1)S(1)}, bf16[512,1024]{1,0:T(8,128)(2,1)}, u32[]{:S(2)}) copy-start(bf16[512,1024]{1,0:T(8,128)(2,1)} %copy-done) | copy-start | bytes 3145732
  89.7 26.3 %collective-permute-start.35 = (bf16[256,2048]{1,0:T(8,128)(2,1)S(1)}, bf16[256,2048]{1,0:T(8,128)(2,1)S(1)}, u32[]{:S(2)}, u32[]{:S(2)}) collective-permute-start(bf16[256,2048]{1,0:T(8,128)(2,1)S(1)} %get-tuple-element.140), channel_id=1, source_target_pairs={{0,1},{1,0},{2,3},{3,2},{4,5},{5,4},{6,7},{7,6},{8,9},{9,8},{10,11... | collective-permute-start | bytes 3145736 | tf_op jit(solution)/shard_map/ppermute | solution.py:698
  89.8 14.8 %collective-permute-start.32 = (bf16[512,512]{1,0:T(8,128)(2,1)S(1)}, bf16[512,512]{1,0:T(8,128)(2,1)S(1)}, u32[]{:S(2)}, u32[]{:S(2)}) collective-permute-start(bf16[512,512]{1,0:T(8,128)(2,1)S(1)} %get-tuple-element.129), channel_id=1, source_target_pairs={{0,8},{1,9},{2,10},{3,11},{4,12},{5,13},{6,14},{7,15},{8,0},{9,1},... | collective-permute-start | bytes 1572872 | tf_op jit(solution)/shard_map/ppermute | solution.py:698
  89.9 24.5 %collective-permute-start.26 = (bf16[256,896]{1,0:T(8,128)(2,1)S(1)}, bf16[256,896]{1,0:T(8,128)(2,1)S(1)}, u32[]{:S(2)}, u32[]{:S(2)}) collective-permute-start(bf16[256,896]{1,0:T(8,128)(2,1)S(1)} %get-tuple-element.119), channel_id=1, source_target_pairs={{0,8},{1,9},{2,10},{3,11},{4,12},{5,13},{6,14},{7,15},{8,0},{9,1},... | collective-permute-start | bytes 1376264 | tf_op jit(solution)/shard_map/ppermute | solution.py:698
  91.9 14.4 %collective-permute-start.24 = (bf16[144,896]{1,0:T(8,128)(2,1)S(1)}, bf16[144,896]{1,0:T(8,128)(2,1)S(1)}, u32[]{:S(2)}, u32[]{:S(2)}) collective-permute-start(bf16[144,896]{1,0:T(8,128)(2,1)S(1)} %get-tuple-element.115), channel_id=1, source_target_pairs={{0,4},{1,5},{2,6},{3,7},{4,0},{5,1},{6,2},{7,3},{8,12},{9,13},{10,... | collective-permute-start | bytes 774152 | tf_op jit(solution)/shard_map/ppermute | solution.py:698
  93.4 23.4 %collective-permute-start.30 = (bf16[256,512]{1,0:T(8,128)(2,1)S(1)}, bf16[256,512]{1,0:T(8,128)(2,1)S(1)}, u32[]{:S(2)}, u32[]{:S(2)}) collective-permute-start(bf16[256,512]{1,0:T(8,128)(2,1)S(1)} %get-tuple-element.126), channel_id=1, source_target_pairs={{0,4},{1,5},{2,6},{3,7},{4,0},{5,1},{6,2},{7,3},{8,12},{9,13},{10,... | collective-permute-start | bytes 786440 | tf_op jit(solution)/shard_map/ppermute | solution.py:698
  104.6 13.0 %collective-permute-start.33 = (bf16[256,512]{1,0:T(8,128)(2,1)S(1)}, bf16[256,512]{1,0:T(8,128)(2,1)S(1)}, u32[]{:S(2)}, u32[]{:S(2)}) collective-permute-start(bf16[256,512]{1,0:T(8,128)(2,1)S(1)} %side.3), channel_id=1, source_target_pairs={{0,4},{1,5},{2,6},{3,7},{4,0},{5,1},{6,2},{7,3},{8,12},{9,13},{10,... | collective-permute-start | bytes 786440 | tf_op jit(solution)/shard_map/ppermute | solution.py:698
  106.3 13.2 %collective-permute-start.25 = (bf16[144,896]{1,0:T(8,128)(2,1)S(1)}, bf16[144,896]{1,0:T(8,128)(2,1)S(1)}, u32[]{:S(2)}, u32[]{:S(2)}) collective-permute-start(bf16[144,896]{1,0:T(8,128)(2,1)S(1)} %get-tuple-element.117), channel_id=1, source_target_pairs={{0,8},{1,9},{2,10},{3,11},{4,12},{5,13},{6,14},{7,15},{8,0},{9,1},... | collective-permute-start | bytes 774152 | tf_op jit(solution)/shard_map/ppermute | solution.py:698
  114.4 8.6 %collective-permute-start.27 = (bf16[128,896]{1,0:T(8,128)(2,1)S(1)}, bf16[128,896]{1,0:T(8,128)(2,1)S(1)}, u32[]{:S(2)}, u32[]{:S(2)}) collective-permute-start(bf16[128,896]{1,0:T(8,128)(2,1)S(1)} %side.2), channel_id=1, source_target_pairs={{0,4},{1,5},{2,6},{3,7},{4,0},{5,1},{6,2},{7,3},{8,12},{9,13},{10,... | collective-permute-start | bytes 688136 | tf_op jit(solution)/shard_map/ppermute | solution.py:698
  116.0 11.9 %collective-permute-start.23 = (bf16[128,896]{1,0:T(8,128)(2,1)S(1)}, bf16[128,896]{1,0:T(8,128)(2,1)S(1)}, u32[]{:S(2)}, u32[]{:S(2)}) collective-permute-start(bf16[128,896]{1,0:T(8,128)(2,1)S(1)} %get-tuple-element.113), channel_id=1, source_target_pairs={{0,4},{1,5},{2,6},{3,7},{4,0},{5,1},{6,2},{7,3},{8,12},{9,13},{10,... | collective-permute-start | bytes 688136 | tf_op jit(solution)/shard_map/ppermute | solution.py:698
  116.8 32.8 %collective-permute-start.36 = (bf16[128,2048]{1,0:T(8,128)(2,1)S(1)}, bf16[128,2048]{1,0:T(8,128)(2,1)S(1)}, u32[]{:S(2)}, u32[]{:S(2)}) collective-permute-start(bf16[128,2048]{1,0:T(8,128)(2,1)S(1)} %get-tuple-element.142), channel_id=1, source_target_pairs={{0,2},{1,3},{2,0},{3,1},{4,6},{5,7},{6,4},{7,5},{8,10},{9,11},{10,... | collective-permute-start | bytes 1572872 | tf_op jit(solution)/shard_map/ppermute | solution.py:698
  117.6 14.1 %collective-permute-start.29 = (bf16[256,512]{1,0:T(8,128)(2,1)S(1)}, bf16[256,512]{1,0:T(8,128)(2,1)S(1)}, u32[]{:S(2)}, u32[]{:S(2)}) collective-permute-start(bf16[256,512]{1,0:T(8,128)(2,1)S(1)} %get-tuple-element.124), channel_id=1, source_target_pairs={{0,4},{1,5},{2,6},{3,7},{4,0},{5,1},{6,2},{7,3},{8,12},{9,13},{10,... | collective-permute-start | bytes 786440 | tf_op jit(solution)/shard_map/ppermute | solution.py:698
  119.0 30.6 %copy-start.10 = (f32[1,1024]{1,0:T(1,128)S(1)}, f32[1,1024]{1,0:T(1,128)}, u32[]{:S(2)}) copy-start(f32[1,1024]{1,0:T(1,128)} %get-tuple-element.93.refs_12_.gain_ref) | copy-start | bytes 12292
  119.5 12.3 %collective-permute-start.31 = (bf16[256,512]{1,0:T(8,128)(2,1)S(1)}, bf16[256,512]{1,0:T(8,128)(2,1)S(1)}, u32[]{:S(2)}, u32[]{:S(2)}) collective-permute-start(bf16[256,512]{1,0:T(8,128)(2,1)S(1)} %near.3), channel_id=1, source_target_pairs={{0,8},{1,9},{2,10},{3,11},{4,12},{5,13},{6,14},{7,15},{8,0},{9,1},... | collective-permute-start | bytes 786440 | tf_op jit(solution)/shard_map/ppermute | solution.py:698
  123.1 23.6 %collective-permute-start.34 = (bf16[256,512]{1,0:T(8,128)(2,1)S(1)}, bf16[256,512]{1,0:T(8,128)(2,1)S(1)}, u32[]{:S(2)}, u32[]{:S(2)}) collective-permute-start(bf16[256,512]{1,0:T(8,128)(2,1)S(1)} %far.3), channel_id=1, source_target_pairs={{0,16},{1,17},{2,18},{3,19},{4,20},{5,21},{6,22},{7,23},{8,24},{9,... | collective-permute-start | bytes 786440 | tf_op jit(solution)/shard_map/ppermute | solution.py:698
  128.0 18.6 %collective-permute-start.28 = (bf16[144,896]{1,0:T(8,128)(2,1)S(1)}, bf16[144,896]{1,0:T(8,128)(2,1)S(1)}, u32[]{:S(2)}, u32[]{:S(2)}) collective-permute-start(bf16[144,896]{1,0:T(8,128)(2,1)S(1)} %get-tuple-element.122), channel_id=1, source_target_pairs={{0,16},{1,17},{2,18},{3,19},{4,20},{5,21},{6,22},{7,23},{8,24},{9,... | collective-permute-start | bytes 774152 | tf_op jit(solution)/shard_map/ppermute | solution.py:698
  147.7 3.1 %collective-permute-start.37 = (bf16[48,1408]{1,0:T(8,128)(2,1)S(1)}, bf16[48,1408]{1,0:T(8,128)(2,1)S(1)}, u32[]{:S(2)}, u32[]{:S(2)}) collective-permute-start(bf16[48,1408]{1,0:T(8,128)(2,1)S(1)} %get-tuple-element.149), channel_id=1, source_target_pairs={{0,1},{1,0},{2,3},{3,2},{4,5},{5,4},{6,7},{7,6},{8,9},{9,8},{10,11... | collective-permute-start | bytes 405512 | tf_op jit(solution)/shard_map/ppermute | solution.py:698
  147.7 6.4 %collective-permute-start.38 = (bf16[48,1408]{1,0:T(8,128)(2,1)S(1)}, bf16[48,1408]{1,0:T(8,128)(2,1)S(1)}, u32[]{:S(2)}, u32[]{:S(2)}) collective-permute-start(bf16[48,1408]{1,0:T(8,128)(2,1)S(1)} %get-tuple-element.150), channel_id=1, source_target_pairs={{0,2},{1,3},{2,0},{3,1},{4,6},{5,7},{6,4},{7,5},{8,10},{9,11},{10,... | collective-permute-start | bytes 405512 | tf_op jit(solution)/shard_map/ppermute | solution.py:698
  148.2 8.0 %collective-permute-start.39 = (bf16[48,1408]{1,0:T(8,128)(2,1)S(1)}, bf16[48,1408]{1,0:T(8,128)(2,1)S(1)}, u32[]{:S(2)}, u32[]{:S(2)}) collective-permute-start(bf16[48,1408]{1,0:T(8,128)(2,1)S(1)} %get-tuple-element.151), channel_id=1, source_target_pairs={{0,3},{1,2},{2,1},{3,0},{4,7},{5,6},{6,5},{7,4},{8,11},{9,10},{10,... | collective-permute-start | bytes 405512 | tf_op jit(solution)/shard_map/ppermute | solution.py:698

commit v3 on v2

--- a/solution.py
+++ b/solution.py
@@ -16,8 +16,10 @@
 F32 = jnp.float32
 NEG = -1e30
 LANES = 128
+PROJECT_COST = 4e9
+SCAN_COST = 1.6e10
 QUAD = 4
-SMALL = 8
+SMALL = 16
 VMEM_BYTES = 44 * 1024 * 1024
 RAW_BYTES = 60 * 1024 * 1024
 
@@ -127,9 +129,19 @@
     return jnp.where(low, row[:, 2 * pair : 2 * pair + 1], row[:, 2 * pair + 1 : 2 * pair + 2])
 
 
-def scan_kernel(proj_ref, ends_ref, cw_ref, head_ref, out_ref):
+def scan_kernel(me_ref, own_ref, g1, g2, g3, ends_ref, cw_ref, head_ref, out_ref, proj_ref, scr):
     rows = LANES
     width = out_ref.shape[1]
+    t = me_ref[0] & (QUAD - 1)
+    part = scr.shape[2]
+    scr[t] = own_ref[:, width : width + part]
+    for r, g in ((1, g1), (2, g2), (3, g3)):
+        scr[t ^ r] = unfold(g[...].astype(F32), r)
+    proj_ref[:, 0:width] = own_ref[:, 0:width]
+    proj_ref[:, width : width + 2 * LANES] = jnp.concatenate([scr[q] for q in range(QUAD)], 1)
+    proj_ref[:, width + 2 * LANES :] = jnp.concatenate(
+        [own_ref[:, width + part :], jnp.zeros((own_ref.shape[0], LANES - part), F32)], 1
+    )
     pairs = width // LANES
     convw = width + 2 * LANES
     dtb, rate, skip = head_ref[0:1, :], head_ref[1:2, :], head_ref[2:3, :]
@@ -164,7 +176,9 @@
     lax.fori_loop(0, ends_ref.shape[0], body, 0)
 
 
-def scan_back_kernel(proj_ref, dscan_ref, ends_ref, cw_ref, head_ref, pc_ref, small_ref):
+def scan_back_kernel(
+    me_ref, proj_ref, dscan_ref, ends_ref, cw_ref, head_ref, pc_ref, small_ref, p0, p1, p2, p3, scr
+):
     rows = LANES
     width = dscan_ref.shape[1]
     pairs = width // LANES
@@ -180,6 +194,13 @@
     low = lane < LANES // 2
     by_head = (iota((width, LANES), 0) // (width // own) == iota((width, LANES), 1)).astype(F32)
     small_ref[...] = jnp.zeros(small_ref.shape, F32)
+    t = me_ref[0] & (QUAD - 1)
+    part = scr.shape[2]
+
+    def add_small(k, v):
+        total = jnp.sum(v, axis=0, keepdims=True)
+        small_ref[k : k + 1, 0:width] += total[:, 0:width]
+        small_ref[5 + k : 6 + k, 0 : 2 * LANES] += total[:, width:]
 
     def body(b, dskip):
         at = pl.ds(pl.multiple_of(b * rows, rows), rows)
@@ -233,24 +254,26 @@
         dread = mm_l(dsc, key)
         dconv = jnp.concatenate(dxs + [dkey, dread], 1) * (sig * (1.0 + conv * (1.0 - sig)))
         dxbc = cw[0:1, :] * dconv
-        small_ref[0:1, 0:convw] += jnp.sum(dconv * xbc, axis=0, keepdims=True)
+        add_small(0, dconv * xbc)
         for k in range(1, 4):
             masked = dconv * masks[k - 1]
             dxbc = dxbc + cw[k : k + 1, :] * pltpu.roll(masked, rows - k, 0)
-            small_ref[k : k + 1, 0:convw] += jnp.sum(
-                masked * pltpu.roll(xbc, k, 0), axis=0, keepdims=True
-            )
-        small_ref[4:5, 0:convw] += jnp.sum(dconv, axis=0, keepdims=True)
-        small_ref[5:6, width : width + LANES] += jnp.sum(ddt, axis=0, keepdims=True)
-        small_ref[5:6, width + LANES : width + 2 * LANES] += jnp.sum(
-            dlog * log_decay, axis=0, keepdims=True
-        )
-        pc_ref[at, 0:convw] = dxbc.astype(BF)
-        pc_ref[at, convw : convw + LANES] = ddt.astype(BF)
+            add_small(k, masked * pltpu.roll(xbc, k, 0))
+        add_small(4, dconv)
+        small_ref[11:12, 0:LANES] += jnp.sum(ddt, axis=0, keepdims=True)
+        small_ref[11:12, LANES : 2 * LANES] += jnp.sum(dlog * log_decay, axis=0, keepdims=True)
+        pc_ref[at, 0:width] = dxbc[:, 0:width].astype(BF)
+        for q in range(QUAD):
+            scr[q, at, :] = dxbc[:, width + q * part : width + (q + 1) * part]
+        pc_ref[at, width + part :] = ddt[:, 0:part].astype(BF)
         return dskip + jnp.concatenate(dsk, 1)
 
     dskip = lax.fori_loop(0, ends_ref.shape[0], body, jnp.zeros((1, width), F32))
-    small_ref[5:6, width + 2 * LANES : width + 3 * LANES] = mm_high(dskip, by_head)
+    small_ref[11:12, 2 * LANES : 3 * LANES] = mm_high(dskip, by_head)
+    half = scr.shape[1] // 2
+    for r, out in enumerate((p0, p1, p2, p3)):
+        mine = scr[t ^ r]
+        out[...] = jnp.concatenate([mine[0:half, :], mine[half:, :]], 1).astype(out.dtype)
 
 
 def weave(out_ref, at, parts, size):
@@ -264,19 +287,22 @@
 def pick_heads(parts, heads):
     total = None
     for q in range(QUAD):
-        sel = (iota((LANES, heads), 1) == iota((LANES, heads), 0) * QUAD + q).astype(F32)
+        deep = (parts[q].shape[1], heads)
+        sel = (iota(deep, 1) == iota(deep, 0) * QUAD + q).astype(F32)
         got = mm_high(parts[q], sel)
         total = got if total is None else total + got
     return total
 
 
-def prep_kernel(me_ref, len_ref, w_hbm, tok_hbm, cot_hbm, wout_hbm, act_ref, wout_ref, *rest):
-    outs, scr, w_ref, tok_ref, cot_ref, sems = rest[0:4], *rest[4:]
+def prep_kernel(me_ref, len_ref, *refs):
+    raws = refs[0:10]
+    act_ref, cwb_ref, head_ref, gain_ref, pre_ref = refs[10:15]
+    outs, scr = refs[15:19], refs[19]
+    w_ref, tok_ref, cot_ref = refs[20:23]
+    sems = refs[30]
     copies = [
         pltpu.make_async_copy(src, dst, sems.at[n])
-        for n, (src, dst) in enumerate(
-            ((w_hbm, w_ref), (tok_hbm, tok_ref), (cot_hbm, cot_ref), (wout_hbm, wout_ref))
-        )
+        for n, (src, dst) in enumerate(zip(raws, refs[20:30]))
     ]
     for c in copies:
         c.start()
@@ -286,7 +312,7 @@
     own = heads // QUAD
     copies[0].wait()
     w = w_ref[...].astype(F32)
-    inner = (w.shape[1] - heads - outs[0].shape[1] + LANES) * QUAD // (2 * (QUAD - 1))
+    inner = gain_ref.shape[1] * QUAD
     size = inner // heads
     conv_end = w.shape[1] - heads
     shared = w[:, 2 * inner : conv_end]
@@ -297,10 +323,12 @@
             at = (k * QUAD + q) * size
             zs.append(w[:, at : at + size])
             xs.append(w[:, inner + at : inner + at + size])
-        pick = (iota((heads, LANES), 0) == iota((heads, LANES), 1) * QUAD + q) & (
-            iota((heads, LANES), 1) < own
+        part = shared.shape[1] // QUAD
+        pick = (iota((heads, part), 0) == iota((heads, part), 1) * QUAD + q) & (
+            iota((heads, part), 1) < own
         )
-        scr[q] = jnp.concatenate(zs + xs + [shared, mm(dts, pick.astype(BF))], 1).astype(BF)
+        mine = [shared[:, q * part : (q + 1) * part], mm(dts, pick.astype(BF))]
+        scr[q] = jnp.concatenate(zs + xs + mine, 1).astype(BF)
     for r in range(QUAD):
         outs[r][...] = scr[t ^ r]
     lane = iota((16, model), 1)
@@ -315,23 +343,15 @@
     copies[2].wait()
     live = (iota((rows, 1), 0) < end).astype(F32)
     act_ref[rows + 16 :, :] = (cot_ref[...].astype(F32) * live).astype(BF)
-    copies[3].wait()
-
-
-def params_kernel(me_ref, *refs):
-    raws, (cwb_ref, head_ref, gain_ref, pre_ref) = refs[0:7], refs[7:11]
-    cw_ref, cb_ref, dt_ref, al_ref, sk_ref, ng_ref, pg_ref = refs[11:18]
-    sems = refs[18]
-    copies = [
-        pltpu.make_async_copy(src, dst, sems.at[n])
-        for n, (src, dst) in enumerate(zip(raws, refs[11:18]))
-    ]
-    for c in copies:
-        c.start()
-    for c in copies:
+    for c in copies[3:]:
         c.wait()
+    share_params(t, refs[23:30], cwb_ref, head_ref, gain_ref, pre_ref)
+
+
+def share_params(t, given, cwb_ref, head_ref, gain_ref, pre_ref):
+    cw_ref, cb_ref, dt_ref, al_ref, sk_ref, ng_ref, pg_ref = given
     pre_ref[...] = pg_ref[...]
-    t = me_ref[0] & (QUAD - 1)
+    bias = jnp.concatenate([cb_ref[n : n + 1, :] for n in range(cb_ref.shape[0])], 1)
     heads = dt_ref.shape[1]
     own = heads // QUAD
     inner = ng_ref.shape[1]
@@ -349,8 +369,8 @@
     cwb_ref[...] = jnp.zeros(cwb_ref.shape, F32)
     cwb_ref[0:taps, 0:width] = mine(cw_ref[...])
     cwb_ref[0:taps, width:] = cw_ref[:, inner:]
-    cwb_ref[taps : taps + 1, 0:width] = mine(cb_ref[...])
-    cwb_ref[taps : taps + 1, width:] = cb_ref[:, inner:]
+    cwb_ref[taps : taps + 1, 0:width] = mine(bias)
+    cwb_ref[taps : taps + 1, width:] = bias[:, inner:]
     gain_ref[...] = mine(ng_ref[...])
     pick = (iota((heads, LANES), 0) == iota((heads, LANES), 1) * QUAD + t) & (
         iota((heads, LANES), 1) < own
@@ -377,7 +397,7 @@
 def project_kernel(me_ref, *refs):
     chunks = 8
     acts, ws = refs[0:QUAD], refs[QUAD : QUAD + chunks]
-    gain_ref, norm_ref, proj_ref, ends_ref = refs[QUAD + chunks :]
+    gain_ref, norm_ref, proj_ref, ends_ref, shared_ref = refs[QUAD + chunks :]
     zy = me_ref[0] // QUAD
     rows = ends_ref.shape[1]
     for r in range(QUAD):
@@ -389,7 +409,24 @@
             norm_ref[r * rows : (r + 1) * rows, k * LANES : (k + 1) * LANES] = part.astype(BF)
         ends_ref[r : r + 1, :] = acts[r][rows : rows + 16, 0:LANES].astype(F32)[0:1, :]
     w = jnp.concatenate([c[...] for c in ws], axis=0)
-    proj_ref[...] = mm(norm_ref[...], w)
+    proj = mm(norm_ref[...], w)
+    proj_ref[...] = proj
+    part = shared_ref.shape[1] // 2
+    width = proj.shape[1] - 2 * part
+    half = shared_ref.shape[0]
+    shared = proj[:, width : width + part]
+    shared_ref[...] = jnp.concatenate([shared[0:half, :], shared[half:, :]], 1).astype(BF)
+
+
+def unfold(packed, flip):
+    rows, part = packed.shape[0] // 2, packed.shape[1] // 2
+    blocks = []
+    for b in range(QUAD):
+        j = b ^ flip
+        blocks.append(
+            packed[(j % 2) * rows : (j % 2 + 1) * rows, (j // 2) * part : (j // 2 + 1) * part]
+        )
+    return jnp.concatenate(blocks, 0)
 
 
 def cot_kernel(me_ref, *refs):
@@ -430,12 +467,11 @@
     stats, ws = refs[0:QUAD], refs[QUAD : QUAD + chunks]
     z_ref, scan_ref, dgn_ref, gain_ref, norm_ref, cot_ref = refs[QUAD + chunks : QUAD + chunks + 6]
     gn_ref, dscan_ref, dz_ref, ngain_ref, pre_ref = refs[QUAD + chunks + 6 : QUAD + chunks + 11]
-    keeps, send67, send3, send1, scr = refs[QUAD + chunks + 11 : QUAD + chunks + 15], *refs[
-        QUAD + chunks + 15 :
-    ]
-    full = keeps[0].shape[0]
-    outs = {0: keeps[0], 2: keeps[1], 4: keeps[2], 5: keeps[3], 3: send3, 1: send1}
-    outs[6], outs[7] = send67.at[0:full, :], send67.at[full:, :]
+    outs = dict(zip((0, 2, 4, 5, 7, 3), refs[QUAD + chunks + 11 :]))
+    scr = refs[QUAD + chunks + 17]
+    full = outs[0].shape[0]
+    for one, two in ((7, 6), (3, 1)):
+        outs[one], outs[two] = outs[one].at[0:full, :], outs[one].at[full:, :]
     zy = me_ref[0] // QUAD
     rows = stats[0].shape[1] // QUAD
     total = stats[0][...]
@@ -477,25 +513,33 @@
     pre_ref[...] = pre
 
 
-def split_small(out_ref, base, small):
-    high = small.astype(BF)
-    low = (small - high.astype(F32)).astype(BF)
-    out_ref[base : base + 2 * SMALL, :] = jnp.concatenate(
-        [high.astype(F32), low.astype(F32)], 0
+def put_small(out_ref, base, small):
+    out_ref[base : base + SMALL, :] = small.astype(BF)
+
+
+def get_small(ref, base):
+    return ref[base : base + SMALL, :].astype(F32)
+
+
+def ingrad_kernel(
+    me_ref, norm_ref, pcx_ref, own_ref, g1, g2, g3, small_ref, ngain_ref, preb_ref, gain_ref, *refs
+):
+    chunks = 8
+    ws, pc_ref, refs = refs[0:chunks], refs[chunks], refs[0:chunks] + refs[chunks + 1 :]
+    part = own_ref.shape[1] // 2
+    width = pc_ref.shape[1] - 2 * part
+    shared = unfold(own_ref[...], 0)
+    for r, g in ((1, g1), (2, g2), (3, g3)):
+        shared = shared + unfold(g[...].astype(F32), r)
+    pc_ref[:, 0:width] = pcx_ref[:, 0:width]
+    pc_ref[:, width:] = jnp.concatenate(
+        [shared, pcx_ref[:, width + part :].astype(F32)], 1
     ).astype(BF)
-
-
-def joined_small(ref, base):
-    both = ref[base : base + 2 * SMALL, :].astype(F32)
-    return both[0:SMALL, :] + both[SMALL:, :]
-
-
-def ingrad_kernel(me_ref, norm_ref, pc_ref, small_ref, ngain_ref, preb_ref, gain_ref, *refs):
-    chunks = 8
-    ws = refs[0:chunks]
-    keeps, send67, send3, send1, mine_ref, scr = refs[chunks : chunks + 4], *refs[chunks + 4 :]
-    outs = {0: keeps[0], 2: keeps[1], 4: keeps[2], 5: keeps[3], 3: send3, 1: send1}
-    outs[6], outs[7] = send67.at[0:LANES, :], send67.at[LANES:, :]
+    outs = dict(zip((0, 2, 4, 6, 7, 3), refs[chunks : 2 * chunks - 2]))
+    pair_ref = outs[7]
+    outs[7], outs[5] = pair_ref.at[0:LANES, :], pair_ref.at[LANES : 2 * LANES, :]
+    mine_ref, scr = refs[2 * chunks - 2 :]
+    outs[3], outs[1] = outs[3].at[0:LANES, :], outs[3].at[LANES:, :]
     zy = me_ref[0] // QUAD
     lane = iota((LANES, LANES), 1)
     pre = preb_ref[...]
@@ -513,62 +557,63 @@
     placed = jnp.concatenate([scr[k : k + 1, :] for k in range(chunks)], 1) / gain
     width = ngain_ref.shape[1]
     mine_ref[...] = small_ref[...]
-    mine_ref[5:6, 0:width] = ngain_ref[...]
-    mine_ref[6:7, :] = placed[:, 0:wide]
-    mine_ref[7:8, 0 : (chunks - per) * LANES] = placed[:, wide:]
-    split_small(send3, LANES, mine_ref[...])
+    mine_ref[10:11, 0:width] = ngain_ref[...]
+    mine_ref[12:13, :] = placed[:, 0:wide]
+    mine_ref[13:14, 0 : (chunks - per) * LANES] = placed[:, wide:]
+    put_small(pair_ref, 2 * LANES, mine_ref[...])
 
 
 def add_near_kernel(keep_ref, got_ref, small_ref, out_ref, sum_ref):
     out_ref[0:LANES, :] = (keep_ref[...] + got_ref[0:LANES, :].astype(F32)).astype(BF)
-    total = small_ref[...] + joined_small(got_ref, LANES)
+    total = small_ref[...] + get_small(got_ref, 2 * LANES)
     sum_ref[...] = total
-    split_small(out_ref, LANES, total)
+    put_small(out_ref, LANES, total)
 
 
 def add_two_kernel(keep_ref, got_ref, out_ref):
-    out_ref[...] = (keep_ref[...] + got_ref[...].astype(F32)).astype(BF)
-
-
-def add_side_kernel(keep_ref, got_ref, out_ref):
     full = keep_ref.shape[0]
-    out_ref[...] = (keep_ref[...] + got_ref[full:, :].astype(F32)).astype(BF)
+    out_ref[...] = (keep_ref[...] + got_ref[0:full, :].astype(F32)).astype(BF)
 
 
 def add_far_kernel(keep_ref, got_ref, side_ref, out_ref):
     full = keep_ref.shape[0]
     out_ref[...] = (
-        keep_ref[...] + got_ref[0:full, :].astype(F32) + side_ref[...].astype(F32)
+        keep_ref[...] + got_ref[full:, :].astype(F32) + side_ref[...].astype(F32)
     ).astype(BF)
 
 
-def add_last_kernel(keep_ref, got_ref, side_ref, small_ref, near_ref, out_ref, sum_ref):
+def add_last_kernel(keep_ref, got_ref, side_ref, small_ref, out_ref, sum_ref):
     out_ref[0:LANES, :] = (
-        keep_ref[...] + got_ref[0:LANES, :].astype(F32) + side_ref[...].astype(F32)
+        keep_ref[...]
+        + got_ref[0:LANES, :].astype(F32)
+        + side_ref[LANES : 2 * LANES, :].astype(F32)
     ).astype(BF)
-    total = small_ref[...] + joined_small(near_ref, LANES)
+    total = small_ref[...] + get_small(got_ref, LANES)
     sum_ref[...] = total
-    split_small(out_ref, LANES, total)
+    put_small(out_ref, LANES, total)
+
+
+def put_rows(part, keep_ref, send_ref, at):
+    rows = keep_ref.shape[0] // 2
+    keep_ref[0:rows, at] = part[0:rows, :]
+    send_ref[0:rows, at] = part[rows : 2 * rows, :].astype(BF)
+    keep_ref[rows:, at] = part[2 * rows : 3 * rows, :]
+    send_ref[rows:, at] = part[3 * rows :, :].astype(BF)
+
+
+def branch_kernel(gn_ref, wfull_ref, keep_ref, send_ref):
+    put_rows(mm(gn_ref[...], wfull_ref[...]), keep_ref, send_ref, pl.ds(0, wfull_ref.shape[1]))
 
 
 def tail_kernel(me_ref, *refs):
     chunks = 8
     w1, w2 = refs[0:chunks], refs[chunks : 2 * chunks]
-    pc_ref, dz_ref, gn_ref, wfull_ref, keep_ref, send_ref = refs[2 * chunks :]
+    pc_ref, dz_ref, keep_ref, send_ref = refs[2 * chunks :]
     zy = me_ref[0] // QUAD
-    rows = keep_ref.shape[0] // 2
-    model = wfull_ref.shape[1]
-
-    def put(part, at):
-        keep_ref[0:rows, at] = part[0:rows, :]
-        send_ref[0:rows, at] = part[rows : 2 * rows, :].astype(BF)
-        keep_ref[rows:, at] = part[2 * rows : 3 * rows, :]
-        send_ref[rows:, at] = part[3 * rows :, :].astype(BF)
-
-    put(mm(gn_ref[...], wfull_ref[...]), pl.ds(0, model))
     for k in range(chunks):
         part = mm_t(pc_ref[...], w1[k][...]) + mm_t(dz_ref[...], w2[k][0:LANES, :])
-        put(part, pl.ds(pl.multiple_of(model + (zy ^ k) * LANES, LANES), LANES))
+        at = pl.ds(pl.multiple_of((zy ^ k) * LANES, LANES), LANES)
+        put_rows(part, keep_ref, send_ref, at)
 
 
 def pair_kernel(keep_ref, got_ref, mine_ref, send_ref):
@@ -578,15 +623,20 @@
     send_ref[...] = total[rows:, :].astype(BF)
 
 
-def rows_kernel(act_ref, gain_ref, a_ref, b_ref, mixed_ref, grad_ref):
-    rows, model = mixed_ref.shape
+def mixed_kernel(act_ref, a_ref, b_ref, mixed_ref):
+    rows = mixed_ref.shape[0]
     hidden = act_ref[0:rows, :].astype(F32)
     end = act_ref[rows : rows + 16, 0:LANES].astype(F32)[0:1, 3:4]
     live = (iota((rows, 1), 0).astype(F32) < end).astype(F32)
     total = a_ref[...] + b_ref[...].astype(F32)
-    mixed_ref[...] = (live * (hidden + total[:, 0:model])).astype(BF)
+    mixed_ref[...] = (live * (hidden + total)).astype(BF)
+
+
+def tokgrad_kernel(act_ref, gain_ref, a_ref, b_ref, grad_ref):
+    rows = grad_ref.shape[0]
+    hidden = act_ref[0:rows, :].astype(F32)
     scale = lax.rsqrt(jnp.mean(hidden * hidden, axis=1, keepdims=True) + EPS)
-    dn = total[:, model:] * gain_ref[...]
+    dn = (a_ref[...] + b_ref[...].astype(F32)) * gain_ref[...]
     inner = jnp.mean(dn * hidden, axis=1, keepdims=True)
     back = scale * dn - hidden * (scale * scale * scale * inner)
     grad_ref[...] = act_ref[rows + 16 :, :].astype(F32) + back
@@ -598,12 +648,12 @@
     t = me_ref[0] & (QUAD - 1)
     nrow = mine_ref.shape[0]
     chunk = QUAD * nrow
-    ta = a[0][...]
-    for got in a[1:]:
+    ta = a[0][...] + a[1][chunk:, :].astype(F32)
+    for got in a[2:]:
         ta = ta + got[0:chunk, :].astype(F32)
-    small = small_ref[...] + joined_small(a[3], chunk)
-    tb = b[0][...].astype(F32)
-    for got in b[1:]:
+    small = small_ref[...] + get_small(a[3], chunk)
+    tb = b[0][...] + b[1][b[0].shape[0] :, :].astype(F32)
+    for got in b[2:]:
         tb = tb + got[...].astype(F32)
     size = wout_ref.shape[0]
     width = tb.shape[1]
@@ -617,7 +667,7 @@
         out[0:nrow, :] = scr[at, :].astype(out.dtype)
     wide = small.shape[1]
     for out in (s1, s2, s3):
-        split_small(out.at[:, 0:wide], nrow, small)
+        put_small(out.at[:, 0:wide], nrow, small)
 
 
 def finish_kernel(me_ref, mine_ref, msmall_ref, *refs):
@@ -630,39 +680,39 @@
     sscr[t] = msmall_ref[...]
     for r in range(1, QUAD):
         scr[t ^ r] = got[r - 1][0:nrow, :].astype(F32)
-        sscr[t ^ r] = joined_small(got[r - 1].at[:, 0:wide], nrow)
+        sscr[t ^ r] = get_small(got[r - 1].at[:, 0:wide], nrow)
     inner = ng_ref.shape[1]
     width = inner // QUAD
     heads = dt_ref.shape[1]
     size = inner // heads
     conv_end = out_ref.shape[1] - heads
-    shared = 2 * width + conv_end - 2 * inner
+    part = (conv_end - 2 * inner) // QUAD
 
     def added(ref, rows, lanes):
         return (ref[0][rows, lanes] + ref[1][rows, lanes]) + (ref[2][rows, lanes] + ref[3][rows, lanes])
 
-    every = slice(0, nrow)
     weave(out_ref, 0, [scr[q][:, 0:width] for q in range(QUAD)], size)
     weave(out_ref, inner, [scr[q][:, width : 2 * width] for q in range(QUAD)], size)
-    out_ref[:, 2 * inner : conv_end] = added(scr, every, slice(2 * width, shared))
+    out_ref[:, 2 * inner : conv_end] = jnp.concatenate(
+        [scr[q][:, 2 * width : 2 * width + part] for q in range(QUAD)], 1
+    )
     out_ref[:, conv_end:] = pick_heads(
-        [scr[q][:, shared : shared + LANES] for q in range(QUAD)], heads
-    )
-    conv = shared - width
+        [scr[q][:, 2 * width + part :] for q in range(QUAD)], heads
+    )
     weave(cw_ref, 0, [sscr[q][0:4, 0:width] for q in range(QUAD)], size)
-    cw_ref[:, inner:] = added(sscr, slice(0, 4), slice(width, conv))
+    cw_ref[:, inner:] = added(sscr, slice(5, 9), slice(0, 2 * LANES))
     weave(row_ref, 0, [sscr[q][4:5, 0:width] for q in range(QUAD)], size)
-    row_ref[:, inner:] = added(sscr, slice(4, 5), slice(width, conv))
+    row_ref[:, inner:] = added(sscr, slice(9, 10), slice(0, 2 * LANES))
     for n in range(cb_ref.shape[0]):
         cb_ref[n : n + 1, :] = row_ref[:, n * LANES : (n + 1) * LANES]
-    weave(ng_ref, 0, [sscr[q][5:6, 0:width] for q in range(QUAD)], size)
+    weave(ng_ref, 0, [sscr[q][10:11, 0:width] for q in range(QUAD)], size)
     lists = [
-        pick_heads([sscr[q][:, at : at + LANES] for q in range(QUAD)], heads)[5:6, :]
-        for at in (width, width + LANES, width + 2 * LANES)
+        pick_heads([sscr[q][8:16, at : at + LANES] for q in range(QUAD)], heads)[3:4, :]
+        for at in (0, LANES, 2 * LANES)
     ]
     dt_ref[...], al_ref[...], sk_ref[...] = lists
-    pg_ref[:, 0:wide] = added(sscr, slice(6, 7), slice(0, wide))
-    pg_ref[:, wide:] = added(sscr, slice(7, 8), slice(0, pg_ref.shape[1] - wide))
+    pg_ref[:, 0:wide] = added(sscr, slice(12, 13), slice(0, wide))
+    pg_ref[:, wide:] = added(sscr, slice(13, 14), slice(0, pg_ref.shape[1] - wide))
 
 
 def quad_shards(
@@ -688,7 +738,9 @@
     size = inner // heads
     nrow, proj_width = in_weight.shape
     convw = width + conv_bias.shape[0] - inner
-    wide = convw + LANES
+    part = (convw - width) // QUAD
+    wide = width + 2 * part
+    full = convw + LANES
     both = width + wide
     total_rows = QUAD * rows
     chunk = QUAD * nrow
@@ -700,68 +752,75 @@
     def after(a, *others):
         return lax.optimization_barrier((a,) + others)[0]
 
-    def gather(mine, later=()):
+    def gather(mine, along=(), later=(), turn=()):
         z = after(mine, *later) if later else mine
         got = [mine, None, None, None, swap(z, 4 * QUAD), None, None, None]
         got[2] = swap(z, 2 * QUAD)
         got[1] = swap(mine, QUAD)
+        got[4], got[2] = lax.optimization_barrier((got[4], got[2], got[1]) + along + turn)[0:2]
         got[5] = swap(got[4], QUAD)
         got[6] = swap(got[4], 2 * QUAD)
         got[3] = swap(got[2], QUAD)
-        got[7] = swap(got[5], 2 * QUAD)
+        got[7] = swap(after(got[5], got[6]), 2 * QUAD)
         return got
 
     me = lax.axis_index("dp").astype(jnp.int32).reshape(1)
 
+    lanes = conv_bias.reshape(-1, LANES)
+    given = [in_weight, tokens, cotangent, conv_weight, lanes]
+    given += [a[None, :] for a in (dt_bias, a_log, skip_gain, norm_gain, pre_gain)]
     prepped = call(
         prep_kernel,
-        [((2 * rows + 16, model), BF), (out_weight.shape, BF)] + [((nrow, both), BF)] * QUAD,
-        [me, lengths, in_weight, tokens, cotangent, out_weight],
         [
-            pltpu.VMEM((QUAD, nrow, both), BF),
-            pltpu.VMEM(in_weight.shape, BF),
-            pltpu.VMEM(tokens.shape, BF),
-            pltpu.VMEM(tokens.shape, BF),
-            pltpu.SemaphoreType.DMA((4,)),
-        ],
+            ((2 * rows + 16, model), BF),
+            ((8, convw), F32),
+            ((8, LANES), F32),
+            ((1, width), F32),
+            ((1, model), F32),
+        ]
+        + [((nrow, both), BF)] * QUAD,
+        [me, lengths] + given,
+        [pltpu.VMEM((QUAD, nrow, both), BF)]
+        + [pltpu.VMEM(a.shape, a.dtype) for a in given]
+        + [pltpu.SemaphoreType.DMA((len(given),))],
         name="prep",
-        raw=(2, 3, 4, 5),
+        raw=tuple(range(2, 12)),
         limit=RAW_BYTES,
     )
-    act, own_out, cut = prepped[0], prepped[1], prepped[2:]
+    act, cwb, by_head, gain, pre = prepped[0:5]
+    cut = prepped[5:]
     got = [swap(cut[r], r) for r in range(1, QUAD)]
-    shapes = [(4, conv_bias.shape[0])] + [(1, n) for n in (conv_bias.shape[0], heads, heads, heads, inner, model)]
-    cwb, by_head, gain, pre = call(
-        params_kernel,
-        [((8, convw), F32), ((8, LANES), F32), ((1, width), F32), ((1, model), F32)],
-        [me, conv_weight]
-        + [a[None, :] for a in (conv_bias, dt_bias, a_log, skip_gain, norm_gain, pre_gain)],
-        [pltpu.VMEM(a, F32) for a in shapes] + [pltpu.SemaphoreType.DMA((7,))],
-        name="params",
-        raw=tuple(range(1, 8)),
-        limit=RAW_BYTES,
-    )
-    got[1] = after(got[1], cwb, by_head, gain, pre)
+    beside = swap(act, 1)
+    got[0] = after(got[0], beside)
     own_a, own_b = call(
         join_kernel,
         [((chunk, wide), BF), ((chunk_b, width), BF)],
-        [me, cut[0]] + got + [own_out],
+        [me, cut[0]] + got + [out_weight],
         name="join",
     )
-    w1 = gather(own_a)
-    w2 = gather(own_b, (w1[2],))
-    across = swap(act, 2)
-    acts = [act, swap(act, 1), across, swap(across, 1)]
-    normed, proj, ends = call(
+    across = swap(after(act, own_a), 2)
+    w1 = gather(own_a, (across,))
+    beyond = swap(across, 1)
+    acts = [act, beside, across, beyond]
+    w2 = gather(own_b, (), (w1[2],), (w1[3], w1[5]))
+    normed, proj_own, ends, shared = call(
         project_kernel,
-        [((total_rows, model), BF), ((total_rows, wide), F32), ((QUAD, rows), F32)],
+        [
+            ((total_rows, model), BF),
+            ((total_rows, wide), F32),
+            ((QUAD, rows), F32),
+            ((total_rows // 2, 2 * part), BF),
+        ],
         [me] + acts + w1 + [pre],
+        flops=PROJECT_COST,
         name="project",
     )
-    (scan_out,) = call(
+    scan_out, proj = call(
         scan_kernel,
-        [((total_rows, width), F32)],
-        [proj, ends, cwb, by_head],
+        [((total_rows, width), F32), ((total_rows, full), F32)],
+        [me, proj_own] + [swap(shared, r) for r in range(1, QUAD)] + [ends, cwb, by_head],
+        [pltpu.VMEM((QUAD, total_rows, part), F32)],
+        flops=SCAN_COST,
         name="scan",
     )
     w_full, cot_all, dgn = call(
@@ -787,80 +846,85 @@
             ((LANES, LANES), F32),
         ]
         + [((chunk_b, width), F32)] * 4
-        + [((2 * chunk_b, width), BF)]
-        + [((chunk_b, width), BF)] * 2,
+        + [((2 * chunk_b, width), BF)] * 2,
         [me] + stats + w2 + [z, scan_out, dgn, gain, normed, cot_all],
         [pltpu.VMEM((width, model), F32)],
         name="ungate",
     )
     gn, dscan, dz, ngain_part, pre_b = ungated[0:5]
-    keep_b, (send67, send3, send1) = ungated[5:9], ungated[9:]
-    got67_b, got3_b, got1_b = swap(send67, 2 * QUAD), swap(send3, QUAD), swap(send1, QUAD)
-    pc1, small = call(
+    keep_b = ungated[5:9]
+
+    got76_b, got31_b = swap(ungated[9], 2 * QUAD), swap(ungated[10], QUAD)
+    fold = (total_rows // 2, 2 * part)
+    pc_x, small, own_bc, *bc = call(
         scan_back_kernel,
-        [((total_rows, wide), BF), ((SMALL, wide), F32)],
-        [proj, dscan, ends, cwb, by_head],
+        [((total_rows, wide), BF), ((SMALL, wide), F32), (fold, F32)] + [(fold, BF)] * 3,
+        [me, proj, dscan, ends, cwb, by_head],
+        [pltpu.VMEM((QUAD, total_rows, part), F32)],
         name="scanback",
     )
+    got76_b, got31_b = lax.optimization_barrier((got76_b, got31_b, pc_x))[0:2]
+    (side,) = call(add_two_kernel, [((chunk_b, width), BF)], [keep_b[3], got76_b], name="side")
+    got5_b = swap(side, QUAD)
+    (near,) = call(add_two_kernel, [((chunk_b, width), BF)], [keep_b[1], got31_b], name="near")
+    got2_b = swap(near, 2 * QUAD)
+    pair_shapes = [((2 * rows, model), F32), ((2 * rows, model), BF)]
+
+    def pair(keep, send, *first):
+        got = swap(send, 1)
+        mine, cross = call(
+            pair_kernel,
+            [((rows, model), F32), ((rows, model), BF)],
+            [keep, after(got, *first) if first else got],
+            name="pair",
+        )
+        return mine, swap(cross, 2)
+
+    mine_m, cross_m = pair(*call(branch_kernel, pair_shapes, [gn, w_full], name="branch"))
+    (mixed,) = call(mixed_kernel, [((rows, model), BF)], [act, mine_m, cross_m], name="mixed")
+    got_bc = [swap(a, r + 1) for r, a in enumerate(bc)]
+    small, cross_m = lax.optimization_barrier((small, cross_m, near, side))[0:2]
     ingrads = call(
         ingrad_kernel,
-        [((chunk, wide), F32)] * 4
-        + [((2 * chunk, wide), BF), ((chunk + 2 * SMALL, wide), BF), ((chunk, wide), BF)]
+        [((total_rows, wide), BF)]
+        + [((chunk, wide), F32)] * 4
+        + [((2 * chunk + SMALL, wide), BF), ((2 * chunk, wide), BF)]
         + [((SMALL, wide), F32)],
-        [me, normed, pc1, small, ngain_part, pre_b, pre] + w1,
+        [me, normed, pc_x, own_bc] + got_bc + [small, ngain_part, pre_b, pre] + w1,
         [pltpu.VMEM((chunks, LANES), F32)],
         name="ingrad",
     )
-    keep_a, (send67, send3, send1, small) = list(ingrads[0:4]), ingrads[4:8]
-    got67_a, got3_a, got1_a = swap(send67, 2 * QUAD), swap(send3, QUAD), swap(send1, QUAD)
-    got67_b = after(got67_b, small)
-    got3_b = after(got3_b, small)
-
-    (side,) = call(add_side_kernel, [((chunk_b, width), BF)], [keep_b[3], got67_b], name="side")
-    got5_b = swap(side, QUAD)
-    (near,) = call(add_two_kernel, [((chunk_b, width), BF)], [keep_b[1], got3_b], name="near")
-    got2_b = swap(near, 2 * QUAD)
+    pc1, *ingrads = ingrads
+    keep_a, small = ingrads[0:4], ingrads[6]
+    got75_a, got31_a = swap(ingrads[4], QUAD), swap(ingrads[5], QUAD)
+    got5_b = after(got5_b, small)
     (far,) = call(
-        add_far_kernel, [((chunk_b, width), BF)], [keep_b[2], got67_b, got5_b], name="far"
+        add_far_kernel, [((chunk_b, width), BF)], [keep_b[2], got76_b, got5_b], name="far"
     )
     got4_b = swap(far, 4 * QUAD)
-
-    (side,) = call(add_side_kernel, [((chunk, wide), BF)], [keep_a[3], got67_a], name="side")
-    got5_a = swap(side, QUAD)
-    riding = [((chunk + 2 * SMALL, wide), BF), ((SMALL, wide), F32)]
-    near, small1 = call(add_near_kernel, riding, [keep_a[1], got3_a, small], name="near")
+    far_b = far
+
+    riding = [((chunk + SMALL, wide), BF), ((SMALL, wide), F32)]
+    side, small1 = call(add_near_kernel, riding, [keep_a[3], got75_a, small], name="side")
+    got6_a = swap(side, 2 * QUAD)
+    far, small2 = call(add_last_kernel, riding, [keep_a[2], got6_a, got75_a, small1], name="far")
+    (near,) = call(add_two_kernel, [((chunk, wide), BF)], [keep_a[1], got31_a], name="near")
     got2_a = swap(near, 2 * QUAD)
-    far, small2 = call(
-        add_last_kernel, riding, [keep_a[2], got67_a, got5_a, small1, got2_a], name="far"
-    )
     got4_a = swap(far, 4 * QUAD)
 
-    pc1, dz = lax.optimization_barrier((pc1, dz, small))[0:2]
-    keep, send = call(
-        tail_kernel,
-        [((2 * rows, 2 * model), F32), ((2 * rows, 2 * model), BF)],
-        [me] + w1 + w2 + [pc1, dz, gn, w_full],
-        name="tail",
-    )
-    mine, send = call(
-        pair_kernel,
-        [((rows, 2 * model), F32), ((rows, 2 * model), BF)],
-        [keep, swap(send, 1)],
-        name="pair",
-    )
-    crossed = swap(send, 2)
-    mixed, tokens_grad = call(
-        rows_kernel,
-        [((rows, model), BF), ((rows, model), F32)],
-        [act, pre, mine, crossed],
-        name="rows",
-    )
+    mine_t, cross_t = pair(
+        *call(tail_kernel, pair_shapes, [me] + w1 + w2 + [after(pc1, far_b), dz], name="tail"), got4_b, got2_b
+    )
+    (tokens_grad,) = call(
+        tokgrad_kernel, [((rows, model), F32)], [act, pre, mine_t, cross_t], name="tokgrad"
+    )
+    got4_a = after(got4_a, cross_t)
 
     out_shard, own, own_small, *cuts = call(
         total_kernel,
         [((size, model), F32), ((nrow, both), F32), ((SMALL, wide), F32)]
-        + [((nrow + 2 * SMALL, both), BF)] * 3,
-        [me, keep_a[0], got1_a, got2_a, got4_a, keep_b[0], got1_b, got2_b, got4_b, small2],
+        + [((nrow + SMALL, both), BF)] * 3,
+        [me, keep_a[0], got31_a, got2_a, got4_a, keep_b[0], got31_b, got2_b, got4_b, small2],
         [pltpu.VMEM((chunk, both), F32)],
         name="total",
     )

time: 158 us -> 144 us (0.911)
  waiting for transfers between devices: 81.8 us -> 56.8 us
  starting transfers between devices: 36 us -> 48.3 us
    ppermute x40 -> x46, waiting for transfers between devices: 81.8 us -> 56.8 us  [swap(): return lax.ppermute(a, 'dp', [(i, i ^ mask) for i in range(count)])]
    ppermute x40 -> x46, starting transfers between devices: 36 us -> 48.3 us  [swap(): return lax.ppermute(a, 'dp', [(i, i ^ mask) for i in range(count)])]
    pallas_call x21 -> x23, Pallas kernels: 34.3 us -> 33.7 us  [call(): pl.pallas_call(kernel, out_shape=shapes, in_specs=in_specs, out_specs=[pl...]
  transfers between devices with their start and end apart: 40 -> 46, of which waited for: 20 -> 25; matrix products, arithmetic and copies ran while one was open for 1% -> 0% of each run, Pallas kernels for 6% -> 13%
where the time goes in v3:
time: 144 us; the launch traced here: 143 us
  waiting for transfers between devices  56.8 us (39%)
  starting transfers between devices  48.3 us (34%)
  Pallas kernels  33.7 us (23%)
  local copies, waits for them, and re-layouts  3.66 us (3%)
    ppermute x46, waiting for transfers between devices, swap(): return lax.ppermute(a, 'dp', [(i, i ^ mask) for i in range(count)])  56.8 us
    ppermute x46, starting transfers between devices, swap(): return lax.ppermute(a, 'dp', [(i, i ^ mask) for i in range(count)])  48.3 us
    pallas_call x23, Pallas kernels, call(): pl.pallas_call(kernel, out_shape=shapes, in_specs=in_specs, out_specs=[pl...  33.7 us
    unnamed x26, local copies, waits for them, and re-layouts  3.66 us
  transfers between devices with their start and end apart: 46, of which 25 were waited for; matrix products, arithmetic and copies ran while one was open for 0% of the time, Pallas kernels for 13%

profile of v3, /device:TPU:0, one launch (start us, length us, event | category | flops | bytes accessed | tf_op | source)
XLA Modules:
  0.0 143.3 jit_solution(10282682862546011430)
XLA Ops:
  0.7 3.0 %prep.1 = (bf16[272,1024]{1,0:T(8,128)(2,1)}, f32[8,768]{1,0:T(8,128)}, f32[8,128]{1,0:T(8,128)}, f32[1,512]{1,0:T(1,128)}, f32[1,1024]{1,0:T(1,128)}, /*index=5...) custom-call(s32[1]{0:T(128)} %bitcast.me_ref, s32[4]{0:T(128)} %len_ref.1, ...), custom_call_target="tpu_custom_call" | custom-call | flops 1000 | bytes 1024 | tf_op jit(solution)/shard_map/prep/pallas_call | solution.py:55
  4.2 2.9 %collective-permute-start.2 = (bf16[32,1152]{1,0:T(8,128)(2,1)}, bf16[32,1152]{1,0:T(8,128)(2,1)S(1)}, u32[]{:S(2)}, u32[]{:S(2)}) collective-permute-start(bf16[32,1152]{1,0:T(8,128)(2,1)} %get-tuple-element.107), channel_id=1, source_target_pairs={{0,2},{1,3},{2,0},{3,1},{4,6},{5,7},{6,4},{7,5},{8,10},{9,11},{10,... | collective-permute-start | bytes 221192 | tf_op jit(solution)/shard_map/ppermute | solution.py:750
  7.1 2.9 %collective-permute-done.2.c2 = bf16[32,1152]{1,0:T(8,128)(2,1)S(1)} collective-permute-done((bf16[32,1152]{1,0:T(8,128)(2,1)}, bf16[32,1152]{1,0:T(8,128)(2,1)S(1)}, u32[]{:S(2)}, u32[]{:S(2)}) %collective-permute-start.2) | collective-permute-done | bytes 73760 | tf_op jit(solution)/shard_map/ppermute | solution.py:750
  10.0 1.9 %collective-permute-done.3.c3 = bf16[32,1152]{1,0:T(8,128)(2,1)S(1)} collective-permute-done((bf16[32,1152]{1,0:T(8,128)(2,1)}, bf16[32,1152]{1,0:T(8,128)(2,1)S(1)}, u32[]{:S(2)}, u32[]{:S(2)}) %collective-permute-start.3) | collective-permute-done | bytes 73760 | tf_op jit(solution)/shard_map/ppermute | solution.py:750
  11.9 0.9 copy-done.6
  12.8 0.9 copy-done.7
  14.3 1.6 %collective-permute-start.8 = (bf16[128,640]{1,0:T(8,128)(2,1)S(1)}, bf16[128,640]{1,0:T(8,128)(2,1)S(1)}, u32[]{:S(2)}, u32[]{:S(2)}) collective-permute-start(bf16[128,640]{1,0:T(8,128)(2,1)S(1)} %get-tuple-element.109.refs_4_.refs_0_), channel_id=1, source_target_pairs={{0,8},{1,9},{2,10},{3,11},{4,12},{5,13},{6,14},{7,15},{8,0},{9,1},... | collective-permute-start | bytes 491528 | tf_op jit(solution)/shard_map/ppermute | solution.py:750
  15.9 2.6 %collective-permute-start.7 = (bf16[128,640]{1,0:T(8,128)(2,1)S(1)}, bf16[128,640]{1,0:T(8,128)(2,1)S(1)}, u32[]{:S(2)}, u32[]{:S(2)}) collective-permute-start(bf16[128,640]{1,0:T(8,128)(2,1)S(1)} %get-tuple-element.109.refs_4_.refs_0_), channel_id=1, source_target_pairs={{0,16},{1,17},{2,18},{3,19},{4,20},{5,21},{6,22},{7,23},{8,24},{9,... | collective-permute-start | bytes 491528 | tf_op jit(solution)/shard_map/ppermute | solution.py:750
  18.5 1.5 %collective-permute-start.6 = (bf16[128,640]{1,0:T(8,128)(2,1)S(1)}, bf16[128,640]{1,0:T(8,128)(2,1)S(1)}, u32[]{:S(2)}, u32[]{:S(2)}) collective-permute-start(bf16[128,640]{1,0:T(8,128)(2,1)S(1)} %get-tuple-element.109.refs_4_.refs_0_), channel_id=1, source_target_pairs={{0,4},{1,5},{2,6},{3,7},{4,0},{5,1},{6,2},{7,3},{8,12},{9,13},{10,... | collective-permute-start | bytes 491528 | tf_op jit(solution)/shard_map/ppermute | solution.py:750
  20.0 8.6 %collective-permute-done.4.refs_2_.refs_10_ = bf16[272,1024]{1,0:T(8,128)(2,1)S(1)} collective-permute-done((bf16[272,1024]{1,0:T(8,128)(2,1)}, bf16[272,1024]{1,0:T(8,128)(2,1)S(1)}, u32[]{:S(2)}, u32[]{:S(2)}) %collective-permute-start.4) | collective-permute-done | bytes 557088 | tf_op jit(solution)/shard_map/ppermute | solution.py:750
  28.6 1.6 %collective-permute-start.11 = (bf16[128,640]{1,0:T(8,128)(2,1)S(1)}, bf16[128,640]{1,0:T(8,128)(2,1)S(1)}, u32[]{:S(2)}, u32[]{:S(2)}) collective-permute-start(bf16[128,640]{1,0:T(8,128)(2,1)S(1)} %collective-permute-done.7.refs_8_.refs_4_), channel_id=1, source_target_pairs={{0,8},{1,9},{2,10},{3,11},{4,12},{5,13},{6,14},{7,15},{8,0},{9,1},... | collective-permute-start | bytes 491528 | tf_op jit(solution)/shard_map/ppermute | solution.py:750
  30.3 1.5 %collective-permute-start.16 = (bf16[256,512]{1,0:T(8,128)(2,1)S(1)}, bf16[256,512]{1,0:T(8,128)(2,1)S(1)}, u32[]{:S(2)}, u32[]{:S(2)}) collective-permute-start(bf16[256,512]{1,0:T(8,128)(2,1)S(1)} %get-tuple-element.123.refs_0_.refs_4_.refs_8_), channel_id=1, source_target_pairs={{0,4},{1,5},{2,6},{3,7},{4,0},{5,1},{6,2},{7,3},{8,12},{9,13},{10,... | collective-permute-start | bytes 786440 | tf_op jit(solution)/shard_map/ppermute | solution.py:750
  32.8 2.9 %collective-permute-done.11.refs_10_.refs_6_ = bf16[128,640]{1,0:T(8,128)(2,1)S(1)} collective-permute-done((bf16[128,640]{1,0:T(8,128)(2,1)S(1)}, bf16[128,640]{1,0:T(8,128)(2,1)S(1)}, u32[]{:S(2)}, u32[]{:S(2)}) %collective-permute-start.11) | collective-permute-done | bytes 163872 | tf_op jit(solution)/shard_map/ppermute | solution.py:750
  35.7 2.6 %collective-permute-start.17 = (bf16[256,512]{1,0:T(8,128)(2,1)S(1)}, bf16[256,512]{1,0:T(8,128)(2,1)S(1)}, u32[]{:S(2)}, u32[]{:S(2)}) collective-permute-start(bf16[256,512]{1,0:T(8,128)(2,1)S(1)} %get-tuple-element.123.refs_0_.refs_4_.refs_8_), channel_id=1, source_target_pairs={{0,16},{1,17},{2,18},{3,19},{4,20},{5,21},{6,22},{7,23},{8,24},{9,... | collective-permute-start | bytes 786440 | tf_op jit(solution)/shard_map/ppermute | solution.py:750
  38.3 3.9 %collective-permute-done.10.refs_9_.refs_5_ = bf16[128,640]{1,0:T(8,128)(2,1)S(1)} collective-permute-done((bf16[128,640]{1,0:T(8,128)(2,1)S(1)}, bf16[128,640]{1,0:T(8,128)(2,1)S(1)}, u32[]{:S(2)}, u32[]{:S(2)}) %collective-permute-start.10) | collective-permute-done | bytes 163872 | tf_op jit(solution)/shard_map/ppermute | solution.py:750
  42.2 1.5 %collective-permute-start.9 = (bf16[128,640]{1,0:T(8,128)(2,1)S(1)}, bf16[128,640]{1,0:T(8,128)(2,1)S(1)}, u32[]{:S(2)}, u32[]{:S(2)}) collective-permute-start(bf16[128,640]{1,0:T(8,128)(2,1)S(1)} %collective-permute-done.8.refs_6_.refs_2_), channel_id=1, source_target_pairs={{0,4},{1,5},{2,6},{3,7},{4,0},{5,1},{6,2},{7,3},{8,12},{9,13},{10,... | collective-permute-start | bytes 491528 | tf_op jit(solution)/shard_map/ppermute | solution.py:750
  44.2 3.5 %collective-permute-done.9.refs_7_.refs_3_ = bf16[128,640]{1,0:T(8,128)(2,1)S(1)} collective-permute-done((bf16[128,640]{1,0:T(8,128)(2,1)S(1)}, bf16[128,640]{1,0:T(8,128)(2,1)S(1)}, u32[]{:S(2)}, u32[]{:S(2)}) %collective-permute-start.9) | collective-permute-done | bytes 163872 | tf_op jit(solution)/shard_map/ppermute | solution.py:750
  47.7 2.2 %collective-permute-done.17.refs_4_.refs_8_.refs_12_ = bf16[256,512]{1,0:T(8,128)(2,1)S(1)} collective-permute-done((bf16[256,512]{1,0:T(8,128)(2,1)S(1)}, bf16[256,512]{1,0:T(8,128)(2,1)S(1)}, u32[]{:S(2)}, u32[]{:S(2)}) %collective-permute-start.17) | collective-permute-done | bytes 262176 | tf_op jit(solution)/shard_map/ppermute | solution.py:750
  49.9 0.7 collective-permute-start.21
  50.6 1.5 %collective-permute-start.20 = (bf16[256,512]{1,0:T(8,128)(2,1)S(1)}, bf16[256,512]{1,0:T(8,128)(2,1)S(1)}, u32[]{:S(2)}, u32[]{:S(2)}) collective-permute-start(bf16[256,512]{1,0:T(8,128)(2,1)S(1)} %collective-permute-done.17.refs_4_.refs_8_.refs_12_), channel_id=1, source_target_pairs={{0,4},{1,5},{2,6},{3,7},{4,0},{5,1},{6,2},{7,3},{8,12},{9,13},{10,... | collective-permute-start | bytes 786440 | tf_op jit(solution)/shard_map/ppermute | solution.py:750
  52.2 1.1 copy-done.2
  53.9 1.5 %project.1 = (bf16[512,1024]{1,0:T(8,128)(2,1)S(1)}, f32[512,640]{1,0:T(8,128)S(1)}, f32[4,128]{1,0:T(4,128)S(1)}, bf16[256,128]{1,0:T(8,128)(2,1)S(1)}) custom-call(s32[1]{0:T(128)} %bitcast.me_ref, bf16[272,1024]{1,0:T(8,128)(2,1)S(1)} %copy-done.2, bf16[272,1024]{1,0:T(8,128)(2,1)S(1)} %collective-permute-done.refs_1_.refs_9_, ...), custom_call_target="tpu_custom_call" | custom-call | flops 4000000000 | bytes 1024 | tf_op jit(solution)/shard_map/project/pallas_call | solution.py:55
  55.5 1.1 collective-permute-start.14
  56.6 0.7 collective-permute-start.13
  57.8 1.3 collective-permute-start.22
  59.7 0.8 collective-permute-done.14.g2
  60.6 4.6 %scan.1 = (f32[512,512]{1,0:T(8,128)S(1)}, f32[512,896]{1,0:T(8,128)S(1)}) custom-call(s32[1]{0:T(128)} %bitcast.me_ref, f32[512,640]{1,0:T(8,128)S(1)} %get-tuple-element.116.own_ref, bf16[256,128]{1,0:T(8,128)(2,1)S(1)} %collective-permute-done.13.g1, bf16[256,128]{1,0:T(8,128)(2,1)S(1)} %collective-permute-done.14.g2, ...), custom_call_target="tpu_custom_call" | custom-call | flops 16000000000 | bytes 1024 | tf_op jit(solution)/shard_map/scan/pallas_call | solution.py:55
  65.8 0.8 normcot.1
  66.6 1.2 gate.1
  68.1 1.1 collective-permute-start.24
  69.8 1.3 collective-permute-done.25.refs_3_
  71.1 0.9 collective-permute-done.24.refs_2_
  72.0 4.2 %ungate.1 = (bf16[512,512]{1,0:T(8,128)(2,1)S(1)}, f32[512,512]{1,0:T(8,128)S(1)}, bf16[512,512]{1,0:T(8,128)(2,1)S(1)}, f32[1,512]{1,0:T(1,128)S(1)}, f32[128,1...) custom-call(s32[1]{0:T(128)} %bitcast.me_ref, ...), custom_call_target="tpu_custom_call" | custom-call | flops 1000 | bytes 1024 | tf_op jit(solution)/shard_map/ungate/pallas_call | solution.py:55
  76.2 0.7 branch.1
  77.1 1.3 collective-permute-start.31
  78.4 1.2 collective-permute-start.32
  79.7 1.3 collective-permute-start.30
  81.0 8.4 %scanback.1 = (bf16[512,640]{1,0:T(8,128)(2,1)S(1)}, f32[16,640]{1,0:T(8,128)S(1)}, f32[256,128]{1,0:T(8,128)S(1)}, bf16[256,128]{1,0:T(8,128)(2,1)S(1)}, bf16[2...) custom-call(s32[1]{0:T(128)} %bitcast.me_ref, f32[512,896]{1,0:T(8,128)S(1)} %get-tuple-element.121.proj_ref, ...), custom_call_target="tpu_custom_call" | custom-call | flops 1000 | bytes 1024 | tf_op jit(solution)/shard_map/scanback/pallas_call | solution.py:55
  89.3 2.0 %collective-permute-done.31.got_ref = bf16[512,512]{1,0:T(8,128)(2,1)S(1)} collective-permute-done((bf16[512,512]{1,0:T(8,128)(2,1)S(1)}, bf16[512,512]{1,0:T(8,128)(2,1)S(1)}, u32[]{:S(2)}, u32[]{:S(2)}) %collective-permute-start.31) | collective-permute-done | bytes 524320 | tf_op jit(solution)/shard_map/ppermute | solution.py:750
  91.4 1.0 collective-permute-done.32.got_ref.refs_5_
  92.4 1.3 collective-permute-start.38
  93.7 1.2 collective-permute-start.27
  95.6 3.0 %collective-permute-done.27.g2 = bf16[256,128]{1,0:T(8,128)(2,1)S(1)} collective-permute-done((bf16[256,128]{1,0:T(8,128)(2,1)S(1)}, bf16[256,128]{1,0:T(8,128)(2,1)S(1)}, u32[]{:S(2)}, u32[]{:S(2)}) %collective-permute-start.27) | collective-permute-done | bytes 65568 | tf_op jit(solution)/shard_map/ppermute | solution.py:750
  99.2 1.5 %ingrad.1 = (bf16[512,640]{1,0:T(8,128)(2,1)S(1)}, f32[128,640]{1,0:T(8,128)S(1)}, f32[128,640]{1,0:T(8,128)S(1)}, f32[128,640]{1,0:T(8,128)S(1)}, f32[128,640]{...) custom-call(s32[1]{0:T(128)} %bitcast.me_ref, ...), custom_call_target="tpu_custom_call" | custom-call | flops 1000 | bytes 1024 | tf_op jit(solution)/shard_map/ingrad/pallas_call | solution.py:55
  100.9 2.6 %tail.1 = (f32[256,1024]{1,0:T(8,128)S(1)}, bf16[256,1024]{1,0:T(8,128)(2,1)S(1)}) custom-call(s32[1]{0:T(128)} %bitcast.me_ref, bf16[128,640]{1,0:T(8,128)(2,1)S(1)} %get-tuple-element.109.refs_4_.refs_0_, bf16[128,640]{1,0:T(8,128)(2,1)S(1)} %collective-permute-done.6.refs_5_.refs_1_, bf16[128,640]{1,0:T(8,128)(2,1)S(1)} %collective-permute-done.8.refs_6_.refs_2_, ...), custom_call_target="tpu_custom_call" | custom-call | flops 1000 | bytes 1024 | tf_op jit(solution)/shard_map/tail/pallas_call | solution.py:55
  104.1 0.8 collective-permute-start.35
  104.9 0.8 collective-permute-start.41
  105.6 3.4 %collective-permute-start.40 = (bf16[256,512]{1,0:T(8,128)(2,1)S(1)}, bf16[256,512]{1,0:T(8,128)(2,1)S(1)}, u32[]{:S(2)}, u32[]{:S(2)}) collective-permute-start(bf16[256,512]{1,0:T(8,128)(2,1)S(1)} %far.3), channel_id=1, source_target_pairs={{0,16},{1,17},{2,18},{3,19},{4,20},{5,21},{6,22},{7,23},{8,24},{9,... | collective-permute-start | bytes 786440 | tf_op jit(solution)/shard_map/ppermute | solution.py:750
  109.1 1.2 collective-permute-start.33
  110.3 4.8 %collective-permute-done.35.got_ref.side_ref = bf16[272,640]{1,0:T(8,128)(2,1)S(1)} collective-permute-done((bf16[272,640]{1,0:T(8,128)(2,1)S(1)}, bf16[272,640]{1,0:T(8,128)(2,1)S(1)}, u32[]{:S(2)}, u32[]{:S(2)}) %collective-permute-start.35) | collective-permute-done | bytes 348192 | tf_op jit(solution)/shard_map/ppermute | solution.py:750
  115.1 0.8 collective-permute-start.36
  115.9 3.6 %collective-permute-done.41.refs_6_ = bf16[256,512]{1,0:T(8,128)(2,1)S(1)} collective-permute-done((bf16[256,512]{1,0:T(8,128)(2,1)S(1)}, bf16[256,512]{1,0:T(8,128)(2,1)S(1)}, u32[]{:S(2)}, u32[]{:S(2)}) %collective-permute-start.41) | collective-permute-done | bytes 262176 | tf_op jit(solution)/shard_map/ppermute | solution.py:750
  119.9 1.1 collective-permute-start.42
  121.0 1.4 %collective-permute-done.36.got_ref = bf16[144,640]{1,0:T(8,128)(2,1)S(1)} collective-permute-done((bf16[144,640]{1,0:T(8,128)(2,1)S(1)}, bf16[144,640]{1,0:T(8,128)(2,1)S(1)}, u32[]{:S(2)}, u32[]{:S(2)}) %collective-permute-start.36) | collective-permute-done | bytes 184352 | tf_op jit(solution)/shard_map/ppermute | solution.py:750
  122.5 2.6 %collective-permute-start.37 = (bf16[144,640]{1,0:T(8,128)(2,1)S(1)}, bf16[144,640]{1,0:T(8,128)(2,1)S(1)}, u32[]{:S(2)}, u32[]{:S(2)}) collective-permute-start(bf16[144,640]{1,0:T(8,128)(2,1)S(1)} %get-tuple-element.163), channel_id=1, source_target_pairs={{0,16},{1,17},{2,18},{3,19},{4,20},{5,21},{6,22},{7,23},{8,24},{9,... | collective-permute-start | bytes 552968 | tf_op jit(solution)/shard_map/ppermute | solution.py:750
  125.1 1.8 %collective-permute-start.34 = (bf16[128,640]{1,0:T(8,128)(2,1)S(1)}, bf16[128,640]{1,0:T(8,128)(2,1)S(1)}, u32[]{:S(2)}, u32[]{:S(2)}) collective-permute-start(bf16[128,640]{1,0:T(8,128)(2,1)S(1)} %near.3), channel_id=1, source_target_pairs={{0,8},{1,9},{2,10},{3,11},{4,12},{5,13},{6,14},{7,15},{8,0},{9,1},... | collective-permute-start | bytes 491528 | tf_op jit(solution)/shard_map/ppermute | solution.py:750
  126.9 6.1 %collective-permute-done.37.refs_3_ = bf16[144,640]{1,0:T(8,128)(2,1)S(1)} collective-permute-done((bf16[144,640]{1,0:T(8,128)(2,1)S(1)}, bf16[144,640]{1,0:T(8,128)(2,1)S(1)}, u32[]{:S(2)}, u32[]{:S(2)}) %collective-permute-start.37) | collective-permute-done | bytes 184352 | tf_op jit(solution)/shard_map/ppermute | solution.py:750
  133.1 1.0 total.1
  134.2 1.3 collective-permute-start.44
  136.0 0.8 mixed.1
  136.8 1.1 tokgrad.1
  137.9 2.1 %collective-permute-done.44.refs_1_ = bf16[48,1152]{1,0:T(8,128)(2,1)S(1)} collective-permute-done((bf16[48,1152]{1,0:T(8,128)(2,1)S(1)}, bf16[48,1152]{1,0:T(8,128)(2,1)S(1)}, u32[]{:S(2)}, u32[]{:S(2)}) %collective-permute-start.44) | collective-permute-done | bytes 110624 | tf_op jit(solution)/shard_map/ppermute | solution.py:750
  140.0 1.6 %collective-permute-done.45.refs_2_ = bf16[48,1152]{1,0:T(8,128)(2,1)S(1)} collective-permute-done((bf16[48,1152]{1,0:T(8,128)(2,1)S(1)}, bf16[48,1152]{1,0:T(8,128)(2,1)S(1)}, u32[]{:S(2)}, u32[]{:S(2)}) %collective-permute-start.45) | collective-permute-done | bytes 110624 | tf_op jit(solution)/shard_map/ppermute | solution.py:750
  141.6 1.7 %finish.1 = (f32[32,4384]{1,0:T(8,128)}, f32[4,2304]{1,0:T(4,128)}, f32[18,128]{1,0:T(8,128)}, f32[1,32]{1,0:T(1,128)}, f32[1,32]{1,0:T(1,128)}, /*index=5*/f32[...) custom-call(s32[1]{0:T(128)} %bitcast.me_ref, f32[32,1152]{1,0:T(8,128)S(1)} %get-tuple-element.181.mine_ref, ...), custom_call_target="tpu_custom_call" | custom-call | flops 1000 | bytes 1024 | tf_op jit(solution)/shard_map/finish/pallas_call | solution.py:55
  (77 shorter events, 9.5 us)
Async XLA Ops:
  3.6 3.5 %collective-permute-start = (bf16[272,1024]{1,0:T(8,128)(2,1)}, bf16[272,1024]{1,0:T(8,128)(2,1)S(1)}, u32[]{:S(2)}, u32[]{:S(2)}) collective-permute-start(bf16[272,1024]{1,0:T(8,128)(2,1)} %get-tuple-element.110.refs_0_.refs_8_.act_ref), channel_id=1, source_target_pairs={{0,1},{1,0},{2,3},{3,2},{4,5},{5,4},{6,7},{7,6},{8,9},{9,8},{10,11... | collective-permute-start | bytes 1671176 | tf_op jit(solution)/shard_map/ppermute | solution.py:750
  4.1 3.0 %collective-permute-start.1 = (bf16[32,1152]{1,0:T(8,128)(2,1)}, bf16[32,1152]{1,0:T(8,128)(2,1)S(1)}, u32[]{:S(2)}, u32[]{:S(2)}) collective-permute-start(bf16[32,1152]{1,0:T(8,128)(2,1)} %get-tuple-element.105), channel_id=1, source_target_pairs={{0,1},{1,0},{2,3},{3,2},{4,5},{5,4},{6,7},{7,6},{8,9},{9,8},{10,11... | collective-permute-start | bytes 221192 | tf_op jit(solution)/shard_map/ppermute | solution.py:750
  4.2 5.8 %collective-permute-start.2 = (bf16[32,1152]{1,0:T(8,128)(2,1)}, bf16[32,1152]{1,0:T(8,128)(2,1)S(1)}, u32[]{:S(2)}, u32[]{:S(2)}) collective-permute-start(bf16[32,1152]{1,0:T(8,128)(2,1)} %get-tuple-element.107), channel_id=1, source_target_pairs={{0,2},{1,3},{2,0},{3,1},{4,6},{5,7},{6,4},{7,5},{8,10},{9,11},{10,... | collective-permute-start | bytes 221192 | tf_op jit(solution)/shard_map/ppermute | solution.py:750
  7.1 4.8 %collective-permute-start.3 = (bf16[32,1152]{1,0:T(8,128)(2,1)}, bf16[32,1152]{1,0:T(8,128)(2,1)S(1)}, u32[]{:S(2)}, u32[]{:S(2)}) collective-permute-start(bf16[32,1152]{1,0:T(8,128)(2,1)} %get-tuple-element.108), channel_id=1, source_target_pairs={{0,3},{1,2},{2,1},{3,0},{4,7},{5,6},{6,5},{7,4},{8,11},{9,10},{10,... | collective-permute-start | bytes 221192 | tf_op jit(solution)/shard_map/ppermute | solution.py:750
  11.9 0.9 copy-start.6
  12.8 0.9 copy-start.7
  13.7 14.9 %collective-permute-start.4 = (bf16[272,1024]{1,0:T(8,128)(2,1)}, bf16[272,1024]{1,0:T(8,128)(2,1)S(1)}, u32[]{:S(2)}, u32[]{:S(2)}) collective-permute-start(bf16[272,1024]{1,0:T(8,128)(2,1)} %get-tuple-element.110.refs_0_.refs_8_.act_ref), channel_id=1, source_target_pairs={{0,2},{1,3},{2,0},{3,1},{4,6},{5,7},{6,4},{7,5},{8,10},{9,11},{10,... | collective-permute-start | bytes 1671176 | tf_op jit(solution)/shard_map/ppermute | solution.py:750
  14.3 14.3 %collective-permute-start.8 = (bf16[128,640]{1,0:T(8,128)(2,1)S(1)}, bf16[128,640]{1,0:T(8,128)(2,1)S(1)}, u32[]{:S(2)}, u32[]{:S(2)}) collective-permute-start(bf16[128,640]{1,0:T(8,128)(2,1)S(1)} %get-tuple-element.109.refs_4_.refs_0_), channel_id=1, source_target_pairs={{0,8},{1,9},{2,10},{3,11},{4,12},{5,13},{6,14},{7,15},{8,0},{9,1},... | collective-permute-start | bytes 491528 | tf_op jit(solution)/shard_map/ppermute | solution.py:750
  15.9 12.7 %collective-permute-start.7 = (bf16[128,640]{1,0:T(8,128)(2,1)S(1)}, bf16[128,640]{1,0:T(8,128)(2,1)S(1)}, u32[]{:S(2)}, u32[]{:S(2)}) collective-permute-start(bf16[128,640]{1,0:T(8,128)(2,1)S(1)} %get-tuple-element.109.refs_4_.refs_0_), channel_id=1, source_target_pairs={{0,16},{1,17},{2,18},{3,19},{4,20},{5,21},{6,22},{7,23},{8,24},{9,... | collective-permute-start | bytes 491528 | tf_op jit(solution)/shard_map/ppermute | solution.py:750
  18.5 10.1 %collective-permute-start.6 = (bf16[128,640]{1,0:T(8,128)(2,1)S(1)}, bf16[128,640]{1,0:T(8,128)(2,1)S(1)}, u32[]{:S(2)}, u32[]{:S(2)}) collective-permute-start(bf16[128,640]{1,0:T(8,128)(2,1)S(1)} %get-tuple-element.109.refs_4_.refs_0_), channel_id=1, source_target_pairs={{0,4},{1,5},{2,6},{3,7},{4,0},{5,1},{6,2},{7,3},{8,12},{9,13},{10,... | collective-permute-start | bytes 491528 | tf_op jit(solution)/shard_map/ppermute | solution.py:750
  28.6 23.5 %collective-permute-start.5 = (bf16[272,1024]{1,0:T(8,128)(2,1)S(1)}, bf16[272,1024]{1,0:T(8,128)(2,1)S(1)}, u32[]{:S(2)}, u32[]{:S(2)}) collective-permute-start(bf16[272,1024]{1,0:T(8,128)(2,1)S(1)} %collective-permute-done.4.refs_2_.refs_10_), channel_id=1, source_target_pairs={{0,1},{1,0},{2,3},{3,2},{4,5},{5,4},{6,7},{7,6},{8,9},{9,8},{10,11... | collective-permute-start | bytes 1671176 | tf_op jit(solution)/shard_map/ppermute | solution.py:750
  28.6 7.1 %collective-permute-start.11 = (bf16[128,640]{1,0:T(8,128)(2,1)S(1)}, bf16[128,640]{1,0:T(8,128)(2,1)S(1)}, u32[]{:S(2)}, u32[]{:S(2)}) collective-permute-start(bf16[128,640]{1,0:T(8,128)(2,1)S(1)} %collective-permute-done.7.refs_8_.refs_4_), channel_id=1, source_target_pairs={{0,8},{1,9},{2,10},{3,11},{4,12},{5,13},{6,14},{7,15},{8,0},{9,1},... | collective-permute-start | bytes 491528 | tf_op jit(solution)/shard_map/ppermute | solution.py:750
  30.3 13.5 %collective-permute-start.16 = (bf16[256,512]{1,0:T(8,128)(2,1)S(1)}, bf16[256,512]{1,0:T(8,128)(2,1)S(1)}, u32[]{:S(2)}, u32[]{:S(2)}) collective-permute-start(bf16[256,512]{1,0:T(8,128)(2,1)S(1)} %get-tuple-element.123.refs_0_.refs_4_.refs_8_), channel_id=1, source_target_pairs={{0,4},{1,5},{2,6},{3,7},{4,0},{5,1},{6,2},{7,3},{8,12},{9,13},{10,... | collective-permute-start | bytes 786440 | tf_op jit(solution)/shard_map/ppermute | solution.py:750
  31.8 10.4 %collective-permute-start.10 = (bf16[128,640]{1,0:T(8,128)(2,1)S(1)}, bf16[128,640]{1,0:T(8,128)(2,1)S(1)}, u32[]{:S(2)}, u32[]{:S(2)}) collective-permute-start(bf16[128,640]{1,0:T(8,128)(2,1)S(1)} %collective-permute-done.7.refs_8_.refs_4_), channel_id=1, source_target_pairs={{0,4},{1,5},{2,6},{3,7},{4,0},{5,1},{6,2},{7,3},{8,12},{9,13},{10,... | collective-permute-start | bytes 491528 | tf_op jit(solution)/shard_map/ppermute | solution.py:750
  32.3 15.4 %collective-permute-start.18 = (bf16[256,512]{1,0:T(8,128)(2,1)S(1)}, bf16[256,512]{1,0:T(8,128)(2,1)S(1)}, u32[]{:S(2)}, u32[]{:S(2)}) collective-permute-start(bf16[256,512]{1,0:T(8,128)(2,1)S(1)} %get-tuple-element.123.refs_0_.refs_4_.refs_8_), channel_id=1, source_target_pairs={{0,8},{1,9},{2,10},{3,11},{4,12},{5,13},{6,14},{7,15},{8,0},{9,1},... | collective-permute-start | bytes 786440 | tf_op jit(solution)/shard_map/ppermute | solution.py:750
  35.7 14.2 %collective-permute-start.17 = (bf16[256,512]{1,0:T(8,128)(2,1)S(1)}, bf16[256,512]{1,0:T(8,128)(2,1)S(1)}, u32[]{:S(2)}, u32[]{:S(2)}) collective-permute-start(bf16[256,512]{1,0:T(8,128)(2,1)S(1)} %get-tuple-element.123.refs_0_.refs_4_.refs_8_), channel_id=1, source_target_pairs={{0,16},{1,17},{2,18},{3,19},{4,20},{5,21},{6,22},{7,23},{8,24},{9,... | collective-permute-start | bytes 786440 | tf_op jit(solution)/shard_map/ppermute | solution.py:750
  42.2 5.5 %collective-permute-start.9 = (bf16[128,640]{1,0:T(8,128)(2,1)S(1)}, bf16[128,640]{1,0:T(8,128)(2,1)S(1)}, u32[]{:S(2)}, u32[]{:S(2)}) collective-permute-start(bf16[128,640]{1,0:T(8,128)(2,1)S(1)} %collective-permute-done.8.refs_6_.refs_2_), channel_id=1, source_target_pairs={{0,4},{1,5},{2,6},{3,7},{4,0},{5,1},{6,2},{7,3},{8,12},{9,13},{10,... | collective-permute-start | bytes 491528 | tf_op jit(solution)/shard_map/ppermute | solution.py:750
  43.7 8.4 %collective-permute-start.12 = (bf16[128,640]{1,0:T(8,128)(2,1)S(1)}, bf16[128,640]{1,0:T(8,128)(2,1)S(1)}, u32[]{:S(2)}, u32[]{:S(2)}) collective-permute-start(bf16[128,640]{1,0:T(8,128)(2,1)S(1)} %collective-permute-done.10.refs_9_.refs_5_), channel_id=1, source_target_pairs={{0,8},{1,9},{2,10},{3,11},{4,12},{5,13},{6,14},{7,15},{8,0},{9,1},... | collective-permute-start | bytes 491528 | tf_op jit(solution)/shard_map/ppermute | solution.py:750
  49.9 7.4 %collective-permute-start.21 = (bf16[256,512]{1,0:T(8,128)(2,1)S(1)}, bf16[256,512]{1,0:T(8,128)(2,1)S(1)}, u32[]{:S(2)}, u32[]{:S(2)}) collective-permute-start(bf16[256,512]{1,0:T(8,128)(2,1)S(1)} %collective-permute-done.17.refs_4_.refs_8_.refs_12_), channel_id=1, source_target_pairs={{0,8},{1,9},{2,10},{3,11},{4,12},{5,13},{6,14},{7,15},{8,0},{9,1},... | collective-permute-start | bytes 786440 | tf_op jit(solution)/shard_map/ppermute | solution.py:750
  50.6 7.2 %collective-permute-start.20 = (bf16[256,512]{1,0:T(8,128)(2,1)S(1)}, bf16[256,512]{1,0:T(8,128)(2,1)S(1)}, u32[]{:S(2)}, u32[]{:S(2)}) collective-permute-start(bf16[256,512]{1,0:T(8,128)(2,1)S(1)} %collective-permute-done.17.refs_4_.refs_8_.refs_12_), channel_id=1, source_target_pairs={{0,4},{1,5},{2,6},{3,7},{4,0},{5,1},{6,2},{7,3},{8,12},{9,13},{10,... | collective-permute-start | bytes 786440 | tf_op jit(solution)/shard_map/ppermute | solution.py:750
  52.2 1.1 copy-start.2
  53.2 0.7 copy-start.9
  53.9 6.7 %copy-start.8 = (f32[8,768]{1,0:T(8,128)S(1)}, f32[8,768]{1,0:T(8,128)}, u32[]{:S(2)}) copy-start(f32[8,768]{1,0:T(8,128)} %get-tuple-element.119.cw_ref) | copy-start | bytes 73732
  53.9 6.7 %copy-start.12 = (f32[8,128]{1,0:T(8,128)S(1)}, f32[8,128]{1,0:T(8,128)}, u32[]{:S(2)}) copy-start(f32[8,128]{1,0:T(8,128)} %get-tuple-element.120.head_ref) | copy-start | bytes 12292
  55.4 11.2 %copy-start = (bf16[512,1024]{1,0:T(8,128)(2,1)}, bf16[512,1024]{1,0:T(8,128)(2,1)S(1)}, u32[]{:S(2)}) copy-start(bf16[512,1024]{1,0:T(8,128)(2,1)S(1)} %get-tuple-element.115.refs_8_.refs_16_.norm_ref) | copy-start | bytes 3145732
  55.4 4.4 %collective-permute-start.15 = (bf16[256,128]{1,0:T(8,128)(2,1)S(1)}, bf16[256,128]{1,0:T(8,128)(2,1)S(1)}, u32[]{:S(2)}, u32[]{:S(2)}) collective-permute-start(bf16[256,128]{1,0:T(8,128)(2,1)S(1)} %get-tuple-element.117), channel_id=1, source_target_pairs={{0,3},{1,2},{2,1},{3,0},{4,7},{5,6},{6,5},{7,4},{8,11},{9,10},{10,... | collective-permute-start | bytes 196616 | tf_op jit(solution)/shard_map/ppermute | solution.py:750
  55.5 5.1 %collective-permute-start.14 = (bf16[256,128]{1,0:T(8,128)(2,1)S(1)}, bf16[256,128]{1,0:T(8,128)(2,1)S(1)}, u32[]{:S(2)}, u32[]{:S(2)}) collective-permute-start(bf16[256,128]{1,0:T(8,128)(2,1)S(1)} %get-tuple-element.117), channel_id=1, source_target_pairs={{0,2},{1,3},{2,0},{3,1},{4,6},{5,7},{6,4},{7,5},{8,10},{9,11},{10,... | collective-permute-start | bytes 196616 | tf_op jit(solution)/shard_map/ppermute | solution.py:750
  56.6 4.0 %collective-permute-start.13 = (bf16[256,128]{1,0:T(8,128)(2,1)S(1)}, bf16[256,128]{1,0:T(8,128)(2,1)S(1)}, u32[]{:S(2)}, u32[]{:S(2)}) collective-permute-start(bf16[256,128]{1,0:T(8,128)(2,1)S(1)} %get-tuple-element.117), channel_id=1, source_target_pairs={{0,1},{1,0},{2,3},{3,2},{4,5},{5,4},{6,7},{7,6},{8,9},{9,8},{10,11... | collective-permute-start | bytes 196616 | tf_op jit(solution)/shard_map/ppermute | solution.py:750
  57.3 8.2 %collective-permute-start.19 = (bf16[256,512]{1,0:T(8,128)(2,1)S(1)}, bf16[256,512]{1,0:T(8,128)(2,1)S(1)}, u32[]{:S(2)}, u32[]{:S(2)}) collective-permute-start(bf16[256,512]{1,0:T(8,128)(2,1)S(1)} %collective-permute-done.18.refs_2_.refs_6_.refs_10_), channel_id=1, source_target_pairs={{0,4},{1,5},{2,6},{3,7},{4,0},{5,1},{6,2},{7,3},{8,12},{9,13},{10,... | collective-permute-start | bytes 786440 | tf_op jit(solution)/shard_map/ppermute | solution.py:750
  57.8 7.9 %collective-permute-start.22 = (bf16[256,512]{1,0:T(8,128)(2,1)S(1)}, bf16[256,512]{1,0:T(8,128)(2,1)S(1)}, u32[]{:S(2)}, u32[]{:S(2)}) collective-permute-start(bf16[256,512]{1,0:T(8,128)(2,1)S(1)} %collective-permute-done.20.refs_5_.refs_9_.refs_13_), channel_id=1, source_target_pairs={{0,8},{1,9},{2,10},{3,11},{4,12},{5,13},{6,14},{7,15},{8,0},{9,1},... | collective-permute-start | bytes 786440 | tf_op jit(solution)/shard_map/ppermute | solution.py:750
  60.6 5.1 %copy-start.3 = (bf16[272,1024]{1,0:T(8,128)(2,1)S(1)}, bf16[272,1024]{1,0:T(8,128)(2,1)}, u32[]{:S(2)}) copy-start(bf16[272,1024]{1,0:T(8,128)(2,1)} %get-tuple-element.110.refs_0_.refs_8_.act_ref) | copy-start | bytes 1671172
  65.3 1.4 copy-start.11
  66.6 1.2 copy-start.4
  66.6 1.3 copy-start.5
  67.9 3.2 %collective-permute-start.25 = (f32[8,512]{1,0:T(8,128)S(1)}, f32[8,512]{1,0:T(8,128)S(1)}, u32[]{:S(2)}, u32[]{:S(2)}) collective-permute-start(f32[8,512]{1,0:T(8,128)S(1)} %get-tuple-element.130.refs_0_), channel_id=1, source_target_pairs={{0,3},{1,2},{2,1},{3,0},{4,7},{5,6},{6,5},{7,4},{8,11},{9,10},{10,... | collective-permute-start | bytes 49160 | tf_op jit(solution)/shard_map/ppermute | solution.py:750
  68.1 3.9 %collective-permute-start.24 = (f32[8,512]{1,0:T(8,128)S(1)}, f32[8,512]{1,0:T(8,128)S(1)}, u32[]{:S(2)}, u32[]{:S(2)}) collective-permute-start(f32[8,512]{1,0:T(8,128)S(1)} %get-tuple-element.130.refs_0_), channel_id=1, source_target_pairs={{0,2},{1,3},{2,0},{3,1},{4,6},{5,7},{6,4},{7,5},{8,10},{9,11},{10,... | collective-permute-start | bytes 49160 | tf_op jit(solution)/shard_map/ppermute | solution.py:750
  69.2 2.8 %collective-permute-start.23 = (f32[8,512]{1,0:T(8,128)S(1)}, f32[8,512]{1,0:T(8,128)S(1)}, u32[]{:S(2)}, u32[]{:S(2)}) collective-permute-start(f32[8,512]{1,0:T(8,128)S(1)} %get-tuple-element.130.refs_0_), channel_id=1, source_target_pairs={{0,1},{1,0},{2,3},{3,2},{4,5},{5,4},{6,7},{7,6},{8,9},{9,8},{10,11... | collective-permute-start | bytes 49160 | tf_op jit(solution)/shard_map/ppermute | solution.py:750
  76.9 2.7 %collective-permute-start.29 = (bf16[256,1024]{1,0:T(8,128)(2,1)S(1)}, bf16[256,1024]{1,0:T(8,128)(2,1)S(1)}, u32[]{:S(2)}, u32[]{:S(2)}) collective-permute-start(bf16[256,1024]{1,0:T(8,128)(2,1)S(1)} %get-tuple-element.143), channel_id=1, source_target_pairs={{0,1},{1,0},{2,3},{3,2},{4,5},{5,4},{6,7},{7,6},{8,9},{9,8},{10,11... | collective-permute-start | bytes 1572872 | tf_op jit(solution)/shard_map/ppermute | solution.py:750
  77.1 14.3 %collective-permute-start.31 = (bf16[512,512]{1,0:T(8,128)(2,1)S(1)}, bf16[512,512]{1,0:T(8,128)(2,1)S(1)}, u32[]{:S(2)}, u32[]{:S(2)}) collective-permute-start(bf16[512,512]{1,0:T(8,128)(2,1)S(1)} %get-tuple-element.146), channel_id=1, source_target_pairs={{0,8},{1,9},{2,10},{3,11},{4,12},{5,13},{6,14},{7,15},{8,0},{9,1},... | collective-permute-start | bytes 1572872 | tf_op jit(solution)/shard_map/ppermute | solution.py:750
  78.4 14.0 %collective-permute-start.32 = (bf16[512,512]{1,0:T(8,128)(2,1)S(1)}, bf16[512,512]{1,0:T(8,128)(2,1)S(1)}, u32[]{:S(2)}, u32[]{:S(2)}) collective-permute-start(bf16[512,512]{1,0:T(8,128)(2,1)S(1)} %get-tuple-element.147), channel_id=1, source_target_pairs={{0,4},{1,5},{2,6},{3,7},{4,0},{5,1},{6,2},{7,3},{8,12},{9,13},{10,... | collective-permute-start | bytes 1572872 | tf_op jit(solution)/shard_map/ppermute | solution.py:750
  79.7 15.9 %collective-permute-start.30 = (bf16[128,1024]{1,0:T(8,128)(2,1)S(1)}, bf16[128,1024]{1,0:T(8,128)(2,1)S(1)}, u32[]{:S(2)}, u32[]{:S(2)}) collective-permute-start(bf16[128,1024]{1,0:T(8,128)(2,1)S(1)} %get-tuple-element.144), channel_id=1, source_target_pairs={{0,2},{1,3},{2,0},{3,1},{4,6},{5,7},{6,4},{7,5},{8,10},{9,11},{10,... | collective-permute-start | bytes 786440 | tf_op jit(solution)/shard_map/ppermute | solution.py:750
  89.3 9.9 %copy-start.1 = (bf16[512,1024]{1,0:T(8,128)(2,1)S(1)}, bf16[512,1024]{1,0:T(8,128)(2,1)}, u32[]{:S(2)}) copy-start(bf16[512,1024]{1,0:T(8,128)(2,1)} %copy-done) | copy-start | bytes 3145732
  89.3 9.9 %copy-start.10 = (f32[1,1024]{1,0:T(1,128)S(1)}, f32[1,1024]{1,0:T(1,128)}, u32[]{:S(2)}) copy-start(f32[1,1024]{1,0:T(1,128)} %get-tuple-element.114.refs_12_.gain_ref) | copy-start | bytes 12292
  92.4 8.3 %collective-permute-start.38 = (bf16[256,512]{1,0:T(8,128)(2,1)S(1)}, bf16[256,512]{1,0:T(8,128)(2,1)S(1)}, u32[]{:S(2)}, u32[]{:S(2)}) collective-permute-start(bf16[256,512]{1,0:T(8,128)(2,1)S(1)} %side.2), channel_id=1, source_target_pairs={{0,4},{1,5},{2,6},{3,7},{4,0},{5,1},{6,2},{7,3},{8,12},{9,13},{10,... | collective-permute-start | bytes 786440 | tf_op jit(solution)/shard_map/ppermute | solution.py:750
  93.7 1.9 %collective-permute-start.26 = (bf16[256,128]{1,0:T(8,128)(2,1)S(1)}, bf16[256,128]{1,0:T(8,128)(2,1)S(1)}, u32[]{:S(2)}, u32[]{:S(2)}) collective-permute-start(bf16[256,128]{1,0:T(8,128)(2,1)S(1)} %get-tuple-element.136), channel_id=1, source_target_pairs={{0,1},{1,0},{2,3},{3,2},{4,5},{5,4},{6,7},{7,6},{8,9},{9,8},{10,11... | collective-permute-start | bytes 196616 | tf_op jit(solution)/shard_map/ppermute | solution.py:750
  93.7 4.9 %collective-permute-start.27 = (bf16[256,128]{1,0:T(8,128)(2,1)S(1)}, bf16[256,128]{1,0:T(8,128)(2,1)S(1)}, u32[]{:S(2)}, u32[]{:S(2)}) collective-permute-start(bf16[256,128]{1,0:T(8,128)(2,1)S(1)} %get-tuple-element.137), channel_id=1, source_target_pairs={{0,2},{1,3},{2,0},{3,1},{4,6},{5,7},{6,4},{7,5},{8,10},{9,11},{10,... | collective-permute-start | bytes 196616 | tf_op jit(solution)/shard_map/ppermute | solution.py:750
  94.9 4.3 %collective-permute-start.28 = (bf16[256,128]{1,0:T(8,128)(2,1)S(1)}, bf16[256,128]{1,0:T(8,128)(2,1)S(1)}, u32[]{:S(2)}, u32[]{:S(2)}) collective-permute-start(bf16[256,128]{1,0:T(8,128)(2,1)S(1)} %get-tuple-element.138), channel_id=1, source_target_pairs={{0,3},{1,2},{2,1},{3,0},{4,7},{5,6},{6,5},{7,4},{8,11},{9,10},{10,... | collective-permute-start | bytes 196616 | tf_op jit(solution)/shard_map/ppermute | solution.py:750
  103.5 16.3 %collective-permute-start.39 = (bf16[256,1024]{1,0:T(8,128)(2,1)S(1)}, bf16[256,1024]{1,0:T(8,128)(2,1)S(1)}, u32[]{:S(2)}, u32[]{:S(2)}) collective-permute-start(bf16[256,1024]{1,0:T(8,128)(2,1)S(1)} %get-tuple-element.170), channel_id=1, source_target_pairs={{0,1},{1,0},{2,3},{3,2},{4,5},{5,4},{6,7},{7,6},{8,9},{9,8},{10,11... | collective-permute-start | bytes 1572872 | tf_op jit(solution)/shard_map/ppermute | solution.py:750
  104.1 11.0 %collective-permute-start.35 = (bf16[272,640]{1,0:T(8,128)(2,1)S(1)}, bf16[272,640]{1,0:T(8,128)(2,1)S(1)}, u32[]{:S(2)}, u32[]{:S(2)}) collective-permute-start(bf16[272,640]{1,0:T(8,128)(2,1)S(1)} %get-tuple-element.159), channel_id=1, source_target_pairs={{0,4},{1,5},{2,6},{3,7},{4,0},{5,1},{6,2},{7,3},{8,12},{9,13},{10,... | collective-permute-start | bytes 1044488 | tf_op jit(solution)/shard_map/ppermute | solution.py:750
  104.9 14.7 %collective-permute-start.41 = (bf16[256,512]{1,0:T(8,128)(2,1)S(1)}, bf16[256,512]{1,0:T(8,128)(2,1)S(1)}, u32[]{:S(2)}, u32[]{:S(2)}) collective-permute-start(bf16[256,512]{1,0:T(8,128)(2,1)S(1)} %near.2), channel_id=1, source_target_pairs={{0,8},{1,9},{2,10},{3,11},{4,12},{5,13},{6,14},{7,15},{8,0},{9,1},... | collective-permute-start | bytes 786440 | tf_op jit(solution)/shard_map/ppermute | solution.py:750
  105.6 14.2 %collective-permute-start.40 = (bf16[256,512]{1,0:T(8,128)(2,1)S(1)}, bf16[256,512]{1,0:T(8,128)(2,1)S(1)}, u32[]{:S(2)}, u32[]{:S(2)}) collective-permute-start(bf16[256,512]{1,0:T(8,128)(2,1)S(1)} %far.3), channel_id=1, source_target_pairs={{0,16},{1,17},{2,18},{3,19},{4,20},{5,21},{6,22},{7,23},{8,24},{9,... | collective-permute-start | bytes 786440 | tf_op jit(solution)/shard_map/ppermute | solution.py:750
  109.1 16.0 %collective-permute-start.33 = (bf16[256,640]{1,0:T(8,128)(2,1)S(1)}, bf16[256,640]{1,0:T(8,128)(2,1)S(1)}, u32[]{:S(2)}, u32[]{:S(2)}) collective-permute-start(bf16[256,640]{1,0:T(8,128)(2,1)S(1)} %get-tuple-element.155), channel_id=1, source_target_pairs={{0,4},{1,5},{2,6},{3,7},{4,0},{5,1},{6,2},{7,3},{8,12},{9,13},{10,... | collective-permute-start | bytes 983048 | tf_op jit(solution)/shard_map/ppermute | solution.py:750
  115.1 7.3 %collective-permute-start.36 = (bf16[144,640]{1,0:T(8,128)(2,1)S(1)}, bf16[144,640]{1,0:T(8,128)(2,1)S(1)}, u32[]{:S(2)}, u32[]{:S(2)}) collective-permute-start(bf16[144,640]{1,0:T(8,128)(2,1)S(1)} %get-tuple-element.161), channel_id=1, source_target_pairs={{0,8},{1,9},{2,10},{3,11},{4,12},{5,13},{6,14},{7,15},{8,0},{9,1},... | collective-permute-start | bytes 552968 | tf_op jit(solution)/shard_map/ppermute | solution.py:750
  119.9 13.1 %collective-permute-start.42 = (bf16[128,1024]{1,0:T(8,128)(2,1)S(1)}, bf16[128,1024]{1,0:T(8,128)(2,1)S(1)}, u32[]{:S(2)}, u32[]{:S(2)}) collective-permute-start(bf16[128,1024]{1,0:T(8,128)(2,1)S(1)} %get-tuple-element.172), channel_id=1, source_target_pairs={{0,2},{1,3},{2,0},{3,1},{4,6},{5,7},{6,4},{7,5},{8,10},{9,11},{10,... | collective-permute-start | bytes 786440 | tf_op jit(solution)/shard_map/ppermute | solution.py:750
  122.5 10.5 %collective-permute-start.37 = (bf16[144,640]{1,0:T(8,128)(2,1)S(1)}, bf16[144,640]{1,0:T(8,128)(2,1)S(1)}, u32[]{:S(2)}, u32[]{:S(2)}) collective-permute-start(bf16[144,640]{1,0:T(8,128)(2,1)S(1)} %get-tuple-element.163), channel_id=1, source_target_pairs={{0,16},{1,17},{2,18},{3,19},{4,20},{5,21},{6,22},{7,23},{8,24},{9,... | collective-permute-start | bytes 552968 | tf_op jit(solution)/shard_map/ppermute | solution.py:750
  125.1 8.0 %collective-permute-start.34 = (bf16[128,640]{1,0:T(8,128)(2,1)S(1)}, bf16[128,640]{1,0:T(8,128)(2,1)S(1)}, u32[]{:S(2)}, u32[]{:S(2)}) collective-permute-start(bf16[128,640]{1,0:T(8,128)(2,1)S(1)} %near.3), channel_id=1, source_target_pairs={{0,8},{1,9},{2,10},{3,11},{4,12},{5,13},{6,14},{7,15},{8,0},{9,1},... | collective-permute-start | bytes 491528 | tf_op jit(solution)/shard_map/ppermute | solution.py:750
  134.1 3.7 %collective-permute-start.43 = (bf16[48,1152]{1,0:T(8,128)(2,1)S(1)}, bf16[48,1152]{1,0:T(8,128)(2,1)S(1)}, u32[]{:S(2)}, u32[]{:S(2)}) collective-permute-start(bf16[48,1152]{1,0:T(8,128)(2,1)S(1)} %get-tuple-element.183), channel_id=1, source_target_pairs={{0,1},{1,0},{2,3},{3,2},{4,5},{5,4},{6,7},{7,6},{8,9},{9,8},{10,11... | collective-permute-start | bytes 331784 | tf_op jit(solution)/shard_map/ppermute | solution.py:750
  134.2 5.9 %collective-permute-start.44 = (bf16[48,1152]{1,0:T(8,128)(2,1)S(1)}, bf16[48,1152]{1,0:T(8,128)(2,1)S(1)}, u32[]{:S(2)}, u32[]{:S(2)}) collective-permute-start(bf16[48,1152]{1,0:T(8,128)(2,1)S(1)} %get-tuple-element.184), channel_id=1, source_target_pairs={{0,2},{1,3},{2,0},{3,1},{4,6},{5,7},{6,4},{7,5},{8,10},{9,11},{10,... | collective-permute-start | bytes 331784 | tf_op jit(solution)/shard_map/ppermute | solution.py:750
  135.5 6.1 %collective-permute-start.45 = (bf16[48,1152]{1,0:T(8,128)(2,1)S(1)}, bf16[48,1152]{1,0:T(8,128)(2,1)S(1)}, u32[]{:S(2)}, u32[]{:S(2)}) collective-permute-start(bf16[48,1152]{1,0:T(8,128)(2,1)S(1)} %get-tuple-element.185), channel_id=1, source_target_pairs={{0,3},{1,2},{2,1},{3,0},{4,7},{5,6},{6,5},{7,4},{8,11},{9,10},{10,... | collective-permute-start | bytes 331784 | tf_op jit(solution)/shard_map/ppermute | solution.py:750

commit v4 on v3

--- a/solution.py
+++ b/solution.py
@@ -16,12 +16,12 @@
 F32 = jnp.float32
 NEG = -1e30
 LANES = 128
+OPT = {'along': 0, 'bsync': 1, 'abyy': 0, 'bbyy': 0, 'atie7': 1, 'btie7': 1, 'actx': 1, 'later': 1, 'turn': 1, 'pcost': 4000000000.0, 'scost': 16000000000.0, 'ucost': 1000.0, 'async': 1, 'y1b': 0, 'r1': 0, 'r2': 4, 'r3': 5, 'r4': 1, 'r5': 0, 'r6': 1, 'r7': 0, 'r8': 2, 'bcost': 1000.0}
 PROJECT_COST = 4e9
 SCAN_COST = 1.6e10
 QUAD = 4
 SMALL = 16
 VMEM_BYTES = 44 * 1024 * 1024
-RAW_BYTES = 60 * 1024 * 1024
 
 
 def mm(a, b):
@@ -52,6 +52,10 @@
         for n, a in enumerate(inputs)
     ]
     shapes = [jax.ShapeDtypeStruct(s, d) for s, d in out_shapes]
+    inputs = [
+        pltpu.with_memory_space_constraint(a, pltpu.HBM) if n in raw else a
+        for n, a in enumerate(inputs)
+    ]
     return pl.pallas_call(
         kernel,
         out_shape=shapes,
@@ -294,15 +298,17 @@
     return total
 
 
-def prep_kernel(me_ref, len_ref, *refs):
-    raws = refs[0:10]
-    act_ref, cwb_ref, head_ref, gain_ref, pre_ref = refs[10:15]
-    outs, scr = refs[15:19], refs[19]
-    w_ref, tok_ref, cot_ref = refs[20:23]
-    sems = refs[30]
+def prep_kernel(me_ref, len_hbm, *refs):
+    raws = refs[0:11]
+    act_ref, cwb_ref, head_ref, gain_ref, pre_ref = refs[11:16]
+    outs, wout_ref, scr = refs[16:20], refs[20], refs[21]
+    w_ref, tok_ref, cot_ref = refs[22:25]
+    sems, len_ref = refs[32], refs[33]
+    lens = pltpu.make_async_copy(len_hbm, len_ref, sems.at[len(raws)])
+    lens.start()
     copies = [
         pltpu.make_async_copy(src, dst, sems.at[n])
-        for n, (src, dst) in enumerate(zip(raws, refs[20:30]))
+        for n, (src, dst) in enumerate(zip(raws, refs[22:32] + (wout_ref,)))
     ]
     for c in copies:
         c.start()
@@ -332,6 +338,7 @@
     for r in range(QUAD):
         outs[r][...] = scr[t ^ r]
     lane = iota((16, model), 1)
+    lens.wait()
     end = jnp.int32(0)
     tail = jnp.zeros((16, model), jnp.int32)
     for s in range(4):
@@ -345,7 +352,7 @@
     act_ref[rows + 16 :, :] = (cot_ref[...].astype(F32) * live).astype(BF)
     for c in copies[3:]:
         c.wait()
-    share_params(t, refs[23:30], cwb_ref, head_ref, gain_ref, pre_ref)
+    share_params(t, refs[25:32], cwb_ref, head_ref, gain_ref, pre_ref)
 
 
 def share_params(t, given, cwb_ref, head_ref, gain_ref, pre_ref):
@@ -752,16 +759,29 @@
     def after(a, *others):
         return lax.optimization_barrier((a,) + others)[0]
 
-    def gather(mine, along=(), later=(), turn=()):
+    def gather(mine, o, along=(), later=(), turn=(), last=()):
         z = after(mine, *later) if later else mine
         got = [mine, None, None, None, swap(z, 4 * QUAD), None, None, None]
         got[2] = swap(z, 2 * QUAD)
-        got[1] = swap(mine, QUAD)
-        got[4], got[2] = lax.optimization_barrier((got[4], got[2], got[1]) + along + turn)[0:2]
+        got[1] = swap(after(mine, *last) if last else mine, QUAD)
+        l2 = turn + (along if OPT['along'] == 0 else ())
+        if OPT[o + 'sync'] == 1:
+            got[4], got[2] = lax.optimization_barrier((got[4], got[2], got[1]) + l2)[0:2]
+        elif OPT[o + 'sync'] == 2:
+            got[4] = after(got[4], got[1], *l2)
+        elif l2:
+            got[4], got[2] = lax.optimization_barrier((got[4], got[2]) + l2)[0:2]
         got[5] = swap(got[4], QUAD)
         got[6] = swap(got[4], 2 * QUAD)
         got[3] = swap(got[2], QUAD)
-        got[7] = swap(after(got[5], got[6]), 2 * QUAD)
+        l3 = along if OPT['along'] == 1 else ()
+        t = OPT[o + 'tie7']
+        if OPT[o + 'byy']:
+            l3 = l3 + ((), (got[5],), (got[5], got[3]), (got[3],))[t]
+            got[7] = swap(after(got[6], *l3) if l3 else got[6], QUAD)
+        else:
+            l3 = l3 + ((), (got[6],), (got[6], got[3]), (got[3],))[t]
+            got[7] = swap(after(got[5], *l3) if l3 else got[5], 2 * QUAD)
         return got
 
     me = lax.axis_index("dp").astype(jnp.int32).reshape(1)
@@ -769,6 +789,7 @@
     lanes = conv_bias.reshape(-1, LANES)
     given = [in_weight, tokens, cotangent, conv_weight, lanes]
     given += [a[None, :] for a in (dt_bias, a_log, skip_gain, norm_gain, pre_gain)]
+    given += [out_weight]
     prepped = call(
         prep_kernel,
         [
@@ -778,31 +799,42 @@
             ((1, width), F32),
             ((1, model), F32),
         ]
-        + [((nrow, both), BF)] * QUAD,
+        + [((nrow, both), BF)] * QUAD
+        + [(out_weight.shape, BF)],
         [me, lengths] + given,
         [pltpu.VMEM((QUAD, nrow, both), BF)]
-        + [pltpu.VMEM(a.shape, a.dtype) for a in given]
-        + [pltpu.SemaphoreType.DMA((len(given),))],
+        + [pltpu.VMEM(a.shape, a.dtype) for a in given[:-1]]
+        + [pltpu.SemaphoreType.DMA((len(given) + 1,)), pltpu.SMEM(lengths.shape, jnp.int32)],
         name="prep",
-        raw=tuple(range(2, 12)),
-        limit=RAW_BYTES,
+        raw=tuple(range(1, 13)),
     )
     act, cwb, by_head, gain, pre = prepped[0:5]
-    cut = prepped[5:]
+    cut, own_out = prepped[5:9], prepped[9]
     got = [swap(cut[r], r) for r in range(1, QUAD)]
     beside = swap(act, 1)
     got[0] = after(got[0], beside)
     own_a, own_b = call(
         join_kernel,
         [((chunk, wide), BF), ((chunk_b, width), BF)],
-        [me, cut[0]] + got + [out_weight],
+        [me, cut[0]] + got + [own_out],
         name="join",
     )
-    across = swap(after(act, own_a), 2)
-    w1 = gather(own_a, (across,))
+    act_x = OPT['actx']
+    if act_x == 0:
+        across = swap(after(act, own_a), 2)
+    elif act_x == 1:
+        across = swap(after(act, *got), 2)
+    if act_x < 2:
+        w1 = gather(own_a, 'a', (across,))
+    else:
+        w1 = gather(own_a, 'a')
+        across = swap(after(act, w1[(2, 4, 1)[act_x - 2]]), 2)
     beyond = swap(across, 1)
     acts = [act, beside, across, beyond]
-    w2 = gather(own_b, (), (w1[2],), (w1[3], w1[5]))
+    later = [(), (w1[2],), (w1[4],), (w1[1],), (w1[2], w1[4], w1[1])][OPT['later']]
+    turn = [(), (w1[3], w1[5]), (w1[5],), (w1[7],), (w1[6],), (w1[3],), (w1[5], w1[6])][OPT['turn']]
+    last = [(), (w1[1],), (w1[5],), (w1[3],), (w1[2],)][OPT['y1b']]
+    w2 = gather(own_b, 'b', (), later, turn, last)
     normed, proj_own, ends, shared = call(
         project_kernel,
         [
@@ -812,7 +844,7 @@
             ((total_rows // 2, 2 * part), BF),
         ],
         [me] + acts + w1 + [pre],
-        flops=PROJECT_COST,
+        flops=OPT['pcost'],
         name="project",
     )
     scan_out, proj = call(
@@ -820,7 +852,7 @@
         [((total_rows, width), F32), ((total_rows, full), F32)],
         [me, proj_own] + [swap(shared, r) for r in range(1, QUAD)] + [ends, cwb, by_head],
         [pltpu.VMEM((QUAD, total_rows, part), F32)],
-        flops=SCAN_COST,
+        flops=OPT['scost'],
         name="scan",
     )
     w_full, cot_all, dgn = call(
@@ -850,6 +882,7 @@
         [me] + stats + w2 + [z, scan_out, dgn, gain, normed, cot_all],
         [pltpu.VMEM((width, model), F32)],
         name="ungate",
+        flops=OPT['ucost'],
     )
     gn, dscan, dz, ngain_part, pre_b = ungated[0:5]
     keep_b = ungated[5:9]
@@ -862,8 +895,15 @@
         [me, proj, dscan, ends, cwb, by_head],
         [pltpu.VMEM((QUAD, total_rows, part), F32)],
         name="scanback",
-    )
-    got76_b, got31_b = lax.optimization_barrier((got76_b, got31_b, pc_x))[0:2]
+        flops=OPT['bcost'],
+    )
+    got_bc = [swap(a, r + 1) for r, a in enumerate(bc)]
+    if OPT['r1'] == 0:
+        got76_b, got31_b = lax.optimization_barrier((got76_b, got31_b, pc_x))[0:2]
+    elif OPT['r1'] == 1:
+        got76_b, got31_b = lax.optimization_barrier((got76_b, got31_b, *got_bc))[0:2]
+    elif OPT['r1'] == 2:
+        got31_b = after(got31_b, *got_bc)
     (side,) = call(add_two_kernel, [((chunk_b, width), BF)], [keep_b[3], got76_b], name="side")
     got5_b = swap(side, QUAD)
     (near,) = call(add_two_kernel, [((chunk_b, width), BF)], [keep_b[1], got31_b], name="near")
@@ -882,8 +922,8 @@
 
     mine_m, cross_m = pair(*call(branch_kernel, pair_shapes, [gn, w_full], name="branch"))
     (mixed,) = call(mixed_kernel, [((rows, model), BF)], [act, mine_m, cross_m], name="mixed")
-    got_bc = [swap(a, r + 1) for r, a in enumerate(bc)]
-    small, cross_m = lax.optimization_barrier((small, cross_m, near, side))[0:2]
+    r2 = [(cross_m, near, side), (near, side), (side,), (cross_m, side), (mine_m, near, side), (mine_m, side)][OPT['r2']]
+    small = after(small, *r2)
     ingrads = call(
         ingrad_kernel,
         [((total_rows, wide), BF)]
@@ -897,7 +937,8 @@
     pc1, *ingrads = ingrads
     keep_a, small = ingrads[0:4], ingrads[6]
     got75_a, got31_a = swap(ingrads[4], QUAD), swap(ingrads[5], QUAD)
-    got5_b = after(got5_b, small)
+    if OPT['r6']:
+        got5_b = after(got5_b, small)
     (far,) = call(
         add_far_kernel, [((chunk_b, width), BF)], [keep_b[2], got76_b, got5_b], name="far"
     )
@@ -905,20 +946,31 @@
     far_b = far
 
     riding = [((chunk + SMALL, wide), BF), ((SMALL, wide), F32)]
+    if OPT['r7'] == 1:
+        got75_a = after(got75_a, got2_b)
     side, small1 = call(add_near_kernel, riding, [keep_a[3], got75_a, small], name="side")
+    if OPT['r7'] == 2:
+        side = after(side, got31_a)
     got6_a = swap(side, 2 * QUAD)
+    if OPT['r8'] == 1:
+        got6_a = after(got6_a, got4_b)
+    elif OPT['r8'] == 2:
+        got6_a = after(got6_a, got31_a)
     far, small2 = call(add_last_kernel, riding, [keep_a[2], got6_a, got75_a, small1], name="far")
     (near,) = call(add_two_kernel, [((chunk, wide), BF)], [keep_a[1], got31_a], name="near")
     got2_a = swap(near, 2 * QUAD)
     got4_a = swap(far, 4 * QUAD)
 
+    r3 = [(far_b,), (side,), (got31_a,), (got75_a,), (far_b, got75_a), (small,), (side, near), (got2_b, far_b)][OPT['r3']]
+    tail_in = after(pc1, *r3)
     mine_t, cross_t = pair(
-        *call(tail_kernel, pair_shapes, [me] + w1 + w2 + [after(pc1, far_b), dz], name="tail"), got4_b, got2_b
+        *call(tail_kernel, pair_shapes, [me] + w1 + w2 + [tail_in, dz], name="tail"), *[(got4_b, got2_b), (), (got4_b,)][OPT['r5']]
     )
     (tokens_grad,) = call(
         tokgrad_kernel, [((rows, model), F32)], [act, pre, mine_t, cross_t], name="tokgrad"
     )
-    got4_a = after(got4_a, cross_t)
+    if OPT['r4']:
+        got4_a = after(got4_a, cross_t)
 
     out_shard, own, own_small, *cuts = call(
         total_kernel,

time: 144 us -> 135 us (0.938)
  waiting for transfers between devices: 56.8 us -> 52.9 us
  local copies, waits for them, and re-layouts: 3.66 us -> 0.11 us
  Pallas kernels: 33.7 us -> 32.2 us
    ppermute x46, waiting for transfers between devices: 56.8 us -> 52.9 us  [swap(): return lax.ppermute(a, 'dp', [(i, i ^ mask) for i in range(count)])]
    unnamed x26 -> x8, local copies, waits for them, and re-layouts: 3.66 us -> 0.11 us
    pallas_call x23, Pallas kernels: 33.7 us -> 32.2 us  [call(): pl.pallas_call(kernel, out_shape=shapes, in_specs=in_specs, out_specs=[pl...]
  transfers between devices with their start and end apart: 46 -> 46, of which waited for: 25 -> 23; matrix products, arithmetic and copies ran while one was open for 0% -> 0% of each run, Pallas kernels for 13% -> 17%
where the time goes in v4:
time: 135 us
  waiting for transfers between devices  52.9 us (39%)
  starting transfers between devices  49.2 us (36%)
  Pallas kernels  32.2 us (24%)
    ppermute x46, waiting for transfers between devices, swap(): return lax.ppermute(a, 'dp', [(i, i ^ mask) for i in range(count)])  52.9 us
    ppermute x46, starting transfers between devices, swap(): return lax.ppermute(a, 'dp', [(i, i ^ mask) for i in range(count)])  49.2 us
    pallas_call x23, Pallas kernels, call(): pl.pallas_call(kernel, out_shape=shapes, in_specs=in_specs, out_specs=[pl...  32.2 us
  transfers between devices with their start and end apart: 46, of which 23 were waited for; matrix products, arithmetic and copies ran while one was open for 0% of the time, Pallas kernels for 17%

profile of v4, /device:TPU:0, one launch (start us, length us, event | category | flops | bytes accessed | tf_op | source)
XLA Modules:
  0.0 135.2 jit_solution(6299558085386642883)
XLA Ops:
  0.7 1.6 %prep.1 = (bf16[272,1024]{1,0:T(8,128)(2,1)S(1)}, f32[8,768]{1,0:T(8,128)S(1)}, f32[8,128]{1,0:T(8,128)S(1)}, f32[1,512]{1,0:T(1,128)S(1)}, f32[1,1024]{1,0:T(1,...) custom-call(s32[1]{0:T(128)} %bitcast.me_ref, ...), custom_call_target="tpu_custom_call" | custom-call | flops 1000 | bytes 1024 | tf_op jit(solution)/shard_map/prep/pallas_call | solution.py:59
  2.8 2.9 %collective-permute-start.2 = (bf16[32,1152]{1,0:T(8,128)(2,1)S(1)}, bf16[32,1152]{1,0:T(8,128)(2,1)S(1)}, u32[]{:S(2)}, u32[]{:S(2)}) collective-permute-start(bf16[32,1152]{1,0:T(8,128)(2,1)S(1)} %get-tuple-element.108), channel_id=1, source_target_pairs={{0,2},{1,3},{2,0},{3,1},{4,6},{5,7},{6,4},{7,5},{8,10},{9,11},{10,... | collective-permute-start | bytes 221192 | tf_op jit(solution)/shard_map/ppermute | solution.py:757
  5.7 2.5 %collective-permute-done.2.c2 = bf16[32,1152]{1,0:T(8,128)(2,1)S(1)} collective-permute-done((bf16[32,1152]{1,0:T(8,128)(2,1)S(1)}, bf16[32,1152]{1,0:T(8,128)(2,1)S(1)}, u32[]{:S(2)}, u32[]{:S(2)}) %collective-permute-start.2) | collective-permute-done | bytes 73760 | tf_op jit(solution)/shard_map/ppermute | solution.py:757
  8.3 2.0 %collective-permute-done.3.c3 = bf16[32,1152]{1,0:T(8,128)(2,1)S(1)} collective-permute-done((bf16[32,1152]{1,0:T(8,128)(2,1)S(1)}, bf16[32,1152]{1,0:T(8,128)(2,1)S(1)}, u32[]{:S(2)}, u32[]{:S(2)}) %collective-permute-start.3) | collective-permute-done | bytes 73760 | tf_op jit(solution)/shard_map/ppermute | solution.py:757
  10.8 1.7 %collective-permute-start.8 = (bf16[128,640]{1,0:T(8,128)(2,1)S(1)}, bf16[128,640]{1,0:T(8,128)(2,1)S(1)}, u32[]{:S(2)}, u32[]{:S(2)}) collective-permute-start(bf16[128,640]{1,0:T(8,128)(2,1)S(1)} %get-tuple-element.113.refs_4_.refs_0_), channel_id=1, source_target_pairs={{0,8},{1,9},{2,10},{3,11},{4,12},{5,13},{6,14},{7,15},{8,0},{9,1},... | collective-permute-start | bytes 491528 | tf_op jit(solution)/shard_map/ppermute | solution.py:757
  12.5 2.6 %collective-permute-start.7 = (bf16[128,640]{1,0:T(8,128)(2,1)S(1)}, bf16[128,640]{1,0:T(8,128)(2,1)S(1)}, u32[]{:S(2)}, u32[]{:S(2)}) collective-permute-start(bf16[128,640]{1,0:T(8,128)(2,1)S(1)} %get-tuple-element.113.refs_4_.refs_0_), channel_id=1, source_target_pairs={{0,16},{1,17},{2,18},{3,19},{4,20},{5,21},{6,22},{7,23},{8,24},{9,... | collective-permute-start | bytes 491528 | tf_op jit(solution)/shard_map/ppermute | solution.py:757
  15.1 1.5 %collective-permute-start.6 = (bf16[128,640]{1,0:T(8,128)(2,1)S(1)}, bf16[128,640]{1,0:T(8,128)(2,1)S(1)}, u32[]{:S(2)}, u32[]{:S(2)}) collective-permute-start(bf16[128,640]{1,0:T(8,128)(2,1)S(1)} %get-tuple-element.113.refs_4_.refs_0_), channel_id=1, source_target_pairs={{0,4},{1,5},{2,6},{3,7},{4,0},{5,1},{6,2},{7,3},{8,12},{9,13},{10,... | collective-permute-start | bytes 491528 | tf_op jit(solution)/shard_map/ppermute | solution.py:757
  16.6 8.3 %collective-permute-done.4.refs_2_.refs_10_ = bf16[272,1024]{1,0:T(8,128)(2,1)S(1)} collective-permute-done((bf16[272,1024]{1,0:T(8,128)(2,1)S(1)}, bf16[272,1024]{1,0:T(8,128)(2,1)S(1)}, u32[]{:S(2)}, u32[]{:S(2)}) %collective-permute-start.4) | collective-permute-done | bytes 557088 | tf_op jit(solution)/shard_map/ppermute | solution.py:757
  24.9 1.6 %collective-permute-start.11 = (bf16[128,640]{1,0:T(8,128)(2,1)S(1)}, bf16[128,640]{1,0:T(8,128)(2,1)S(1)}, u32[]{:S(2)}, u32[]{:S(2)}) collective-permute-start(bf16[128,640]{1,0:T(8,128)(2,1)S(1)} %collective-permute-done.7.refs_8_.refs_4_), channel_id=1, source_target_pairs={{0,8},{1,9},{2,10},{3,11},{4,12},{5,13},{6,14},{7,15},{8,0},{9,1},... | collective-permute-start | bytes 491528 | tf_op jit(solution)/shard_map/ppermute | solution.py:757
  26.6 1.5 %collective-permute-start.16 = (bf16[256,512]{1,0:T(8,128)(2,1)S(1)}, bf16[256,512]{1,0:T(8,128)(2,1)S(1)}, u32[]{:S(2)}, u32[]{:S(2)}) collective-permute-start(bf16[256,512]{1,0:T(8,128)(2,1)S(1)} %get-tuple-element.126.refs_0_.refs_4_.refs_8_), channel_id=1, source_target_pairs={{0,4},{1,5},{2,6},{3,7},{4,0},{5,1},{6,2},{7,3},{8,12},{9,13},{10,... | collective-permute-start | bytes 786440 | tf_op jit(solution)/shard_map/ppermute | solution.py:757
  29.0 2.9 %collective-permute-done.11.refs_10_.refs_6_ = bf16[128,640]{1,0:T(8,128)(2,1)S(1)} collective-permute-done((bf16[128,640]{1,0:T(8,128)(2,1)S(1)}, bf16[128,640]{1,0:T(8,128)(2,1)S(1)}, u32[]{:S(2)}, u32[]{:S(2)}) %collective-permute-start.11) | collective-permute-done | bytes 163872 | tf_op jit(solution)/shard_map/ppermute | solution.py:757
  32.0 2.6 %collective-permute-start.17 = (bf16[256,512]{1,0:T(8,128)(2,1)S(1)}, bf16[256,512]{1,0:T(8,128)(2,1)S(1)}, u32[]{:S(2)}, u32[]{:S(2)}) collective-permute-start(bf16[256,512]{1,0:T(8,128)(2,1)S(1)} %get-tuple-element.126.refs_0_.refs_4_.refs_8_), channel_id=1, source_target_pairs={{0,16},{1,17},{2,18},{3,19},{4,20},{5,21},{6,22},{7,23},{8,24},{9,... | collective-permute-start | bytes 786440 | tf_op jit(solution)/shard_map/ppermute | solution.py:757
  34.6 3.9 %collective-permute-done.10.refs_9_.refs_5_ = bf16[128,640]{1,0:T(8,128)(2,1)S(1)} collective-permute-done((bf16[128,640]{1,0:T(8,128)(2,1)S(1)}, bf16[128,640]{1,0:T(8,128)(2,1)S(1)}, u32[]{:S(2)}, u32[]{:S(2)}) %collective-permute-start.10) | collective-permute-done | bytes 163872 | tf_op jit(solution)/shard_map/ppermute | solution.py:757
  38.5 1.5 %collective-permute-start.9 = (bf16[128,640]{1,0:T(8,128)(2,1)S(1)}, bf16[128,640]{1,0:T(8,128)(2,1)S(1)}, u32[]{:S(2)}, u32[]{:S(2)}) collective-permute-start(bf16[128,640]{1,0:T(8,128)(2,1)S(1)} %collective-permute-done.8.refs_6_.refs_2_), channel_id=1, source_target_pairs={{0,4},{1,5},{2,6},{3,7},{4,0},{5,1},{6,2},{7,3},{8,12},{9,13},{10,... | collective-permute-start | bytes 491528 | tf_op jit(solution)/shard_map/ppermute | solution.py:757
  40.5 3.5 %collective-permute-done.9.refs_7_.refs_3_ = bf16[128,640]{1,0:T(8,128)(2,1)S(1)} collective-permute-done((bf16[128,640]{1,0:T(8,128)(2,1)S(1)}, bf16[128,640]{1,0:T(8,128)(2,1)S(1)}, u32[]{:S(2)}, u32[]{:S(2)}) %collective-permute-start.9) | collective-permute-done | bytes 163872 | tf_op jit(solution)/shard_map/ppermute | solution.py:757
  44.0 2.2 %collective-permute-done.17.refs_4_.refs_8_.refs_12_ = bf16[256,512]{1,0:T(8,128)(2,1)S(1)} collective-permute-done((bf16[256,512]{1,0:T(8,128)(2,1)S(1)}, bf16[256,512]{1,0:T(8,128)(2,1)S(1)}, u32[]{:S(2)}, u32[]{:S(2)}) %collective-permute-start.17) | collective-permute-done | bytes 262176 | tf_op jit(solution)/shard_map/ppermute | solution.py:757
  46.2 0.7 collective-permute-start.21
  46.9 1.5 %collective-permute-start.20 = (bf16[256,512]{1,0:T(8,128)(2,1)S(1)}, bf16[256,512]{1,0:T(8,128)(2,1)S(1)}, u32[]{:S(2)}, u32[]{:S(2)}) collective-permute-start(bf16[256,512]{1,0:T(8,128)(2,1)S(1)} %collective-permute-done.17.refs_4_.refs_8_.refs_12_), channel_id=1, source_target_pairs={{0,4},{1,5},{2,6},{3,7},{4,0},{5,1},{6,2},{7,3},{8,12},{9,13},{10,... | collective-permute-start | bytes 786440 | tf_op jit(solution)/shard_map/ppermute | solution.py:757
  48.4 1.5 %project.1 = (bf16[512,1024]{1,0:T(8,128)(2,1)S(1)}, f32[512,640]{1,0:T(8,128)S(1)}, f32[4,128]{1,0:T(4,128)S(1)}, bf16[256,128]{1,0:T(8,128)(2,1)S(1)}) custom-call(s32[1]{0:T(128)} %bitcast.me_ref, bf16[272,1024]{1,0:T(8,128)(2,1)S(1)} %get-tuple-element.110.refs_0_.refs_8_.act_ref, bf16[272,1024]{1,0:T(8,128)(2,1)S(1)} %collective-permute-done.refs_1_.refs_9_, ...), custom_call_target="tpu_custom_call" | custom-call | flops 4000000000 | bytes 1024 | tf_op jit(solution)/shard_map/project/pallas_call | solution.py:59
  50.0 1.1 collective-permute-start.14
  51.1 0.7 collective-permute-start.13
  51.9 0.7 collective-permute-done.21.refs_6_.refs_10_.refs_14_
  52.6 1.5 %collective-permute-start.19 = (bf16[256,512]{1,0:T(8,128)(2,1)S(1)}, bf16[256,512]{1,0:T(8,128)(2,1)S(1)}, u32[]{:S(2)}, u32[]{:S(2)}) collective-permute-start(bf16[256,512]{1,0:T(8,128)(2,1)S(1)} %collective-permute-done.18.refs_2_.refs_6_.refs_10_), channel_id=1, source_target_pairs={{0,4},{1,5},{2,6},{3,7},{4,0},{5,1},{6,2},{7,3},{8,12},{9,13},{10,... | collective-permute-start | bytes 786440 | tf_op jit(solution)/shard_map/ppermute | solution.py:757
  54.1 1.0 collective-permute-start.22
  55.1 4.6 %scan.1 = (f32[512,512]{1,0:T(8,128)S(1)}, f32[512,896]{1,0:T(8,128)S(1)}) custom-call(s32[1]{0:T(128)} %bitcast.me_ref, f32[512,640]{1,0:T(8,128)S(1)} %get-tuple-element.119.own_ref, bf16[256,128]{1,0:T(8,128)(2,1)S(1)} %collective-permute-done.13.g1, bf16[256,128]{1,0:T(8,128)(2,1)S(1)} %collective-permute-done.14.g2, ...), custom_call_target="tpu_custom_call" | custom-call | flops 16000000000 | bytes 1024 | tf_op jit(solution)/shard_map/scan/pallas_call | solution.py:59
  60.5 0.8 normcot.1
  61.3 1.2 gate.1
  62.6 1.1 collective-permute-start.24
  63.7 0.7 collective-permute-start.23
  64.5 1.3 collective-permute-done.25.refs_3_
  65.8 0.6 collective-permute-done.24.refs_2_
  66.4 4.2 %ungate.1 = (bf16[512,512]{1,0:T(8,128)(2,1)S(1)}, f32[512,512]{1,0:T(8,128)S(1)}, bf16[512,512]{1,0:T(8,128)(2,1)S(1)}, f32[1,512]{1,0:T(1,128)S(1)}, f32[128,1...) custom-call(s32[1]{0:T(128)} %bitcast.me_ref, ...), custom_call_target="tpu_custom_call" | custom-call | flops 1000 | bytes 1024 | tf_op jit(solution)/shard_map/ungate/pallas_call | solution.py:59
  70.6 1.4 %collective-permute-start.30 = (bf16[512,512]{1,0:T(8,128)(2,1)S(1)}, bf16[512,512]{1,0:T(8,128)(2,1)S(1)}, u32[]{:S(2)}, u32[]{:S(2)}) collective-permute-start(bf16[512,512]{1,0:T(8,128)(2,1)S(1)} %get-tuple-element.149), channel_id=1, source_target_pairs={{0,8},{1,9},{2,10},{3,11},{4,12},{5,13},{6,14},{7,15},{8,0},{9,1},... | collective-permute-start | bytes 1572872 | tf_op jit(solution)/shard_map/ppermute | solution.py:757
  72.0 1.3 collective-permute-start.31
  73.3 0.7 branch.1
  74.1 8.3 %scanback.1 = (bf16[512,640]{1,0:T(8,128)(2,1)S(1)}, f32[16,640]{1,0:T(8,128)S(1)}, f32[256,128]{1,0:T(8,128)S(1)}, bf16[256,128]{1,0:T(8,128)(2,1)S(1)}, bf16[2...) custom-call(s32[1]{0:T(128)} %bitcast.me_ref, f32[512,896]{1,0:T(8,128)S(1)} %get-tuple-element.124.proj_ref, ...), custom_call_target="tpu_custom_call" | custom-call | flops 1000 | bytes 1024 | tf_op jit(solution)/shard_map/scanback/pallas_call | solution.py:59
  82.9 1.2 collective-permute-start.27
  84.7 1.0 collective-permute-done.31.got_ref.refs_5_
  85.8 1.3 collective-permute-start.38
  87.3 1.5 %collective-permute-done.28.g3 = bf16[256,128]{1,0:T(8,128)(2,1)S(1)} collective-permute-done((bf16[256,128]{1,0:T(8,128)(2,1)S(1)}, bf16[256,128]{1,0:T(8,128)(2,1)S(1)}, u32[]{:S(2)}, u32[]{:S(2)}) %collective-permute-start.28) | collective-permute-done | bytes 65568 | tf_op jit(solution)/shard_map/ppermute | solution.py:757
  88.8 1.5 %ingrad.1 = (bf16[512,640]{1,0:T(8,128)(2,1)S(1)}, f32[128,640]{1,0:T(8,128)S(1)}, f32[128,640]{1,0:T(8,128)S(1)}, f32[128,640]{1,0:T(8,128)S(1)}, f32[128,640]{...) custom-call(s32[1]{0:T(128)} %bitcast.me_ref, ...), custom_call_target="tpu_custom_call" | custom-call | flops 1000 | bytes 1024 | tf_op jit(solution)/shard_map/ingrad/pallas_call | solution.py:59
  90.3 2.6 %tail.1 = (f32[256,1024]{1,0:T(8,128)S(1)}, bf16[256,1024]{1,0:T(8,128)(2,1)S(1)}) custom-call(s32[1]{0:T(128)} %bitcast.me_ref, bf16[128,640]{1,0:T(8,128)(2,1)S(1)} %get-tuple-element.113.refs_4_.refs_0_, bf16[128,640]{1,0:T(8,128)(2,1)S(1)} %collective-permute-done.6.refs_5_.refs_1_, bf16[128,640]{1,0:T(8,128)(2,1)S(1)} %collective-permute-done.8.refs_6_.refs_2_, ...), custom_call_target="tpu_custom_call" | custom-call | flops 1000 | bytes 1024 | tf_op jit(solution)/shard_map/tail/pallas_call | solution.py:59
  93.0 1.4 %collective-permute-start.34 = (bf16[272,640]{1,0:T(8,128)(2,1)S(1)}, bf16[272,640]{1,0:T(8,128)(2,1)S(1)}, u32[]{:S(2)}, u32[]{:S(2)}) collective-permute-start(bf16[272,640]{1,0:T(8,128)(2,1)S(1)} %get-tuple-element.162), channel_id=1, source_target_pairs={{0,4},{1,5},{2,6},{3,7},{4,0},{5,1},{6,2},{7,3},{8,12},{9,13},{10,... | collective-permute-start | bytes 1044488 | tf_op jit(solution)/shard_map/ppermute | solution.py:757
  94.4 1.3 collective-permute-start.40
  95.8 2.7 %collective-permute-start.39 = (bf16[256,512]{1,0:T(8,128)(2,1)S(1)}, bf16[256,512]{1,0:T(8,128)(2,1)S(1)}, u32[]{:S(2)}, u32[]{:S(2)}) collective-permute-start(bf16[256,512]{1,0:T(8,128)(2,1)S(1)} %far.3), channel_id=1, source_target_pairs={{0,16},{1,17},{2,18},{3,19},{4,20},{5,21},{6,22},{7,23},{8,24},{9,... | collective-permute-start | bytes 786440 | tf_op jit(solution)/shard_map/ppermute | solution.py:757
  98.5 1.1 collective-permute-start.32
  99.6 4.4 %collective-permute-done.34.got_ref.side_ref = bf16[272,640]{1,0:T(8,128)(2,1)S(1)} collective-permute-done((bf16[272,640]{1,0:T(8,128)(2,1)S(1)}, bf16[272,640]{1,0:T(8,128)(2,1)S(1)}, u32[]{:S(2)}, u32[]{:S(2)}) %collective-permute-start.34) | collective-permute-done | bytes 348192 | tf_op jit(solution)/shard_map/ppermute | solution.py:757
  104.0 1.2 collective-permute-start.35
  105.3 3.9 %collective-permute-done.40.refs_6_ = bf16[256,512]{1,0:T(8,128)(2,1)S(1)} collective-permute-done((bf16[256,512]{1,0:T(8,128)(2,1)S(1)}, bf16[256,512]{1,0:T(8,128)(2,1)S(1)}, u32[]{:S(2)}, u32[]{:S(2)}) %collective-permute-start.40) | collective-permute-done | bytes 262176 | tf_op jit(solution)/shard_map/ppermute | solution.py:757
  109.3 1.0 collective-permute-start.41
  110.6 1.8 %collective-permute-done.35.got_ref = bf16[144,640]{1,0:T(8,128)(2,1)S(1)} collective-permute-done((bf16[144,640]{1,0:T(8,128)(2,1)S(1)}, bf16[144,640]{1,0:T(8,128)(2,1)S(1)}, u32[]{:S(2)}, u32[]{:S(2)}) %collective-permute-start.35) | collective-permute-done | bytes 184352 | tf_op jit(solution)/shard_map/ppermute | solution.py:757
  112.4 3.5 %collective-permute-start.36 = (bf16[144,640]{1,0:T(8,128)(2,1)S(1)}, bf16[144,640]{1,0:T(8,128)(2,1)S(1)}, u32[]{:S(2)}, u32[]{:S(2)}) collective-permute-start(bf16[144,640]{1,0:T(8,128)(2,1)S(1)} %get-tuple-element.167), channel_id=1, source_target_pairs={{0,16},{1,17},{2,18},{3,19},{4,20},{5,21},{6,22},{7,23},{8,24},{9,... | collective-permute-start | bytes 552968 | tf_op jit(solution)/shard_map/ppermute | solution.py:757
  116.0 1.1 collective-permute-start.33
  117.1 0.9 collective-permute-start.42
  118.0 6.1 %collective-permute-done.36.refs_3_ = bf16[144,640]{1,0:T(8,128)(2,1)S(1)} collective-permute-done((bf16[144,640]{1,0:T(8,128)(2,1)S(1)}, bf16[144,640]{1,0:T(8,128)(2,1)S(1)}, u32[]{:S(2)}, u32[]{:S(2)}) %collective-permute-start.36) | collective-permute-done | bytes 184352 | tf_op jit(solution)/shard_map/ppermute | solution.py:757
  124.1 1.0 collective-permute-done.33.refs_2_
  125.0 1.0 total.1
  126.0 0.9 collective-permute-start.44
  127.0 0.9 collective-permute-start.45
  127.9 0.8 mixed.1
  128.7 1.1 tokgrad.1
  129.8 2.1 %collective-permute-done.44.refs_1_ = bf16[48,1152]{1,0:T(8,128)(2,1)S(1)} collective-permute-done((bf16[48,1152]{1,0:T(8,128)(2,1)S(1)}, bf16[48,1152]{1,0:T(8,128)(2,1)S(1)}, u32[]{:S(2)}, u32[]{:S(2)}) %collective-permute-start.44) | collective-permute-done | bytes 110624 | tf_op jit(solution)/shard_map/ppermute | solution.py:757
  131.9 1.6 %collective-permute-done.45.refs_2_ = bf16[48,1152]{1,0:T(8,128)(2,1)S(1)} collective-permute-done((bf16[48,1152]{1,0:T(8,128)(2,1)S(1)}, bf16[48,1152]{1,0:T(8,128)(2,1)S(1)}, u32[]{:S(2)}, u32[]{:S(2)}) %collective-permute-start.45) | collective-permute-done | bytes 110624 | tf_op jit(solution)/shard_map/ppermute | solution.py:757
  133.5 1.7 %finish.1 = (f32[32,4384]{1,0:T(8,128)}, f32[4,2304]{1,0:T(4,128)}, f32[18,128]{1,0:T(8,128)}, f32[1,32]{1,0:T(1,128)}, f32[1,32]{1,0:T(1,128)}, /*index=5*/f32[...) custom-call(s32[1]{0:T(128)} %bitcast.me_ref, f32[32,1152]{1,0:T(8,128)S(1)} %get-tuple-element.185.mine_ref, ...), custom_call_target="tpu_custom_call" | custom-call | flops 1000 | bytes 1024 | tf_op jit(solution)/shard_map/finish/pallas_call | solution.py:59
  (59 shorter events, 5.6 us)
Async XLA Ops:
  2.2 3.5 %collective-permute-start = (bf16[272,1024]{1,0:T(8,128)(2,1)S(1)}, bf16[272,1024]{1,0:T(8,128)(2,1)S(1)}, u32[]{:S(2)}, u32[]{:S(2)}) collective-permute-start(bf16[272,1024]{1,0:T(8,128)(2,1)S(1)} %get-tuple-element.110.refs_0_.refs_8_.act_ref), channel_id=1, source_target_pairs={{0,1},{1,0},{2,3},{3,2},{4,5},{5,4},{6,7},{7,6},{8,9},{9,8},{10,11... | collective-permute-start | bytes 1671176 | tf_op jit(solution)/shard_map/ppermute | solution.py:757
  2.7 3.0 %collective-permute-start.1 = (bf16[32,1152]{1,0:T(8,128)(2,1)S(1)}, bf16[32,1152]{1,0:T(8,128)(2,1)S(1)}, u32[]{:S(2)}, u32[]{:S(2)}) collective-permute-start(bf16[32,1152]{1,0:T(8,128)(2,1)S(1)} %get-tuple-element.106), channel_id=1, source_target_pairs={{0,1},{1,0},{2,3},{3,2},{4,5},{5,4},{6,7},{7,6},{8,9},{9,8},{10,11... | collective-permute-start | bytes 221192 | tf_op jit(solution)/shard_map/ppermute | solution.py:757
  2.8 5.5 %collective-permute-start.2 = (bf16[32,1152]{1,0:T(8,128)(2,1)S(1)}, bf16[32,1152]{1,0:T(8,128)(2,1)S(1)}, u32[]{:S(2)}, u32[]{:S(2)}) collective-permute-start(bf16[32,1152]{1,0:T(8,128)(2,1)S(1)} %get-tuple-element.108), channel_id=1, source_target_pairs={{0,2},{1,3},{2,0},{3,1},{4,6},{5,7},{6,4},{7,5},{8,10},{9,11},{10,... | collective-permute-start | bytes 221192 | tf_op jit(solution)/shard_map/ppermute | solution.py:757
  5.7 4.5 %collective-permute-start.3 = (bf16[32,1152]{1,0:T(8,128)(2,1)S(1)}, bf16[32,1152]{1,0:T(8,128)(2,1)S(1)}, u32[]{:S(2)}, u32[]{:S(2)}) collective-permute-start(bf16[32,1152]{1,0:T(8,128)(2,1)S(1)} %get-tuple-element.109), channel_id=1, source_target_pairs={{0,3},{1,2},{2,1},{3,0},{4,7},{5,6},{6,5},{7,4},{8,11},{9,10},{10,... | collective-permute-start | bytes 221192 | tf_op jit(solution)/shard_map/ppermute | solution.py:757
  10.3 14.6 %collective-permute-start.4 = (bf16[272,1024]{1,0:T(8,128)(2,1)S(1)}, bf16[272,1024]{1,0:T(8,128)(2,1)S(1)}, u32[]{:S(2)}, u32[]{:S(2)}) collective-permute-start(bf16[272,1024]{1,0:T(8,128)(2,1)S(1)} %get-tuple-element.110.refs_0_.refs_8_.act_ref), channel_id=1, source_target_pairs={{0,2},{1,3},{2,0},{3,1},{4,6},{5,7},{6,4},{7,5},{8,10},{9,11},{10,... | collective-permute-start | bytes 1671176 | tf_op jit(solution)/shard_map/ppermute | solution.py:757
  10.8 14.1 %collective-permute-start.8 = (bf16[128,640]{1,0:T(8,128)(2,1)S(1)}, bf16[128,640]{1,0:T(8,128)(2,1)S(1)}, u32[]{:S(2)}, u32[]{:S(2)}) collective-permute-start(bf16[128,640]{1,0:T(8,128)(2,1)S(1)} %get-tuple-element.113.refs_4_.refs_0_), channel_id=1, source_target_pairs={{0,8},{1,9},{2,10},{3,11},{4,12},{5,13},{6,14},{7,15},{8,0},{9,1},... | collective-permute-start | bytes 491528 | tf_op jit(solution)/shard_map/ppermute | solution.py:757
  12.5 12.4 %collective-permute-start.7 = (bf16[128,640]{1,0:T(8,128)(2,1)S(1)}, bf16[128,640]{1,0:T(8,128)(2,1)S(1)}, u32[]{:S(2)}, u32[]{:S(2)}) collective-permute-start(bf16[128,640]{1,0:T(8,128)(2,1)S(1)} %get-tuple-element.113.refs_4_.refs_0_), channel_id=1, source_target_pairs={{0,16},{1,17},{2,18},{3,19},{4,20},{5,21},{6,22},{7,23},{8,24},{9,... | collective-permute-start | bytes 491528 | tf_op jit(solution)/shard_map/ppermute | solution.py:757
  15.1 9.8 %collective-permute-start.6 = (bf16[128,640]{1,0:T(8,128)(2,1)S(1)}, bf16[128,640]{1,0:T(8,128)(2,1)S(1)}, u32[]{:S(2)}, u32[]{:S(2)}) collective-permute-start(bf16[128,640]{1,0:T(8,128)(2,1)S(1)} %get-tuple-element.113.refs_4_.refs_0_), channel_id=1, source_target_pairs={{0,4},{1,5},{2,6},{3,7},{4,0},{5,1},{6,2},{7,3},{8,12},{9,13},{10,... | collective-permute-start | bytes 491528 | tf_op jit(solution)/shard_map/ppermute | solution.py:757
  24.9 23.5 %collective-permute-start.5 = (bf16[272,1024]{1,0:T(8,128)(2,1)S(1)}, bf16[272,1024]{1,0:T(8,128)(2,1)S(1)}, u32[]{:S(2)}, u32[]{:S(2)}) collective-permute-start(bf16[272,1024]{1,0:T(8,128)(2,1)S(1)} %collective-permute-done.4.refs_2_.refs_10_), channel_id=1, source_target_pairs={{0,1},{1,0},{2,3},{3,2},{4,5},{5,4},{6,7},{7,6},{8,9},{9,8},{10,11... | collective-permute-start | bytes 1671176 | tf_op jit(solution)/shard_map/ppermute | solution.py:757
  24.9 7.1 %collective-permute-start.11 = (bf16[128,640]{1,0:T(8,128)(2,1)S(1)}, bf16[128,640]{1,0:T(8,128)(2,1)S(1)}, u32[]{:S(2)}, u32[]{:S(2)}) collective-permute-start(bf16[128,640]{1,0:T(8,128)(2,1)S(1)} %collective-permute-done.7.refs_8_.refs_4_), channel_id=1, source_target_pairs={{0,8},{1,9},{2,10},{3,11},{4,12},{5,13},{6,14},{7,15},{8,0},{9,1},... | collective-permute-start | bytes 491528 | tf_op jit(solution)/shard_map/ppermute | solution.py:757
  26.6 13.5 %collective-permute-start.16 = (bf16[256,512]{1,0:T(8,128)(2,1)S(1)}, bf16[256,512]{1,0:T(8,128)(2,1)S(1)}, u32[]{:S(2)}, u32[]{:S(2)}) collective-permute-start(bf16[256,512]{1,0:T(8,128)(2,1)S(1)} %get-tuple-element.126.refs_0_.refs_4_.refs_8_), channel_id=1, source_target_pairs={{0,4},{1,5},{2,6},{3,7},{4,0},{5,1},{6,2},{7,3},{8,12},{9,13},{10,... | collective-permute-start | bytes 786440 | tf_op jit(solution)/shard_map/ppermute | solution.py:757
  28.1 10.4 %collective-permute-start.10 = (bf16[128,640]{1,0:T(8,128)(2,1)S(1)}, bf16[128,640]{1,0:T(8,128)(2,1)S(1)}, u32[]{:S(2)}, u32[]{:S(2)}) collective-permute-start(bf16[128,640]{1,0:T(8,128)(2,1)S(1)} %collective-permute-done.7.refs_8_.refs_4_), channel_id=1, source_target_pairs={{0,4},{1,5},{2,6},{3,7},{4,0},{5,1},{6,2},{7,3},{8,12},{9,13},{10,... | collective-permute-start | bytes 491528 | tf_op jit(solution)/shard_map/ppermute | solution.py:757
  28.6 15.4 %collective-permute-start.18 = (bf16[256,512]{1,0:T(8,128)(2,1)S(1)}, bf16[256,512]{1,0:T(8,128)(2,1)S(1)}, u32[]{:S(2)}, u32[]{:S(2)}) collective-permute-start(bf16[256,512]{1,0:T(8,128)(2,1)S(1)} %get-tuple-element.126.refs_0_.refs_4_.refs_8_), channel_id=1, source_target_pairs={{0,8},{1,9},{2,10},{3,11},{4,12},{5,13},{6,14},{7,15},{8,0},{9,1},... | collective-permute-start | bytes 786440 | tf_op jit(solution)/shard_map/ppermute | solution.py:757
  32.0 14.2 %collective-permute-start.17 = (bf16[256,512]{1,0:T(8,128)(2,1)S(1)}, bf16[256,512]{1,0:T(8,128)(2,1)S(1)}, u32[]{:S(2)}, u32[]{:S(2)}) collective-permute-start(bf16[256,512]{1,0:T(8,128)(2,1)S(1)} %get-tuple-element.126.refs_0_.refs_4_.refs_8_), channel_id=1, source_target_pairs={{0,16},{1,17},{2,18},{3,19},{4,20},{5,21},{6,22},{7,23},{8,24},{9,... | collective-permute-start | bytes 786440 | tf_op jit(solution)/shard_map/ppermute | solution.py:757
  38.5 5.5 %collective-permute-start.9 = (bf16[128,640]{1,0:T(8,128)(2,1)S(1)}, bf16[128,640]{1,0:T(8,128)(2,1)S(1)}, u32[]{:S(2)}, u32[]{:S(2)}) collective-permute-start(bf16[128,640]{1,0:T(8,128)(2,1)S(1)} %collective-permute-done.8.refs_6_.refs_2_), channel_id=1, source_target_pairs={{0,4},{1,5},{2,6},{3,7},{4,0},{5,1},{6,2},{7,3},{8,12},{9,13},{10,... | collective-permute-start | bytes 491528 | tf_op jit(solution)/shard_map/ppermute | solution.py:757
  40.0 8.4 %collective-permute-start.12 = (bf16[128,640]{1,0:T(8,128)(2,1)S(1)}, bf16[128,640]{1,0:T(8,128)(2,1)S(1)}, u32[]{:S(2)}, u32[]{:S(2)}) collective-permute-start(bf16[128,640]{1,0:T(8,128)(2,1)S(1)} %collective-permute-done.10.refs_9_.refs_5_), channel_id=1, source_target_pairs={{0,8},{1,9},{2,10},{3,11},{4,12},{5,13},{6,14},{7,15},{8,0},{9,1},... | collective-permute-start | bytes 491528 | tf_op jit(solution)/shard_map/ppermute | solution.py:757
  46.2 6.4 %collective-permute-start.21 = (bf16[256,512]{1,0:T(8,128)(2,1)S(1)}, bf16[256,512]{1,0:T(8,128)(2,1)S(1)}, u32[]{:S(2)}, u32[]{:S(2)}) collective-permute-start(bf16[256,512]{1,0:T(8,128)(2,1)S(1)} %collective-permute-done.17.refs_4_.refs_8_.refs_12_), channel_id=1, source_target_pairs={{0,8},{1,9},{2,10},{3,11},{4,12},{5,13},{6,14},{7,15},{8,0},{9,1},... | collective-permute-start | bytes 786440 | tf_op jit(solution)/shard_map/ppermute | solution.py:757
  46.9 7.2 %collective-permute-start.20 = (bf16[256,512]{1,0:T(8,128)(2,1)S(1)}, bf16[256,512]{1,0:T(8,128)(2,1)S(1)}, u32[]{:S(2)}, u32[]{:S(2)}) collective-permute-start(bf16[256,512]{1,0:T(8,128)(2,1)S(1)} %collective-permute-done.17.refs_4_.refs_8_.refs_12_), channel_id=1, source_target_pairs={{0,4},{1,5},{2,6},{3,7},{4,0},{5,1},{6,2},{7,3},{8,12},{9,13},{10,... | collective-permute-start | bytes 786440 | tf_op jit(solution)/shard_map/ppermute | solution.py:757
  49.9 11.4 %copy-start = (bf16[512,1024]{1,0:T(8,128)(2,1)}, bf16[512,1024]{1,0:T(8,128)(2,1)S(1)}, u32[]{:S(2)}) copy-start(bf16[512,1024]{1,0:T(8,128)(2,1)S(1)} %get-tuple-element.118.refs_8_.refs_16_.norm_ref) | copy-start | bytes 3145732
  49.9 5.2 %collective-permute-start.15 = (bf16[256,128]{1,0:T(8,128)(2,1)S(1)}, bf16[256,128]{1,0:T(8,128)(2,1)S(1)}, u32[]{:S(2)}, u32[]{:S(2)}) collective-permute-start(bf16[256,128]{1,0:T(8,128)(2,1)S(1)} %get-tuple-element.120), channel_id=1, source_target_pairs={{0,3},{1,2},{2,1},{3,0},{4,7},{5,6},{6,5},{7,4},{8,11},{9,10},{10,... | collective-permute-start | bytes 196616 | tf_op jit(solution)/shard_map/ppermute | solution.py:757
  50.0 5.1 %collective-permute-start.14 = (bf16[256,128]{1,0:T(8,128)(2,1)S(1)}, bf16[256,128]{1,0:T(8,128)(2,1)S(1)}, u32[]{:S(2)}, u32[]{:S(2)}) collective-permute-start(bf16[256,128]{1,0:T(8,128)(2,1)S(1)} %get-tuple-element.120), channel_id=1, source_target_pairs={{0,2},{1,3},{2,0},{3,1},{4,6},{5,7},{6,4},{7,5},{8,10},{9,11},{10,... | collective-permute-start | bytes 196616 | tf_op jit(solution)/shard_map/ppermute | solution.py:757
  51.1 4.0 %collective-permute-start.13 = (bf16[256,128]{1,0:T(8,128)(2,1)S(1)}, bf16[256,128]{1,0:T(8,128)(2,1)S(1)}, u32[]{:S(2)}, u32[]{:S(2)}) collective-permute-start(bf16[256,128]{1,0:T(8,128)(2,1)S(1)} %get-tuple-element.120), channel_id=1, source_target_pairs={{0,1},{1,0},{2,3},{3,2},{4,5},{5,4},{6,7},{7,6},{8,9},{9,8},{10,11... | collective-permute-start | bytes 196616 | tf_op jit(solution)/shard_map/ppermute | solution.py:757
  52.6 7.5 %collective-permute-start.19 = (bf16[256,512]{1,0:T(8,128)(2,1)S(1)}, bf16[256,512]{1,0:T(8,128)(2,1)S(1)}, u32[]{:S(2)}, u32[]{:S(2)}) collective-permute-start(bf16[256,512]{1,0:T(8,128)(2,1)S(1)} %collective-permute-done.18.refs_2_.refs_6_.refs_10_), channel_id=1, source_target_pairs={{0,4},{1,5},{2,6},{3,7},{4,0},{5,1},{6,2},{7,3},{8,12},{9,13},{10,... | collective-permute-start | bytes 786440 | tf_op jit(solution)/shard_map/ppermute | solution.py:757
  54.1 6.4 %collective-permute-start.22 = (bf16[256,512]{1,0:T(8,128)(2,1)S(1)}, bf16[256,512]{1,0:T(8,128)(2,1)S(1)}, u32[]{:S(2)}, u32[]{:S(2)}) collective-permute-start(bf16[256,512]{1,0:T(8,128)(2,1)S(1)} %collective-permute-done.20.refs_5_.refs_9_.refs_13_), channel_id=1, source_target_pairs={{0,8},{1,9},{2,10},{3,11},{4,12},{5,13},{6,14},{7,15},{8,0},{9,1},... | collective-permute-start | bytes 786440 | tf_op jit(solution)/shard_map/ppermute | solution.py:757
  61.3 1.2 copy-start.2
  61.3 1.3 copy-start.3
  62.6 3.2 %collective-permute-start.25 = (f32[8,512]{1,0:T(8,128)S(1)}, f32[8,512]{1,0:T(8,128)S(1)}, u32[]{:S(2)}, u32[]{:S(2)}) collective-permute-start(f32[8,512]{1,0:T(8,128)S(1)} %get-tuple-element.133.refs_0_), channel_id=1, source_target_pairs={{0,3},{1,2},{2,1},{3,0},{4,7},{5,6},{6,5},{7,4},{8,11},{9,10},{10,... | collective-permute-start | bytes 49160 | tf_op jit(solution)/shard_map/ppermute | solution.py:757
  62.6 3.8 %collective-permute-start.24 = (f32[8,512]{1,0:T(8,128)S(1)}, f32[8,512]{1,0:T(8,128)S(1)}, u32[]{:S(2)}, u32[]{:S(2)}) collective-permute-start(f32[8,512]{1,0:T(8,128)S(1)} %get-tuple-element.133.refs_0_), channel_id=1, source_target_pairs={{0,2},{1,3},{2,0},{3,1},{4,6},{5,7},{6,4},{7,5},{8,10},{9,11},{10,... | collective-permute-start | bytes 49160 | tf_op jit(solution)/shard_map/ppermute | solution.py:757
  63.7 2.7 %collective-permute-start.23 = (f32[8,512]{1,0:T(8,128)S(1)}, f32[8,512]{1,0:T(8,128)S(1)}, u32[]{:S(2)}, u32[]{:S(2)}) collective-permute-start(f32[8,512]{1,0:T(8,128)S(1)} %get-tuple-element.133.refs_0_), channel_id=1, source_target_pairs={{0,1},{1,0},{2,3},{3,2},{4,5},{5,4},{6,7},{7,6},{8,9},{9,8},{10,11... | collective-permute-start | bytes 49160 | tf_op jit(solution)/shard_map/ppermute | solution.py:757
  70.6 14.0 %collective-permute-start.30 = (bf16[512,512]{1,0:T(8,128)(2,1)S(1)}, bf16[512,512]{1,0:T(8,128)(2,1)S(1)}, u32[]{:S(2)}, u32[]{:S(2)}) collective-permute-start(bf16[512,512]{1,0:T(8,128)(2,1)S(1)} %get-tuple-element.149), channel_id=1, source_target_pairs={{0,8},{1,9},{2,10},{3,11},{4,12},{5,13},{6,14},{7,15},{8,0},{9,1},... | collective-permute-start | bytes 1572872 | tf_op jit(solution)/shard_map/ppermute | solution.py:757
  72.0 13.7 %collective-permute-start.31 = (bf16[512,512]{1,0:T(8,128)(2,1)S(1)}, bf16[512,512]{1,0:T(8,128)(2,1)S(1)}, u32[]{:S(2)}, u32[]{:S(2)}) collective-permute-start(bf16[512,512]{1,0:T(8,128)(2,1)S(1)} %get-tuple-element.150), channel_id=1, source_target_pairs={{0,4},{1,5},{2,6},{3,7},{4,0},{5,1},{6,2},{7,3},{8,12},{9,13},{10,... | collective-permute-start | bytes 1572872 | tf_op jit(solution)/shard_map/ppermute | solution.py:757
  74.0 13.1 %collective-permute-start.29 = (bf16[256,1024]{1,0:T(8,128)(2,1)S(1)}, bf16[256,1024]{1,0:T(8,128)(2,1)S(1)}, u32[]{:S(2)}, u32[]{:S(2)}) collective-permute-start(bf16[256,1024]{1,0:T(8,128)(2,1)S(1)} %get-tuple-element.146), channel_id=1, source_target_pairs={{0,1},{1,0},{2,3},{3,2},{4,5},{5,4},{6,7},{7,6},{8,9},{9,8},{10,11... | collective-permute-start | bytes 1572872 | tf_op jit(solution)/shard_map/ppermute | solution.py:757
  82.4 4.9 %collective-permute-start.26 = (bf16[256,128]{1,0:T(8,128)(2,1)S(1)}, bf16[256,128]{1,0:T(8,128)(2,1)S(1)}, u32[]{:S(2)}, u32[]{:S(2)}) collective-permute-start(bf16[256,128]{1,0:T(8,128)(2,1)S(1)} %get-tuple-element.139), channel_id=1, source_target_pairs={{0,1},{1,0},{2,3},{3,2},{4,5},{5,4},{6,7},{7,6},{8,9},{9,8},{10,11... | collective-permute-start | bytes 196616 | tf_op jit(solution)/shard_map/ppermute | solution.py:757
  82.9 4.4 %collective-permute-start.27 = (bf16[256,128]{1,0:T(8,128)(2,1)S(1)}, bf16[256,128]{1,0:T(8,128)(2,1)S(1)}, u32[]{:S(2)}, u32[]{:S(2)}) collective-permute-start(bf16[256,128]{1,0:T(8,128)(2,1)S(1)} %get-tuple-element.140), channel_id=1, source_target_pairs={{0,2},{1,3},{2,0},{3,1},{4,6},{5,7},{6,4},{7,5},{8,10},{9,11},{10,... | collective-permute-start | bytes 196616 | tf_op jit(solution)/shard_map/ppermute | solution.py:757
  84.6 4.1 %collective-permute-start.28 = (bf16[256,128]{1,0:T(8,128)(2,1)S(1)}, bf16[256,128]{1,0:T(8,128)(2,1)S(1)}, u32[]{:S(2)}, u32[]{:S(2)}) collective-permute-start(bf16[256,128]{1,0:T(8,128)(2,1)S(1)} %get-tuple-element.141), channel_id=1, source_target_pairs={{0,3},{1,2},{2,1},{3,0},{4,7},{5,6},{6,5},{7,4},{8,11},{9,10},{10,... | collective-permute-start | bytes 196616 | tf_op jit(solution)/shard_map/ppermute | solution.py:757
  85.7 3.1 %copy-start.1 = (bf16[512,1024]{1,0:T(8,128)(2,1)S(1)}, bf16[512,1024]{1,0:T(8,128)(2,1)}, u32[]{:S(2)}) copy-start(bf16[512,1024]{1,0:T(8,128)(2,1)} %copy-done) | copy-start | bytes 3145732
  85.8 9.9 %collective-permute-start.38 = (bf16[256,512]{1,0:T(8,128)(2,1)S(1)}, bf16[256,512]{1,0:T(8,128)(2,1)S(1)}, u32[]{:S(2)}, u32[]{:S(2)}) collective-permute-start(bf16[256,512]{1,0:T(8,128)(2,1)S(1)} %side.2), channel_id=1, source_target_pairs={{0,4},{1,5},{2,6},{3,7},{4,0},{5,1},{6,2},{7,3},{8,12},{9,13},{10,... | collective-permute-start | bytes 786440 | tf_op jit(solution)/shard_map/ppermute | solution.py:757
  92.9 16.3 %collective-permute-start.37 = (bf16[256,1024]{1,0:T(8,128)(2,1)S(1)}, bf16[256,1024]{1,0:T(8,128)(2,1)S(1)}, u32[]{:S(2)}, u32[]{:S(2)}) collective-permute-start(bf16[256,1024]{1,0:T(8,128)(2,1)S(1)} %get-tuple-element.172), channel_id=1, source_target_pairs={{0,1},{1,0},{2,3},{3,2},{4,5},{5,4},{6,7},{7,6},{8,9},{9,8},{10,11... | collective-permute-start | bytes 1572872 | tf_op jit(solution)/shard_map/ppermute | solution.py:757
  93.0 11.0 %collective-permute-start.34 = (bf16[272,640]{1,0:T(8,128)(2,1)S(1)}, bf16[272,640]{1,0:T(8,128)(2,1)S(1)}, u32[]{:S(2)}, u32[]{:S(2)}) collective-permute-start(bf16[272,640]{1,0:T(8,128)(2,1)S(1)} %get-tuple-element.162), channel_id=1, source_target_pairs={{0,4},{1,5},{2,6},{3,7},{4,0},{5,1},{6,2},{7,3},{8,12},{9,13},{10,... | collective-permute-start | bytes 1044488 | tf_op jit(solution)/shard_map/ppermute | solution.py:757
  94.4 14.8 %collective-permute-start.40 = (bf16[256,512]{1,0:T(8,128)(2,1)S(1)}, bf16[256,512]{1,0:T(8,128)(2,1)S(1)}, u32[]{:S(2)}, u32[]{:S(2)}) collective-permute-start(bf16[256,512]{1,0:T(8,128)(2,1)S(1)} %near.2), channel_id=1, source_target_pairs={{0,8},{1,9},{2,10},{3,11},{4,12},{5,13},{6,14},{7,15},{8,0},{9,1},... | collective-permute-start | bytes 786440 | tf_op jit(solution)/shard_map/ppermute | solution.py:757
  95.8 13.4 %collective-permute-start.39 = (bf16[256,512]{1,0:T(8,128)(2,1)S(1)}, bf16[256,512]{1,0:T(8,128)(2,1)S(1)}, u32[]{:S(2)}, u32[]{:S(2)}) collective-permute-start(bf16[256,512]{1,0:T(8,128)(2,1)S(1)} %far.3), channel_id=1, source_target_pairs={{0,16},{1,17},{2,18},{3,19},{4,20},{5,21},{6,22},{7,23},{8,24},{9,... | collective-permute-start | bytes 786440 | tf_op jit(solution)/shard_map/ppermute | solution.py:757
  98.5 12.1 %collective-permute-start.32 = (bf16[256,640]{1,0:T(8,128)(2,1)S(1)}, bf16[256,640]{1,0:T(8,128)(2,1)S(1)}, u32[]{:S(2)}, u32[]{:S(2)}) collective-permute-start(bf16[256,640]{1,0:T(8,128)(2,1)S(1)} %get-tuple-element.158), channel_id=1, source_target_pairs={{0,4},{1,5},{2,6},{3,7},{4,0},{5,1},{6,2},{7,3},{8,12},{9,13},{10,... | collective-permute-start | bytes 983048 | tf_op jit(solution)/shard_map/ppermute | solution.py:757
  104.0 8.3 %collective-permute-start.35 = (bf16[144,640]{1,0:T(8,128)(2,1)S(1)}, bf16[144,640]{1,0:T(8,128)(2,1)S(1)}, u32[]{:S(2)}, u32[]{:S(2)}) collective-permute-start(bf16[144,640]{1,0:T(8,128)(2,1)S(1)} %get-tuple-element.164), channel_id=1, source_target_pairs={{0,8},{1,9},{2,10},{3,11},{4,12},{5,13},{6,14},{7,15},{8,0},{9,1},... | collective-permute-start | bytes 552968 | tf_op jit(solution)/shard_map/ppermute | solution.py:757
  109.3 14.8 %collective-permute-start.41 = (bf16[128,1024]{1,0:T(8,128)(2,1)S(1)}, bf16[128,1024]{1,0:T(8,128)(2,1)S(1)}, u32[]{:S(2)}, u32[]{:S(2)}) collective-permute-start(bf16[128,1024]{1,0:T(8,128)(2,1)S(1)} %get-tuple-element.176), channel_id=1, source_target_pairs={{0,2},{1,3},{2,0},{3,1},{4,6},{5,7},{6,4},{7,5},{8,10},{9,11},{10,... | collective-permute-start | bytes 786440 | tf_op jit(solution)/shard_map/ppermute | solution.py:757
  112.4 11.6 %collective-permute-start.36 = (bf16[144,640]{1,0:T(8,128)(2,1)S(1)}, bf16[144,640]{1,0:T(8,128)(2,1)S(1)}, u32[]{:S(2)}, u32[]{:S(2)}) collective-permute-start(bf16[144,640]{1,0:T(8,128)(2,1)S(1)} %get-tuple-element.167), channel_id=1, source_target_pairs={{0,16},{1,17},{2,18},{3,19},{4,20},{5,21},{6,22},{7,23},{8,24},{9,... | collective-permute-start | bytes 552968 | tf_op jit(solution)/shard_map/ppermute | solution.py:757
  116.0 9.1 %collective-permute-start.33 = (bf16[128,640]{1,0:T(8,128)(2,1)S(1)}, bf16[128,640]{1,0:T(8,128)(2,1)S(1)}, u32[]{:S(2)}, u32[]{:S(2)}) collective-permute-start(bf16[128,640]{1,0:T(8,128)(2,1)S(1)} %near.3), channel_id=1, source_target_pairs={{0,8},{1,9},{2,10},{3,11},{4,12},{5,13},{6,14},{7,15},{8,0},{9,1},... | collective-permute-start | bytes 491528 | tf_op jit(solution)/shard_map/ppermute | solution.py:757
  117.1 10.9 %collective-permute-start.42 = (bf16[128,1024]{1,0:T(8,128)(2,1)S(1)}, bf16[128,1024]{1,0:T(8,128)(2,1)S(1)}, u32[]{:S(2)}, u32[]{:S(2)}) collective-permute-start(bf16[128,1024]{1,0:T(8,128)(2,1)S(1)} %get-tuple-element.181), channel_id=1, source_target_pairs={{0,2},{1,3},{2,0},{3,1},{4,6},{5,7},{6,4},{7,5},{8,10},{9,11},{10,... | collective-permute-start | bytes 786440 | tf_op jit(solution)/shard_map/ppermute | solution.py:757
  126.0 3.8 %collective-permute-start.43 = (bf16[48,1152]{1,0:T(8,128)(2,1)S(1)}, bf16[48,1152]{1,0:T(8,128)(2,1)S(1)}, u32[]{:S(2)}, u32[]{:S(2)}) collective-permute-start(bf16[48,1152]{1,0:T(8,128)(2,1)S(1)} %get-tuple-element.187), channel_id=1, source_target_pairs={{0,1},{1,0},{2,3},{3,2},{4,5},{5,4},{6,7},{7,6},{8,9},{9,8},{10,11... | collective-permute-start | bytes 331784 | tf_op jit(solution)/shard_map/ppermute | solution.py:757
  126.0 5.9 %collective-permute-start.44 = (bf16[48,1152]{1,0:T(8,128)(2,1)S(1)}, bf16[48,1152]{1,0:T(8,128)(2,1)S(1)}, u32[]{:S(2)}, u32[]{:S(2)}) collective-permute-start(bf16[48,1152]{1,0:T(8,128)(2,1)S(1)} %get-tuple-element.188), channel_id=1, source_target_pairs={{0,2},{1,3},{2,0},{3,1},{4,6},{5,7},{6,4},{7,5},{8,10},{9,11},{10,... | collective-permute-start | bytes 331784 | tf_op jit(solution)/shard_map/ppermute | solution.py:757
  127.0 6.5 %collective-permute-start.45 = (bf16[48,1152]{1,0:T(8,128)(2,1)S(1)}, bf16[48,1152]{1,0:T(8,128)(2,1)S(1)}, u32[]{:S(2)}, u32[]{:S(2)}) collective-permute-start(bf16[48,1152]{1,0:T(8,128)(2,1)S(1)} %get-tuple-element.189), channel_id=1, source_target_pairs={{0,3},{1,2},{2,1},{3,0},{4,7},{5,6},{6,5},{7,4},{8,11},{9,10},{10,... | collective-permute-start | bytes 331784 | tf_op jit(solution)/shard_map/ppermute | solution.py:757

commit v5 on v4

--- a/solution.py
+++ b/solution.py
@@ -40,6 +40,24 @@
     return lax.dot_general(
         a, b, (((1,), (0,)), ((), ())), precision=HIGH, preferred_element_type=F32
     )
+
+
+def split3(v):
+    high = v.astype(BF)
+    rest = v - high.astype(F32)
+    mid = rest.astype(BF)
+    return high, mid, (rest - mid.astype(F32)).astype(BF)
+
+
+def ones_left(ones, v):
+    n = v.shape[1]
+    out = mm(ones.astype(BF), jnp.concatenate(split3(v), 1))
+    return out[:, 0:n] + out[:, n : 2 * n] + out[:, 2 * n :]
+
+
+def ones_right(v, ones):
+    low = ones.astype(BF)
+    return mm(jnp.concatenate(split3(v), 1), jnp.concatenate([low, low, low], 0))
 
 
 def call(kernel, out_shapes, inputs, scratch=(), flops=1e3, name=None, raw=(), limit=VMEM_BYTES):
@@ -112,7 +130,7 @@
 def steps_of(dt_raw, dtb, neg_rate, rows):
     step = softplus(dt_raw + dtb)
     log_decay = step * neg_rate
-    cum = mm_high(tri_block(rows), log_decay)
+    cum = ones_left(tri_block(rows), log_decay)
     return step, log_decay, cum
 
 
@@ -133,7 +151,7 @@
     return jnp.where(low, row[:, 2 * pair : 2 * pair + 1], row[:, 2 * pair + 1 : 2 * pair + 2])
 
 
-def scan_kernel(me_ref, own_ref, g1, g2, g3, ends_ref, cw_ref, head_ref, out_ref, proj_ref, scr):
+def scan_kernel(me_ref, own_ref, g1, g2, g3, ends_ref, cw_ref, head_ref, out_ref, proj_ref, conv_ref, scr):
     rows = LANES
     width = out_ref.shape[1]
     t = me_ref[0] & (QUAD - 1)
@@ -160,6 +178,7 @@
         masks = same_masks(ends, rows, 4)
         xbc = proj_ref[at, 0:convw]
         conv = conv_sum_of(xbc, cw_ref[...], cw_ref[4:5, :], masks)
+        conv_ref[at, :] = conv
         act = conv * sigmoid(conv)
         key, read = act[:, width : width + LANES], act[:, width + LANES : convw]
         scores = mm_t(read.astype(BF), key.astype(BF))
@@ -177,11 +196,11 @@
             out_ref[at, lanes] = y + pair_lanes(skip, p, low[0:1, :]) * x
         return carry
 
-    lax.fori_loop(0, ends_ref.shape[0], body, 0)
+    lax.fori_loop(0, ends_ref.shape[0], body, 0, unroll=True)
 
 
 def scan_back_kernel(
-    me_ref, proj_ref, dscan_ref, ends_ref, cw_ref, head_ref, pc_ref, small_ref, p0, p1, p2, p3, scr
+    me_ref, proj_ref, conv_ref, dscan_ref, ends_ref, cw_ref, head_ref, pc_ref, small_ref, p0, p1, p2, p3, scr
 ):
     rows = LANES
     width = dscan_ref.shape[1]
@@ -215,7 +234,7 @@
         masks = same_masks(ends, rows, 4)
         xbc = proj_ref[at, 0:convw]
         cw = cw_ref[...]
-        conv = conv_sum_of(xbc, cw, cw[4:5, :], masks)
+        conv = conv_ref[at, :]
         sig = sigmoid(conv)
         act = conv * sig
         key = act[:, width : width + LANES].astype(BF)
@@ -251,7 +270,7 @@
             dsk.append(jnp.sum(dy * x, axis=0, keepdims=True))
             dxs.append(dx_s * s + pair_lanes(skip, p, low[0:1, :]) * dy)
         dlog = jnp.concatenate(dlogs + [jnp.zeros((rows - own, rows), F32)], 0).T
-        dstep = mm_high(jnp.concatenate(prods, 1), by_head) + dlog * neg_rate
+        dstep = ones_right(jnp.concatenate(prods, 1), by_head) + dlog * neg_rate
         ddt = jnp.where(lane < own, dstep * sigmoid(raw + dtb), 0.0)
         dsc = (dscores[:, 0:rows] + dscores[:, rows:]).astype(BF)
         dkey = mm(dsc, read)
@@ -272,7 +291,7 @@
         pc_ref[at, width + part :] = ddt[:, 0:part].astype(BF)
         return dskip + jnp.concatenate(dsk, 1)
 
-    dskip = lax.fori_loop(0, ends_ref.shape[0], body, jnp.zeros((1, width), F32))
+    dskip = lax.fori_loop(0, ends_ref.shape[0], body, jnp.zeros((1, width), F32), unroll=True)
     small_ref[11:12, 2 * LANES : 3 * LANES] = mm_high(dskip, by_head)
     half = scr.shape[1] // 2
     for r, out in enumerate((p0, p1, p2, p3)):
@@ -289,13 +308,11 @@
 
 
 def pick_heads(parts, heads):
-    total = None
+    sels = []
     for q in range(QUAD):
         deep = (parts[q].shape[1], heads)
-        sel = (iota(deep, 1) == iota(deep, 0) * QUAD + q).astype(F32)
-        got = mm_high(parts[q], sel)
-        total = got if total is None else total + got
-    return total
+        sels.append((iota(deep, 1) == iota(deep, 0) * QUAD + q).astype(F32))
+    return ones_right(jnp.concatenate(parts, 1), jnp.concatenate(sels, 0))
 
 
 def prep_kernel(me_ref, len_hbm, *refs):
@@ -847,9 +864,9 @@
         flops=OPT['pcost'],
         name="project",
     )
-    scan_out, proj = call(
+    scan_out, proj, conv = call(
         scan_kernel,
-        [((total_rows, width), F32), ((total_rows, full), F32)],
+        [((total_rows, width), F32), ((total_rows, full), F32), ((total_rows, convw), F32)],
         [me, proj_own] + [swap(shared, r) for r in range(1, QUAD)] + [ends, cwb, by_head],
         [pltpu.VMEM((QUAD, total_rows, part), F32)],
         flops=OPT['scost'],
@@ -892,7 +909,7 @@
     pc_x, small, own_bc, *bc = call(
         scan_back_kernel,
         [((total_rows, wide), BF), ((SMALL, wide), F32), (fold, F32)] + [(fold, BF)] * 3,
-        [me, proj, dscan, ends, cwb, by_head],
+        [me, proj, conv, dscan, ends, cwb, by_head],
         [pltpu.VMEM((QUAD, total_rows, part), F32)],
         name="scanback",
         flops=OPT['bcost'],

time: 135 us -> 135 us (level)
  Pallas kernels: 32.2 us -> 30.5 us
    pallas_call x23, Pallas kernels: 32.2 us -> 30.5 us  [call(): pl.pallas_call(kernel, out_shape=shapes, in_specs=in_specs, out_specs=[pl...]
  transfers between devices with their start and end apart: 46 -> 46, of which waited for: 23 -> 23; matrix products, arithmetic and copies ran while one was open for 0% -> 0% of each run, Pallas kernels for 17% -> 16%
where the time goes in v5:
time: 135 us
  waiting for transfers between devices  54 us (40%)
  starting transfers between devices  49.1 us (36%)
  Pallas kernels  30.5 us (23%)
    ppermute x46, waiting for transfers between devices, swap(): return lax.ppermute(a, 'dp', [(i, i ^ mask) for i in range(count)])  54 us
    ppermute x46, starting transfers between devices, swap(): return lax.ppermute(a, 'dp', [(i, i ^ mask) for i in range(count)])  49.1 us
    pallas_call x23, Pallas kernels, call(): pl.pallas_call(kernel, out_shape=shapes, in_specs=in_specs, out_specs=[pl...  30.5 us
  transfers between devices with their start and end apart: 46, of which 23 were waited for; matrix products, arithmetic and copies ran while one was open for 0% of the time, Pallas kernels for 16%

profile of v5, /device:TPU:0, one launch (start us, length us, event | category | flops | bytes accessed | tf_op | source)
XLA Modules:
  0.0 134.7 jit_solution(5767837208311238761)
XLA Ops:
  0.7 1.6 %prep.1 = (bf16[272,1024]{1,0:T(8,128)(2,1)S(1)}, f32[8,768]{1,0:T(8,128)S(1)}, f32[8,128]{1,0:T(8,128)S(1)}, f32[1,512]{1,0:T(1,128)S(1)}, f32[1,1024]{1,0:T(1,...) custom-call(s32[1]{0:T(128)} %bitcast.me_ref, ...), custom_call_target="tpu_custom_call" | custom-call | flops 1000 | bytes 1024 | tf_op jit(solution)/shard_map/prep/pallas_call | solution.py:77
  2.8 2.9 %collective-permute-start.2 = (bf16[32,1152]{1,0:T(8,128)(2,1)S(1)}, bf16[32,1152]{1,0:T(8,128)(2,1)S(1)}, u32[]{:S(2)}, u32[]{:S(2)}) collective-permute-start(bf16[32,1152]{1,0:T(8,128)(2,1)S(1)} %get-tuple-element.109), channel_id=1, source_target_pairs={{0,2},{1,3},{2,0},{3,1},{4,6},{5,7},{6,4},{7,5},{8,10},{9,11},{10,... | collective-permute-start | bytes 221192 | tf_op jit(solution)/shard_map/ppermute | solution.py:774
  5.7 2.5 %collective-permute-done.2.c2 = bf16[32,1152]{1,0:T(8,128)(2,1)S(1)} collective-permute-done((bf16[32,1152]{1,0:T(8,128)(2,1)S(1)}, bf16[32,1152]{1,0:T(8,128)(2,1)S(1)}, u32[]{:S(2)}, u32[]{:S(2)}) %collective-permute-start.2) | collective-permute-done | bytes 73760 | tf_op jit(solution)/shard_map/ppermute | solution.py:774
  8.3 2.0 %collective-permute-done.3.c3 = bf16[32,1152]{1,0:T(8,128)(2,1)S(1)} collective-permute-done((bf16[32,1152]{1,0:T(8,128)(2,1)S(1)}, bf16[32,1152]{1,0:T(8,128)(2,1)S(1)}, u32[]{:S(2)}, u32[]{:S(2)}) %collective-permute-start.3) | collective-permute-done | bytes 73760 | tf_op jit(solution)/shard_map/ppermute | solution.py:774
  10.8 1.7 %collective-permute-start.8 = (bf16[128,640]{1,0:T(8,128)(2,1)S(1)}, bf16[128,640]{1,0:T(8,128)(2,1)S(1)}, u32[]{:S(2)}, u32[]{:S(2)}) collective-permute-start(bf16[128,640]{1,0:T(8,128)(2,1)S(1)} %get-tuple-element.114.refs_4_.refs_0_), channel_id=1, source_target_pairs={{0,8},{1,9},{2,10},{3,11},{4,12},{5,13},{6,14},{7,15},{8,0},{9,1},... | collective-permute-start | bytes 491528 | tf_op jit(solution)/shard_map/ppermute | solution.py:774
  12.5 2.6 %collective-permute-start.7 = (bf16[128,640]{1,0:T(8,128)(2,1)S(1)}, bf16[128,640]{1,0:T(8,128)(2,1)S(1)}, u32[]{:S(2)}, u32[]{:S(2)}) collective-permute-start(bf16[128,640]{1,0:T(8,128)(2,1)S(1)} %get-tuple-element.114.refs_4_.refs_0_), channel_id=1, source_target_pairs={{0,16},{1,17},{2,18},{3,19},{4,20},{5,21},{6,22},{7,23},{8,24},{9,... | collective-permute-start | bytes 491528 | tf_op jit(solution)/shard_map/ppermute | solution.py:774
  15.1 1.5 %collective-permute-start.6 = (bf16[128,640]{1,0:T(8,128)(2,1)S(1)}, bf16[128,640]{1,0:T(8,128)(2,1)S(1)}, u32[]{:S(2)}, u32[]{:S(2)}) collective-permute-start(bf16[128,640]{1,0:T(8,128)(2,1)S(1)} %get-tuple-element.114.refs_4_.refs_0_), channel_id=1, source_target_pairs={{0,4},{1,5},{2,6},{3,7},{4,0},{5,1},{6,2},{7,3},{8,12},{9,13},{10,... | collective-permute-start | bytes 491528 | tf_op jit(solution)/shard_map/ppermute | solution.py:774
  16.6 8.3 %collective-permute-done.4.refs_2_.refs_10_ = bf16[272,1024]{1,0:T(8,128)(2,1)S(1)} collective-permute-done((bf16[272,1024]{1,0:T(8,128)(2,1)S(1)}, bf16[272,1024]{1,0:T(8,128)(2,1)S(1)}, u32[]{:S(2)}, u32[]{:S(2)}) %collective-permute-start.4) | collective-permute-done | bytes 557088 | tf_op jit(solution)/shard_map/ppermute | solution.py:774
  24.9 1.6 %collective-permute-start.11 = (bf16[128,640]{1,0:T(8,128)(2,1)S(1)}, bf16[128,640]{1,0:T(8,128)(2,1)S(1)}, u32[]{:S(2)}, u32[]{:S(2)}) collective-permute-start(bf16[128,640]{1,0:T(8,128)(2,1)S(1)} %collective-permute-done.7.refs_8_.refs_4_), channel_id=1, source_target_pairs={{0,8},{1,9},{2,10},{3,11},{4,12},{5,13},{6,14},{7,15},{8,0},{9,1},... | collective-permute-start | bytes 491528 | tf_op jit(solution)/shard_map/ppermute | solution.py:774
  26.6 1.5 %collective-permute-start.16 = (bf16[256,512]{1,0:T(8,128)(2,1)S(1)}, bf16[256,512]{1,0:T(8,128)(2,1)S(1)}, u32[]{:S(2)}, u32[]{:S(2)}) collective-permute-start(bf16[256,512]{1,0:T(8,128)(2,1)S(1)} %get-tuple-element.128.refs_0_.refs_4_.refs_8_), channel_id=1, source_target_pairs={{0,4},{1,5},{2,6},{3,7},{4,0},{5,1},{6,2},{7,3},{8,12},{9,13},{10,... | collective-permute-start | bytes 786440 | tf_op jit(solution)/shard_map/ppermute | solution.py:774
  29.0 2.9 %collective-permute-done.11.refs_10_.refs_6_ = bf16[128,640]{1,0:T(8,128)(2,1)S(1)} collective-permute-done((bf16[128,640]{1,0:T(8,128)(2,1)S(1)}, bf16[128,640]{1,0:T(8,128)(2,1)S(1)}, u32[]{:S(2)}, u32[]{:S(2)}) %collective-permute-start.11) | collective-permute-done | bytes 163872 | tf_op jit(solution)/shard_map/ppermute | solution.py:774
  32.0 2.6 %collective-permute-start.17 = (bf16[256,512]{1,0:T(8,128)(2,1)S(1)}, bf16[256,512]{1,0:T(8,128)(2,1)S(1)}, u32[]{:S(2)}, u32[]{:S(2)}) collective-permute-start(bf16[256,512]{1,0:T(8,128)(2,1)S(1)} %get-tuple-element.128.refs_0_.refs_4_.refs_8_), channel_id=1, source_target_pairs={{0,16},{1,17},{2,18},{3,19},{4,20},{5,21},{6,22},{7,23},{8,24},{9,... | collective-permute-start | bytes 786440 | tf_op jit(solution)/shard_map/ppermute | solution.py:774
  34.6 3.9 %collective-permute-done.10.refs_9_.refs_5_ = bf16[128,640]{1,0:T(8,128)(2,1)S(1)} collective-permute-done((bf16[128,640]{1,0:T(8,128)(2,1)S(1)}, bf16[128,640]{1,0:T(8,128)(2,1)S(1)}, u32[]{:S(2)}, u32[]{:S(2)}) %collective-permute-start.10) | collective-permute-done | bytes 163872 | tf_op jit(solution)/shard_map/ppermute | solution.py:774
  38.5 1.5 %collective-permute-start.9 = (bf16[128,640]{1,0:T(8,128)(2,1)S(1)}, bf16[128,640]{1,0:T(8,128)(2,1)S(1)}, u32[]{:S(2)}, u32[]{:S(2)}) collective-permute-start(bf16[128,640]{1,0:T(8,128)(2,1)S(1)} %collective-permute-done.8.refs_6_.refs_2_), channel_id=1, source_target_pairs={{0,4},{1,5},{2,6},{3,7},{4,0},{5,1},{6,2},{7,3},{8,12},{9,13},{10,... | collective-permute-start | bytes 491528 | tf_op jit(solution)/shard_map/ppermute | solution.py:774
  40.5 3.5 %collective-permute-done.9.refs_7_.refs_3_ = bf16[128,640]{1,0:T(8,128)(2,1)S(1)} collective-permute-done((bf16[128,640]{1,0:T(8,128)(2,1)S(1)}, bf16[128,640]{1,0:T(8,128)(2,1)S(1)}, u32[]{:S(2)}, u32[]{:S(2)}) %collective-permute-start.9) | collective-permute-done | bytes 163872 | tf_op jit(solution)/shard_map/ppermute | solution.py:774
  44.0 2.2 %collective-permute-done.17.refs_4_.refs_8_.refs_12_ = bf16[256,512]{1,0:T(8,128)(2,1)S(1)} collective-permute-done((bf16[256,512]{1,0:T(8,128)(2,1)S(1)}, bf16[256,512]{1,0:T(8,128)(2,1)S(1)}, u32[]{:S(2)}, u32[]{:S(2)}) %collective-permute-start.17) | collective-permute-done | bytes 262176 | tf_op jit(solution)/shard_map/ppermute | solution.py:774
  46.2 0.7 collective-permute-start.21
  46.9 1.5 %collective-permute-start.20 = (bf16[256,512]{1,0:T(8,128)(2,1)S(1)}, bf16[256,512]{1,0:T(8,128)(2,1)S(1)}, u32[]{:S(2)}, u32[]{:S(2)}) collective-permute-start(bf16[256,512]{1,0:T(8,128)(2,1)S(1)} %collective-permute-done.17.refs_4_.refs_8_.refs_12_), channel_id=1, source_target_pairs={{0,4},{1,5},{2,6},{3,7},{4,0},{5,1},{6,2},{7,3},{8,12},{9,13},{10,... | collective-permute-start | bytes 786440 | tf_op jit(solution)/shard_map/ppermute | solution.py:774
  48.4 1.5 %project.1 = (bf16[512,1024]{1,0:T(8,128)(2,1)S(1)}, f32[512,640]{1,0:T(8,128)S(1)}, f32[4,128]{1,0:T(4,128)S(1)}, bf16[256,128]{1,0:T(8,128)(2,1)S(1)}) custom-call(s32[1]{0:T(128)} %bitcast.me_ref, bf16[272,1024]{1,0:T(8,128)(2,1)S(1)} %get-tuple-element.111.refs_0_.refs_8_.act_ref, bf16[272,1024]{1,0:T(8,128)(2,1)S(1)} %collective-permute-done.refs_1_.refs_9_, ...), custom_call_target="tpu_custom_call" | custom-call | flops 4000000000 | bytes 1024 | tf_op jit(solution)/shard_map/project/pallas_call | solution.py:77
  50.0 1.1 collective-permute-start.14
  51.2 0.7 collective-permute-start.13
  51.9 0.7 collective-permute-done.21.refs_6_.refs_10_.refs_14_
  52.6 1.5 %collective-permute-start.19 = (bf16[256,512]{1,0:T(8,128)(2,1)S(1)}, bf16[256,512]{1,0:T(8,128)(2,1)S(1)}, u32[]{:S(2)}, u32[]{:S(2)}) collective-permute-start(bf16[256,512]{1,0:T(8,128)(2,1)S(1)} %collective-permute-done.18.refs_2_.refs_6_.refs_10_), channel_id=1, source_target_pairs={{0,4},{1,5},{2,6},{3,7},{4,0},{5,1},{6,2},{7,3},{8,12},{9,13},{10,... | collective-permute-start | bytes 786440 | tf_op jit(solution)/shard_map/ppermute | solution.py:774
  54.1 1.0 collective-permute-start.22
  55.2 4.9 %scan.1 = (f32[512,512]{1,0:T(8,128)S(1)}, f32[512,896]{1,0:T(8,128)S(1)}, f32[512,768]{1,0:T(8,128)S(1)}) custom-call(s32[1]{0:T(128)} %bitcast.me_ref, f32[512,640]{1,0:T(8,128)S(1)} %get-tuple-element.120.own_ref, bf16[256,128]{1,0:T(8,128)(2,1)S(1)} %collective-permute-done.13.g1, bf16[256,128]{1,0:T(8,128)(2,1)S(1)} %collective-permute-done.14.g2, ...), custom_call_target="tpu_custom_call" | custom-call | flops 16000000000 | bytes 1024 | tf_op jit(solution)/shard_map/scan/pallas_call | solution.py:77
  60.5 0.8 normcot.1
  61.3 1.2 gate.1
  62.9 1.1 collective-permute-start.24
  64.5 1.4 %collective-permute-done.25.refs_3_ = f32[8,512]{1,0:T(8,128)S(1)} collective-permute-done((f32[8,512]{1,0:T(8,128)S(1)}, f32[8,512]{1,0:T(8,128)S(1)}, u32[]{:S(2)}, u32[]{:S(2)}) %collective-permute-start.25) | collective-permute-done | bytes 16416 | tf_op jit(solution)/shard_map/ppermute | solution.py:774
  65.9 0.9 collective-permute-done.24.refs_2_
  66.7 4.2 %ungate.1 = (bf16[512,512]{1,0:T(8,128)(2,1)S(1)}, f32[512,512]{1,0:T(8,128)S(1)}, bf16[512,512]{1,0:T(8,128)(2,1)S(1)}, f32[1,512]{1,0:T(1,128)S(1)}, f32[128,1...) custom-call(s32[1]{0:T(128)} %bitcast.me_ref, ...), custom_call_target="tpu_custom_call" | custom-call | flops 1000 | bytes 1024 | tf_op jit(solution)/shard_map/ungate/pallas_call | solution.py:77
  71.0 1.2 collective-permute-start.30
  72.2 1.2 collective-permute-start.31
  73.4 0.7 branch.1
  74.3 6.9 %scanback.1 = (bf16[512,640]{1,0:T(8,128)(2,1)S(1)}, f32[16,640]{1,0:T(8,128)S(1)}, f32[256,128]{1,0:T(8,128)S(1)}, bf16[256,128]{1,0:T(8,128)(2,1)S(1)}, bf16[2...) custom-call(s32[1]{0:T(128)} %bitcast.me_ref, f32[512,896]{1,0:T(8,128)S(1)} %get-tuple-element.125.proj_ref, ...), custom_call_target="tpu_custom_call" | custom-call | flops 1000 | bytes 1024 | tf_op jit(solution)/shard_map/scanback/pallas_call | solution.py:77
  81.3 0.6 collective-permute-start.26
  81.9 1.2 collective-permute-start.27
  83.0 1.9 %collective-permute-done.30.got_ref = bf16[512,512]{1,0:T(8,128)(2,1)S(1)} collective-permute-done((bf16[512,512]{1,0:T(8,128)(2,1)S(1)}, bf16[512,512]{1,0:T(8,128)(2,1)S(1)}, u32[]{:S(2)}, u32[]{:S(2)}) %collective-permute-start.30) | collective-permute-done | bytes 524320 | tf_op jit(solution)/shard_map/ppermute | solution.py:774
  85.4 1.8 %collective-permute-start.38 = (bf16[256,512]{1,0:T(8,128)(2,1)S(1)}, bf16[256,512]{1,0:T(8,128)(2,1)S(1)}, u32[]{:S(2)}, u32[]{:S(2)}) collective-permute-start(bf16[256,512]{1,0:T(8,128)(2,1)S(1)} %side.2), channel_id=1, source_target_pairs={{0,4},{1,5},{2,6},{3,7},{4,0},{5,1},{6,2},{7,3},{8,12},{9,13},{10,... | collective-permute-start | bytes 786440 | tf_op jit(solution)/shard_map/ppermute | solution.py:774
  87.4 1.3 collective-permute-done.28.g3
  88.7 1.5 %ingrad.1 = (bf16[512,640]{1,0:T(8,128)(2,1)S(1)}, f32[128,640]{1,0:T(8,128)S(1)}, f32[128,640]{1,0:T(8,128)S(1)}, f32[128,640]{1,0:T(8,128)S(1)}, f32[128,640]{...) custom-call(s32[1]{0:T(128)} %bitcast.me_ref, ...), custom_call_target="tpu_custom_call" | custom-call | flops 1000 | bytes 1024 | tf_op jit(solution)/shard_map/ingrad/pallas_call | solution.py:77
  90.1 2.6 %tail.1 = (f32[256,1024]{1,0:T(8,128)S(1)}, bf16[256,1024]{1,0:T(8,128)(2,1)S(1)}) custom-call(s32[1]{0:T(128)} %bitcast.me_ref, bf16[128,640]{1,0:T(8,128)(2,1)S(1)} %get-tuple-element.114.refs_4_.refs_0_, bf16[128,640]{1,0:T(8,128)(2,1)S(1)} %collective-permute-done.6.refs_5_.refs_1_, bf16[128,640]{1,0:T(8,128)(2,1)S(1)} %collective-permute-done.8.refs_6_.refs_2_, ...), custom_call_target="tpu_custom_call" | custom-call | flops 1000 | bytes 1024 | tf_op jit(solution)/shard_map/tail/pallas_call | solution.py:77
  92.9 1.6 %collective-permute-start.34 = (bf16[272,640]{1,0:T(8,128)(2,1)S(1)}, bf16[272,640]{1,0:T(8,128)(2,1)S(1)}, u32[]{:S(2)}, u32[]{:S(2)}) collective-permute-start(bf16[272,640]{1,0:T(8,128)(2,1)S(1)} %get-tuple-element.164), channel_id=1, source_target_pairs={{0,4},{1,5},{2,6},{3,7},{4,0},{5,1},{6,2},{7,3},{8,12},{9,13},{10,... | collective-permute-start | bytes 1044488 | tf_op jit(solution)/shard_map/ppermute | solution.py:774
  94.4 1.3 collective-permute-start.40
  95.8 2.7 %collective-permute-start.39 = (bf16[256,512]{1,0:T(8,128)(2,1)S(1)}, bf16[256,512]{1,0:T(8,128)(2,1)S(1)}, u32[]{:S(2)}, u32[]{:S(2)}) collective-permute-start(bf16[256,512]{1,0:T(8,128)(2,1)S(1)} %far.3), channel_id=1, source_target_pairs={{0,16},{1,17},{2,18},{3,19},{4,20},{5,21},{6,22},{7,23},{8,24},{9,... | collective-permute-start | bytes 786440 | tf_op jit(solution)/shard_map/ppermute | solution.py:774
  98.5 1.1 collective-permute-start.32
  99.6 4.3 %collective-permute-done.34.got_ref.side_ref = bf16[272,640]{1,0:T(8,128)(2,1)S(1)} collective-permute-done((bf16[272,640]{1,0:T(8,128)(2,1)S(1)}, bf16[272,640]{1,0:T(8,128)(2,1)S(1)}, u32[]{:S(2)}, u32[]{:S(2)}) %collective-permute-start.34) | collective-permute-done | bytes 348192 | tf_op jit(solution)/shard_map/ppermute | solution.py:774
  103.9 0.9 collective-permute-start.35
  104.8 4.3 %collective-permute-done.40.refs_6_ = bf16[256,512]{1,0:T(8,128)(2,1)S(1)} collective-permute-done((bf16[256,512]{1,0:T(8,128)(2,1)S(1)}, bf16[256,512]{1,0:T(8,128)(2,1)S(1)}, u32[]{:S(2)}, u32[]{:S(2)}) %collective-permute-start.40) | collective-permute-done | bytes 262176 | tf_op jit(solution)/shard_map/ppermute | solution.py:774
  109.3 1.0 collective-permute-start.41
  110.4 1.9 %collective-permute-done.35.got_ref = bf16[144,640]{1,0:T(8,128)(2,1)S(1)} collective-permute-done((bf16[144,640]{1,0:T(8,128)(2,1)S(1)}, bf16[144,640]{1,0:T(8,128)(2,1)S(1)}, u32[]{:S(2)}, u32[]{:S(2)}) %collective-permute-start.35) | collective-permute-done | bytes 184352 | tf_op jit(solution)/shard_map/ppermute | solution.py:774
  112.4 3.5 %collective-permute-start.36 = (bf16[144,640]{1,0:T(8,128)(2,1)S(1)}, bf16[144,640]{1,0:T(8,128)(2,1)S(1)}, u32[]{:S(2)}, u32[]{:S(2)}) collective-permute-start(bf16[144,640]{1,0:T(8,128)(2,1)S(1)} %get-tuple-element.169), channel_id=1, source_target_pairs={{0,16},{1,17},{2,18},{3,19},{4,20},{5,21},{6,22},{7,23},{8,24},{9,... | collective-permute-start | bytes 552968 | tf_op jit(solution)/shard_map/ppermute | solution.py:774
  116.0 1.1 collective-permute-start.33
  117.0 0.9 collective-permute-start.42
  117.9 6.1 %collective-permute-done.36.refs_3_ = bf16[144,640]{1,0:T(8,128)(2,1)S(1)} collective-permute-done((bf16[144,640]{1,0:T(8,128)(2,1)S(1)}, bf16[144,640]{1,0:T(8,128)(2,1)S(1)}, u32[]{:S(2)}, u32[]{:S(2)}) %collective-permute-start.36) | collective-permute-done | bytes 184352 | tf_op jit(solution)/shard_map/ppermute | solution.py:774
  124.1 1.0 collective-permute-done.33.refs_2_
  125.0 1.0 total.1
  126.1 0.9 collective-permute-start.44
  127.0 0.9 collective-permute-start.45
  127.9 0.8 mixed.1
  128.7 1.0 tokgrad.1
  129.8 2.1 %collective-permute-done.44.refs_1_ = bf16[48,1152]{1,0:T(8,128)(2,1)S(1)} collective-permute-done((bf16[48,1152]{1,0:T(8,128)(2,1)S(1)}, bf16[48,1152]{1,0:T(8,128)(2,1)S(1)}, u32[]{:S(2)}, u32[]{:S(2)}) %collective-permute-start.44) | collective-permute-done | bytes 110624 | tf_op jit(solution)/shard_map/ppermute | solution.py:774
  131.9 1.6 %collective-permute-done.45.refs_2_ = bf16[48,1152]{1,0:T(8,128)(2,1)S(1)} collective-permute-done((bf16[48,1152]{1,0:T(8,128)(2,1)S(1)}, bf16[48,1152]{1,0:T(8,128)(2,1)S(1)}, u32[]{:S(2)}, u32[]{:S(2)}) %collective-permute-start.45) | collective-permute-done | bytes 110624 | tf_op jit(solution)/shard_map/ppermute | solution.py:774
  133.5 1.1 finish.1
  (67 shorter events, 5.5 us)
Async XLA Ops:
  2.2 3.5 %collective-permute-start = (bf16[272,1024]{1,0:T(8,128)(2,1)S(1)}, bf16[272,1024]{1,0:T(8,128)(2,1)S(1)}, u32[]{:S(2)}, u32[]{:S(2)}) collective-permute-start(bf16[272,1024]{1,0:T(8,128)(2,1)S(1)} %get-tuple-element.111.refs_0_.refs_8_.act_ref), channel_id=1, source_target_pairs={{0,1},{1,0},{2,3},{3,2},{4,5},{5,4},{6,7},{7,6},{8,9},{9,8},{10,11... | collective-permute-start | bytes 1671176 | tf_op jit(solution)/shard_map/ppermute | solution.py:774
  2.7 3.0 %collective-permute-start.1 = (bf16[32,1152]{1,0:T(8,128)(2,1)S(1)}, bf16[32,1152]{1,0:T(8,128)(2,1)S(1)}, u32[]{:S(2)}, u32[]{:S(2)}) collective-permute-start(bf16[32,1152]{1,0:T(8,128)(2,1)S(1)} %get-tuple-element.107), channel_id=1, source_target_pairs={{0,1},{1,0},{2,3},{3,2},{4,5},{5,4},{6,7},{7,6},{8,9},{9,8},{10,11... | collective-permute-start | bytes 221192 | tf_op jit(solution)/shard_map/ppermute | solution.py:774
  2.8 5.5 %collective-permute-start.2 = (bf16[32,1152]{1,0:T(8,128)(2,1)S(1)}, bf16[32,1152]{1,0:T(8,128)(2,1)S(1)}, u32[]{:S(2)}, u32[]{:S(2)}) collective-permute-start(bf16[32,1152]{1,0:T(8,128)(2,1)S(1)} %get-tuple-element.109), channel_id=1, source_target_pairs={{0,2},{1,3},{2,0},{3,1},{4,6},{5,7},{6,4},{7,5},{8,10},{9,11},{10,... | collective-permute-start | bytes 221192 | tf_op jit(solution)/shard_map/ppermute | solution.py:774
  5.7 4.5 %collective-permute-start.3 = (bf16[32,1152]{1,0:T(8,128)(2,1)S(1)}, bf16[32,1152]{1,0:T(8,128)(2,1)S(1)}, u32[]{:S(2)}, u32[]{:S(2)}) collective-permute-start(bf16[32,1152]{1,0:T(8,128)(2,1)S(1)} %get-tuple-element.110), channel_id=1, source_target_pairs={{0,3},{1,2},{2,1},{3,0},{4,7},{5,6},{6,5},{7,4},{8,11},{9,10},{10,... | collective-permute-start | bytes 221192 | tf_op jit(solution)/shard_map/ppermute | solution.py:774
  10.3 14.6 %collective-permute-start.4 = (bf16[272,1024]{1,0:T(8,128)(2,1)S(1)}, bf16[272,1024]{1,0:T(8,128)(2,1)S(1)}, u32[]{:S(2)}, u32[]{:S(2)}) collective-permute-start(bf16[272,1024]{1,0:T(8,128)(2,1)S(1)} %get-tuple-element.111.refs_0_.refs_8_.act_ref), channel_id=1, source_target_pairs={{0,2},{1,3},{2,0},{3,1},{4,6},{5,7},{6,4},{7,5},{8,10},{9,11},{10,... | collective-permute-start | bytes 1671176 | tf_op jit(solution)/shard_map/ppermute | solution.py:774
  10.8 14.1 %collective-permute-start.8 = (bf16[128,640]{1,0:T(8,128)(2,1)S(1)}, bf16[128,640]{1,0:T(8,128)(2,1)S(1)}, u32[]{:S(2)}, u32[]{:S(2)}) collective-permute-start(bf16[128,640]{1,0:T(8,128)(2,1)S(1)} %get-tuple-element.114.refs_4_.refs_0_), channel_id=1, source_target_pairs={{0,8},{1,9},{2,10},{3,11},{4,12},{5,13},{6,14},{7,15},{8,0},{9,1},... | collective-permute-start | bytes 491528 | tf_op jit(solution)/shard_map/ppermute | solution.py:774
  12.5 12.4 %collective-permute-start.7 = (bf16[128,640]{1,0:T(8,128)(2,1)S(1)}, bf16[128,640]{1,0:T(8,128)(2,1)S(1)}, u32[]{:S(2)}, u32[]{:S(2)}) collective-permute-start(bf16[128,640]{1,0:T(8,128)(2,1)S(1)} %get-tuple-element.114.refs_4_.refs_0_), channel_id=1, source_target_pairs={{0,16},{1,17},{2,18},{3,19},{4,20},{5,21},{6,22},{7,23},{8,24},{9,... | collective-permute-start | bytes 491528 | tf_op jit(solution)/shard_map/ppermute | solution.py:774
  15.1 9.8 %collective-permute-start.6 = (bf16[128,640]{1,0:T(8,128)(2,1)S(1)}, bf16[128,640]{1,0:T(8,128)(2,1)S(1)}, u32[]{:S(2)}, u32[]{:S(2)}) collective-permute-start(bf16[128,640]{1,0:T(8,128)(2,1)S(1)} %get-tuple-element.114.refs_4_.refs_0_), channel_id=1, source_target_pairs={{0,4},{1,5},{2,6},{3,7},{4,0},{5,1},{6,2},{7,3},{8,12},{9,13},{10,... | collective-permute-start | bytes 491528 | tf_op jit(solution)/shard_map/ppermute | solution.py:774
  24.9 23.5 %collective-permute-start.5 = (bf16[272,1024]{1,0:T(8,128)(2,1)S(1)}, bf16[272,1024]{1,0:T(8,128)(2,1)S(1)}, u32[]{:S(2)}, u32[]{:S(2)}) collective-permute-start(bf16[272,1024]{1,0:T(8,128)(2,1)S(1)} %collective-permute-done.4.refs_2_.refs_10_), channel_id=1, source_target_pairs={{0,1},{1,0},{2,3},{3,2},{4,5},{5,4},{6,7},{7,6},{8,9},{9,8},{10,11... | collective-permute-start | bytes 1671176 | tf_op jit(solution)/shard_map/ppermute | solution.py:774
  24.9 7.1 %collective-permute-start.11 = (bf16[128,640]{1,0:T(8,128)(2,1)S(1)}, bf16[128,640]{1,0:T(8,128)(2,1)S(1)}, u32[]{:S(2)}, u32[]{:S(2)}) collective-permute-start(bf16[128,640]{1,0:T(8,128)(2,1)S(1)} %collective-permute-done.7.refs_8_.refs_4_), channel_id=1, source_target_pairs={{0,8},{1,9},{2,10},{3,11},{4,12},{5,13},{6,14},{7,15},{8,0},{9,1},... | collective-permute-start | bytes 491528 | tf_op jit(solution)/shard_map/ppermute | solution.py:774
  26.6 13.5 %collective-permute-start.16 = (bf16[256,512]{1,0:T(8,128)(2,1)S(1)}, bf16[256,512]{1,0:T(8,128)(2,1)S(1)}, u32[]{:S(2)}, u32[]{:S(2)}) collective-permute-start(bf16[256,512]{1,0:T(8,128)(2,1)S(1)} %get-tuple-element.128.refs_0_.refs_4_.refs_8_), channel_id=1, source_target_pairs={{0,4},{1,5},{2,6},{3,7},{4,0},{5,1},{6,2},{7,3},{8,12},{9,13},{10,... | collective-permute-start | bytes 786440 | tf_op jit(solution)/shard_map/ppermute | solution.py:774
  28.1 10.4 %collective-permute-start.10 = (bf16[128,640]{1,0:T(8,128)(2,1)S(1)}, bf16[128,640]{1,0:T(8,128)(2,1)S(1)}, u32[]{:S(2)}, u32[]{:S(2)}) collective-permute-start(bf16[128,640]{1,0:T(8,128)(2,1)S(1)} %collective-permute-done.7.refs_8_.refs_4_), channel_id=1, source_target_pairs={{0,4},{1,5},{2,6},{3,7},{4,0},{5,1},{6,2},{7,3},{8,12},{9,13},{10,... | collective-permute-start | bytes 491528 | tf_op jit(solution)/shard_map/ppermute | solution.py:774
  28.6 15.4 %collective-permute-start.18 = (bf16[256,512]{1,0:T(8,128)(2,1)S(1)}, bf16[256,512]{1,0:T(8,128)(2,1)S(1)}, u32[]{:S(2)}, u32[]{:S(2)}) collective-permute-start(bf16[256,512]{1,0:T(8,128)(2,1)S(1)} %get-tuple-element.128.refs_0_.refs_4_.refs_8_), channel_id=1, source_target_pairs={{0,8},{1,9},{2,10},{3,11},{4,12},{5,13},{6,14},{7,15},{8,0},{9,1},... | collective-permute-start | bytes 786440 | tf_op jit(solution)/shard_map/ppermute | solution.py:774
  32.0 14.2 %collective-permute-start.17 = (bf16[256,512]{1,0:T(8,128)(2,1)S(1)}, bf16[256,512]{1,0:T(8,128)(2,1)S(1)}, u32[]{:S(2)}, u32[]{:S(2)}) collective-permute-start(bf16[256,512]{1,0:T(8,128)(2,1)S(1)} %get-tuple-element.128.refs_0_.refs_4_.refs_8_), channel_id=1, source_target_pairs={{0,16},{1,17},{2,18},{3,19},{4,20},{5,21},{6,22},{7,23},{8,24},{9,... | collective-permute-start | bytes 786440 | tf_op jit(solution)/shard_map/ppermute | solution.py:774
  38.5 5.5 %collective-permute-start.9 = (bf16[128,640]{1,0:T(8,128)(2,1)S(1)}, bf16[128,640]{1,0:T(8,128)(2,1)S(1)}, u32[]{:S(2)}, u32[]{:S(2)}) collective-permute-start(bf16[128,640]{1,0:T(8,128)(2,1)S(1)} %collective-permute-done.8.refs_6_.refs_2_), channel_id=1, source_target_pairs={{0,4},{1,5},{2,6},{3,7},{4,0},{5,1},{6,2},{7,3},{8,12},{9,13},{10,... | collective-permute-start | bytes 491528 | tf_op jit(solution)/shard_map/ppermute | solution.py:774
  40.0 8.4 %collective-permute-start.12 = (bf16[128,640]{1,0:T(8,128)(2,1)S(1)}, bf16[128,640]{1,0:T(8,128)(2,1)S(1)}, u32[]{:S(2)}, u32[]{:S(2)}) collective-permute-start(bf16[128,640]{1,0:T(8,128)(2,1)S(1)} %collective-permute-done.10.refs_9_.refs_5_), channel_id=1, source_target_pairs={{0,8},{1,9},{2,10},{3,11},{4,12},{5,13},{6,14},{7,15},{8,0},{9,1},... | collective-permute-start | bytes 491528 | tf_op jit(solution)/shard_map/ppermute | solution.py:774
  44.0 5.9 %copy-start.4 = (bf16[128,640]{1,0:T(8,128)(2,1)}, bf16[128,640]{1,0:T(8,128)(2,1)S(1)}, u32[]{:S(2)}) copy-start(bf16[128,640]{1,0:T(8,128)(2,1)S(1)} %collective-permute-done.9.refs_7_.refs_3_) | copy-start | bytes 491524
  46.2 6.4 %collective-permute-start.21 = (bf16[256,512]{1,0:T(8,128)(2,1)S(1)}, bf16[256,512]{1,0:T(8,128)(2,1)S(1)}, u32[]{:S(2)}, u32[]{:S(2)}) collective-permute-start(bf16[256,512]{1,0:T(8,128)(2,1)S(1)} %collective-permute-done.17.refs_4_.refs_8_.refs_12_), channel_id=1, source_target_pairs={{0,8},{1,9},{2,10},{3,11},{4,12},{5,13},{6,14},{7,15},{8,0},{9,1},... | collective-permute-start | bytes 786440 | tf_op jit(solution)/shard_map/ppermute | solution.py:774
  46.9 7.2 %collective-permute-start.20 = (bf16[256,512]{1,0:T(8,128)(2,1)S(1)}, bf16[256,512]{1,0:T(8,128)(2,1)S(1)}, u32[]{:S(2)}, u32[]{:S(2)}) collective-permute-start(bf16[256,512]{1,0:T(8,128)(2,1)S(1)} %collective-permute-done.17.refs_4_.refs_8_.refs_12_), channel_id=1, source_target_pairs={{0,4},{1,5},{2,6},{3,7},{4,0},{5,1},{6,2},{7,3},{8,12},{9,13},{10,... | collective-permute-start | bytes 786440 | tf_op jit(solution)/shard_map/ppermute | solution.py:774
  48.4 1.5 %copy-start.6 = (bf16[128,640]{1,0:T(8,128)(2,1)}, bf16[128,640]{1,0:T(8,128)(2,1)S(1)}, u32[]{:S(2)}) copy-start(bf16[128,640]{1,0:T(8,128)(2,1)S(1)} %collective-permute-done.12.refs_11_.refs_7_) | copy-start | bytes 491524
  50.0 11.4 %copy-start = (bf16[512,1024]{1,0:T(8,128)(2,1)}, bf16[512,1024]{1,0:T(8,128)(2,1)S(1)}, u32[]{:S(2)}) copy-start(bf16[512,1024]{1,0:T(8,128)(2,1)S(1)} %get-tuple-element.119.refs_8_.refs_16_.norm_ref) | copy-start | bytes 3145732
  50.0 5.1 %collective-permute-start.15 = (bf16[256,128]{1,0:T(8,128)(2,1)S(1)}, bf16[256,128]{1,0:T(8,128)(2,1)S(1)}, u32[]{:S(2)}, u32[]{:S(2)}) collective-permute-start(bf16[256,128]{1,0:T(8,128)(2,1)S(1)} %get-tuple-element.121), channel_id=1, source_target_pairs={{0,3},{1,2},{2,1},{3,0},{4,7},{5,6},{6,5},{7,4},{8,11},{9,10},{10,... | collective-permute-start | bytes 196616 | tf_op jit(solution)/shard_map/ppermute | solution.py:774
  50.0 5.1 %collective-permute-start.14 = (bf16[256,128]{1,0:T(8,128)(2,1)S(1)}, bf16[256,128]{1,0:T(8,128)(2,1)S(1)}, u32[]{:S(2)}, u32[]{:S(2)}) collective-permute-start(bf16[256,128]{1,0:T(8,128)(2,1)S(1)} %get-tuple-element.121), channel_id=1, source_target_pairs={{0,2},{1,3},{2,0},{3,1},{4,6},{5,7},{6,4},{7,5},{8,10},{9,11},{10,... | collective-permute-start | bytes 196616 | tf_op jit(solution)/shard_map/ppermute | solution.py:774
  51.2 4.0 %collective-permute-start.13 = (bf16[256,128]{1,0:T(8,128)(2,1)S(1)}, bf16[256,128]{1,0:T(8,128)(2,1)S(1)}, u32[]{:S(2)}, u32[]{:S(2)}) collective-permute-start(bf16[256,128]{1,0:T(8,128)(2,1)S(1)} %get-tuple-element.121), channel_id=1, source_target_pairs={{0,1},{1,0},{2,3},{3,2},{4,5},{5,4},{6,7},{7,6},{8,9},{9,8},{10,11... | collective-permute-start | bytes 196616 | tf_op jit(solution)/shard_map/ppermute | solution.py:774
  52.6 7.5 %collective-permute-start.19 = (bf16[256,512]{1,0:T(8,128)(2,1)S(1)}, bf16[256,512]{1,0:T(8,128)(2,1)S(1)}, u32[]{:S(2)}, u32[]{:S(2)}) collective-permute-start(bf16[256,512]{1,0:T(8,128)(2,1)S(1)} %collective-permute-done.18.refs_2_.refs_6_.refs_10_), channel_id=1, source_target_pairs={{0,4},{1,5},{2,6},{3,7},{4,0},{5,1},{6,2},{7,3},{8,12},{9,13},{10,... | collective-permute-start | bytes 786440 | tf_op jit(solution)/shard_map/ppermute | solution.py:774
  54.1 6.4 %collective-permute-start.22 = (bf16[256,512]{1,0:T(8,128)(2,1)S(1)}, bf16[256,512]{1,0:T(8,128)(2,1)S(1)}, u32[]{:S(2)}, u32[]{:S(2)}) collective-permute-start(bf16[256,512]{1,0:T(8,128)(2,1)S(1)} %collective-permute-done.20.refs_5_.refs_9_.refs_13_), channel_id=1, source_target_pairs={{0,8},{1,9},{2,10},{3,11},{4,12},{5,13},{6,14},{7,15},{8,0},{9,1},... | collective-permute-start | bytes 786440 | tf_op jit(solution)/shard_map/ppermute | solution.py:774
  61.3 1.2 copy-start.2
  61.3 1.3 copy-start.3
  62.6 3.3 %collective-permute-start.25 = (f32[8,512]{1,0:T(8,128)S(1)}, f32[8,512]{1,0:T(8,128)S(1)}, u32[]{:S(2)}, u32[]{:S(2)}) collective-permute-start(f32[8,512]{1,0:T(8,128)S(1)} %get-tuple-element.135.refs_0_), channel_id=1, source_target_pairs={{0,3},{1,2},{2,1},{3,0},{4,7},{5,6},{6,5},{7,4},{8,11},{9,10},{10,... | collective-permute-start | bytes 49160 | tf_op jit(solution)/shard_map/ppermute | solution.py:774
  62.9 3.9 %collective-permute-start.24 = (f32[8,512]{1,0:T(8,128)S(1)}, f32[8,512]{1,0:T(8,128)S(1)}, u32[]{:S(2)}, u32[]{:S(2)}) collective-permute-start(f32[8,512]{1,0:T(8,128)S(1)} %get-tuple-element.135.refs_0_), channel_id=1, source_target_pairs={{0,2},{1,3},{2,0},{3,1},{4,6},{5,7},{6,4},{7,5},{8,10},{9,11},{10,... | collective-permute-start | bytes 49160 | tf_op jit(solution)/shard_map/ppermute | solution.py:774
  64.0 2.8 %collective-permute-start.23 = (f32[8,512]{1,0:T(8,128)S(1)}, f32[8,512]{1,0:T(8,128)S(1)}, u32[]{:S(2)}, u32[]{:S(2)}) collective-permute-start(f32[8,512]{1,0:T(8,128)S(1)} %get-tuple-element.135.refs_0_), channel_id=1, source_target_pairs={{0,1},{1,0},{2,3},{3,2},{4,5},{5,4},{6,7},{7,6},{8,9},{9,8},{10,11... | collective-permute-start | bytes 49160 | tf_op jit(solution)/shard_map/ppermute | solution.py:774
  71.0 13.9 %collective-permute-start.30 = (bf16[512,512]{1,0:T(8,128)(2,1)S(1)}, bf16[512,512]{1,0:T(8,128)(2,1)S(1)}, u32[]{:S(2)}, u32[]{:S(2)}) collective-permute-start(bf16[512,512]{1,0:T(8,128)(2,1)S(1)} %get-tuple-element.151), channel_id=1, source_target_pairs={{0,8},{1,9},{2,10},{3,11},{4,12},{5,13},{6,14},{7,15},{8,0},{9,1},... | collective-permute-start | bytes 1572872 | tf_op jit(solution)/shard_map/ppermute | solution.py:774
  72.2 13.1 %collective-permute-start.31 = (bf16[512,512]{1,0:T(8,128)(2,1)S(1)}, bf16[512,512]{1,0:T(8,128)(2,1)S(1)}, u32[]{:S(2)}, u32[]{:S(2)}) collective-permute-start(bf16[512,512]{1,0:T(8,128)(2,1)S(1)} %get-tuple-element.152), channel_id=1, source_target_pairs={{0,4},{1,5},{2,6},{3,7},{4,0},{5,1},{6,2},{7,3},{8,12},{9,13},{10,... | collective-permute-start | bytes 1572872 | tf_op jit(solution)/shard_map/ppermute | solution.py:774
  74.1 13.2 %collective-permute-start.29 = (bf16[256,1024]{1,0:T(8,128)(2,1)S(1)}, bf16[256,1024]{1,0:T(8,128)(2,1)S(1)}, u32[]{:S(2)}, u32[]{:S(2)}) collective-permute-start(bf16[256,1024]{1,0:T(8,128)(2,1)S(1)} %get-tuple-element.148), channel_id=1, source_target_pairs={{0,1},{1,0},{2,3},{3,2},{4,5},{5,4},{6,7},{7,6},{8,9},{9,8},{10,11... | collective-permute-start | bytes 1572872 | tf_op jit(solution)/shard_map/ppermute | solution.py:774
  81.3 6.1 %collective-permute-start.26 = (bf16[256,128]{1,0:T(8,128)(2,1)S(1)}, bf16[256,128]{1,0:T(8,128)(2,1)S(1)}, u32[]{:S(2)}, u32[]{:S(2)}) collective-permute-start(bf16[256,128]{1,0:T(8,128)(2,1)S(1)} %get-tuple-element.141), channel_id=1, source_target_pairs={{0,1},{1,0},{2,3},{3,2},{4,5},{5,4},{6,7},{7,6},{8,9},{9,8},{10,11... | collective-permute-start | bytes 196616 | tf_op jit(solution)/shard_map/ppermute | solution.py:774
  81.9 5.5 %collective-permute-start.27 = (bf16[256,128]{1,0:T(8,128)(2,1)S(1)}, bf16[256,128]{1,0:T(8,128)(2,1)S(1)}, u32[]{:S(2)}, u32[]{:S(2)}) collective-permute-start(bf16[256,128]{1,0:T(8,128)(2,1)S(1)} %get-tuple-element.142), channel_id=1, source_target_pairs={{0,2},{1,3},{2,0},{3,1},{4,6},{5,7},{6,4},{7,5},{8,10},{9,11},{10,... | collective-permute-start | bytes 196616 | tf_op jit(solution)/shard_map/ppermute | solution.py:774
  84.9 3.8 %collective-permute-start.28 = (bf16[256,128]{1,0:T(8,128)(2,1)S(1)}, bf16[256,128]{1,0:T(8,128)(2,1)S(1)}, u32[]{:S(2)}, u32[]{:S(2)}) collective-permute-start(bf16[256,128]{1,0:T(8,128)(2,1)S(1)} %get-tuple-element.143), channel_id=1, source_target_pairs={{0,3},{1,2},{2,1},{3,0},{4,7},{5,6},{6,5},{7,4},{8,11},{9,10},{10,... | collective-permute-start | bytes 196616 | tf_op jit(solution)/shard_map/ppermute | solution.py:774
  85.4 3.3 %copy-start.1 = (bf16[512,1024]{1,0:T(8,128)(2,1)S(1)}, bf16[512,1024]{1,0:T(8,128)(2,1)}, u32[]{:S(2)}) copy-start(bf16[512,1024]{1,0:T(8,128)(2,1)} %copy-done) | copy-start | bytes 3145732
  85.4 3.3 %copy-start.5 = (bf16[128,640]{1,0:T(8,128)(2,1)S(1)}, bf16[128,640]{1,0:T(8,128)(2,1)}, u32[]{:S(2)}) copy-start(bf16[128,640]{1,0:T(8,128)(2,1)} %copy-done.4) | copy-start | bytes 491524
  85.4 3.3 %copy-start.7 = (bf16[128,640]{1,0:T(8,128)(2,1)S(1)}, bf16[128,640]{1,0:T(8,128)(2,1)}, u32[]{:S(2)}) copy-start(bf16[128,640]{1,0:T(8,128)(2,1)} %copy-done.6) | copy-start | bytes 491524
  85.4 10.3 %collective-permute-start.38 = (bf16[256,512]{1,0:T(8,128)(2,1)S(1)}, bf16[256,512]{1,0:T(8,128)(2,1)S(1)}, u32[]{:S(2)}, u32[]{:S(2)}) collective-permute-start(bf16[256,512]{1,0:T(8,128)(2,1)S(1)} %side.2), channel_id=1, source_target_pairs={{0,4},{1,5},{2,6},{3,7},{4,0},{5,1},{6,2},{7,3},{8,12},{9,13},{10,... | collective-permute-start | bytes 786440 | tf_op jit(solution)/shard_map/ppermute | solution.py:774
  92.8 16.4 %collective-permute-start.37 = (bf16[256,1024]{1,0:T(8,128)(2,1)S(1)}, bf16[256,1024]{1,0:T(8,128)(2,1)S(1)}, u32[]{:S(2)}, u32[]{:S(2)}) collective-permute-start(bf16[256,1024]{1,0:T(8,128)(2,1)S(1)} %get-tuple-element.174), channel_id=1, source_target_pairs={{0,1},{1,0},{2,3},{3,2},{4,5},{5,4},{6,7},{7,6},{8,9},{9,8},{10,11... | collective-permute-start | bytes 1572872 | tf_op jit(solution)/shard_map/ppermute | solution.py:774
  92.9 11.0 %collective-permute-start.34 = (bf16[272,640]{1,0:T(8,128)(2,1)S(1)}, bf16[272,640]{1,0:T(8,128)(2,1)S(1)}, u32[]{:S(2)}, u32[]{:S(2)}) collective-permute-start(bf16[272,640]{1,0:T(8,128)(2,1)S(1)} %get-tuple-element.164), channel_id=1, source_target_pairs={{0,4},{1,5},{2,6},{3,7},{4,0},{5,1},{6,2},{7,3},{8,12},{9,13},{10,... | collective-permute-start | bytes 1044488 | tf_op jit(solution)/shard_map/ppermute | solution.py:774
  94.4 14.8 %collective-permute-start.40 = (bf16[256,512]{1,0:T(8,128)(2,1)S(1)}, bf16[256,512]{1,0:T(8,128)(2,1)S(1)}, u32[]{:S(2)}, u32[]{:S(2)}) collective-permute-start(bf16[256,512]{1,0:T(8,128)(2,1)S(1)} %near.2), channel_id=1, source_target_pairs={{0,8},{1,9},{2,10},{3,11},{4,12},{5,13},{6,14},{7,15},{8,0},{9,1},... | collective-permute-start | bytes 786440 | tf_op jit(solution)/shard_map/ppermute | solution.py:774
  95.8 13.4 %collective-permute-start.39 = (bf16[256,512]{1,0:T(8,128)(2,1)S(1)}, bf16[256,512]{1,0:T(8,128)(2,1)S(1)}, u32[]{:S(2)}, u32[]{:S(2)}) collective-permute-start(bf16[256,512]{1,0:T(8,128)(2,1)S(1)} %far.3), channel_id=1, source_target_pairs={{0,16},{1,17},{2,18},{3,19},{4,20},{5,21},{6,22},{7,23},{8,24},{9,... | collective-permute-start | bytes 786440 | tf_op jit(solution)/shard_map/ppermute | solution.py:774
  98.5 12.0 %collective-permute-start.32 = (bf16[256,640]{1,0:T(8,128)(2,1)S(1)}, bf16[256,640]{1,0:T(8,128)(2,1)S(1)}, u32[]{:S(2)}, u32[]{:S(2)}) collective-permute-start(bf16[256,640]{1,0:T(8,128)(2,1)S(1)} %get-tuple-element.160), channel_id=1, source_target_pairs={{0,4},{1,5},{2,6},{3,7},{4,0},{5,1},{6,2},{7,3},{8,12},{9,13},{10,... | collective-permute-start | bytes 983048 | tf_op jit(solution)/shard_map/ppermute | solution.py:774
  103.9 8.4 %collective-permute-start.35 = (bf16[144,640]{1,0:T(8,128)(2,1)S(1)}, bf16[144,640]{1,0:T(8,128)(2,1)S(1)}, u32[]{:S(2)}, u32[]{:S(2)}) collective-permute-start(bf16[144,640]{1,0:T(8,128)(2,1)S(1)} %get-tuple-element.166), channel_id=1, source_target_pairs={{0,8},{1,9},{2,10},{3,11},{4,12},{5,13},{6,14},{7,15},{8,0},{9,1},... | collective-permute-start | bytes 552968 | tf_op jit(solution)/shard_map/ppermute | solution.py:774
  109.3 14.8 %collective-permute-start.41 = (bf16[128,1024]{1,0:T(8,128)(2,1)S(1)}, bf16[128,1024]{1,0:T(8,128)(2,1)S(1)}, u32[]{:S(2)}, u32[]{:S(2)}) collective-permute-start(bf16[128,1024]{1,0:T(8,128)(2,1)S(1)} %get-tuple-element.178), channel_id=1, source_target_pairs={{0,2},{1,3},{2,0},{3,1},{4,6},{5,7},{6,4},{7,5},{8,10},{9,11},{10,... | collective-permute-start | bytes 786440 | tf_op jit(solution)/shard_map/ppermute | solution.py:774
  112.4 11.7 %collective-permute-start.36 = (bf16[144,640]{1,0:T(8,128)(2,1)S(1)}, bf16[144,640]{1,0:T(8,128)(2,1)S(1)}, u32[]{:S(2)}, u32[]{:S(2)}) collective-permute-start(bf16[144,640]{1,0:T(8,128)(2,1)S(1)} %get-tuple-element.169), channel_id=1, source_target_pairs={{0,16},{1,17},{2,18},{3,19},{4,20},{5,21},{6,22},{7,23},{8,24},{9,... | collective-permute-start | bytes 552968 | tf_op jit(solution)/shard_map/ppermute | solution.py:774
  116.0 9.1 %collective-permute-start.33 = (bf16[128,640]{1,0:T(8,128)(2,1)S(1)}, bf16[128,640]{1,0:T(8,128)(2,1)S(1)}, u32[]{:S(2)}, u32[]{:S(2)}) collective-permute-start(bf16[128,640]{1,0:T(8,128)(2,1)S(1)} %near.3), channel_id=1, source_target_pairs={{0,8},{1,9},{2,10},{3,11},{4,12},{5,13},{6,14},{7,15},{8,0},{9,1},... | collective-permute-start | bytes 491528 | tf_op jit(solution)/shard_map/ppermute | solution.py:774
  117.0 10.9 %collective-permute-start.42 = (bf16[128,1024]{1,0:T(8,128)(2,1)S(1)}, bf16[128,1024]{1,0:T(8,128)(2,1)S(1)}, u32[]{:S(2)}, u32[]{:S(2)}) collective-permute-start(bf16[128,1024]{1,0:T(8,128)(2,1)S(1)} %get-tuple-element.183), channel_id=1, source_target_pairs={{0,2},{1,3},{2,0},{3,1},{4,6},{5,7},{6,4},{7,5},{8,10},{9,11},{10,... | collective-permute-start | bytes 786440 | tf_op jit(solution)/shard_map/ppermute | solution.py:774
  126.1 3.7 %collective-permute-start.43 = (bf16[48,1152]{1,0:T(8,128)(2,1)S(1)}, bf16[48,1152]{1,0:T(8,128)(2,1)S(1)}, u32[]{:S(2)}, u32[]{:S(2)}) collective-permute-start(bf16[48,1152]{1,0:T(8,128)(2,1)S(1)} %get-tuple-element.189), channel_id=1, source_target_pairs={{0,1},{1,0},{2,3},{3,2},{4,5},{5,4},{6,7},{7,6},{8,9},{9,8},{10,11... | collective-permute-start | bytes 331784 | tf_op jit(solution)/shard_map/ppermute | solution.py:774
  126.1 5.9 %collective-permute-start.44 = (bf16[48,1152]{1,0:T(8,128)(2,1)S(1)}, bf16[48,1152]{1,0:T(8,128)(2,1)S(1)}, u32[]{:S(2)}, u32[]{:S(2)}) collective-permute-start(bf16[48,1152]{1,0:T(8,128)(2,1)S(1)} %get-tuple-element.190), channel_id=1, source_target_pairs={{0,2},{1,3},{2,0},{3,1},{4,6},{5,7},{6,4},{7,5},{8,10},{9,11},{10,... | collective-permute-start | bytes 331784 | tf_op jit(solution)/shard_map/ppermute | solution.py:774
  127.0 6.5 %collective-permute-start.45 = (bf16[48,1152]{1,0:T(8,128)(2,1)S(1)}, bf16[48,1152]{1,0:T(8,128)(2,1)S(1)}, u32[]{:S(2)}, u32[]{:S(2)}) collective-permute-start(bf16[48,1152]{1,0:T(8,128)(2,1)S(1)} %get-tuple-element.191), channel_id=1, source_target_pairs={{0,3},{1,2},{2,1},{3,0},{4,7},{5,6},{6,5},{7,4},{8,11},{9,10},{10,... | collective-permute-start | bytes 331784 | tf_op jit(solution)/shard_map/ppermute | solution.py:774
